TPU v7x, 32 devices: a whole 2x2x4 slice. The times are simulated.
32 devices in a mesh: dp: 8 (over z, core), tensor: 4 (over y, x).
Axes of the slice: x: 2, y: 2, z: 4, core: 2. Of those that a mesh axis runs over, the one named last changes fastest.
Arguments:
- tokens: bfloat16 [6144, 3072], P('dp'), may hold values from -6 to 6
- assign: int32 [6144, 2], P('dp'), may hold values from 0 to 7, as said below
- combine: float32 [6144, 2], P('dp'), may hold values from 0.1 to 1
- cotangent: bfloat16 [6144, 3072], P('dp'), may hold values from -6 to 6
- w_gate: bfloat16 [3072, 8192], P('dp', 'tensor'), may hold values from -0.109375 to 0.109375
- w_up: bfloat16 [3072, 8192], P('dp', 'tensor'), may hold values from -0.109375 to 0.109375
- w_down_t: bfloat16 [3072, 8192], P('dp', 'tensor'), may hold values from -0.0625 to 0.0625
Outputs:
- mixed: bfloat16 [6144, 3072], P('dp', 'tensor')
- input_grad: bfloat16 [6144, 3072], P('dp', 'tensor')
- weight_grad: float32 [6144], P('dp')
- gate_weight_grad: bfloat16 [3072, 8192], P('dp', 'tensor')
- up_weight_grad: bfloat16 [3072, 8192], P('dp', 'tensor')
- down_weight_grad: bfloat16 [3072, 8192], P('dp', 'tensor')
Inputs may be any that keep to these rules, and one draw needn't show every extreme that they name: `assign`: each token names 2 different experts. Of the 768 tokens of one index of dp at most 384 name expert 0, and in every draw the tokens of some index of dp name it exactly 384 times.
All inputs are finite; a program needn't handle non-finite values.
Results may differ from a plain program's by a relative error of at most 0.028.
Values may be sent and summed in bfloat16 or wider, within the bound.
No kernel may reach another device: no remote copies, remote signals or barrier semaphores. Data moves between devices by JAX's collectives and lax.ppermute only.
A program may use at most 192 MiB of HBM per device.

v0:
```python
import jax
import jax.numpy as jnp
from jax import lax
from jax.sharding import PartitionSpec as P


def select_rows(assign_block, combine_block, row_limit):
    token_total = assign_block.shape[0]
    expert_hit = assign_block == 0
    routed = jnp.any(expert_hit, axis=1)
    weight = jnp.sum(
        jnp.where(expert_hit, combine_block, jnp.zeros((), combine_block.dtype)), axis=1
    )
    place = jnp.cumsum(routed.astype(jnp.int32)) - 1
    match = routed[None, :] & (place[None, :] == jnp.arange(row_limit, dtype=jnp.int32)[:, None])
    positions = jnp.arange(token_total, dtype=jnp.int32)
    row_index = jnp.sum(jnp.where(match, positions[None, :], 0), axis=1)
    valid = jnp.any(match, axis=1)
    row_weight = jnp.where(valid, weight[row_index], jnp.zeros((), weight.dtype))
    return (row_index, valid, row_weight)


def place_rows(rows, valid, row_index, token_total):
    shape = (token_total,) + rows.shape[1:]
    mask = valid.reshape(valid.shape + (1,) * (rows.ndim - 1))
    values = jnp.where(mask, rows.astype(jnp.float32), jnp.zeros((), jnp.float32))
    return jnp.zeros(shape, jnp.float32).at[row_index].add(values)


def contract_last(left, right):
    return lax.dot_general(
        left, right, (((1,), (1,)), ((), ())), preferred_element_type=jnp.float32
    )


def contract_first(left, right):
    return lax.dot_general(
        left, right, (((0,), (0,)), ((), ())), preferred_element_type=jnp.float32
    )


def local(tokens, assign, combine, cotangent, w_gate, w_up, w_down_t):
    token_total = tokens.shape[0]
    row_index, valid, row_weight = select_rows(assign, combine, token_total // 2)
    keep = valid[:, None]
    rows_in = jnp.where(keep, tokens[row_index], jnp.zeros((), tokens.dtype))
    rows_grad = jnp.where(keep, cotangent[row_index], jnp.zeros((), cotangent.dtype))
    gate_full, up_full = (
        lax.all_gather(w_gate, "dp", axis=0, tiled=True),
        lax.all_gather(w_up, "dp", axis=0, tiled=True),
    )
    gate_pre = jnp.dot(rows_in, gate_full, preferred_element_type=jnp.float32)
    up_pre = jnp.dot(rows_in, up_full, preferred_element_type=jnp.float32)
    sigmoid_gate = jax.nn.sigmoid(gate_pre)
    hidden = (gate_pre * sigmoid_gate * up_pre).astype(jnp.bfloat16)
    down_full = lax.all_gather(w_down_t, "dp", axis=0, tiled=True)
    partial_value = contract_last(hidden, down_full)
    width_part = tokens.shape[1] // lax.axis_size("tensor")
    column_start = lax.axis_index("tensor") * width_part
    out_cols = lax.psum_scatter(
        partial_value.astype(jnp.bfloat16), "tensor", scatter_dimension=1, tiled=True
    ).astype(jnp.float32)
    grad_cols = lax.dynamic_slice_in_dim(rows_grad, column_start, width_part, 1)
    weight_rows = lax.psum(jnp.sum(grad_cols.astype(jnp.float32) * out_cols, axis=1), "tensor")
    mixed_rows = (row_weight[:, None] * out_cols).astype(jnp.bfloat16)
    mixed = place_rows(mixed_rows, valid, row_index, token_total).astype(jnp.bfloat16)
    weight_grad = place_rows(weight_rows, valid, row_index, token_total)
    out_grad = (row_weight[:, None] * rows_grad.astype(jnp.float32)).astype(jnp.bfloat16)
    hidden_grad = jnp.dot(out_grad, down_full, preferred_element_type=jnp.float32)
    gate_grad = (
        hidden_grad * up_pre * sigmoid_gate * (1.0 + gate_pre * (1.0 - sigmoid_gate))
    ).astype(jnp.bfloat16)
    up_grad = (hidden_grad * gate_pre * sigmoid_gate).astype(jnp.bfloat16)
    input_part = contract_last(gate_grad, gate_full) + contract_last(up_grad, up_full)
    input_cols = lax.psum_scatter(
        input_part.astype(jnp.bfloat16), "tensor", scatter_dimension=1, tiled=True
    )
    input_grad = place_rows(input_cols, valid, row_index, token_total).astype(jnp.bfloat16)
    both_grads = jnp.concatenate([gate_grad, up_grad], axis=1)
    grads = lax.psum_scatter(
        jnp.concatenate(
            [contract_first(rows_in, both_grads), contract_first(out_grad, hidden)], axis=1
        ).astype(jnp.bfloat16),
        "dp",
        scatter_dimension=0,
        tiled=True,
    ).astype(jnp.float32)
    hidden_part = w_gate.shape[1]
    grads = grads.astype(jnp.bfloat16)
    return (
        mixed,
        input_grad,
        weight_grad,
        grads[:, :hidden_part],
        grads[:, hidden_part : 2 * hidden_part],
        grads[:, 2 * hidden_part :],
    )


def solution(mesh):
    return jax.shard_map(
        local,
        mesh=mesh,
        in_specs=(
            P("dp", None),
            P("dp", None),
            P("dp", None),
            P("dp", None),
            P("dp", "tensor"),
            P("dp", "tensor"),
            P("dp", "tensor"),
        ),
        out_specs=(
            P("dp", "tensor"),
            P("dp", "tensor"),
            P("dp"),
            P("dp", "tensor"),
            P("dp", "tensor"),
            P("dp", "tensor"),
        ),
        check_vma=False,
    )
```

profile of v0, /device:TPU:0, one launch (start us, length us, event | category | flops | bytes accessed | tf_op | source)
XLA Modules:
  0.0 840.8 jit_solution(11356976767499175872)
XLA Ops:
  7.2 0.0 copy-start.1
  7.2 0.0 copy-start.2
  7.2 0.0 all-gather.6.cloned.1.call-start
  7.2 0.7 all-gather.6.cloned.1.call-update
  7.9 0.0 all-gather.4.cloned.1.call-start
  8.0 0.7 all-gather.4.cloned.1.call-update
  8.7 0.0 all-gather.8.cloned.1.call-start
  8.7 0.7 all-gather.8.cloned.1.call-update
  9.4 0.0 reduce-scatter.4.cloned.1.call-start
  9.5 0.3 reduce-window.9
  9.8 0.1 slice.16
  9.9 0.1 slice_reduce_fusion
  10.0 0.1 add_bitcast_fusion
  10.1 0.3 select_reduce_fusion
  10.5 1.9 gather_fusion
  12.4 9.7 %gather_fusion.1 = bf16[384,3072]{1,0:T(8,128)(2,1)} fusion(bf16[768,3072]{1,0:T(8,128)(2,1)} %param.7, s32[1024]{0:T(1024)S(1)} %pad_clamp_fusion), kind=kCustom, calls=%fused_computation.1 | custom fusion | bytes 4720128 | tf_op jit(solution)/shard_map/gather | solution.py:46
  22.1 9.9 %gather_fusion.2 = bf16[384,3072]{1,0:T(8,128)(2,1)S(1)} fusion(bf16[768,3072]{1,0:T(8,128)(2,1)} %param.10, s32[1024]{0:T(1024)S(1)} %pad_clamp_fusion), kind=kCustom, calls=%fused_computation.2 | custom fusion | bytes 4720128 | tf_op jit(solution)/shard_map/gather | solution.py:47
  32.0 0.2 fusion.14
  32.3 1.6 broadcast_select_fusion
  33.9 95.3 %all-gather.6.cloned.1.call-done = bf16[3072,2048]{1,0:T(8,128)(2,1)} async-done(((bf16[384,2048]{1,0:T(8,128)(2,1)}), bf16[3072,2048]{1,0:T(8,128)(2,1)}) %all-gather.6.cloned.1.call-update) | async-done | bytes 12582928 | tf_op jit(solution)/shard_map/all_gather | solution.py:50
  129.1 11.5 %fusion.27 = f32[384,2048]{1,0:T(8,128)} fusion(bf16[3072,2048]{1,0:T(8,128)(2,1)} %all-gather.6.cloned.1.call-done, bf16[384,3072]{1,0:T(8,128)(2,1)} %gather_fusion.1, pred[384]{0:T(512)(128)(4,1)S(1)} %fusion.14), kind=kOutput, calls=%fused_computation.57 | convolution fusion | flops 4833017856 | bytes 18088320 | tf_op jit(solution)/shard_map/dot_general | solution.py:53
  140.6 105.1 %all-gather.4.cloned.1.call-done = bf16[3072,2048]{1,0:T(8,128)(2,1)} async-done(((bf16[384,2048]{1,0:T(8,128)(2,1)}), bf16[3072,2048]{1,0:T(8,128)(2,1)}) %all-gather.4.cloned.1.call-update) | async-done | bytes 12582928 | tf_op jit(solution)/shard_map/all_gather | solution.py:49
  245.8 11.5 %fusion.28 = f32[384,2048]{1,0:T(8,128)} fusion(bf16[3072,2048]{1,0:T(8,128)(2,1)} %all-gather.4.cloned.1.call-done, bf16[384,3072]{1,0:T(8,128)(2,1)} %gather_fusion.1, pred[384]{0:T(512)(128)(4,1)S(1)} %fusion.14), kind=kOutput, calls=%fused_computation.58 | convolution fusion | flops 4833017856 | bytes 18088320 | tf_op jit(solution)/shard_map/dot_general | solution.py:52
  257.2 105.2 %all-gather.8.cloned.1.call-done = bf16[3072,2048]{1,0:T(8,128)(2,1)} async-done(((bf16[384,2048]{1,0:T(8,128)(2,1)}), bf16[3072,2048]{1,0:T(8,128)(2,1)}) %all-gather.8.cloned.1.call-update) | async-done | bytes 12582928 | tf_op jit(solution)/shard_map/all_gather | solution.py:56
  362.4 14.0 %multiply_convert_fusion.1 = (bf16[384,2048]{1,0:T(8,128)(2,1)}, bf16[384,2048]{1,0:T(8,128)(2,1)}, bf16[384,2048]{1,0:T(8,128)(2,1)S(1)}) fusion(f32[384,2048]{1,0:T(8,128)} %fusion.28, f32[384,2048]{1,0:T(8,128)} %fusion.27, bf16[3072,2048]{1,0:T(8,128)(2,1)} %all-gather.8.cloned.1.call-done, bf16[384,3072]{1,0:T(8,128)(2,1)S(1)} %copy-done, ...), kind=kOutput, calls=%fused_computation.15 | convolution fusion | flops 4847960064 | bytes 25953792 | tf_op jit(solution)/shard_map/dot_general | solution.py:69
  376.4 1.1 copy-done.4
  377.6 6.4 convolution_convert_fusion.2
  384.0 0.0 reduce-scatter.4.cloned.1.call-update
  384.0 0.0 reduce-scatter.6.cloned.1.call-start
  384.0 0.0 copy-start.5
  384.0 8.6 %fusion.30 = f32[384,3072]{1,0:T(8,128)S(1)} fusion(bf16[384,2048]{1,0:T(8,128)(2,1)} %get-tuple-element.7, bf16[3072,2048]{1,0:T(8,128)(2,1)} %all-gather.4.cloned.1.call-done), kind=kOutput, calls=%fused_computation.60 | convolution fusion | flops 4831838208 | bytes 18874368 | tf_op jit(solution)/shard_map/dot_general | solution.py:31
  392.7 14.6 %add_convert_fusion = bf16[384,3072]{1,0:T(8,128)(2,1)} fusion(f32[384,3072]{1,0:T(8,128)S(1)} %fusion.30, bf16[384,2048]{1,0:T(8,128)(2,1)S(1)} %copy-done.5, bf16[3072,2048]{1,0:T(8,128)(2,1)} %all-gather.6.cloned.1.call-done), kind=kOutput, calls=%fused_computation.9 | convolution fusion | flops 4834197504 | bytes 21233664 | tf_op jit(solution)/shard_map/dot_general | solution.py:31
  407.3 0.0 reduce-scatter.6.cloned.1.call-update
  407.4 0.0 reduce-scatter.8.cloned.1.call-start
  407.4 11.4 %convolution_convert_fusion.1 = bf16[3072,2048]{1,0:T(8,128)(2,1)} fusion(bf16[384,2048]{1,0:T(8,128)(2,1)} %copy-done.4, bf16[384,3072]{1,0:T(8,128)(2,1)S(1)} %copy-done, f32[384]{0:T(512)S(1)} %broadcast_select_fusion.3), kind=kOutput, calls=%fused_computation.8 | convolution fusion | flops 4841668608 | bytes 16516608 | tf_op jit(solution)/shard_map/dot_general | solution.py:37
  418.8 20.6 %convolution_convert_fusion = bf16[3072,4096]{1,0:T(8,128)(2,1)} fusion(bf16[384,2048]{1,0:T(8,128)(2,1)} %get-tuple-element.6, bf16[384,2048]{1,0:T(8,128)(2,1)} %get-tuple-element.7, bf16[384,3072]{1,0:T(8,128)(2,1)} %gather_fusion.1, pred[384]{0:T(512)(128)(4,1)S(1)} %fusion.14), kind=kOutput, calls=%fused_computation.7 | convolution fusion | flops 9683730432 | bytes 30671232 | tf_op jit(solution)/shard_map/dot_general | solution.py:37
  439.4 25.9 %pad_maximum_fusion = bf16[3072,6144]{1,0:T(8,128)(2,1)} fusion(bf16[3072,2048]{1,0:T(8,128)(2,1)} %convolution_convert_fusion.1, bf16[3072,4096]{1,0:T(8,128)(2,1)} %convolution_convert_fusion), kind=kLoop, calls=%fused_computation.6 | loop fusion | flops 75497472 | bytes 75497472 | tf_op jit(solution)/shard_map/concatenate | solution.py:81
  465.3 0.0 reduce-scatter.8.cloned.1.call-update
  465.4 0.0 reduce-scatter.4.cloned.1.call-done
  465.4 1.3 fusion.4
  466.7 9.8 %psum.7 = f32[384]{0:T(512)S(1)} all-reduce(f32[384]{0:T(512)S(1)} %fusion.4), channel_id=1, replica_groups=mesh['dp'=8,'tensor'=4] {'tensor'}, use_global_device_ids=true, to_apply=%region_11.12 | all-reduce | flops 384 | bytes 3072 | tf_op jit(solution)/shard_map/psum | solution.py:64
  476.5 4.7 scatter_custom_fusion.2
  481.2 4.4 scatter_custom_fusion
  485.5 1.1 convert_element_type.59
  486.7 4.3 scatter_custom_fusion.1
  491.0 1.1 convert_element_type.66
  492.1 336.7 %reduce-scatter.8.cloned.1.call-done = bf16[384,6144]{1,0:T(8,128)(2,1)} async-done(((bf16[3072,6144]{1,0:T(8,128)(2,1)}), bf16[384,6144]{1,0:T(8,128)(2,1)}) %reduce-scatter.8.cloned.1.call-update) | async-done | bytes 4718608 | tf_op jit(solution)/shard_map/reduce_scatter | solution.py:80
  828.8 4.7 fusion.29
  (17 shorter events, 0.1 us)
Async XLA Ops:
  7.2 2.3 copy-start.1
  7.2 3.3 copy-start.2
  7.2 121.9 %all-gather.6.cloned.1.call-start = ((), (), s32[]{:S(2)}) async-start(), calls=%async_computation.4 | async-start | bytes 14155776 | tf_op jit(solution)/shard_map/all_gather | solution.py:50
  7.9 237.8 %all-gather.4.cloned.1.call-start = ((), (), s32[]{:S(2)}) async-start(), calls=%async_computation.3 | async-start | bytes 14155776 | tf_op jit(solution)/shard_map/all_gather | solution.py:49
  8.7 353.7 %all-gather.8.cloned.1.call-start = ((), (), s32[]{:S(2)}) async-start(), calls=%async_computation.5 | async-start | bytes 14155776 | tf_op jit(solution)/shard_map/all_gather | solution.py:56
  9.4 456.0 %reduce-scatter.4.cloned.1.call-start = ((), (), s32[]{:S(2)}) async-start(), calls=%async_computation.6 | async-start | bytes 2949120 | tf_op jit(solution)/shard_map/reduce_scatter | solution.py:60
  140.6 221.8 %copy-start = (bf16[384,3072]{1,0:T(8,128)(2,1)S(1)}, bf16[384,3072]{1,0:T(8,128)(2,1)}, u32[]{:S(2)}) copy-start(bf16[384,3072]{1,0:T(8,128)(2,1)} %broadcast_select_fusion) | copy-start | bytes 7077892
  362.4 15.2 %copy-start.3 = (bf16[3072,2048]{1,0:T(8,128)(2,1)S(1)}, bf16[3072,2048]{1,0:T(8,128)(2,1)}, u32[]{:S(2)}) copy-start(bf16[3072,2048]{1,0:T(8,128)(2,1)} %all-gather.8.cloned.1.call-done) | copy-start | bytes 37748740
  376.4 1.1 copy-start.4
  384.0 102.7 %reduce-scatter.6.cloned.1.call-start = ((), (), s32[]{:S(2)}) async-start(), calls=%async_computation.7 | async-start | bytes 2949120 | tf_op jit(solution)/shard_map/reduce_scatter | solution.py:75
  384.0 8.7 %copy-start.5 = (bf16[384,2048]{1,0:T(8,128)(2,1)S(1)}, bf16[384,2048]{1,0:T(8,128)(2,1)}, u32[]{:S(2)}) copy-start(bf16[384,2048]{1,0:T(8,128)(2,1)} %get-tuple-element.6) | copy-start | bytes 4718596
  407.4 421.4 %reduce-scatter.8.cloned.1.call-start = ((), (), s32[]{:S(2)}) async-start(), calls=%async_computation.8 | async-start | bytes 42467328 | tf_op jit(solution)/shard_map/reduce_scatter | solution.py:80
Sparse Core Ops, SparseCore 0:
  9.7 119.4 all-gather.5
  130.8 114.9 all-gather.3
  247.4 114.9 all-gather.7
  384.1 35.6 reduce-scatter.3
  422.7 37.3 reduce-scatter.5
  465.5 363.2 reduce-scatter.7
where the time goes:
time: 850 us; the launch traced here: 841 us
  waiting for transfers between devices  644 us (76%)
  matrix products  98.6 us (12%)
  other arithmetic  45.5 us (5%)
  local copies, waits for them, and re-layouts  27.6 us (3%)
  between operations  14.7 us (2%)
  blocking collectives  9.79 us (1%)
    reduce_scatter x1, waiting for transfers between devices, local(): lax.psum_scatter(jnp.concatenate([contract_first(rows_in, both_grads), co...  337 us
    all_gather x1, waiting for transfers between devices, local(): down_full = lax.all_gather(w_down_t, 'dp', axis=0, tiled=True)  105 us
    all_gather x1, waiting for transfers between devices, local(): lax.all_gather(w_gate, 'dp', axis=0, tiled=True)  105 us
    all_gather x1, waiting for transfers between devices, local(): lax.all_gather(w_up, 'dp', axis=0, tiled=True)  95.3 us
    dot_general x2, matrix products, contract_first(): lax.dot_general(left, right, (((0,), (0,)), ((), ())), preferred_element_...  32 us
    dot_general x3, matrix products, contract_last(): lax.dot_general(left, right, (((1,), (1,)), ((), ())), preferred_element_...  29.7 us
    concatenate x1, other arithmetic, local(): jnp.concatenate([contract_first(rows_in, both_grads), contract_first(out_...  25.9 us
  transfers between devices with their start and end apart: 6, of which 4 were waited for; matrix products, arithmetic and copies ran while one was open for 17% of the time, Pallas kernels for 0%

commit v1 on v0

v1 whole, which is shorter than its diff:
```python
import jax
import jax.numpy as jnp
from jax import lax
from jax.sharding import PartitionSpec as P

BF16 = jnp.bfloat16
F32 = jnp.float32


def dot(left, right, dims):
    return lax.dot_general(left, right, (dims, ((), ())), preferred_element_type=F32)


def mm(left, right):
    return dot(left, right, ((1,), (0,)))


def mm_last(left, right):
    return dot(left, right, ((1,), (1,)))


def mm_first(left, right):
    return dot(left, right, ((0,), (0,)))


def swap(value, axis, distance):
    size = lax.axis_size(axis)
    return lax.ppermute(value, axis, [(i, i ^ distance) for i in range(size)])


def select_rows(assign_block, combine_block, row_limit):
    expert_hit = assign_block == 0
    routed = jnp.any(expert_hit, axis=1)
    weight = jnp.sum(
        jnp.where(expert_hit, combine_block, jnp.zeros((), combine_block.dtype)), axis=1
    )
    place = jnp.cumsum(routed.astype(jnp.int32)) - 1
    match = routed[None, :] & (place[None, :] == jnp.arange(row_limit, dtype=jnp.int32)[:, None])
    row_weight = jnp.sum(jnp.where(match, weight[None, :], 0.0), axis=1)
    return (match, row_weight)


def pick(flag, first, second):
    return jnp.where(flag, first, second)


def halves(value, upper, axis):
    width = value.shape[axis] // 2
    start = upper * width
    mine = lax.dynamic_slice_in_dim(value, start, width, axis)
    other = lax.dynamic_slice_in_dim(value, width - start, width, axis)
    return mine, other


def join(mine, other, upper, axis):
    return pick(
        upper == 0,
        jnp.concatenate([mine, other], axis=axis),
        jnp.concatenate([other, mine], axis=axis),
    )


def gather_tensor(value):
    size = lax.axis_size("tensor")
    me = lax.axis_index("tensor")
    rows, width = value.shape
    full = jnp.zeros((rows, width * size), value.dtype)
    full = lax.dynamic_update_slice_in_dim(full, value, me * width, 1)
    for k in range(1, size):
        full = lax.dynamic_update_slice_in_dim(full, swap(value, "tensor", k), (me ^ k) * width, 1)
    return full


def scatter_tensor(value, bits):
    size = lax.axis_size("tensor")
    me = lax.axis_index("tensor")
    rows, depth = value.shape
    width = depth // size
    def part(k):
        return lax.dynamic_slice_in_dim(value, (me ^ k) * width, width, 1)

    parts = {k: part(k) for k in range(size)}
    for bit in bits:
        gone = [k for k in parts if k & bit]
        kept = [k for k in parts if not k & bit]
        sent = jnp.concatenate([parts[k].astype(BF16) for k in gone], axis=1)
        got = swap(sent, "tensor", bit)
        parts = {
            k: parts[k].astype(F32) + got[:, i * width : (i + 1) * width].astype(F32)
            for i, k in enumerate(kept)
        }
    return parts[0]


def local(tokens, assign, combine, cotangent, w_gate, w_up, w_down_t):
    token_total, depth = tokens.shape
    row_limit = token_total // 2
    n_dp = lax.axis_size("dp")
    n_tensor = lax.axis_size("tensor")
    half = n_dp // 2
    upper = lax.axis_index("dp") // half
    me_t = lax.axis_index("tensor")
    width = depth // n_tensor
    groups = [list(range(half)), list(range(half, n_dp))]
    bits = [1 << i for i in range(n_tensor.bit_length() - 1)]

    def gather_half(value):
        return lax.all_gather(value, "dp", axis=0, tiled=True, axis_index_groups=groups)

    def scatter_half(value):
        return lax.psum_scatter(
            value, "dp", scatter_dimension=0, tiled=True, axis_index_groups=groups
        )

    match, row_weight = select_rows(assign, combine, row_limit)
    hot = match.astype(BF16)
    rows_in = mm(hot, tokens).astype(BF16)
    rows_grad = mm(hot, cotangent).astype(BF16)
    out_grad = (row_weight[:, None] * rows_grad.astype(F32)).astype(BF16)

    def partner_rows(rows):
        mine = lax.dynamic_slice_in_dim(rows, me_t * width, width, 1)
        return gather_tensor(swap(mine, "dp", half))

    both_in = jnp.concatenate([rows_in, partner_rows(rows_in)], axis=0)
    both_out = jnp.concatenate([out_grad, partner_rows(out_grad)], axis=0)
    in_own, in_far = halves(both_in, upper, 1)
    out_own, out_far = halves(both_out, upper, 1)

    def panel(block):
        mine, other = halves(block, upper, 1)
        return gather_half(mine), gather_half(swap(other, "dp", half))

    gate_own, gate_far = panel(w_gate)
    up_own, up_far = panel(w_up)
    down_own, down_far = panel(w_down_t)

    gate_pre = mm(in_own, gate_own) + mm(in_far, gate_far)
    up_pre = mm(in_own, up_own) + mm(in_far, up_far)
    sigmoid_gate = jax.nn.sigmoid(gate_pre)
    hidden = (gate_pre * sigmoid_gate * up_pre).astype(BF16)

    def panel_grad(left_own, left_far, right):
        far = swap(scatter_half(mm_first(left_far, right).astype(BF16)), "dp", half)
        own = scatter_half(mm_first(left_own, right).astype(BF16))
        return join(own, far, upper, 1)

    down_grad = panel_grad(out_own, out_far, hidden)

    hidden_grad = mm(out_own, down_own) + mm(out_far, down_far)
    gate_grad = (
        hidden_grad * up_pre * sigmoid_gate * (1.0 + gate_pre * (1.0 - sigmoid_gate))
    ).astype(BF16)
    up_grad = (hidden_grad * gate_pre * sigmoid_gate).astype(BF16)

    gate_weight_grad = panel_grad(in_own, in_far, gate_grad)
    up_weight_grad = panel_grad(in_own, in_far, up_grad)

    def whole(own, far):
        return join(own.astype(BF16), far.astype(BF16), upper, 1)

    def reduce_rows(value):
        far = scatter_tensor(value[row_limit:], bits)
        got = swap(far.astype(BF16), "dp", half)
        return scatter_tensor(value[:row_limit], bits[::-1]) + got.astype(F32)

    expert_cols = reduce_rows(whole(mm_last(hidden, down_own), mm_last(hidden, down_far)))
    input_cols = reduce_rows(
        whole(
            mm_last(gate_grad, gate_own) + mm_last(up_grad, up_own),
            mm_last(gate_grad, gate_far) + mm_last(up_grad, up_far),
        )
    )

    grad_cols = lax.dynamic_slice_in_dim(rows_grad, me_t * width, width, 1)
    weight_rows = jnp.sum(grad_cols.astype(F32) * expert_cols, axis=1)
    for bit in bits:
        weight_rows = weight_rows + swap(weight_rows, "tensor", bit)
    weight_grad = jnp.sum(jnp.where(match, weight_rows[:, None], 0.0), axis=0)

    mixed = mm_first(hot, (row_weight[:, None] * expert_cols).astype(BF16)).astype(BF16)
    input_grad = mm_first(hot, input_cols.astype(BF16)).astype(BF16)
    return (mixed, input_grad, weight_grad, gate_weight_grad, up_weight_grad, down_grad)


def solution(mesh):
    return jax.shard_map(
        local,
        mesh=mesh,
        in_specs=(
            P("dp", None),
            P("dp", None),
            P("dp", None),
            P("dp", None),
            P("dp", "tensor"),
            P("dp", "tensor"),
            P("dp", "tensor"),
        ),
        out_specs=(
            P("dp", "tensor"),
            P("dp", "tensor"),
            P("dp"),
            P("dp", "tensor"),
            P("dp", "tensor"),
            P("dp", "tensor"),
        ),
        check_vma=False,
    )
```

time: 850 us -> 765 us (0.900)
  waiting for transfers between devices: 644 us -> 566 us
  starting transfers between devices: 0.24 us -> 32.9 us
  other arithmetic: 45.5 us -> 22.1 us
  local copies, waits for them, and re-layouts: 27.6 us -> 15 us
  matrix products: 98.6 us -> 110 us
  blocking collectives: 9.79 us -> 0 us
    ppermute x0 -> x26, waiting for transfers between devices: none -> 303 us  [swap(): return lax.ppermute(value, axis, [(i, i ^ distance) for i in range(size)])]
    all_gather x3 -> x6, waiting for transfers between devices: 306 us -> 91.3 us  [gather_half(): lax.all_gather(value, 'dp', axis=0, tiled=True, axis_index_groups=groups)]
    reduce_scatter x3 -> x6, waiting for transfers between devices: 337 us -> 170 us  [scatter_half(): lax.psum_scatter(value, 'dp', scatter_dimension=0, tiled=True, axis_index...]
    ppermute x0 -> x26, starting transfers between devices: none -> 32.1 us  [swap(): return lax.ppermute(value, axis, [(i, i ^ distance) for i in range(size)])]
    concatenate x1 -> x5, other arithmetic: 25.9 us -> 2.85 us  [the longest x1 2.52 us: local(): both_in = jnp.concatenate([rows_in, partner_rows(rows_in)], axis=0)]
    gather x3 -> x0, local copies, waits for them, and re-layouts: 21.5 us -> none  [the longest x1 9.95 us: local(): cotangent[row_index]]
    scatter-add x3 -> x0, other arithmetic: 13.4 us -> none  [place_rows(): return jnp.zeros(shape, jnp.float32).at[row_index].add(values)]
    select_n x4 -> x5, other arithmetic: 1.65 us -> 13.6 us  [pick(): return jnp.where(flag, first, second)]
  transfers between devices with their start and end apart: 6 -> 38, of which waited for: 4 -> 24; matrix products, arithmetic and copies ran while one was open for 17% -> 15% of each run, Pallas kernels for 0% -> 0%
where the time goes in v1:
time: 765 us; the launch traced here: 761 us
  waiting for transfers between devices  566 us (74%)
  matrix products  110 us (14%)
  starting transfers between devices  32.9 us (4%)
  other arithmetic  22.1 us (3%)
  between operations  15.1 us (2%)
  local copies, waits for them, and re-layouts  15 us (2%)
    ppermute x26, waiting for transfers between devices, swap(): return lax.ppermute(value, axis, [(i, i ^ distance) for i in range(size)])  303 us
    reduce_scatter x6, waiting for transfers between devices, scatter_half(): lax.psum_scatter(value, 'dp', scatter_dimension=0, tiled=True, axis_index...  170 us
    dot_general x22, matrix products, dot(): lax.dot_general(left, right, (dims, ((), ())), preferred_element_type=F32)  110 us
    all_gather x6, waiting for transfers between devices, gather_half(): lax.all_gather(value, 'dp', axis=0, tiled=True, axis_index_groups=groups)  91.3 us
    ppermute x26, starting transfers between devices, swap(): return lax.ppermute(value, axis, [(i, i ^ distance) for i in range(size)])  32.1 us
  transfers between devices with their start and end apart: 38, of which 24 were waited for; matrix products, arithmetic and copies ran while one was open for 15% of the time, Pallas kernels for 0%

profile of v1, /device:TPU:0, one launch (start us, length us, event | category | flops | bytes accessed | tf_op | source)
XLA Modules:
  0.0 761.0 jit_solution(7875966342012958808)
XLA Ops:
  9.7 4.0 collective-permute-start.4
  13.8 34.4 %collective-permute-done.4 = bf16[384,1024]{1,0:T(8,128)(2,1)S(1)} collective-permute-done((bf16[384,1024]{1,0:T(8,128)(2,1)S(1)}, bf16[384,1024]{1,0:T(8,128)(2,1)S(1)}, u32[]{:S(2)}, u32[]{:S(2)}) %collective-permute-start.4) | collective-permute-done | bytes 786464 | tf_op jit(solution)/shard_map/ppermute | solution.py:28
  50.2 36.5 %collective-permute-done.5 = bf16[384,1024]{1,0:T(8,128)(2,1)S(1)} collective-permute-done((bf16[384,1024]{1,0:T(8,128)(2,1)S(1)}, bf16[384,1024]{1,0:T(8,128)(2,1)S(1)}, u32[]{:S(2)}, u32[]{:S(2)}) %collective-permute-start.5) | collective-permute-done | bytes 786464 | tf_op jit(solution)/shard_map/ppermute | solution.py:28
  90.0 35.6 %collective-permute-done.6 = bf16[384,1024]{1,0:T(8,128)(2,1)S(1)} collective-permute-done((bf16[384,1024]{1,0:T(8,128)(2,1)S(1)}, bf16[384,1024]{1,0:T(8,128)(2,1)S(1)}, u32[]{:S(2)}, u32[]{:S(2)}) %collective-permute-start.6) | collective-permute-done | bytes 786464 | tf_op jit(solution)/shard_map/ppermute | solution.py:28
  127.2 4.4 convolution_convert_fusion.1
  131.7 27.2 %collective-permute-done = bf16[384,768]{1,0:T(8,128)(2,1)S(1)} collective-permute-done((bf16[384,768]{1,0:T(8,128)(2,1)S(1)}, bf16[384,768]{1,0:T(8,128)(2,1)S(1)}, u32[]{:S(2)}, u32[]{:S(2)}) %collective-permute-start) | collective-permute-done | bytes 589856 | tf_op jit(solution)/shard_map/ppermute | solution.py:28
  163.1 12.2 %collective-permute-done.1 = bf16[384,768]{1,0:T(8,128)(2,1)} collective-permute-done((bf16[384,768]{1,0:T(8,128)(2,1)S(1)}, bf16[384,768]{1,0:T(8,128)(2,1)}, u32[]{:S(2)}, u32[]{:S(2)}) %collective-permute-start.1) | collective-permute-done | bytes 589856 | tf_op jit(solution)/shard_map/ppermute | solution.py:28
  176.4 7.1 collective-permute-done.2
  184.8 2.5 fusion.3
  187.3 7.0 fusion.30
  194.4 7.0 fusion.31
  201.4 6.4 convolution_add_fusion.2
  207.8 29.7 %all-gather.11.cloned.1.call-done = bf16[1536,1024]{1,0:T(8,128)(2,1)} async-done(((bf16[384,1024]{1,0:T(8,128)(2,1)}), bf16[1536,1024]{1,0:T(8,128)(2,1)}) %all-gather.11.cloned.1.call-update) | async-done | bytes 3145744 | tf_op jit(solution)/shard_map/all_gather | solution.py:108
  237.5 7.3 multiply_convert_fusion.3
  244.8 29.4 %all-gather.17.cloned.1.call-done = bf16[1536,1024]{1,0:T(8,128)(2,1)} async-done(((bf16[384,1024]{1,0:T(8,128)(2,1)}), bf16[1536,1024]{1,0:T(8,128)(2,1)}) %all-gather.17.cloned.1.call-update) | async-done | bytes 3145744 | tf_op jit(solution)/shard_map/all_gather | solution.py:108
  274.1 5.0 convolution_convert_fusion.8
  279.2 32.2 %all-gather.15.cloned.1.call-done = bf16[1536,1024]{1,0:T(8,128)(2,1)} async-done(((bf16[384,1024]{1,0:T(8,128)(2,1)}), bf16[1536,1024]{1,0:T(8,128)(2,1)}) %all-gather.15.cloned.1.call-update) | async-done | bytes 3145744 | tf_op jit(solution)/shard_map/all_gather | solution.py:108
  311.4 5.0 convolution_convert_fusion.9
  321.9 25.2 %collective-permute-done.9 = bf16[384,1536]{1,0:T(8,128)(2,1)S(1)} collective-permute-done((bf16[384,1536]{1,0:T(8,128)(2,1)S(1)}, bf16[384,1536]{1,0:T(8,128)(2,1)S(1)}, u32[]{:S(2)}, u32[]{:S(2)}) %collective-permute-start.9) | collective-permute-done | bytes 1179680 | tf_op jit(solution)/shard_map/ppermute | solution.py:28
  350.6 12.0 %collective-permute-done.10 = bf16[384,768]{1,0:T(8,128)(2,1)S(1)} collective-permute-done((bf16[384,768]{1,0:T(8,128)(2,1)S(1)}, bf16[384,768]{1,0:T(8,128)(2,1)S(1)}, u32[]{:S(2)}, u32[]{:S(2)}) %collective-permute-start.10) | collective-permute-done | bytes 589856 | tf_op jit(solution)/shard_map/ppermute | solution.py:28
  367.3 23.0 %collective-permute-done.11 = bf16[384,768]{1,0:T(8,128)(2,1)S(1)} collective-permute-done((bf16[384,768]{1,0:T(8,128)(2,1)S(1)}, bf16[384,768]{1,0:T(8,128)(2,1)S(1)}, u32[]{:S(2)}, u32[]{:S(2)}) %collective-permute-start.11) | collective-permute-done | bytes 589856 | tf_op jit(solution)/shard_map/ppermute | solution.py:28
  399.9 25.5 %collective-permute-done.12 = bf16[384,768]{1,0:T(8,128)(2,1)S(1)} collective-permute-done((bf16[384,768]{1,0:T(8,128)(2,1)S(1)}, bf16[384,768]{1,0:T(8,128)(2,1)S(1)}, u32[]{:S(2)}, u32[]{:S(2)}) %collective-permute-start.12) | collective-permute-done | bytes 589856 | tf_op jit(solution)/shard_map/ppermute | solution.py:28
  429.3 12.3 %collective-permute-done.13 = bf16[384,768]{1,0:T(8,128)(2,1)S(1)} collective-permute-done((bf16[384,768]{1,0:T(8,128)(2,1)S(1)}, bf16[384,768]{1,0:T(8,128)(2,1)S(1)}, u32[]{:S(2)}, u32[]{:S(2)}) %collective-permute-start.13) | collective-permute-done | bytes 589856 | tf_op jit(solution)/shard_map/ppermute | solution.py:28
  441.7 12.8 %collective-permute-done.14 = bf16[384,768]{1,0:T(8,128)(2,1)S(1)} collective-permute-done((bf16[384,768]{1,0:T(8,128)(2,1)S(1)}, bf16[384,768]{1,0:T(8,128)(2,1)S(1)}, u32[]{:S(2)}, u32[]{:S(2)}) %collective-permute-start.14) | collective-permute-done | bytes 589856 | tf_op jit(solution)/shard_map/ppermute | solution.py:28
  454.7 2.6 fusion.25
  459.3 5.6 multiply_convert_fusion.2
  466.1 4.0 convolution_convert_fusion.6
  470.3 6.4 convolution_convert_fusion.4
  476.8 6.5 convolution_convert_fusion.2
  483.4 6.6 convolution_convert_fusion.7
  490.1 6.6 convolution_convert_fusion.5
  496.7 6.5 convolution_convert_fusion.3
  503.2 5.2 fusion.33
  508.4 3.1 add_convert_fusion
  511.6 2.6 fusion.32
  514.3 2.9 add_convert_fusion.1
  521.6 24.5 %collective-permute-done.18 = bf16[384,1536]{1,0:T(8,128)(2,1)S(1)} collective-permute-done((bf16[384,1536]{1,0:T(8,128)(2,1)S(1)}, bf16[384,1536]{1,0:T(8,128)(2,1)S(1)}, u32[]{:S(2)}, u32[]{:S(2)}) %collective-permute-start.18) | collective-permute-done | bytes 1179680 | tf_op jit(solution)/shard_map/ppermute | solution.py:28
  549.9 10.3 %collective-permute-done.19 = bf16[384,768]{1,0:T(8,128)(2,1)S(1)} collective-permute-done((bf16[384,768]{1,0:T(8,128)(2,1)S(1)}, bf16[384,768]{1,0:T(8,128)(2,1)S(1)}, u32[]{:S(2)}, u32[]{:S(2)}) %collective-permute-start.19) | collective-permute-done | bytes 589856 | tf_op jit(solution)/shard_map/ppermute | solution.py:28
  561.2 2.9 collective-permute-start.23
  564.2 3.3 convolution_convert_fusion.11
  567.5 23.6 %reduce-scatter.17.cloned.1.call-done = bf16[384,1024]{1,0:T(8,128)(2,1)} async-done(((bf16[1536,1024]{1,0:T(8,128)(2,1)}), bf16[384,1024]{1,0:T(8,128)(2,1)}) %reduce-scatter.17.cloned.1.call-update) | async-done | bytes 786448 | tf_op jit(solution)/shard_map/reduce_scatter | solution.py:111
  592.9 3.6 convolution_convert_fusion.10
  596.5 55.0 %reduce-scatter.7.cloned.1.call-done = bf16[384,1024]{1,0:T(8,128)(2,1)} async-done(((bf16[1536,1024]{1,0:T(8,128)(2,1)}), bf16[384,1024]{1,0:T(8,128)(2,1)}) %reduce-scatter.7.cloned.1.call-update) | async-done | bytes 786448 | tf_op jit(solution)/shard_map/reduce_scatter | solution.py:111
  651.5 3.7 maximum_select_fusion.2
  655.2 57.9 %reduce-scatter.11.cloned.1.call-done = bf16[384,1024]{1,0:T(8,128)(2,1)} async-done(((bf16[1536,1024]{1,0:T(8,128)(2,1)}), bf16[384,1024]{1,0:T(8,128)(2,1)}) %reduce-scatter.11.cloned.1.call-update) | async-done | bytes 786448 | tf_op jit(solution)/shard_map/reduce_scatter | solution.py:111
  713.0 3.7 maximum_select_fusion.3
  716.7 34.0 %reduce-scatter.15.cloned.1.call-done = bf16[384,1024]{1,0:T(8,128)(2,1)} async-done(((bf16[1536,1024]{1,0:T(8,128)(2,1)}), bf16[384,1024]{1,0:T(8,128)(2,1)}) %reduce-scatter.15.cloned.1.call-update) | async-done | bytes 786448 | tf_op jit(solution)/shard_map/reduce_scatter | solution.py:111
  750.7 3.2 maximum_select_fusion.4
  (167 shorter events, 57.7 us)
Async XLA Ops:
  7.2 42.0 %copy-start.5 = (bf16[384,2048]{1,0:T(8,128)(2,1)S(1)}, bf16[384,2048]{1,0:T(8,128)(2,1)}, u32[]{:S(2)}) copy-start(bf16[384,2048]{1,0:T(8,128)(2,1)} %param.12) | copy-start | bytes 4718596
  7.2 180.2 %all-gather.9.cloned.1.call-start = ((), (), s32[]{:S(2)}) async-start(), calls=%async_computation.7 | async-start | bytes 3932160 | tf_op jit(solution)/shard_map/all_gather | solution.py:108
  9.7 38.4 %collective-permute-start.4 = (bf16[384,1024]{1,0:T(8,128)(2,1)S(1)}, bf16[384,1024]{1,0:T(8,128)(2,1)S(1)}, u32[]{:S(2)}, u32[]{:S(2)}) collective-permute-start(bf16[384,1024]{1,0:T(8,128)(2,1)S(1)} %get-tuple-element.27), channel_id=1, source_target_pairs={{0,16},{4,20},{8,24},{12,28},{16,0},{20,4},{24,8},{28,12},{1,17},{... | collective-permute-start | bytes 2359304 | tf_op jit(solution)/shard_map/ppermute | solution.py:28
  49.1 39.9 %copy-start.6 = (bf16[384,2048]{1,0:T(8,128)(2,1)S(1)}, bf16[384,2048]{1,0:T(8,128)(2,1)}, u32[]{:S(2)}) copy-start(bf16[384,2048]{1,0:T(8,128)(2,1)} %param.13) | copy-start | bytes 4718596
  49.1 145.3 %all-gather.13.cloned.1.call-start = ((), (), s32[]{:S(2)}) async-start(), calls=%async_computation.9 | async-start | bytes 3932160 | tf_op jit(solution)/shard_map/all_gather | solution.py:108
  50.2 36.5 %collective-permute-start.5 = (bf16[384,1024]{1,0:T(8,128)(2,1)S(1)}, bf16[384,1024]{1,0:T(8,128)(2,1)S(1)}, u32[]{:S(2)}, u32[]{:S(2)}) collective-permute-start(bf16[384,1024]{1,0:T(8,128)(2,1)S(1)} %get-tuple-element.29), channel_id=1, source_target_pairs={{0,16},{4,20},{8,24},{12,28},{16,0},{20,4},{24,8},{28,12},{1,17},{... | collective-permute-start | bytes 2359304 | tf_op jit(solution)/shard_map/ppermute | solution.py:28
  87.6 113.8 %all-gather.7.cloned.1.call-start = ((), (), s32[]{:S(2)}) async-start(), calls=%async_computation.6 | async-start | bytes 3932160 | tf_op jit(solution)/shard_map/all_gather | solution.py:108
  88.3 149.2 %all-gather.11.cloned.1.call-start = ((), (), s32[]{:S(2)}) async-start(), calls=%async_computation.8 | async-start | bytes 3932160 | tf_op jit(solution)/shard_map/all_gather | solution.py:108
  88.4 38.2 %copy-start.13 = (s32[768,2]{0,1:T(2,128)S(1)}, s32[768,2]{0,1:T(2,128)}, u32[]{:S(2)}) copy-start(s32[768,2]{0,1:T(2,128)} %param.8) | copy-start | bytes 18436
  88.9 185.2 %all-gather.17.cloned.1.call-start = ((), (), s32[]{:S(2)}) async-start(), calls=%async_computation.11 | async-start | bytes 3932160 | tf_op jit(solution)/shard_map/all_gather | solution.py:108
  90.0 35.6 %collective-permute-start.6 = (bf16[384,1024]{1,0:T(8,128)(2,1)S(1)}, bf16[384,1024]{1,0:T(8,128)(2,1)S(1)}, u32[]{:S(2)}, u32[]{:S(2)}) collective-permute-start(bf16[384,1024]{1,0:T(8,128)(2,1)S(1)} %get-tuple-element.25), channel_id=1, source_target_pairs={{0,16},{4,20},{8,24},{12,28},{16,0},{20,4},{24,8},{28,12},{1,17},{... | collective-permute-start | bytes 2359304 | tf_op jit(solution)/shard_map/ppermute | solution.py:28
  126.5 184.8 %all-gather.15.cloned.1.call-start = ((), (), s32[]{:S(2)}) async-start(), calls=%async_computation.10 | async-start | bytes 3932160 | tf_op jit(solution)/shard_map/all_gather | solution.py:108
  131.7 27.3 %collective-permute-start = (bf16[384,768]{1,0:T(8,128)(2,1)S(1)}, bf16[384,768]{1,0:T(8,128)(2,1)S(1)}, u32[]{:S(2)}, u32[]{:S(2)}) collective-permute-start(bf16[384,768]{1,0:T(8,128)(2,1)S(1)} %constant_dynamic-slice_fusion.15), channel_id=1, source_target_pairs={{0,16},{4,20},{8,24},{12,28},{16,0},{20,4},{24,8},{28,12},{1,17},{... | collective-permute-start | bytes 1769480 | tf_op jit(solution)/shard_map/ppermute | solution.py:28
  158.9 16.4 %collective-permute-start.1 = (bf16[384,768]{1,0:T(8,128)(2,1)S(1)}, bf16[384,768]{1,0:T(8,128)(2,1)}, u32[]{:S(2)}, u32[]{:S(2)}) collective-permute-start(bf16[384,768]{1,0:T(8,128)(2,1)S(1)} %collective-permute-done), channel_id=1, source_target_pairs={{0,1},{1,0},{2,3},{3,2},{4,5},{5,4},{6,7},{7,6},{8,9},{9,8},{10,11... | collective-permute-start | bytes 1769480 | tf_op jit(solution)/shard_map/ppermute | solution.py:28
  159.0 24.5 %collective-permute-start.2 = (bf16[384,768]{1,0:T(8,128)(2,1)S(1)}, bf16[384,768]{1,0:T(8,128)(2,1)}, u32[]{:S(2)}, u32[]{:S(2)}) collective-permute-start(bf16[384,768]{1,0:T(8,128)(2,1)S(1)} %collective-permute-done), channel_id=1, source_target_pairs={{0,2},{1,3},{2,0},{3,1},{4,6},{5,7},{6,4},{7,5},{8,10},{9,11},{10,... | collective-permute-start | bytes 1769480 | tf_op jit(solution)/shard_map/ppermute | solution.py:28
  160.5 24.2 %collective-permute-start.3 = (bf16[384,768]{1,0:T(8,128)(2,1)S(1)}, bf16[384,768]{1,0:T(8,128)(2,1)S(1)}, u32[]{:S(2)}, u32[]{:S(2)}) collective-permute-start(bf16[384,768]{1,0:T(8,128)(2,1)S(1)} %collective-permute-done), channel_id=1, source_target_pairs={{0,3},{1,2},{2,1},{3,0},{4,7},{5,6},{6,5},{7,4},{8,11},{9,10},{10,... | collective-permute-start | bytes 1769480 | tf_op jit(solution)/shard_map/ppermute | solution.py:28
  162.5 398.8 %reduce-scatter.9.cloned.1.call-start = ((), (), s32[]{:S(2)}) async-start(), calls=%async_computation.13 | async-start | bytes 3932160 | tf_op jit(solution)/shard_map/reduce_scatter | solution.py:111
  318.5 46.7 %slice-start = ((s8[4718592]{0:T(1024)(128)(4,1)}), s8[4194304]{0:T(1024)(128)(4,1)S(1)}, s32[]{:S(2)}) async-start(s8[4718592]{0:T(1024)(128)(4,1)} %bitcast.38), calls=%async_computation.18 | async-start | bytes 8388608
  318.6 28.6 %collective-permute-start.9 = (bf16[384,1536]{1,0:T(8,128)(2,1)S(1)}, bf16[384,1536]{1,0:T(8,128)(2,1)S(1)}, u32[]{:S(2)}, u32[]{:S(2)}) collective-permute-start(bf16[384,1536]{1,0:T(8,128)(2,1)S(1)} %pad_maximum_fusion.1), channel_id=1, source_target_pairs={{0,1},{1,0},{2,3},{3,2},{4,5},{5,4},{6,7},{7,6},{8,9},{9,8},{10,11... | collective-permute-start | bytes 3538952 | tf_op jit(solution)/shard_map/ppermute | solution.py:28
  320.3 45.0 %slice-start.1 = ((s8[4718592]{0:T(1024)(128)(4,1)}), s8[524288]{0:T(1024)(128)(4,1)S(1)}, s32[]{:S(2)}) async-start(s8[4718592]{0:T(1024)(128)(4,1)} %bitcast.38), calls=%async_computation.19 | async-start | bytes 1048576
  320.4 28.5 %collective-permute-start.7 = (bf16[384,1536]{1,0:T(8,128)(2,1)S(1)}, bf16[384,1536]{1,0:T(8,128)(2,1)S(1)}, u32[]{:S(2)}, u32[]{:S(2)}) collective-permute-start(bf16[384,1536]{1,0:T(8,128)(2,1)S(1)} %pad_maximum_fusion), channel_id=1, source_target_pairs={{0,2},{1,3},{2,0},{3,1},{4,6},{5,7},{6,4},{7,5},{8,10},{9,11},{10,... | collective-permute-start | bytes 3538952 | tf_op jit(solution)/shard_map/ppermute | solution.py:28
  347.4 15.2 %collective-permute-start.10 = (bf16[384,768]{1,0:T(8,128)(2,1)S(1)}, bf16[384,768]{1,0:T(8,128)(2,1)S(1)}, u32[]{:S(2)}, u32[]{:S(2)}) collective-permute-start(bf16[384,768]{1,0:T(8,128)(2,1)S(1)} %add_convert_fusion.7), channel_id=1, source_target_pairs={{0,2},{1,3},{2,0},{3,1},{4,6},{5,7},{6,4},{7,5},{8,10},{9,11},{10,... | collective-permute-start | bytes 1769480 | tf_op jit(solution)/shard_map/ppermute | solution.py:28
  349.1 18.2 %collective-permute-start.8 = (bf16[384,768]{1,0:T(8,128)(2,1)S(1)}, bf16[384,768]{1,0:T(8,128)(2,1)S(1)}, u32[]{:S(2)}, u32[]{:S(2)}) collective-permute-start(bf16[384,768]{1,0:T(8,128)(2,1)S(1)} %add_convert_fusion.8), channel_id=1, source_target_pairs={{0,1},{1,0},{2,3},{3,2},{4,5},{5,4},{6,7},{7,6},{8,9},{9,8},{10,11... | collective-permute-start | bytes 1769480 | tf_op jit(solution)/shard_map/ppermute | solution.py:28
  362.8 27.6 %collective-permute-start.11 = (bf16[384,768]{1,0:T(8,128)(2,1)S(1)}, bf16[384,768]{1,0:T(8,128)(2,1)S(1)}, u32[]{:S(2)}, u32[]{:S(2)}) collective-permute-start(bf16[384,768]{1,0:T(8,128)(2,1)S(1)} %add_convert_fusion.6), channel_id=1, source_target_pairs={{0,16},{4,20},{8,24},{12,28},{16,0},{20,4},{24,8},{28,12},{1,17},{... | collective-permute-start | bytes 1769480 | tf_op jit(solution)/shard_map/ppermute | solution.py:28
  367.3 28.9 %copy-start.14 = (f32[768,2]{0,1:T(2,128)S(1)}, f32[768,2]{0,1:T(2,128)}, u32[]{:S(2)}) copy-start(f32[768,2]{0,1:T(2,128)} %param.9) | copy-start | bytes 18436
  367.3 31.7 %copy-start.10 = (bf16[384,768]{1,0:T(8,128)(2,1)}, bf16[384,768]{1,0:T(8,128)(2,1)S(1)}, u32[]{:S(2)}) copy-start(bf16[384,768]{1,0:T(8,128)(2,1)S(1)} %collective-permute-done.8) | copy-start | bytes 1769476
  390.8 3.6 collective-permute-start.21
  394.5 3.6 collective-permute-start.22
  399.8 57.6 %copy-start.1 = (bf16[384,3072]{1,0:T(8,128)(2,1)}, bf16[384,3072]{1,0:T(8,128)(2,1)S(1)}, u32[]{:S(2)}) copy-start(bf16[384,3072]{1,0:T(8,128)(2,1)S(1)} %multiply_convert_fusion) | copy-start | bytes 7077892
  399.9 25.6 %collective-permute-start.12 = (bf16[384,768]{1,0:T(8,128)(2,1)S(1)}, bf16[384,768]{1,0:T(8,128)(2,1)S(1)}, u32[]{:S(2)}, u32[]{:S(2)}) collective-permute-start(bf16[384,768]{1,0:T(8,128)(2,1)S(1)} %constant_dynamic-slice_fusion.4), channel_id=1, source_target_pairs={{0,16},{4,20},{8,24},{12,28},{16,0},{20,4},{24,8},{28,12},{1,17},{... | collective-permute-start | bytes 1769480 | tf_op jit(solution)/shard_map/ppermute | solution.py:28
  425.4 16.2 %collective-permute-start.13 = (bf16[384,768]{1,0:T(8,128)(2,1)S(1)}, bf16[384,768]{1,0:T(8,128)(2,1)S(1)}, u32[]{:S(2)}, u32[]{:S(2)}) collective-permute-start(bf16[384,768]{1,0:T(8,128)(2,1)S(1)} %collective-permute-done.12), channel_id=1, source_target_pairs={{0,1},{1,0},{2,3},{3,2},{4,5},{5,4},{6,7},{7,6},{8,9},{9,8},{10,11... | collective-permute-start | bytes 1769480 | tf_op jit(solution)/shard_map/ppermute | solution.py:28
  426.9 27.6 %collective-permute-start.14 = (bf16[384,768]{1,0:T(8,128)(2,1)S(1)}, bf16[384,768]{1,0:T(8,128)(2,1)S(1)}, u32[]{:S(2)}, u32[]{:S(2)}) collective-permute-start(bf16[384,768]{1,0:T(8,128)(2,1)S(1)} %collective-permute-done.12), channel_id=1, source_target_pairs={{0,2},{1,3},{2,0},{3,1},{4,6},{5,7},{6,4},{7,5},{8,10},{9,11},{10,... | collective-permute-start | bytes 1769480 | tf_op jit(solution)/shard_map/ppermute | solution.py:28
  428.4 26.2 %collective-permute-start.15 = (bf16[384,768]{1,0:T(8,128)(2,1)S(1)}, bf16[384,768]{1,0:T(8,128)(2,1)S(1)}, u32[]{:S(2)}, u32[]{:S(2)}) collective-permute-start(bf16[384,768]{1,0:T(8,128)(2,1)S(1)} %collective-permute-done.12), channel_id=1, source_target_pairs={{0,3},{1,2},{2,1},{3,0},{4,7},{5,6},{6,5},{7,4},{8,11},{9,10},{10,... | collective-permute-start | bytes 1769480 | tf_op jit(solution)/shard_map/ppermute | solution.py:28
  429.2 25.5 %copy-start.18 = (bf16[1536,1024]{1,0:T(8,128)(2,1)S(1)}, bf16[1536,1024]{1,0:T(8,128)(2,1)}, u32[]{:S(2)}) copy-start(bf16[1536,1024]{1,0:T(8,128)(2,1)} %all-gather.17.cloned.1.call-done) | copy-start | bytes 9437188
  470.1 94.0 %reduce-scatter.13.cloned.1.call-start = ((), (), s32[]{:S(2)}) async-start(), calls=%async_computation.15 | async-start | bytes 3932160 | tf_op jit(solution)/shard_map/reduce_scatter | solution.py:111
  476.8 114.4 %reduce-scatter.17.cloned.1.call-start = ((), (), s32[]{:S(2)}) async-start(), calls=%async_computation.17 | async-start | bytes 3932160 | tf_op jit(solution)/shard_map/reduce_scatter | solution.py:111
  483.4 168.1 %reduce-scatter.7.cloned.1.call-start = ((), (), s32[]{:S(2)}) async-start(), calls=%async_computation.12 | async-start | bytes 3932160 | tf_op jit(solution)/shard_map/reduce_scatter | solution.py:111
  490.0 223.0 %reduce-scatter.11.cloned.1.call-start = ((), (), s32[]{:S(2)}) async-start(), calls=%async_computation.14 | async-start | bytes 3932160 | tf_op jit(solution)/shard_map/reduce_scatter | solution.py:111
  496.6 254.0 %reduce-scatter.15.cloned.1.call-start = ((), (), s32[]{:S(2)}) async-start(), calls=%async_computation.16 | async-start | bytes 3932160 | tf_op jit(solution)/shard_map/reduce_scatter | solution.py:111
  518.8 29.0 %copy-start = (bf16[384,3072]{1,0:T(8,128)(2,1)}, bf16[384,3072]{1,0:T(8,128)(2,1)S(1)}, u32[]{:S(2)}) copy-start(bf16[384,3072]{1,0:T(8,128)(2,1)S(1)} %get-tuple-element.10) | copy-start | bytes 7077892
  519.0 27.1 %collective-permute-start.18 = (bf16[384,1536]{1,0:T(8,128)(2,1)S(1)}, bf16[384,1536]{1,0:T(8,128)(2,1)S(1)}, u32[]{:S(2)}, u32[]{:S(2)}) collective-permute-start(bf16[384,1536]{1,0:T(8,128)(2,1)S(1)} %pad_maximum_fusion.3), channel_id=1, source_target_pairs={{0,1},{1,0},{2,3},{3,2},{4,5},{5,4},{6,7},{7,6},{8,9},{9,8},{10,11... | collective-permute-start | bytes 3538952 | tf_op jit(solution)/shard_map/ppermute | solution.py:28
  520.7 27.1 %collective-permute-start.16 = (bf16[384,1536]{1,0:T(8,128)(2,1)S(1)}, bf16[384,1536]{1,0:T(8,128)(2,1)S(1)}, u32[]{:S(2)}, u32[]{:S(2)}) collective-permute-start(bf16[384,1536]{1,0:T(8,128)(2,1)S(1)} %pad_maximum_fusion.2), channel_id=1, source_target_pairs={{0,2},{1,3},{2,0},{3,1},{4,6},{5,7},{6,4},{7,5},{8,10},{9,11},{10,... | collective-permute-start | bytes 3538952 | tf_op jit(solution)/shard_map/ppermute | solution.py:28
  546.3 13.8 %collective-permute-start.19 = (bf16[384,768]{1,0:T(8,128)(2,1)S(1)}, bf16[384,768]{1,0:T(8,128)(2,1)S(1)}, u32[]{:S(2)}, u32[]{:S(2)}) collective-permute-start(bf16[384,768]{1,0:T(8,128)(2,1)S(1)} %add_convert_fusion.4), channel_id=1, source_target_pairs={{0,2},{1,3},{2,0},{3,1},{4,6},{5,7},{6,4},{7,5},{8,10},{9,11},{10,... | collective-permute-start | bytes 1769480 | tf_op jit(solution)/shard_map/ppermute | solution.py:28
  549.0 44.0 %collective-permute-start.17 = (bf16[384,768]{1,0:T(8,128)(2,1)}, bf16[384,768]{1,0:T(8,128)(2,1)}, u32[]{:S(2)}, u32[]{:S(2)}) collective-permute-start(bf16[384,768]{1,0:T(8,128)(2,1)} %add_convert_fusion.5), channel_id=1, source_target_pairs={{0,1},{1,0},{2,3},{3,2},{4,5},{5,4},{6,7},{7,6},{8,9},{9,8},{10,11... | collective-permute-start | bytes 1769480 | tf_op jit(solution)/shard_map/ppermute | solution.py:28
  561.2 31.7 %collective-permute-start.20 = (bf16[384,768]{1,0:T(8,128)(2,1)}, bf16[384,768]{1,0:T(8,128)(2,1)}, u32[]{:S(2)}, u32[]{:S(2)}) collective-permute-start(bf16[384,768]{1,0:T(8,128)(2,1)} %add_convert_fusion.3), channel_id=1, source_target_pairs={{0,16},{4,20},{8,24},{12,28},{16,0},{20,4},{24,8},{28,12},{1,17},{... | collective-permute-start | bytes 1769480 | tf_op jit(solution)/shard_map/ppermute | solution.py:28
  561.2 90.2 %collective-permute-start.23 = (bf16[384,1024]{1,0:T(8,128)(2,1)}, bf16[384,1024]{1,0:T(8,128)(2,1)}, u32[]{:S(2)}, u32[]{:S(2)}) collective-permute-start(bf16[384,1024]{1,0:T(8,128)(2,1)} %reduce-scatter.9.cloned.1.call-done), channel_id=1, source_target_pairs={{0,16},{4,20},{8,24},{12,28},{16,0},{20,4},{24,8},{28,12},{1,17},{... | collective-permute-start | bytes 2359304 | tf_op jit(solution)/shard_map/ppermute | solution.py:28
  564.2 148.9 %collective-permute-start.24 = (bf16[384,1024]{1,0:T(8,128)(2,1)}, bf16[384,1024]{1,0:T(8,128)(2,1)}, u32[]{:S(2)}, u32[]{:S(2)}) collective-permute-start(bf16[384,1024]{1,0:T(8,128)(2,1)} %reduce-scatter.13.cloned.1.call-done), channel_id=1, source_target_pairs={{0,16},{4,20},{8,24},{12,28},{16,0},{20,4},{24,8},{28,12},{1,17},{... | collective-permute-start | bytes 2359304 | tf_op jit(solution)/shard_map/ppermute | solution.py:28
  591.1 159.5 %collective-permute-start.25 = (bf16[384,1024]{1,0:T(8,128)(2,1)}, bf16[384,1024]{1,0:T(8,128)(2,1)S(1)}, u32[]{:S(2)}, u32[]{:S(2)}) collective-permute-start(bf16[384,1024]{1,0:T(8,128)(2,1)} %reduce-scatter.17.cloned.1.call-done), channel_id=1, source_target_pairs={{0,16},{4,20},{8,24},{12,28},{16,0},{20,4},{24,8},{28,12},{1,17},{... | collective-permute-start | bytes 2359304 | tf_op jit(solution)/shard_map/ppermute | solution.py:28
  (17 other events, 60.8 us)
Sparse Core Ops, SparseCore 0:
  49.2 58.4 all-gather.8
  109.8 53.8 all-gather.12
  165.8 34.4 all-gather.6
  202.3 35.1 all-gather.10
  238.9 35.1 all-gather.16
  276.1 35.1 all-gather.14
  470.2 33.4 reduce-scatter.8
  506.0 34.2 reduce-scatter.12
  542.6 48.5 reduce-scatter.16
  593.3 58.1 reduce-scatter.6
  653.8 59.2 reduce-scatter.10
  715.2 35.4 reduce-scatter.14

commit v2 on v1

v2 whole, which is shorter than its diff:
```python
import jax
import jax.numpy as jnp
from jax import lax
from jax.sharding import PartitionSpec as P

BF16 = jnp.bfloat16
F32 = jnp.float32


def dot(left, right, dims):
    return lax.dot_general(left, right, (dims, ((), ())), preferred_element_type=F32)


def mm(left, right):
    return dot(left, right, ((1,), (0,)))


def mm_last(left, right):
    return dot(left, right, ((1,), (1,)))


def mm_first(left, right):
    return dot(left, right, ((0,), (0,)))


def swap(value, axis, distance):
    size = lax.axis_size(axis)
    return lax.ppermute(value, axis, [(i, i ^ distance) for i in range(size)])


def fence(*values):
    return lax.optimization_barrier(values)


def select_rows(assign_block, combine_block, row_limit):
    expert_hit = assign_block == 0
    routed = jnp.any(expert_hit, axis=1)
    weight = jnp.sum(
        jnp.where(expert_hit, combine_block, jnp.zeros((), combine_block.dtype)), axis=1
    )
    place = jnp.cumsum(routed.astype(jnp.int32)) - 1
    match = routed[None, :] & (place[None, :] == jnp.arange(row_limit, dtype=jnp.int32)[:, None])
    row_weight = jnp.sum(jnp.where(match, weight[None, :], 0.0), axis=1)
    return (match, row_weight)


def halves(value, upper, axis):
    width = value.shape[axis] // 2
    start = upper * width
    mine = lax.dynamic_slice_in_dim(value, start, width, axis)
    other = lax.dynamic_slice_in_dim(value, width - start, width, axis)
    return mine, other


def join(mine, other, upper, axis):
    return jnp.where(
        upper == 0,
        jnp.concatenate([mine, other], axis=axis),
        jnp.concatenate([other, mine], axis=axis),
    )


def columns(value, places, width):
    return jnp.concatenate(
        [lax.dynamic_slice_in_dim(value, p * width, width, 1) for p in places], axis=1
    )


def cat(*values):
    return jnp.concatenate(values, axis=0)


def local(tokens, assign, combine, cotangent, w_gate, w_up, w_down_t):
    token_total, depth = tokens.shape
    row_limit = token_total // 2
    n_dp = lax.axis_size("dp")
    n_tensor = lax.axis_size("tensor")
    me = lax.axis_index("dp")
    me_t = lax.axis_index("tensor")
    far = n_dp // 2
    upper = me // far
    rows_w = w_gate.shape[0]
    width = depth // n_tensor
    mids = [1 << i for i in range(1, far.bit_length() - 1)][::-1]
    t_bits = [1 << i for i in range(n_tensor.bit_length() - 1)]

    own_even = [0]
    for bit in mids:
        own_even = own_even + [k ^ bit for k in own_even]
    even = own_even + [k ^ far for k in own_even]
    odd = [k ^ 1 for k in even]
    n_own = len(own_even)

    def grow(block):
        for bit in mids:
            block = cat(block, swap(block, "dp", bit))
        return block

    def z_far(block):
        return swap(block, "dp", far)

    def core(block):
        return swap(block, "dp", 1)

    (gate_0, gate_1), (up_0, up_1), (down_0, down_1) = (
        halves(w, upper, 1) for w in (w_gate, w_up, w_down_t)
    )
    gate_own = grow(gate_0)
    gate_4 = z_far(gate_1)
    match, row_weight = select_rows(assign, combine, row_limit)
    hot = match.astype(BF16)
    rows_in = mm(hot, tokens).astype(BF16)
    rows_grad = mm(hot, cotangent).astype(BF16)
    out_grad = (row_weight[:, None] * rows_grad.astype(F32)).astype(BF16)
    quarter = jnp.concatenate(
        [lax.dynamic_slice_in_dim(v, me_t * width, width, 1) for v in (rows_in, out_grad)], axis=1
    )
    gate_own, gate_4, rows_in, out_grad, quarter, up_0 = fence(
        gate_own, gate_4, rows_in, out_grad, quarter, up_0
    )

    quarter = z_far(quarter)
    gate_far = grow(gate_4)
    up_own = grow(up_0)
    quarter, gate_far, up_own, up_1, down_0 = fence(quarter, gate_far, up_own, up_1, down_0)

    quarters = [quarter] + [swap(quarter, "tensor", k) for k in range(1, n_tensor)]
    up_4 = z_far(up_1)
    down_own = grow(down_0)
    gate_even = cat(gate_own, gate_far)
    gate_odd = core(gate_even)
    *quarters, up_4, down_own, gate_odd, down_1 = fence(
        *quarters, up_4, down_own, gate_odd, down_1
    )

    def rows_far(part):
        wide = jnp.concatenate(
            [q[:, part * width : (part + 1) * width] for q in quarters], axis=1
        )
        return columns(wide, [me_t ^ k for k in range(n_tensor)], width)

    def relative(value, order):
        return columns(value, [me ^ k for k in order], rows_w)

    both_in = cat(rows_in, rows_far(0))
    both_out = cat(out_grad, rows_far(1))
    in_even, in_odd = relative(both_in, even), relative(both_in, odd)
    out_even, out_odd = relative(both_out, even), relative(both_out, odd)
    down_4 = z_far(down_1)
    up_far = grow(up_4)
    gate_pre = mm(in_even, gate_even) + mm(in_odd, gate_odd)
    down_4, up_far, gate_pre = fence(down_4, up_far, gate_pre)

    up_even = cat(up_own, up_far)
    up_odd = core(up_even)
    down_far = grow(down_4)
    up_pre_even = mm(in_even, up_even)
    up_odd, down_far, up_pre_even = fence(up_odd, down_far, up_pre_even)

    down_even = cat(down_own, down_far)
    down_odd = core(down_even)
    up_pre = up_pre_even + mm(in_odd, up_odd)
    sigmoid_gate = jax.nn.sigmoid(gate_pre)
    hidden = (gate_pre * sigmoid_gate * up_pre).astype(BF16)
    g_down_odd = mm_first(out_odd, hidden).astype(BF16)
    hidden_grad_even = mm(out_even, down_even)
    down_odd, g_down_odd, hidden, hidden_grad_even = fence(
        down_odd, g_down_odd, hidden, hidden_grad_even
    )

    g_down_got = core(g_down_odd)
    hidden_grad = hidden_grad_even + mm(out_odd, down_odd)
    gate_grad = (
        hidden_grad * up_pre * sigmoid_gate * (1.0 + gate_pre * (1.0 - sigmoid_gate))
    ).astype(BF16)
    up_grad = (hidden_grad * gate_pre * sigmoid_gate).astype(BF16)
    g_down_got, gate_grad, up_grad = fence(g_down_got, gate_grad, up_grad)

    def even_grad(left, right, got):
        return (mm_first(left, right) + got.astype(F32)).astype(BF16)

    def shrink(value):
        for bit in mids[::-1]:
            size = value.shape[0] // 2
            got = swap(value[size:], "dp", bit)
            value = (value[:size].astype(F32) + got.astype(F32)).astype(BF16)
        return value

    cut = n_own * rows_w

    g_down = even_grad(out_even, hidden, g_down_got)
    g_down_own, g_down_4 = shrink(g_down[:cut]), shrink(g_down[cut:])
    g_gate_odd = mm_first(in_odd, gate_grad).astype(BF16)
    g_up_odd = mm_first(in_odd, up_grad).astype(BF16)

    def true_order(even_part, odd_part):
        whole = jnp.concatenate([even_part.astype(BF16), odd_part.astype(BF16)], axis=1)
        order = even + odd
        place = [order.index(k) for k in range(n_dp)]
        table = jnp.array(place, jnp.int32)
        return columns(whole, [table[me ^ b] for b in range(n_dp)], rows_w)

    expert_part = true_order(mm_last(hidden, down_even), mm_last(hidden, down_odd))
    g_down_own, g_down_4, g_gate_odd, g_up_odd, expert_part = fence(
        g_down_own, g_down_4, g_gate_odd, g_up_odd, expert_part
    )

    def split_parts(value):
        return {
            k: lax.dynamic_slice_in_dim(value, (me_t ^ k) * width, width, 1)
            for k in range(n_tensor)
        }

    def tensor_step(parts, bit):
        gone = [k for k in parts if k & bit]
        kept = [k for k in parts if not k & bit]
        got = swap(jnp.concatenate([parts[k] for k in gone], axis=1), "tensor", bit)
        return {
            k: (parts[k].astype(F32) + got[:, i * width : (i + 1) * width].astype(F32)).astype(BF16)
            for i, k in enumerate(kept)
        }

    def steps_1(value):
        near, away = split_parts(value[:row_limit]), split_parts(value[row_limit:])
        return tensor_step(near, t_bits[0]), tensor_step(away, t_bits[-1])

    def steps_2(near, away):
        for bit in t_bits[1:]:
            near = tensor_step(near, bit)
        for bit in t_bits[:-1][::-1]:
            away = tensor_step(away, bit)
        return near[0], away[0]

    g_down_far = z_far(g_down_4)
    g_gate_got = core(g_gate_odd)
    g_up_got = core(g_up_odd)
    expert_near, expert_away = steps_1(expert_part)
    input_part = true_order(
        mm_last(gate_grad, gate_even) + mm_last(up_grad, up_even),
        mm_last(gate_grad, gate_odd) + mm_last(up_grad, up_odd),
    )
    g_down_far, g_gate_got, g_up_got, expert_near, expert_away, input_part = fence(
        g_down_far, g_gate_got, g_up_got, expert_near, expert_away, input_part
    )

    g_gate = even_grad(in_even, gate_grad, g_gate_got)
    g_gate_own, g_gate_4 = shrink(g_gate[:cut]), shrink(g_gate[cut:])
    g_up = even_grad(in_even, up_grad, g_up_got)
    expert_near, expert_away = steps_2(expert_near, expert_away)
    input_near, input_away = steps_1(input_part)
    (g_gate_own, g_gate_4, g_up, expert_near, expert_away, input_near, input_away) = fence(
        g_gate_own, g_gate_4, g_up, expert_near, expert_away, input_near, input_away
    )

    g_gate_far = z_far(g_gate_4)
    g_up_own, g_up_4 = shrink(g_up[:cut]), shrink(g_up[cut:])
    expert_got = z_far(expert_away)
    input_near, input_away = steps_2(input_near, input_away)
    g_gate_far, g_up_own, g_up_4, expert_got, input_near, input_away = fence(
        g_gate_far, g_up_own, g_up_4, expert_got, input_near, input_away
    )

    g_up_far = z_far(g_up_4)
    input_got = z_far(input_away)
    expert_cols = expert_near.astype(F32) + expert_got.astype(F32)
    grad_cols = lax.dynamic_slice_in_dim(rows_grad, me_t * width, width, 1)
    weight_rows = jnp.sum(grad_cols.astype(F32) * expert_cols, axis=1)
    for bit in t_bits:
        weight_rows = weight_rows + swap(weight_rows, "tensor", bit)
    weight_grad = jnp.sum(jnp.where(match, weight_rows[:, None], 0.0), axis=0)
    mixed = mm_first(hot, (row_weight[:, None] * expert_cols).astype(BF16)).astype(BF16)
    input_cols = (input_near.astype(F32) + input_got.astype(F32)).astype(BF16)
    input_grad = mm_first(hot, input_cols).astype(BF16)
    return (
        mixed,
        input_grad,
        weight_grad,
        join(g_gate_own, g_gate_far, upper, 1),
        join(g_up_own, g_up_far, upper, 1),
        join(g_down_own, g_down_far, upper, 1),
    )


def solution(mesh):
    return jax.shard_map(
        local,
        mesh=mesh,
        in_specs=(
            P("dp", None),
            P("dp", None),
            P("dp", None),
            P("dp", None),
            P("dp", "tensor"),
            P("dp", "tensor"),
            P("dp", "tensor"),
        ),
        out_specs=(
            P("dp", "tensor"),
            P("dp", "tensor"),
            P("dp"),
            P("dp", "tensor"),
            P("dp", "tensor"),
            P("dp", "tensor"),
        ),
        check_vma=False,
    )
```

time: 765 us -> 583 us (0.76)
  waiting for transfers between devices: 566 us -> 333 us
  other arithmetic: 22.1 us -> 69.4 us
  matrix products: 110 us -> 94 us
  local copies, waits for them, and re-layouts: 15 us -> 29.4 us
  starting transfers between devices: 32.9 us -> 42.7 us
  between operations: 15.1 us -> 7.26 us
    reduce_scatter x6 -> x0, waiting for transfers between devices: 170 us -> none  [scatter_half(): lax.psum_scatter(value, 'dp', scatter_dimension=0, tiled=True, axis_index...]
    all_gather x6 -> x0, waiting for transfers between devices: 91.3 us -> none  [gather_half(): lax.all_gather(value, 'dp', axis=0, tiled=True, axis_index_groups=groups)]
    concatenate x5 -> x17, other arithmetic: 2.85 us -> 42.6 us  [the longest x8 41 us: cat(): return jnp.concatenate(values, axis=0)]
    ppermute x26 -> x40, waiting for transfers between devices: 303 us -> 333 us  [swap(): return lax.ppermute(value, axis, [(i, i ^ distance) for i in range(size)])]
    dot_general x22, matrix products: 110 us -> 94 us  [dot(): lax.dot_general(left, right, (dims, ((), ())), preferred_element_type=F32)]
    convert_element_type x7 -> x13, other arithmetic: 3.78 us -> 14.4 us  [the longest x8 6.93 us: tensor_step(): (parts[k].astype(F32) + got[:, i * width:(i + 1) * width].astype(F32)).as...]
    ppermute x26 -> x40, starting transfers between devices: 32.1 us -> 42.7 us  [swap(): return lax.ppermute(value, axis, [(i, i ^ distance) for i in range(size)])]
    select_n x5 -> x3, other arithmetic: 13.6 us -> 5.21 us  [join(): jnp.where(upper == 0, jnp.concatenate([mine, other], axis=axis), jnp.conc...]
  transfers between devices with their start and end apart: 38 -> 40, of which waited for: 24 -> 23; matrix products, arithmetic and copies ran while one was open for 15% -> 24% of each run, Pallas kernels for 0% -> 0%
where the time goes in v2:
time: 583 us; the launch traced here: 575 us
  waiting for transfers between devices  333 us (57%)
  matrix products  94 us (16%)
  other arithmetic  69.4 us (12%)
  starting transfers between devices  42.7 us (7%)
  local copies, waits for them, and re-layouts  29.4 us (5%)
  between operations  7.26 us (1%)
    ppermute x40, waiting for transfers between devices, swap(): return lax.ppermute(value, axis, [(i, i ^ distance) for i in range(size)])  333 us
    dot_general x22, matrix products, dot(): lax.dot_general(left, right, (dims, ((), ())), preferred_element_type=F32)  94 us
    ppermute x40, starting transfers between devices, swap(): return lax.ppermute(value, axis, [(i, i ^ distance) for i in range(size)])  42.7 us
    concatenate x8, other arithmetic, cat(): return jnp.concatenate(values, axis=0)  41 us
  transfers between devices with their start and end apart: 40, of which 23 were waited for; matrix products, arithmetic and copies ran while one was open for 24% of the time, Pallas kernels for 0%

profile of v2, /device:TPU:0, one launch (start us, length us, event | category | flops | bytes accessed | tf_op | source)
XLA Modules:
  0.0 575.5 jit_solution(3725017520595892459)
XLA Ops:
  0.7 2.4 constant_dynamic-slice_fusion.38
  3.1 4.0 collective-permute-start.1
  9.6 5.9 %multiply_convert_fusion = (bf16[384,3072]{1,0:T(8,128)(2,1)S(1)}, bf16[384,3072]{1,0:T(8,128)(2,1)}) fusion(f32[384]{0:T(512)S(1)} %select_reduce_fusion.1, bf16[768,3072]{1,0:T(8,128)(2,1)} %param.12, s32[768]{0:T(1024)S(1)} %add_bitcast_fusion, pred[768]{0:T(1024)(128)(4,1)S(1)} %fusion.48), kind=kOutput, calls=%fused_computation.39 | convolution fusion | flops 1817247744 | bytes 9442560 | tf_op jit(solution)/shard_map/dot_general | solution.py:11
  15.6 3.5 convolution_convert_fusion.1
  21.7 19.3 %collective-permute-done = bf16[384,1024]{1,0:T(8,128)(2,1)} collective-permute-done((bf16[384,1024]{1,0:T(8,128)(2,1)S(1)}, bf16[384,1024]{1,0:T(8,128)(2,1)}, u32[]{:S(2)}, u32[]{:S(2)}) %collective-permute-start) | collective-permute-done | bytes 786464 | tf_op jit(solution)/shard_map/ppermute | solution.py:28
  42.3 2.5 collective-permute-start.2
  49.1 39.1 %collective-permute-done.3 = bf16[384,1024]{1,0:T(8,128)(2,1)S(1)} collective-permute-done((bf16[384,1024]{1,0:T(8,128)(2,1)}, bf16[384,1024]{1,0:T(8,128)(2,1)S(1)}, u32[]{:S(2)}, u32[]{:S(2)}) %collective-permute-start.3) | collective-permute-done | bytes 786464 | tf_op jit(solution)/shard_map/ppermute | solution.py:28
  89.5 14.3 %collective-permute-done.4 = bf16[384,1024]{1,0:T(8,128)(2,1)S(1)} collective-permute-done((bf16[384,1024]{1,0:T(8,128)(2,1)S(1)}, bf16[384,1024]{1,0:T(8,128)(2,1)S(1)}, u32[]{:S(2)}, u32[]{:S(2)}) %collective-permute-start.4) | collective-permute-done | bytes 786464 | tf_op jit(solution)/shard_map/ppermute | solution.py:28
  106.9 2.4 collective-permute-start.7
  110.4 14.8 %collective-permute-done.9 = bf16[384,1024]{1,0:T(8,128)(2,1)S(1)} collective-permute-done((bf16[384,1024]{1,0:T(8,128)(2,1)S(1)}, bf16[384,1024]{1,0:T(8,128)(2,1)S(1)}, u32[]{:S(2)}, u32[]{:S(2)}) %collective-permute-start.9) | collective-permute-done | bytes 786464 | tf_op jit(solution)/shard_map/ppermute | solution.py:28
  126.0 2.8 collective-permute-start.8
  131.5 32.2 %collective-permute-done.8 = bf16[384,1024]{1,0:T(8,128)(2,1)} collective-permute-done((bf16[384,1024]{1,0:T(8,128)(2,1)}, bf16[384,1024]{1,0:T(8,128)(2,1)}, u32[]{:S(2)}, u32[]{:S(2)}) %collective-permute-start.8) | collective-permute-done | bytes 786464 | tf_op jit(solution)/shard_map/ppermute | solution.py:28
  164.4 3.5 collective-permute-start.12
  175.0 17.9 %maximum_maximum_fusion = bf16[768,3072]{1,0:T(8,128)(2,1)S(1)} fusion(bf16[384,768]{1,0:T(8,128)(2,1)S(1)} %get-tuple-element.212, bf16[384,768]{1,0:T(8,128)(2,1)S(1)} %get-tuple-element.211, bf16[384,768]{1,0:T(8,128)(2,1)S(1)} %get-tuple-element.210, bf16[384,768]{1,0:T(8,128)(2,1)S(1)} %get-tuple-element.213, bf16[384,3072]{1,0:T(8,128)(2,1)S(1)} %copy-done.2), kind=kLoop, calls=%fused_computation.35 | loop fusion | flops 23592960 | bytes 9437184 | tf_op jit(solution)/shard_map/concatenate | solution.py:70
  193.8 6.2 %fusion.54 = f32[768,1024]{1,0:T(8,128)S(1)} fusion(bf16[1536,1024]{1,0:T(8,128)(2,1)} %collective-permute-done.10, bf16[768,384]{1,0:T(8,128)(2,1)S(1)} %get-tuple-element.143, bf16[768,384]{1,0:T(8,128)(2,1)S(1)} %get-tuple-element.144, bf16[768,384]{1,0:T(8,128)(2,1)S(1)} %get-tuple-element.145, bf16[768,384]{1,0:T(8,128)(2,1)S(1)} %get-tuple-element.146), kind=kOutput, calls=%fused_computation.200 | convolution fusion | flops 2425356288 | bytes 8650752 | tf_op jit(solution)/shard_map/dot_general | solution.py:11
  200.1 4.5 convolution_add_fusion
  215.2 4.6 fusion.55
  219.8 13.6 %collective-permute-done.14 = bf16[384,1024]{1,0:T(8,128)(2,1)S(1)} collective-permute-done((bf16[384,1024]{1,0:T(8,128)(2,1)}, bf16[384,1024]{1,0:T(8,128)(2,1)S(1)}, u32[]{:S(2)}, u32[]{:S(2)}) %collective-permute-start.14) | collective-permute-done | bytes 786464 | tf_op jit(solution)/shard_map/ppermute | solution.py:28
  235.7 17.8 %maximum_maximum_fusion.1 = bf16[768,3072]{1,0:T(8,128)(2,1)S(1)} fusion(bf16[384,768]{1,0:T(8,128)(2,1)S(1)} %copy-done.6, bf16[384,768]{1,0:T(8,128)(2,1)S(1)} %copy-done.7, bf16[384,768]{1,0:T(8,128)(2,1)S(1)} %copy-done.8, bf16[384,768]{1,0:T(8,128)(2,1)S(1)} %copy-done.5, bf16[384,3072]{1,0:T(8,128)(2,1)S(1)} %copy-done.1), kind=kLoop, calls=%fused_computation.36 | loop fusion | flops 23592960 | bytes 9437184 | tf_op jit(solution)/shard_map/concatenate | solution.py:70
  255.2 4.7 fusion.53
  261.5 4.4 convolution_convert_fusion.4
  266.0 2.6 fusion.46
  268.6 2.9 convolution_convert_fusion.6
  271.6 4.9 convolution_convert_fusion.5
  279.7 4.5 fusion.47
  286.0 7.3 %fusion.67 = f32[768,1536]{1,0:T(8,128)} fusion(bf16[768,1024]{1,0:T(8,128)(2,1)S(1)} %get-tuple-element.97, bf16[1536,1024]{1,0:T(8,128)(2,1)} %collective-permute-done.13), kind=kOutput, calls=%fused_computation.213 | convolution fusion | flops 2415919104 | bytes 9437184 | tf_op jit(solution)/shard_map/dot_general | solution.py:11
  293.3 6.2 %fusion.66 = f32[768,1536]{1,0:T(8,128)} fusion(bf16[768,1024]{1,0:T(8,128)(2,1)S(1)} %get-tuple-element.97, bf16[1536,1024]{1,0:T(8,128)(2,1)} %constant_dynamic-update-slice_fusion.2), kind=kOutput, calls=%fused_computation.212 | convolution fusion | flops 2415919104 | bytes 9437184 | tf_op jit(solution)/shard_map/dot_general | solution.py:11
  299.5 3.3 convolution_convert_fusion.2
  302.8 3.2 add_convert_fusion.2
  306.0 3.2 convolution_convert_fusion.3
  309.2 5.5 add_convert_fusion.3
  317.0 4.8 add_convert_fusion.4
  321.8 13.5 %collective-permute-done.18 = bf16[384,1024]{1,0:T(8,128)(2,1)S(1)} collective-permute-done((bf16[384,1024]{1,0:T(8,128)(2,1)S(1)}, bf16[384,1024]{1,0:T(8,128)(2,1)S(1)}, u32[]{:S(2)}, u32[]{:S(2)}) %collective-permute-start.18) | collective-permute-done | bytes 786464 | tf_op jit(solution)/shard_map/ppermute | solution.py:28
  335.3 16.4 %collective-permute-done.17 = bf16[384,1024]{1,0:T(8,128)(2,1)S(1)} collective-permute-done((bf16[384,1024]{1,0:T(8,128)(2,1)S(1)}, bf16[384,1024]{1,0:T(8,128)(2,1)S(1)}, u32[]{:S(2)}, u32[]{:S(2)}) %collective-permute-start.17) | collective-permute-done | bytes 786464 | tf_op jit(solution)/shard_map/ppermute | solution.py:28
  360.3 22.0 %collective-permute-done.22 = bf16[384,1536]{1,0:T(8,128)(2,1)S(1)} collective-permute-done((bf16[384,1536]{1,0:T(8,128)(2,1)S(1)}, bf16[384,1536]{1,0:T(8,128)(2,1)S(1)}, u32[]{:S(2)}, u32[]{:S(2)}) %collective-permute-start.22) | collective-permute-done | bytes 1179680 | tf_op jit(solution)/shard_map/ppermute | solution.py:28
  384.2 11.8 %collective-permute-done.19 = bf16[384,1024]{1,0:T(8,128)(2,1)S(1)} collective-permute-done((bf16[384,1024]{1,0:T(8,128)(2,1)S(1)}, bf16[384,1024]{1,0:T(8,128)(2,1)S(1)}, u32[]{:S(2)}, u32[]{:S(2)}) %collective-permute-start.19) | collective-permute-done | bytes 786464 | tf_op jit(solution)/shard_map/ppermute | solution.py:28
  396.8 4.8 add_convert_fusion.1
  402.9 2.0 collective-permute-start.24
  407.3 9.7 %collective-permute-done.26 = bf16[384,768]{1,0:T(8,128)(2,1)S(1)} collective-permute-done((bf16[384,768]{1,0:T(8,128)(2,1)S(1)}, bf16[384,768]{1,0:T(8,128)(2,1)S(1)}, u32[]{:S(2)}, u32[]{:S(2)}) %collective-permute-start.26) | collective-permute-done | bytes 589856 | tf_op jit(solution)/shard_map/ppermute | solution.py:28
  417.4 3.2 add_convert_fusion
  423.4 15.3 %collective-permute-done.24 = bf16[384,1024]{1,0:T(8,128)(2,1)S(1)} collective-permute-done((bf16[384,1024]{1,0:T(8,128)(2,1)S(1)}, bf16[384,1024]{1,0:T(8,128)(2,1)S(1)}, u32[]{:S(2)}, u32[]{:S(2)}) %collective-permute-start.24) | collective-permute-done | bytes 786464 | tf_op jit(solution)/shard_map/ppermute | solution.py:28
  447.6 2.0 collective-permute-start.31
  451.4 8.3 %collective-permute-done.34 = bf16[384,768]{1,0:T(8,128)(2,1)} collective-permute-done((bf16[384,768]{1,0:T(8,128)(2,1)}, bf16[384,768]{1,0:T(8,128)(2,1)}, u32[]{:S(2)}, u32[]{:S(2)}) %collective-permute-start.34) | collective-permute-done | bytes 589856 | tf_op jit(solution)/shard_map/ppermute | solution.py:28
  461.1 35.6 %collective-permute-done.32 = bf16[384,1024]{1,0:T(8,128)(2,1)S(1)} collective-permute-done((bf16[384,1024]{1,0:T(8,128)(2,1)S(1)}, bf16[384,1024]{1,0:T(8,128)(2,1)S(1)}, u32[]{:S(2)}, u32[]{:S(2)}) %collective-permute-start.32) | collective-permute-done | bytes 786464 | tf_op jit(solution)/shard_map/ppermute | solution.py:28
  496.7 14.1 %collective-permute-done.31 = bf16[384,1024]{1,0:T(8,128)(2,1)S(1)} collective-permute-done((bf16[384,1024]{1,0:T(8,128)(2,1)S(1)}, bf16[384,1024]{1,0:T(8,128)(2,1)S(1)}, u32[]{:S(2)}, u32[]{:S(2)}) %collective-permute-start.31) | collective-permute-done | bytes 786464 | tf_op jit(solution)/shard_map/ppermute | solution.py:28
  517.7 2.0 convolution_convert_fusion.8
  524.1 32.5 %collective-permute-done.36 = bf16[384,768]{1,0:T(8,128)(2,1)S(1)} collective-permute-done((bf16[384,768]{1,0:T(8,128)(2,1)S(1)}, bf16[384,768]{1,0:T(8,128)(2,1)S(1)}, u32[]{:S(2)}, u32[]{:S(2)}) %collective-permute-start.36) | collective-permute-done | bytes 589856 | tf_op jit(solution)/shard_map/ppermute | solution.py:28
  558.4 14.9 %collective-permute-done.39 = bf16[384,1024]{1,0:T(8,128)(2,1)S(1)} collective-permute-done((bf16[384,1024]{1,0:T(8,128)(2,1)S(1)}, bf16[384,1024]{1,0:T(8,128)(2,1)S(1)}, u32[]{:S(2)}, u32[]{:S(2)}) %collective-permute-start.39) | collective-permute-done | bytes 786464 | tf_op jit(solution)/shard_map/ppermute | solution.py:28
  (253 shorter events, 91.5 us)
Async XLA Ops:
  3.1 39.2 %collective-permute-start.1 = (bf16[384,1024]{1,0:T(8,128)(2,1)}, bf16[384,1024]{1,0:T(8,128)(2,1)}, u32[]{:S(2)}, u32[]{:S(2)}) collective-permute-start(bf16[384,1024]{1,0:T(8,128)(2,1)} %get-tuple-element.190), channel_id=1, source_target_pairs={{0,16},{4,20},{8,24},{12,28},{16,0},{20,4},{24,8},{28,12},{1,17},{... | collective-permute-start | bytes 2359304 | tf_op jit(solution)/shard_map/ppermute | solution.py:28
  7.1 33.9 %collective-permute-start = (bf16[384,1024]{1,0:T(8,128)(2,1)S(1)}, bf16[384,1024]{1,0:T(8,128)(2,1)}, u32[]{:S(2)}, u32[]{:S(2)}) collective-permute-start(bf16[384,1024]{1,0:T(8,128)(2,1)S(1)} %get-tuple-element.191), channel_id=1, source_target_pairs={{0,8},{4,12},{8,0},{12,4},{16,24},{20,28},{24,16},{28,20},{1,9},{5... | collective-permute-start | bytes 2359304 | tf_op jit(solution)/shard_map/ppermute | solution.py:28
  21.6 25.2 %copy-start.13 = (bf16[384,2048]{1,0:T(8,128)(2,1)S(1)}, bf16[384,2048]{1,0:T(8,128)(2,1)}, u32[]{:S(2)}) copy-start(bf16[384,2048]{1,0:T(8,128)(2,1)} %param.15) | copy-start | bytes 4718596
  42.3 61.6 %collective-permute-start.2 = (bf16[384,1536]{1,0:T(8,128)(2,1)S(1)}, bf16[384,1536]{1,0:T(8,128)(2,1)S(1)}, u32[]{:S(2)}, u32[]{:S(2)}) collective-permute-start(bf16[384,1536]{1,0:T(8,128)(2,1)S(1)} %pad_maximum_fusion.12), channel_id=1, source_target_pairs={{0,16},{4,20},{8,24},{12,28},{16,0},{20,4},{24,8},{28,12},{1,17},{... | collective-permute-start | bytes 3538952 | tf_op jit(solution)/shard_map/ppermute | solution.py:28
  44.8 43.4 %collective-permute-start.3 = (bf16[384,1024]{1,0:T(8,128)(2,1)}, bf16[384,1024]{1,0:T(8,128)(2,1)S(1)}, u32[]{:S(2)}, u32[]{:S(2)}) collective-permute-start(bf16[384,1024]{1,0:T(8,128)(2,1)} %collective-permute-done.1), channel_id=1, source_target_pairs={{0,8},{4,12},{8,0},{12,4},{16,24},{20,28},{24,16},{28,20},{1,9},{5... | collective-permute-start | bytes 2359304 | tf_op jit(solution)/shard_map/ppermute | solution.py:28
  45.9 57.9 %collective-permute-start.4 = (bf16[384,1024]{1,0:T(8,128)(2,1)S(1)}, bf16[384,1024]{1,0:T(8,128)(2,1)S(1)}, u32[]{:S(2)}, u32[]{:S(2)}) collective-permute-start(bf16[384,1024]{1,0:T(8,128)(2,1)S(1)} %get-tuple-element.69), channel_id=1, source_target_pairs={{0,8},{4,12},{8,0},{12,4},{16,24},{20,28},{24,16},{28,20},{1,9},{5... | collective-permute-start | bytes 2359304 | tf_op jit(solution)/shard_map/ppermute | solution.py:28
  105.2 58.4 %collective-permute-start.10 = (bf16[1536,1024]{1,0:T(8,128)(2,1)}, bf16[1536,1024]{1,0:T(8,128)(2,1)}, u32[]{:S(2)}, u32[]{:S(2)}) collective-permute-start(bf16[1536,1024]{1,0:T(8,128)(2,1)} %constant_dynamic-update-slice_fusion), channel_id=1, source_target_pairs={{0,4},{4,0},{8,12},{12,8},{16,20},{20,16},{24,28},{28,24},{1,5},{5... | collective-permute-start | bytes 9437192 | tf_op jit(solution)/shard_map/ppermute | solution.py:28
  105.2 20.0 %collective-permute-start.9 = (bf16[384,1024]{1,0:T(8,128)(2,1)S(1)}, bf16[384,1024]{1,0:T(8,128)(2,1)S(1)}, u32[]{:S(2)}, u32[]{:S(2)}) collective-permute-start(bf16[384,1024]{1,0:T(8,128)(2,1)S(1)} %get-tuple-element.72), channel_id=1, source_target_pairs={{0,8},{4,12},{8,0},{12,4},{16,24},{20,28},{24,16},{28,20},{1,9},{5... | collective-permute-start | bytes 2359304 | tf_op jit(solution)/shard_map/ppermute | solution.py:28
  106.9 56.8 %collective-permute-start.7 = (bf16[384,1536]{1,0:T(8,128)(2,1)S(1)}, bf16[384,1536]{1,0:T(8,128)(2,1)}, u32[]{:S(2)}, u32[]{:S(2)}) collective-permute-start(bf16[384,1536]{1,0:T(8,128)(2,1)S(1)} %collective-permute-done.2), channel_id=1, source_target_pairs={{0,3},{1,2},{2,1},{3,0},{4,7},{5,6},{6,5},{7,4},{8,11},{9,10},{10,... | collective-permute-start | bytes 3538952 | tf_op jit(solution)/shard_map/ppermute | solution.py:28
  109.3 54.3 %collective-permute-start.6 = (bf16[384,1536]{1,0:T(8,128)(2,1)S(1)}, bf16[384,1536]{1,0:T(8,128)(2,1)}, u32[]{:S(2)}, u32[]{:S(2)}) collective-permute-start(bf16[384,1536]{1,0:T(8,128)(2,1)S(1)} %collective-permute-done.2), channel_id=1, source_target_pairs={{0,2},{1,3},{2,0},{3,1},{4,6},{5,7},{6,4},{7,5},{8,10},{9,11},{10,... | collective-permute-start | bytes 3538952 | tf_op jit(solution)/shard_map/ppermute | solution.py:28
  109.8 53.8 %collective-permute-start.5 = (bf16[384,1536]{1,0:T(8,128)(2,1)S(1)}, bf16[384,1536]{1,0:T(8,128)(2,1)}, u32[]{:S(2)}, u32[]{:S(2)}) collective-permute-start(bf16[384,1536]{1,0:T(8,128)(2,1)S(1)} %collective-permute-done.2), channel_id=1, source_target_pairs={{0,1},{1,0},{2,3},{3,2},{4,5},{5,4},{6,7},{7,6},{8,9},{9,8},{10,11... | collective-permute-start | bytes 3538952 | tf_op jit(solution)/shard_map/ppermute | solution.py:28
  126.0 37.6 %collective-permute-start.8 = (bf16[384,1024]{1,0:T(8,128)(2,1)}, bf16[384,1024]{1,0:T(8,128)(2,1)}, u32[]{:S(2)}, u32[]{:S(2)}) collective-permute-start(bf16[384,1024]{1,0:T(8,128)(2,1)} %get-tuple-element.71), channel_id=1, source_target_pairs={{0,16},{4,20},{8,24},{12,28},{16,0},{20,4},{24,8},{28,12},{1,17},{... | collective-permute-start | bytes 2359304 | tf_op jit(solution)/shard_map/ppermute | solution.py:28
  130.2 33.5 %copy-start.15 = (bf16[384,1024]{1,0:T(8,128)(2,1)S(1)}, bf16[384,1024]{1,0:T(8,128)(2,1)}, u32[]{:S(2)}) copy-start(bf16[384,1024]{1,0:T(8,128)(2,1)} %get-tuple-element.81) | copy-start | bytes 2359300
  163.7 42.1 %collective-permute-start.11 = (bf16[384,1024]{1,0:T(8,128)(2,1)S(1)}, bf16[384,1024]{1,0:T(8,128)(2,1)S(1)}, u32[]{:S(2)}, u32[]{:S(2)}) collective-permute-start(bf16[384,1024]{1,0:T(8,128)(2,1)S(1)} %copy-done.15), channel_id=1, source_target_pairs={{0,16},{4,20},{8,24},{12,28},{16,0},{20,4},{24,8},{28,12},{1,17},{... | collective-permute-start | bytes 2359304 | tf_op jit(solution)/shard_map/ppermute | solution.py:28
  164.4 40.2 %collective-permute-start.12 = (bf16[384,1024]{1,0:T(8,128)(2,1)}, bf16[384,1024]{1,0:T(8,128)(2,1)S(1)}, u32[]{:S(2)}, u32[]{:S(2)}) collective-permute-start(bf16[384,1024]{1,0:T(8,128)(2,1)} %collective-permute-done.8), channel_id=1, source_target_pairs={{0,8},{4,12},{8,0},{12,4},{16,24},{20,28},{24,16},{28,20},{1,9},{5... | collective-permute-start | bytes 2359304 | tf_op jit(solution)/shard_map/ppermute | solution.py:28
  207.4 26.2 %collective-permute-start.13 = (bf16[1536,1024]{1,0:T(8,128)(2,1)}, bf16[1536,1024]{1,0:T(8,128)(2,1)}, u32[]{:S(2)}, u32[]{:S(2)}) collective-permute-start(bf16[1536,1024]{1,0:T(8,128)(2,1)} %constant_dynamic-update-slice_fusion.2), channel_id=1, source_target_pairs={{0,4},{4,0},{8,12},{12,8},{16,20},{20,16},{24,28},{28,24},{1,5},{5... | collective-permute-start | bytes 9437192 | tf_op jit(solution)/shard_map/ppermute | solution.py:28
  213.2 20.2 %collective-permute-start.14 = (bf16[384,1024]{1,0:T(8,128)(2,1)}, bf16[384,1024]{1,0:T(8,128)(2,1)S(1)}, u32[]{:S(2)}, u32[]{:S(2)}) collective-permute-start(bf16[384,1024]{1,0:T(8,128)(2,1)} %copy-done.16), channel_id=1, source_target_pairs={{0,8},{4,12},{8,0},{12,4},{16,24},{20,28},{24,16},{28,20},{1,9},{5... | collective-permute-start | bytes 2359304 | tf_op jit(solution)/shard_map/ppermute | solution.py:28
  215.2 18.2 %copy-start.17 = (bf16[384,1024]{1,0:T(8,128)(2,1)S(1)}, bf16[384,1024]{1,0:T(8,128)(2,1)}, u32[]{:S(2)}) copy-start(bf16[384,1024]{1,0:T(8,128)(2,1)} %copy-done.16) | copy-start | bytes 2359300
  233.7 34.9 %collective-permute-start.15 = (bf16[1536,1024]{1,0:T(8,128)(2,1)S(1)}, bf16[1536,1024]{1,0:T(8,128)(2,1)}, u32[]{:S(2)}, u32[]{:S(2)}) collective-permute-start(bf16[1536,1024]{1,0:T(8,128)(2,1)S(1)} %constant_dynamic-update-slice_fusion.4), channel_id=1, source_target_pairs={{0,4},{4,0},{8,12},{12,8},{16,20},{20,16},{24,28},{28,24},{1,5},{5... | collective-permute-start | bytes 9437192 | tf_op jit(solution)/shard_map/ppermute | solution.py:28
  271.5 14.5 %collective-permute-start.16 = (bf16[1536,1024]{1,0:T(8,128)(2,1)}, bf16[1536,1024]{1,0:T(8,128)(2,1)S(1)}, u32[]{:S(2)}, u32[]{:S(2)}) collective-permute-start(bf16[1536,1024]{1,0:T(8,128)(2,1)} %convolution_convert_fusion.4), channel_id=1, source_target_pairs={{0,4},{4,0},{8,12},{12,8},{16,20},{20,16},{24,28},{28,24},{1,5},{5... | collective-permute-start | bytes 9437192 | tf_op jit(solution)/shard_map/ppermute | solution.py:28
  314.9 20.4 %collective-permute-start.18 = (bf16[384,1024]{1,0:T(8,128)(2,1)S(1)}, bf16[384,1024]{1,0:T(8,128)(2,1)S(1)}, u32[]{:S(2)}, u32[]{:S(2)}) collective-permute-start(bf16[384,1024]{1,0:T(8,128)(2,1)S(1)} %get-tuple-element.168), channel_id=1, source_target_pairs={{0,8},{4,12},{8,0},{12,4},{16,24},{20,28},{24,16},{28,20},{1,9},{5... | collective-permute-start | bytes 2359304 | tf_op jit(solution)/shard_map/ppermute | solution.py:28
  315.2 36.5 %collective-permute-start.17 = (bf16[384,1024]{1,0:T(8,128)(2,1)S(1)}, bf16[384,1024]{1,0:T(8,128)(2,1)S(1)}, u32[]{:S(2)}, u32[]{:S(2)}) collective-permute-start(bf16[384,1024]{1,0:T(8,128)(2,1)S(1)} %get-tuple-element.169), channel_id=1, source_target_pairs={{0,8},{4,12},{8,0},{12,4},{16,24},{20,28},{24,16},{28,20},{1,9},{5... | collective-permute-start | bytes 2359304 | tf_op jit(solution)/shard_map/ppermute | solution.py:28
  353.3 42.7 %collective-permute-start.20 = (bf16[1536,1024]{1,0:T(8,128)(2,1)S(1)}, bf16[1536,1024]{1,0:T(8,128)(2,1)}, u32[]{:S(2)}, u32[]{:S(2)}) collective-permute-start(bf16[1536,1024]{1,0:T(8,128)(2,1)S(1)} %convolution_convert_fusion.3), channel_id=1, source_target_pairs={{0,4},{4,0},{8,12},{12,8},{16,20},{20,16},{24,28},{28,24},{1,5},{5... | collective-permute-start | bytes 9437192 | tf_op jit(solution)/shard_map/ppermute | solution.py:28
  353.3 42.7 %collective-permute-start.21 = (bf16[1536,1024]{1,0:T(8,128)(2,1)S(1)}, bf16[1536,1024]{1,0:T(8,128)(2,1)S(1)}, u32[]{:S(2)}, u32[]{:S(2)}) collective-permute-start(bf16[1536,1024]{1,0:T(8,128)(2,1)S(1)} %convolution_convert_fusion.2), channel_id=1, source_target_pairs={{0,4},{4,0},{8,12},{12,8},{16,20},{20,16},{24,28},{28,24},{1,5},{5... | collective-permute-start | bytes 9437192 | tf_op jit(solution)/shard_map/ppermute | solution.py:28
  354.3 27.9 %collective-permute-start.22 = (bf16[384,1536]{1,0:T(8,128)(2,1)S(1)}, bf16[384,1536]{1,0:T(8,128)(2,1)S(1)}, u32[]{:S(2)}, u32[]{:S(2)}) collective-permute-start(bf16[384,1536]{1,0:T(8,128)(2,1)S(1)} %pad_maximum_fusion.13), channel_id=1, source_target_pairs={{0,1},{1,0},{2,3},{3,2},{4,5},{5,4},{6,7},{7,6},{8,9},{9,8},{10,11... | collective-permute-start | bytes 3538952 | tf_op jit(solution)/shard_map/ppermute | solution.py:28
  356.1 27.7 %collective-permute-start.23 = (bf16[384,1536]{1,0:T(8,128)(2,1)S(1)}, bf16[384,1536]{1,0:T(8,128)(2,1)S(1)}, u32[]{:S(2)}, u32[]{:S(2)}) collective-permute-start(bf16[384,1536]{1,0:T(8,128)(2,1)S(1)} %pad_maximum_fusion.14), channel_id=1, source_target_pairs={{0,2},{1,3},{2,0},{3,1},{4,6},{5,7},{6,4},{7,5},{8,10},{9,11},{10,... | collective-permute-start | bytes 3538952 | tf_op jit(solution)/shard_map/ppermute | solution.py:28
  359.5 36.5 %collective-permute-start.19 = (bf16[384,1024]{1,0:T(8,128)(2,1)S(1)}, bf16[384,1024]{1,0:T(8,128)(2,1)S(1)}, u32[]{:S(2)}, u32[]{:S(2)}) collective-permute-start(bf16[384,1024]{1,0:T(8,128)(2,1)S(1)} %get-tuple-element.98), channel_id=1, source_target_pairs={{0,16},{4,20},{8,24},{12,28},{16,0},{20,4},{24,8},{28,12},{1,17},{... | collective-permute-start | bytes 2359304 | tf_op jit(solution)/shard_map/ppermute | solution.py:28
  401.6 15.3 %collective-permute-start.26 = (bf16[384,768]{1,0:T(8,128)(2,1)S(1)}, bf16[384,768]{1,0:T(8,128)(2,1)S(1)}, u32[]{:S(2)}, u32[]{:S(2)}) collective-permute-start(bf16[384,768]{1,0:T(8,128)(2,1)S(1)} %get-tuple-element.105), channel_id=1, source_target_pairs={{0,2},{1,3},{2,0},{3,1},{4,6},{5,7},{6,4},{7,5},{8,10},{9,11},{10,... | collective-permute-start | bytes 1769480 | tf_op jit(solution)/shard_map/ppermute | solution.py:28
  402.2 19.4 %collective-permute-start.27 = (bf16[384,768]{1,0:T(8,128)(2,1)S(1)}, bf16[384,768]{1,0:T(8,128)(2,1)S(1)}, u32[]{:S(2)}, u32[]{:S(2)}) collective-permute-start(bf16[384,768]{1,0:T(8,128)(2,1)S(1)} %get-tuple-element.107), channel_id=1, source_target_pairs={{0,1},{1,0},{2,3},{3,2},{4,5},{5,4},{6,7},{7,6},{8,9},{9,8},{10,11... | collective-permute-start | bytes 1769480 | tf_op jit(solution)/shard_map/ppermute | solution.py:28
  402.9 20.5 %collective-permute-start.25 = (bf16[384,1024]{1,0:T(8,128)(2,1)S(1)}, bf16[384,1024]{1,0:T(8,128)(2,1)S(1)}, u32[]{:S(2)}, u32[]{:S(2)}) collective-permute-start(bf16[384,1024]{1,0:T(8,128)(2,1)S(1)} %get-tuple-element.164), channel_id=1, source_target_pairs={{0,8},{4,12},{8,0},{12,4},{16,24},{20,28},{24,16},{28,20},{1,9},{5... | collective-permute-start | bytes 2359304 | tf_op jit(solution)/shard_map/ppermute | solution.py:28
  402.9 35.7 %collective-permute-start.24 = (bf16[384,1024]{1,0:T(8,128)(2,1)S(1)}, bf16[384,1024]{1,0:T(8,128)(2,1)S(1)}, u32[]{:S(2)}, u32[]{:S(2)}) collective-permute-start(bf16[384,1024]{1,0:T(8,128)(2,1)S(1)} %get-tuple-element.165), channel_id=1, source_target_pairs={{0,8},{4,12},{8,0},{12,4},{16,24},{20,28},{24,16},{28,20},{1,9},{5... | collective-permute-start | bytes 2359304 | tf_op jit(solution)/shard_map/ppermute | solution.py:28
  405.5 37.0 %collective-permute-start.28 = (bf16[384,1536]{1,0:T(8,128)(2,1)S(1)}, bf16[384,1536]{1,0:T(8,128)(2,1)S(1)}, u32[]{:S(2)}, u32[]{:S(2)}) collective-permute-start(bf16[384,1536]{1,0:T(8,128)(2,1)S(1)} %pad_maximum_fusion.15), channel_id=1, source_target_pairs={{0,1},{1,0},{2,3},{3,2},{4,5},{5,4},{6,7},{7,6},{8,9},{9,8},{10,11... | collective-permute-start | bytes 3538952 | tf_op jit(solution)/shard_map/ppermute | solution.py:28
  416.9 27.0 %collective-permute-start.29 = (bf16[384,1536]{1,0:T(8,128)(2,1)S(1)}, bf16[384,1536]{1,0:T(8,128)(2,1)S(1)}, u32[]{:S(2)}, u32[]{:S(2)}) collective-permute-start(bf16[384,1536]{1,0:T(8,128)(2,1)S(1)} %pad_maximum_fusion.16), channel_id=1, source_target_pairs={{0,2},{1,3},{2,0},{3,1},{4,6},{5,7},{6,4},{7,5},{8,10},{9,11},{10,... | collective-permute-start | bytes 3538952 | tf_op jit(solution)/shard_map/ppermute | solution.py:28
  445.4 14.3 %collective-permute-start.34 = (bf16[384,768]{1,0:T(8,128)(2,1)}, bf16[384,768]{1,0:T(8,128)(2,1)}, u32[]{:S(2)}, u32[]{:S(2)}) collective-permute-start(bf16[384,768]{1,0:T(8,128)(2,1)} %get-tuple-element.114), channel_id=1, source_target_pairs={{0,2},{1,3},{2,0},{3,1},{4,6},{5,7},{6,4},{7,5},{8,10},{9,11},{10,... | collective-permute-start | bytes 1769480 | tf_op jit(solution)/shard_map/ppermute | solution.py:28
  446.9 14.1 %collective-permute-start.35 = (bf16[384,768]{1,0:T(8,128)(2,1)}, bf16[384,768]{1,0:T(8,128)(2,1)S(1)}, u32[]{:S(2)}, u32[]{:S(2)}) collective-permute-start(bf16[384,768]{1,0:T(8,128)(2,1)} %get-tuple-element.116), channel_id=1, source_target_pairs={{0,1},{1,0},{2,3},{3,2},{4,5},{5,4},{6,7},{7,6},{8,9},{9,8},{10,11... | collective-permute-start | bytes 1769480 | tf_op jit(solution)/shard_map/ppermute | solution.py:28
  447.6 49.2 %collective-permute-start.32 = (bf16[384,1024]{1,0:T(8,128)(2,1)S(1)}, bf16[384,1024]{1,0:T(8,128)(2,1)S(1)}, u32[]{:S(2)}, u32[]{:S(2)}) collective-permute-start(bf16[384,1024]{1,0:T(8,128)(2,1)S(1)} %get-tuple-element.160), channel_id=1, source_target_pairs={{0,8},{4,12},{8,0},{12,4},{16,24},{20,28},{24,16},{28,20},{1,9},{5... | collective-permute-start | bytes 2359304 | tf_op jit(solution)/shard_map/ppermute | solution.py:28
  447.6 13.3 %copy-start.11 = (bf16[384,768]{1,0:T(8,128)(2,1)S(1)}, bf16[384,768]{1,0:T(8,128)(2,1)}, u32[]{:S(2)}) copy-start(bf16[384,768]{1,0:T(8,128)(2,1)} %get-tuple-element.115) | copy-start | bytes 1769476
  447.6 63.2 %collective-permute-start.31 = (bf16[384,1024]{1,0:T(8,128)(2,1)S(1)}, bf16[384,1024]{1,0:T(8,128)(2,1)S(1)}, u32[]{:S(2)}, u32[]{:S(2)}) collective-permute-start(bf16[384,1024]{1,0:T(8,128)(2,1)S(1)} %get-tuple-element.161), channel_id=1, source_target_pairs={{0,8},{4,12},{8,0},{12,4},{16,24},{20,28},{24,16},{28,20},{1,9},{5... | collective-permute-start | bytes 2359304 | tf_op jit(solution)/shard_map/ppermute | solution.py:28
  451.4 60.1 %collective-permute-start.33 = (bf16[384,768]{1,0:T(8,128)(2,1)S(1)}, bf16[384,768]{1,0:T(8,128)(2,1)S(1)}, u32[]{:S(2)}, u32[]{:S(2)}) collective-permute-start(bf16[384,768]{1,0:T(8,128)(2,1)S(1)} %copy-done.40), channel_id=1, source_target_pairs={{0,16},{4,20},{8,24},{12,28},{16,0},{20,4},{24,8},{28,12},{1,17},{... | collective-permute-start | bytes 1769480 | tf_op jit(solution)/shard_map/ppermute | solution.py:28
  459.7 52.0 %collective-permute-start.30 = (bf16[384,1024]{1,0:T(8,128)(2,1)S(1)}, bf16[384,1024]{1,0:T(8,128)(2,1)S(1)}, u32[]{:S(2)}, u32[]{:S(2)}) collective-permute-start(bf16[384,1024]{1,0:T(8,128)(2,1)S(1)} %copy-done.14), channel_id=1, source_target_pairs={{0,16},{4,20},{8,24},{12,28},{16,0},{20,4},{24,8},{28,12},{1,17},{... | collective-permute-start | bytes 2359304 | tf_op jit(solution)/shard_map/ppermute | solution.py:28
  461.1 50.6 %copy-start.9 = (bf16[384,768]{1,0:T(8,128)(2,1)S(1)}, bf16[384,768]{1,0:T(8,128)(2,1)}, u32[]{:S(2)}) copy-start(bf16[384,768]{1,0:T(8,128)(2,1)} %add_convert_fusion.19) | copy-start | bytes 1769476
  461.1 56.5 %copy-start.42 = (s32[768]{0:T(1024)S(1)}, s32[768]{0:T(1024)}, u32[]{:S(2)}) copy-start(s32[768]{0:T(1024)} %copy-done.41) | copy-start | bytes 9220
  461.1 56.5 %copy-start.46 = (pred[768]{0:T(1024)(128)(4,1)S(1)}, pred[768]{0:T(1024)(128)(4,1)}, u32[]{:S(2)}) copy-start(pred[768]{0:T(1024)(128)(4,1)} %copy-done.45) | copy-start | bytes 2308
  461.1 56.5 %copy-start.49 = (f32[384]{0:T(512)S(1)}, f32[384]{0:T(512)}, u32[]{:S(2)}) copy-start(f32[384]{0:T(512)} %copy-done.48) | copy-start | bytes 4612
  513.2 6.5 %collective-permute-start.37 = (f32[384]{0:T(512)S(1)}, f32[384]{0:T(512)S(1)}, u32[]{:S(2)}, u32[]{:S(2)}) collective-permute-start(f32[384]{0:T(512)S(1)} %multiply_reduce_fusion), channel_id=1, source_target_pairs={{0,1},{1,0},{2,3},{3,2},{4,5},{5,4},{6,7},{7,6},{8,9},{9,8},{10,11... | collective-permute-start | bytes 4616 | tf_op jit(solution)/shard_map/ppermute | solution.py:28
  514.7 41.8 %collective-permute-start.36 = (bf16[384,768]{1,0:T(8,128)(2,1)S(1)}, bf16[384,768]{1,0:T(8,128)(2,1)S(1)}, u32[]{:S(2)}, u32[]{:S(2)}) collective-permute-start(bf16[384,768]{1,0:T(8,128)(2,1)S(1)} %add_convert_fusion.12), channel_id=1, source_target_pairs={{0,16},{4,20},{8,24},{12,28},{16,0},{20,4},{24,8},{28,12},{1,17},{... | collective-permute-start | bytes 1769480 | tf_op jit(solution)/shard_map/ppermute | solution.py:28
  515.9 57.4 %collective-permute-start.39 = (bf16[384,1024]{1,0:T(8,128)(2,1)S(1)}, bf16[384,1024]{1,0:T(8,128)(2,1)S(1)}, u32[]{:S(2)}, u32[]{:S(2)}) collective-permute-start(bf16[384,1024]{1,0:T(8,128)(2,1)S(1)} %get-tuple-element.123), channel_id=1, source_target_pairs={{0,16},{4,20},{8,24},{12,28},{16,0},{20,4},{24,8},{28,12},{1,17},{... | collective-permute-start | bytes 2359304 | tf_op jit(solution)/shard_map/ppermute | solution.py:28
  519.6 3.6 collective-permute-start.38
  (47 other events, 206.2 us)

commit v3 on v1

v3 whole, which is shorter than its diff:
```python
import jax
import jax.numpy as jnp
from jax import lax
from jax.sharding import PartitionSpec as P

BF16 = jnp.bfloat16
F32 = jnp.float32


def dot(left, right, dims):
    return lax.dot_general(left, right, (dims, ((), ())), preferred_element_type=F32)


def mm(left, right):
    return dot(left, right, ((1,), (0,)))


def mm_last(left, right):
    return dot(left, right, ((1,), (1,)))


def mm_first(left, right):
    return dot(left, right, ((0,), (0,)))


def swap(value, axis, distance):
    size = lax.axis_size(axis)
    return lax.ppermute(value, axis, [(i, i ^ distance) for i in range(size)])


def fence(*values):
    return lax.optimization_barrier(values)


def select_rows(assign_block, combine_block, row_limit):
    expert_hit = assign_block == 0
    routed = jnp.any(expert_hit, axis=1)
    weight = jnp.sum(
        jnp.where(expert_hit, combine_block, jnp.zeros((), combine_block.dtype)), axis=1
    )
    place = jnp.cumsum(routed.astype(jnp.int32)) - 1
    match = routed[None, :] & (place[None, :] == jnp.arange(row_limit, dtype=jnp.int32)[:, None])
    row_weight = jnp.sum(jnp.where(match, weight[None, :], 0.0), axis=1)
    return (match, row_weight)


def join(mine, other, upper, axis):
    return jnp.where(
        upper == 0,
        jnp.concatenate([mine, other], axis=axis),
        jnp.concatenate([other, mine], axis=axis),
    )


def cat(*values):
    return jnp.concatenate(values, axis=0)


def beside(*values):
    return jnp.concatenate(values, axis=1)


def local(tokens, assign, combine, cotangent, w_gate, w_up, w_down_t):
    token_total, depth = tokens.shape
    row_limit = token_total // 2
    n_dp = lax.axis_size("dp")
    n_tensor = lax.axis_size("tensor")
    me = lax.axis_index("dp")
    me_t = lax.axis_index("tensor")
    chip, core = me // 2, me % 2
    far = n_dp // 2
    upper = me // far
    rows_w = w_gate.shape[0]
    pair = 2 * rows_w
    n_chip = n_dp // 2
    hid = w_gate.shape[1] // 4
    width = depth // n_tensor
    half = depth // 2
    mids = [1 << i for i in range(1, far.bit_length() - 1)]
    t_bits = [1 << i for i in range(n_tensor.bit_length() - 1)]

    def z_far(block):
        return swap(block, "dp", far)

    def across(block):
        return swap(block, "dp", 1)

    def grow(block):
        for bit in mids:
            block = cat(block, swap(block, "dp", bit))
        return block

    def shrink(value):
        for bit in mids[::-1]:
            size = value.shape[0] // 2
            got = swap(value[size:], "dp", bit)
            value = (value[:size].astype(F32) + got.astype(F32)).astype(BF16)
        return value

    def part(w, u, c):
        return lax.dynamic_slice_in_dim(w, (u * 2 + c) * hid, hid, 1)

    def to_sibling(w):
        return beside(part(w, upper, 1 - core), part(w, 1 - upper, 1 - core))

    def pair_rows(w, got):
        mine = join(part(w, upper, core), got[:, :hid], core, 0)
        other = join(part(w, 1 - upper, core), got[:, hid:], core, 0)
        return mine, other

    wide = 2 * hid
    gate_0 = lax.dynamic_slice_in_dim(w_gate, upper * wide, wide, 1)
    gate_4 = z_far(lax.dynamic_slice_in_dim(w_gate, (1 - upper) * wide, wide, 1))
    gate_own = grow(gate_0)
    match, row_weight = select_rows(assign, combine, row_limit)
    hot = match.astype(BF16)
    rows_in = mm(hot, tokens).astype(BF16)
    rows_grad = mm(hot, cotangent).astype(BF16)
    out_grad = (row_weight[:, None] * rows_grad.astype(F32)).astype(BF16)
    quarter = beside(
        *(lax.dynamic_slice_in_dim(v, me_t * width, width, 1) for v in (rows_in, out_grad))
    )
    near = jnp.zeros((2 * row_limit, depth), BF16)
    for i, value in enumerate((rows_in, out_grad)):
        for j in range(n_chip):
            block = lax.dynamic_slice_in_dim(value, (chip ^ j) * pair, pair, 1)
            near = lax.dynamic_update_slice(near, block, (i * row_limit, j * pair))
    send = cat(to_sibling(w_up), to_sibling(w_down_t))
    gate_4, gate_own, quarter, near, send = fence(gate_4, gate_own, quarter, near, send)

    quarter = z_far(quarter)
    gate_far = grow(gate_4)
    near_sib = across(near)
    got = across(send)
    up_0, up_1 = pair_rows(w_up, got[:rows_w])
    down_0, down_1 = pair_rows(w_down_t, got[rows_w:])
    quarter, gate_far, near_sib, up_0, up_1, down_0, down_1 = fence(
        quarter, gate_far, near_sib, up_0, up_1, down_0, down_1
    )

    up_4 = z_far(up_1)
    own = grow(beside(up_0, down_0))
    quarters = [quarter] + [swap(quarter, "tensor", k) for k in range(1, n_tensor)]
    gate_all = cat(gate_own, gate_far)
    gate_mine = lax.dynamic_slice_in_dim(gate_all, core * hid, hid, 1)
    gate_send = lax.dynamic_slice_in_dim(gate_all, (1 - core) * hid, hid, 1)
    up_4, own, gate_mine, gate_send, down_1, *quarters = fence(
        up_4, own, gate_mine, gate_send, down_1, *quarters
    )
    up_own, down_own = own[:, :hid], own[:, hid:]

    up_far = grow(up_4)
    down_4 = z_far(down_1)
    gate = join(
        gate_mine.reshape(n_chip, rows_w, hid),
        across(gate_send).reshape(n_chip, rows_w, hid),
        core,
        1,
    ).reshape(depth, hid)
    away = jnp.zeros((2 * row_limit, depth), BF16)
    for i in range(2):
        for k, piece in enumerate(quarters):
            for q in range(width // pair):
                block = piece[:, i * width + q * pair : i * width + (q + 1) * pair]
                place = ((me_t ^ k) * (width // pair) + q) ^ chip
                away = lax.dynamic_update_slice(away, block, (i * row_limit, place * pair))
    away_sib = across(away)
    in_all = cat(near[:row_limit], away[:row_limit], near_sib[:row_limit], away_sib[:row_limit])
    gate_pre = mm(in_all, gate)
    up_far, down_4, in_all, gate_pre, away, away_sib, gate = fence(
        up_far, down_4, in_all, gate_pre, away, away_sib, gate
    )

    down_far = grow(down_4)
    up = cat(up_own, up_far)
    out_all = cat(near[row_limit:], away[row_limit:], near_sib[row_limit:], away_sib[row_limit:])
    up_pre = mm(in_all, up)
    sigmoid_gate = jax.nn.sigmoid(gate_pre)
    hidden = (gate_pre * sigmoid_gate * up_pre).astype(BF16)
    g_down = mm_first(out_all, hidden).astype(BF16)
    g_down, hidden, up_pre, down_far, out_all, up = fence(
        g_down, hidden, up_pre, down_far, out_all, up
    )

    g_down_4 = shrink(g_down[half:])
    g_down_own = shrink(g_down[:half])
    down = cat(down_own, down_far)
    hidden_grad = mm(out_all, down)
    gate_grad = (
        hidden_grad * up_pre * sigmoid_gate * (1.0 + gate_pre * (1.0 - sigmoid_gate))
    ).astype(BF16)
    up_grad = (hidden_grad * gate_pre * sigmoid_gate).astype(BF16)
    g_gate = mm_first(in_all, gate_grad).astype(BF16)
    g_up = mm_first(in_all, up_grad).astype(BF16)
    table = 2 * row_limit
    expert_got = across(mm_last(hidden[table:], down).astype(BF16))
    g_down_4, g_down_own, down, gate_grad, up_grad, g_gate, g_up, expert_got = fence(
        g_down_4, g_down_own, down, gate_grad, up_grad, g_gate, g_up, expert_got
    )

    def features(value, rank):
        count = width // pair
        return beside(
            *(
                lax.dynamic_slice_in_dim(value, ((rank * count + q) ^ chip) * pair, pair, 1)
                for q in range(count)
            )
        )

    def split_parts(value):
        return {k: features(value, me_t ^ k) for k in range(n_tensor)}

    def tensor_step(parts, bit):
        gone = [k for k in parts if k & bit]
        kept = [k for k in parts if not k & bit]
        got = swap(beside(*(parts[k] for k in gone)), "tensor", bit)
        return {
            k: (parts[k].astype(F32) + got[:, i * width : (i + 1) * width].astype(F32)).astype(BF16)
            for i, k in enumerate(kept)
        }

    def steps_1(value):
        return (
            tensor_step(split_parts(value[:row_limit]), t_bits[0]),
            tensor_step(split_parts(value[row_limit:]), t_bits[-1]),
        )

    def steps_2(mine, other):
        for bit in t_bits[1:]:
            mine = tensor_step(mine, bit)
        for bit in t_bits[:-1][::-1]:
            other = tensor_step(other, bit)
        return mine[0], other[0]

    def panel(own, other):
        both = beside(own, other)
        mine = lax.dynamic_slice_in_dim(both, core * rows_w, rows_w, 0)
        got = across(lax.dynamic_slice_in_dim(both, (1 - core) * rows_w, rows_w, 0))
        whole = jnp.zeros((rows_w, 4 * hid), BF16)
        for block, u, c in (
            (mine[:, :hid], upper, core),
            (mine[:, hid:], 1 - upper, core),
            (got[:, :hid], upper, 1 - core),
            (got[:, hid:], 1 - upper, 1 - core),
        ):
            whole = lax.dynamic_update_slice(whole, block, (0, (u * 2 + c) * hid))
        return whole

    g_down_far = z_far(g_down_4)
    g_gate_4 = shrink(g_gate[half:])
    expert_sum = (mm_last(hidden[:table], down) + expert_got.astype(F32)).astype(BF16)
    expert_mine, expert_other = steps_2(*steps_1(expert_sum))
    input_got = across(
        (mm_last(gate_grad[table:], gate) + mm_last(up_grad[table:], up)).astype(BF16)
    )
    input_sum = (
        mm_last(gate_grad[:table], gate)
        + mm_last(up_grad[:table], up)
        + input_got.astype(F32)
    ).astype(BF16)
    g_down_far, g_gate_4, expert_mine, expert_other, input_sum, g_gate, g_up = fence(
        g_down_far, g_gate_4, expert_mine, expert_other, input_sum, g_gate, g_up
    )

    g_gate_far = z_far(g_gate_4)
    g_up_4 = shrink(g_up[half:])
    input_mine, input_other = steps_1(input_sum)
    down_out = panel(g_down_own, g_down_far)
    g_gate_far, g_up_4, input_mine, input_other, g_gate, g_up, down_out = fence(
        g_gate_far, g_up_4, input_mine, input_other, g_gate, g_up, down_out
    )

    g_up_far = z_far(g_up_4)
    g_gate_own = shrink(g_gate[:half])
    expert_got = z_far(expert_other)
    input_mine, input_other = steps_2(input_mine, input_other)
    g_up_far, g_gate_own, expert_got, input_mine, input_other, g_up = fence(
        g_up_far, g_gate_own, expert_got, input_mine, input_other, g_up
    )

    g_up_own = shrink(g_up[:half])
    input_got = z_far(input_other)
    expert_cols = expert_mine.astype(F32) + expert_got.astype(F32)
    grad_cols = lax.dynamic_slice_in_dim(rows_grad, me_t * width, width, 1)
    weight_rows = jnp.sum(grad_cols.astype(F32) * expert_cols, axis=1)
    for bit in t_bits:
        weight_rows = weight_rows + swap(weight_rows, "tensor", bit)
    weight_grad = jnp.sum(jnp.where(match, weight_rows[:, None], 0.0), axis=0)
    mixed = mm_first(hot, (row_weight[:, None] * expert_cols).astype(BF16)).astype(BF16)
    input_cols = (input_mine.astype(F32) + input_got.astype(F32)).astype(BF16)
    input_grad = mm_first(hot, input_cols).astype(BF16)
    return (
        mixed,
        input_grad,
        weight_grad,
        panel(g_gate_own, g_gate_far),
        panel(g_up_own, g_up_far),
        down_out,
    )


def solution(mesh):
    return jax.shard_map(
        local,
        mesh=mesh,
        in_specs=(
            P("dp", None),
            P("dp", None),
            P("dp", None),
            P("dp", None),
            P("dp", "tensor"),
            P("dp", "tensor"),
            P("dp", "tensor"),
        ),
        out_specs=(
            P("dp", "tensor"),
            P("dp", "tensor"),
            P("dp"),
            P("dp", "tensor"),
            P("dp", "tensor"),
            P("dp", "tensor"),
        ),
        check_vma=False,
    )
```

time: 765 us -> 497 us (0.65)
  waiting for transfers between devices: 566 us -> 263 us
  local copies, waits for them, and re-layouts: 15 us -> 65.1 us
  matrix products: 110 us -> 83 us
  between operations: 15.1 us -> 2.14 us
  other arithmetic: 22.1 us -> 33.9 us
  starting transfers between devices: 32.9 us -> 41 us
    reduce_scatter x6 -> x0, waiting for transfers between devices: 170 us -> none  [scatter_half(): lax.psum_scatter(value, 'dp', scatter_dimension=0, tiled=True, axis_index...]
    all_gather x6 -> x0, waiting for transfers between devices: 91.3 us -> none  [gather_half(): lax.all_gather(value, 'dp', axis=0, tiled=True, axis_index_groups=groups)]
    ppermute x26 -> x42, waiting for transfers between devices: 303 us -> 263 us  [swap(): return lax.ppermute(value, axis, [(i, i ^ distance) for i in range(size)])]
    dot_general x22 -> x16, matrix products: 110 us -> 83 us  [dot(): lax.dot_general(left, right, (dims, ((), ())), preferred_element_type=F32)]
    dynamic_update_slice x8 -> x28, local copies, waits for them, and re-layouts: 2.67 us -> 25.6 us  [the longest x8 15.8 us: local(): away = lax.dynamic_update_slice(away, block, (i * row_limit, place * pair))]
    slice x3 -> x16, local copies, waits for them, and re-layouts: 0.72 us -> 20.5 us  [the longest x5 3.46 us: shrink(): got = swap(value[size:], 'dp', bit)]
    concatenate x5 -> x16, other arithmetic: 2.85 us -> 14 us  [the longest x10 12.4 us: cat(): return jnp.concatenate(values, axis=0)]
    select_n x5, other arithmetic: 13.6 us -> 4.01 us  [join(): jnp.where(upper == 0, jnp.concatenate([mine, other], axis=axis), jnp.conc...]
  transfers between devices with their start and end apart: 38 -> 42, of which waited for: 24 -> 22; matrix products, arithmetic and copies ran while one was open for 15% -> 30% of each run, Pallas kernels for 0% -> 0%
where the time goes in v3:
time: 497 us; the launch traced here: 488 us
  waiting for transfers between devices  263 us (53%)
  matrix products  83 us (17%)
  local copies, waits for them, and re-layouts  65.1 us (13%)
  starting transfers between devices  41 us (8%)
  other arithmetic  33.9 us (7%)
    ppermute x42, waiting for transfers between devices, swap(): return lax.ppermute(value, axis, [(i, i ^ distance) for i in range(size)])  263 us
    dot_general x16, matrix products, dot(): lax.dot_general(left, right, (dims, ((), ())), preferred_element_type=F32)  83 us
    ppermute x42, starting transfers between devices, swap(): return lax.ppermute(value, axis, [(i, i ^ distance) for i in range(size)])  41 us
    dynamic_update_slice x8, local copies, waits for them, and re-layouts, local(): away = lax.dynamic_update_slice(away, block, (i * row_limit, place * pair))  15.8 us
    concatenate x10, other arithmetic, cat(): return jnp.concatenate(values, axis=0)  12.4 us
  transfers between devices with their start and end apart: 42, of which 22 were waited for; matrix products, arithmetic and copies ran while one was open for 30% of the time, Pallas kernels for 0%

profile of v3, /device:TPU:0, one launch (start us, length us, event | category | flops | bytes accessed | tf_op | source)
XLA Modules:
  0.0 488.5 jit_solution(10313234665414291922)
XLA Ops:
  0.7 2.4 constant_dynamic-slice_fusion.23
  3.1 4.0 collective-permute-start
  9.3 4.3 convolution_convert_fusion.5
  14.0 2.7 dynamic_update_slice.84
  18.6 5.8 %multiply_convert_fusion = (bf16[384,3072]{1,0:T(8,128)(2,1)S(1)}, bf16[384,3072]{1,0:T(8,128)(2,1)}) fusion(f32[384]{0:T(512)S(1)} %select_reduce_fusion.1, bf16[768,3072]{1,0:T(8,128)(2,1)} %param.10, s32[768]{0:T(1024)S(1)} %add_bitcast_fusion, pred[768]{0:T(1024)(128)(4,1)S(1)} %fusion.25), kind=kOutput, calls=%fused_computation.6 | convolution fusion | flops 1817247744 | bytes 9442560 | tf_op jit(solution)/shard_map/dot_general | solution.py:11
  29.3 3.0 constant_dynamic-slice_fusion.12
  34.8 6.2 %collective-permute-done.1 = bf16[384,1024]{1,0:T(8,128)(2,1)} collective-permute-done((bf16[384,1024]{1,0:T(8,128)(2,1)S(1)}, bf16[384,1024]{1,0:T(8,128)(2,1)}, u32[]{:S(2)}, u32[]{:S(2)}) %collective-permute-start.1) | collective-permute-done | bytes 786464 | tf_op jit(solution)/shard_map/ppermute | solution.py:28
  42.8 2.6 collective-permute-start.3
  46.4 32.7 %collective-permute-done.3 = bf16[384,1024]{1,0:T(8,128)(2,1)} collective-permute-done((bf16[384,1024]{1,0:T(8,128)(2,1)}, bf16[384,1024]{1,0:T(8,128)(2,1)}, u32[]{:S(2)}, u32[]{:S(2)}) %collective-permute-start.3) | collective-permute-done | bytes 786464 | tf_op jit(solution)/shard_map/ppermute | solution.py:28
  85.3 14.4 %collective-permute-done.2 = bf16[384,1536]{1,0:T(8,128)(2,1)} collective-permute-done((bf16[384,1536]{1,0:T(8,128)(2,1)}, bf16[384,1536]{1,0:T(8,128)(2,1)}, u32[]{:S(2)}, u32[]{:S(2)}) %collective-permute-start.2) | collective-permute-done | bytes 1179680 | tf_op jit(solution)/shard_map/ppermute | solution.py:28
  108.2 2.0 constant_dynamic-slice_fusion.10
  110.2 43.7 %collective-permute-done.7 = bf16[768,1024]{1,0:T(8,128)(2,1)} collective-permute-done((bf16[768,1024]{1,0:T(8,128)(2,1)}, bf16[768,1024]{1,0:T(8,128)(2,1)}, u32[]{:S(2)}, u32[]{:S(2)}) %collective-permute-start.7) | collective-permute-done | bytes 1572896 | tf_op jit(solution)/shard_map/ppermute | solution.py:28
  153.9 2.2 pad_maximum_fusion.2
  156.2 2.8 broadcast.36
  162.9 2.0 slice_dynamic-update-slice_fusion.5
  168.9 2.0 slice_dynamic-update-slice_fusion.2
  170.8 2.0 slice_dynamic-update-slice_fusion.1
  174.8 2.8 fusion.30
  178.7 2.7 fusion.31
  186.5 21.9 %collective-permute-done.11 = bf16[768,512]{1,0:T(8,128)(2,1)S(1)} collective-permute-done((bf16[768,512]{1,0:T(8,128)(2,1)S(1)}, bf16[768,512]{1,0:T(8,128)(2,1)S(1)}, u32[]{:S(2)}, u32[]{:S(2)}) %collective-permute-start.11) | collective-permute-done | bytes 786464 | tf_op jit(solution)/shard_map/ppermute | solution.py:28
  212.8 6.9 %fusion.35 = f32[1536,512]{1,0:T(8,128)} fusion(bf16[1536,3072]{1,0:T(8,128)(2,1)S(1)} %pad_maximum_fusion, bf16[3072,512]{1,0:T(8,128)(2,1)S(1)} %bitcast.24), kind=kOutput, calls=%fused_computation.161 | convolution fusion | flops 4831838208 | bytes 15728640 | tf_op jit(solution)/shard_map/dot_general | solution.py:11
  226.1 8.6 %multiply_convert_fusion.3 = (bf16[1536,512]{1,0:T(8,128)(2,1)S(1)}, f32[1536,512]{1,0:T(8,128)}) fusion(f32[1536,512]{1,0:T(8,128)} %fusion.35, bf16[1536,3072]{1,0:T(8,128)(2,1)S(1)} %pad_maximum_fusion, bf16[1536,512]{1,0:T(8,128)(2,1)S(1)} %pad_maximum_fusion.7, bf16[1536,512]{1,0:T(8,128)(2,1)S(1)} %copy-done.1), kind=kOutput, calls=%fused_computation.18 | convolution fusion | flops 4842848256 | bytes 20447232 | tf_op jit(solution)/shard_map/dot_general | solution.py:11
  234.8 5.5 %convolution_convert_fusion.3 = bf16[3072,512]{1,0:T(8,128)(2,1)S(1)} fusion(bf16[1536,3072]{1,0:T(8,128)(2,1)S(1)} %pad_maximum_fusion.1, bf16[1536,512]{1,0:T(8,128)(2,1)S(1)} %get-tuple-element.101), kind=kOutput, calls=%fused_computation.9 | convolution fusion | flops 4833411072 | bytes 14155776 | tf_op jit(solution)/shard_map/dot_general | solution.py:11
  240.3 2.0 pad_maximum_fusion.3
  248.4 6.5 %convolution_convert_fusion = bf16[768,3072]{1,0:T(8,128)(2,1)} fusion(bf16[1536,512]{1,0:T(8,128)(2,1)S(1)} %copy-done.37, bf16[1536,512]{1,0:T(8,128)(2,1)S(1)} %pad_maximum_fusion.8, bf16[1536,512]{1,0:T(8,128)(2,1)S(1)} %copy-done), kind=kOutput, calls=%fused_computation.5 | convolution fusion | flops 2424569856 | bytes 8650752 | tf_op jit(solution)/shard_map/dot_general | solution.py:11
  254.8 9.5 %multiply_convert_fusion.1 = (bf16[1536,512]{1,0:T(8,128)(2,1)}, bf16[1536,512]{1,0:T(8,128)(2,1)}) fusion(f32[1536,512]{1,0:T(8,128)} %fusion.35, f32[1536,512]{1,0:T(8,128)} %get-tuple-element.100, bf16[1536,3072]{1,0:T(8,128)(2,1)S(1)} %pad_maximum_fusion.1, bf16[1536,512]{1,0:T(8,128)(2,1)S(1)} %pad_maximum_fusion.8, bf16[1536,512]{1,0:T(8,128)(2,1)S(1)} %copy-done), kind=kOutput, calls=%fused_computation.16 | convolution fusion | flops 4848353280 | bytes 22020096 | tf_op jit(solution)/shard_map/dot_general | solution.py:11
  264.4 7.0 %convolution_convert_fusion.2 = bf16[3072,512]{1,0:T(8,128)(2,1)S(1)} fusion(bf16[1536,3072]{1,0:T(8,128)(2,1)S(1)} %pad_maximum_fusion, bf16[1536,512]{1,0:T(8,128)(2,1)} %get-tuple-element.106), kind=kOutput, calls=%fused_computation.8 | convolution fusion | flops 4833411072 | bytes 14155776 | tf_op jit(solution)/shard_map/dot_general | solution.py:11
  271.4 6.8 %convolution_convert_fusion.1 = bf16[3072,512]{1,0:T(8,128)(2,1)} fusion(bf16[1536,3072]{1,0:T(8,128)(2,1)S(1)} %pad_maximum_fusion, bf16[1536,512]{1,0:T(8,128)(2,1)S(1)} %copy-done.35), kind=kOutput, calls=%fused_computation.7 | convolution fusion | flops 4833411072 | bytes 14155776 | tf_op jit(solution)/shard_map/dot_general | solution.py:11
  278.5 2.9 collective-permute-done.16
  285.1 2.6 fusion.7
  287.8 4.4 add_convert_fusion.1
  292.2 4.6 add_convert_fusion.2
  300.0 2.6 fusion.12
  302.6 3.8 fusion.10
  306.4 2.1 collective-permute-start.19
  308.5 17.3 %collective-permute-done.21 = bf16[384,1536]{1,0:T(8,128)(2,1)S(1)} collective-permute-done((bf16[384,1536]{1,0:T(8,128)(2,1)S(1)}, bf16[384,1536]{1,0:T(8,128)(2,1)S(1)}, u32[]{:S(2)}, u32[]{:S(2)}) %collective-permute-start.21) | collective-permute-done | bytes 1179680 | tf_op jit(solution)/shard_map/ppermute | solution.py:28
  329.5 2.5 add_convert_fusion.6
  331.9 9.1 %collective-permute-done.22 = bf16[384,768]{1,0:T(8,128)(2,1)S(1)} collective-permute-done((bf16[384,768]{1,0:T(8,128)(2,1)S(1)}, bf16[384,768]{1,0:T(8,128)(2,1)S(1)}, u32[]{:S(2)}, u32[]{:S(2)}) %collective-permute-start.22) | collective-permute-done | bytes 589856 | tf_op jit(solution)/shard_map/ppermute | solution.py:28
  343.5 4.7 add_convert_fusion
  356.7 28.3 %collective-permute-done.27 = bf16[768,512]{1,0:T(8,128)(2,1)S(1)} collective-permute-done((bf16[768,512]{1,0:T(8,128)(2,1)S(1)}, bf16[768,512]{1,0:T(8,128)(2,1)S(1)}, u32[]{:S(2)}, u32[]{:S(2)}) %collective-permute-start.27) | collective-permute-done | bytes 786464 | tf_op jit(solution)/shard_map/ppermute | solution.py:28
  390.4 2.4 collective-permute-start.31
  392.8 6.4 %collective-permute-done.34 = bf16[384,768]{1,0:T(8,128)(2,1)S(1)} collective-permute-done((bf16[384,768]{1,0:T(8,128)(2,1)S(1)}, bf16[384,768]{1,0:T(8,128)(2,1)S(1)}, u32[]{:S(2)}, u32[]{:S(2)}) %collective-permute-start.34) | collective-permute-done | bytes 589856 | tf_op jit(solution)/shard_map/ppermute | solution.py:28
  400.4 20.6 %collective-permute-done.32 = bf16[768,512]{1,0:T(8,128)(2,1)S(1)} collective-permute-done((bf16[768,512]{1,0:T(8,128)(2,1)S(1)}, bf16[768,512]{1,0:T(8,128)(2,1)S(1)}, u32[]{:S(2)}, u32[]{:S(2)}) %collective-permute-start.32) | collective-permute-done | bytes 786464 | tf_op jit(solution)/shard_map/ppermute | solution.py:28
  421.3 15.3 %collective-permute-done.33 = bf16[384,768]{1,0:T(8,128)(2,1)S(1)} collective-permute-done((bf16[384,768]{1,0:T(8,128)(2,1)S(1)}, bf16[384,768]{1,0:T(8,128)(2,1)S(1)}, u32[]{:S(2)}, u32[]{:S(2)}) %collective-permute-start.33) | collective-permute-done | bytes 589856 | tf_op jit(solution)/shard_map/ppermute | solution.py:28
  436.6 20.7 %collective-permute-done.31 = bf16[768,512]{1,0:T(8,128)(2,1)S(1)} collective-permute-done((bf16[768,512]{1,0:T(8,128)(2,1)S(1)}, bf16[768,512]{1,0:T(8,128)(2,1)S(1)}, u32[]{:S(2)}, u32[]{:S(2)}) %collective-permute-start.31) | collective-permute-done | bytes 786464 | tf_op jit(solution)/shard_map/ppermute | solution.py:28
  465.0 2.9 collective-permute-done.38
  468.8 5.9 %collective-permute-done.36 = bf16[384,768]{1,0:T(8,128)(2,1)S(1)} collective-permute-done((bf16[384,768]{1,0:T(8,128)(2,1)S(1)}, bf16[384,768]{1,0:T(8,128)(2,1)S(1)}, u32[]{:S(2)}, u32[]{:S(2)}) %collective-permute-start.36) | collective-permute-done | bytes 589856 | tf_op jit(solution)/shard_map/ppermute | solution.py:28
  476.5 7.4 %collective-permute-done.40 = bf16[768,512]{1,0:T(8,128)(2,1)S(1)} collective-permute-done((bf16[768,512]{1,0:T(8,128)(2,1)S(1)}, bf16[768,512]{1,0:T(8,128)(2,1)S(1)}, u32[]{:S(2)}, u32[]{:S(2)}) %collective-permute-start.40) | collective-permute-done | bytes 786464 | tf_op jit(solution)/shard_map/ppermute | solution.py:28
  (243 shorter events, 104.5 us)
Async XLA Ops:
  3.1 39.2 %collective-permute-start = (bf16[384,1024]{1,0:T(8,128)(2,1)}, bf16[384,1024]{1,0:T(8,128)(2,1)}, u32[]{:S(2)}, u32[]{:S(2)}) collective-permute-start(bf16[384,1024]{1,0:T(8,128)(2,1)} %get-tuple-element.183), channel_id=1, source_target_pairs={{0,16},{4,20},{8,24},{12,28},{16,0},{20,4},{24,8},{28,12},{1,17},{... | collective-permute-start | bytes 2359304 | tf_op jit(solution)/shard_map/ppermute | solution.py:28
  7.1 33.9 %collective-permute-start.1 = (bf16[384,1024]{1,0:T(8,128)(2,1)S(1)}, bf16[384,1024]{1,0:T(8,128)(2,1)}, u32[]{:S(2)}, u32[]{:S(2)}) collective-permute-start(bf16[384,1024]{1,0:T(8,128)(2,1)S(1)} %get-tuple-element.182), channel_id=1, source_target_pairs={{0,8},{4,12},{8,0},{12,4},{16,24},{20,28},{24,16},{28,20},{1,9},{5... | collective-permute-start | bytes 2359304 | tf_op jit(solution)/shard_map/ppermute | solution.py:28
  42.3 57.4 %collective-permute-start.4 = (bf16[768,3072]{1,0:T(8,128)(2,1)}, bf16[768,3072]{1,0:T(8,128)(2,1)}, u32[]{:S(2)}, u32[]{:S(2)}) collective-permute-start(bf16[768,3072]{1,0:T(8,128)(2,1)} %get-tuple-element.70), channel_id=1, source_target_pairs={{0,4},{4,0},{8,12},{12,8},{16,20},{20,16},{24,28},{28,24},{1,5},{5... | collective-permute-start | bytes 14155784 | tf_op jit(solution)/shard_map/ppermute | solution.py:28
  42.3 38.3 %collective-permute-start.5 = (bf16[768,1024]{1,0:T(8,128)(2,1)}, bf16[768,1024]{1,0:T(8,128)(2,1)}, u32[]{:S(2)}, u32[]{:S(2)}) collective-permute-start(bf16[768,1024]{1,0:T(8,128)(2,1)} %maximum_maximum_fusion), channel_id=1, source_target_pairs={{0,4},{4,0},{8,12},{12,8},{16,20},{20,16},{24,28},{28,24},{1,5},{5... | collective-permute-start | bytes 4718600 | tf_op jit(solution)/shard_map/ppermute | solution.py:28
  42.8 36.3 %collective-permute-start.3 = (bf16[384,1024]{1,0:T(8,128)(2,1)}, bf16[384,1024]{1,0:T(8,128)(2,1)}, u32[]{:S(2)}, u32[]{:S(2)}) collective-permute-start(bf16[384,1024]{1,0:T(8,128)(2,1)} %collective-permute-done), channel_id=1, source_target_pairs={{0,8},{4,12},{8,0},{12,4},{16,24},{20,28},{24,16},{28,20},{1,9},{5... | collective-permute-start | bytes 2359304 | tf_op jit(solution)/shard_map/ppermute | solution.py:28
  45.4 54.2 %collective-permute-start.2 = (bf16[384,1536]{1,0:T(8,128)(2,1)}, bf16[384,1536]{1,0:T(8,128)(2,1)}, u32[]{:S(2)}, u32[]{:S(2)}) collective-permute-start(bf16[384,1536]{1,0:T(8,128)(2,1)} %pad_maximum_fusion.9), channel_id=1, source_target_pairs={{0,16},{4,20},{8,24},{12,28},{16,0},{20,4},{24,8},{28,12},{1,17},{... | collective-permute-start | bytes 3538952 | tf_op jit(solution)/shard_map/ppermute | solution.py:28
  101.5 52.4 %collective-permute-start.7 = (bf16[768,1024]{1,0:T(8,128)(2,1)}, bf16[768,1024]{1,0:T(8,128)(2,1)}, u32[]{:S(2)}, u32[]{:S(2)}) collective-permute-start(bf16[768,1024]{1,0:T(8,128)(2,1)} %constant_dynamic-update-slice_fusion), channel_id=1, source_target_pairs={{0,8},{4,12},{8,0},{12,4},{16,24},{20,28},{24,16},{28,20},{1,9},{5... | collective-permute-start | bytes 4718600 | tf_op jit(solution)/shard_map/ppermute | solution.py:28
  101.5 54.6 %collective-permute-start.8 = (bf16[384,1536]{1,0:T(8,128)(2,1)}, bf16[384,1536]{1,0:T(8,128)(2,1)}, u32[]{:S(2)}, u32[]{:S(2)}) collective-permute-start(bf16[384,1536]{1,0:T(8,128)(2,1)} %collective-permute-done.2), channel_id=1, source_target_pairs={{0,1},{1,0},{2,3},{3,2},{4,5},{5,4},{6,7},{7,6},{8,9},{9,8},{10,11... | collective-permute-start | bytes 3538952 | tf_op jit(solution)/shard_map/ppermute | solution.py:28
  103.0 53.2 %collective-permute-start.9 = (bf16[384,1536]{1,0:T(8,128)(2,1)}, bf16[384,1536]{1,0:T(8,128)(2,1)}, u32[]{:S(2)}, u32[]{:S(2)}) collective-permute-start(bf16[384,1536]{1,0:T(8,128)(2,1)} %collective-permute-done.2), channel_id=1, source_target_pairs={{0,2},{1,3},{2,0},{3,1},{4,6},{5,7},{6,4},{7,5},{8,10},{9,11},{10,... | collective-permute-start | bytes 3538952 | tf_op jit(solution)/shard_map/ppermute | solution.py:28
  104.5 51.7 %collective-permute-start.10 = (bf16[384,1536]{1,0:T(8,128)(2,1)}, bf16[384,1536]{1,0:T(8,128)(2,1)}, u32[]{:S(2)}, u32[]{:S(2)}) collective-permute-start(bf16[384,1536]{1,0:T(8,128)(2,1)} %collective-permute-done.2), channel_id=1, source_target_pairs={{0,3},{1,2},{2,1},{3,0},{4,7},{5,6},{6,5},{7,4},{8,11},{9,10},{10,... | collective-permute-start | bytes 3538952 | tf_op jit(solution)/shard_map/ppermute | solution.py:28
  106.1 50.0 %collective-permute-start.6 = (bf16[768,512]{1,0:T(8,128)(2,1)S(1)}, bf16[768,512]{1,0:T(8,128)(2,1)S(1)}, u32[]{:S(2)}, u32[]{:S(2)}) collective-permute-start(bf16[768,512]{1,0:T(8,128)(2,1)S(1)} %copy-done.22), channel_id=1, source_target_pairs={{0,16},{4,20},{8,24},{12,28},{16,0},{20,4},{24,8},{28,12},{1,17},{... | collective-permute-start | bytes 2359304 | tf_op jit(solution)/shard_map/ppermute | solution.py:28
  174.8 35.1 %collective-permute-start.13 = (bf16[768,3072]{1,0:T(8,128)(2,1)}, bf16[768,3072]{1,0:T(8,128)(2,1)}, u32[]{:S(2)}, u32[]{:S(2)}) collective-permute-start(bf16[768,3072]{1,0:T(8,128)(2,1)} %slice_dynamic-update-slice_fusion), channel_id=1, source_target_pairs={{0,4},{4,0},{8,12},{12,8},{16,20},{20,16},{24,28},{28,24},{1,5},{5... | collective-permute-start | bytes 14155784 | tf_op jit(solution)/shard_map/ppermute | solution.py:28
  177.7 30.7 %collective-permute-start.11 = (bf16[768,512]{1,0:T(8,128)(2,1)S(1)}, bf16[768,512]{1,0:T(8,128)(2,1)S(1)}, u32[]{:S(2)}, u32[]{:S(2)}) collective-permute-start(bf16[768,512]{1,0:T(8,128)(2,1)S(1)} %copy-done.24), channel_id=1, source_target_pairs={{0,8},{4,12},{8,0},{12,4},{16,24},{20,28},{24,16},{28,20},{1,9},{5... | collective-permute-start | bytes 2359304 | tf_op jit(solution)/shard_map/ppermute | solution.py:28
  178.4 30.5 %collective-permute-start.14 = (bf16[1536,512]{1,0:T(8,128)(2,1)S(1)}, bf16[1536,512]{1,0:T(8,128)(2,1)S(1)}, u32[]{:S(2)}, u32[]{:S(2)}) collective-permute-start(bf16[1536,512]{1,0:T(8,128)(2,1)S(1)} %copy-done.20), channel_id=1, source_target_pairs={{0,4},{4,0},{8,12},{12,8},{16,20},{20,16},{24,28},{28,24},{1,5},{5... | collective-permute-start | bytes 4718600 | tf_op jit(solution)/shard_map/ppermute | solution.py:28
  183.3 37.7 %collective-permute-start.12 = (bf16[768,512]{1,0:T(8,128)(2,1)S(1)}, bf16[768,512]{1,0:T(8,128)(2,1)}, u32[]{:S(2)}, u32[]{:S(2)}) collective-permute-start(bf16[768,512]{1,0:T(8,128)(2,1)S(1)} %copy-done.21), channel_id=1, source_target_pairs={{0,16},{4,20},{8,24},{12,28},{16,0},{20,4},{24,8},{28,12},{1,17},{... | collective-permute-start | bytes 2359304 | tf_op jit(solution)/shard_map/ppermute | solution.py:28
  186.5 22.4 %copy-start.2 = (bf16[1536,512]{1,0:T(8,128)(2,1)S(1)}, bf16[1536,512]{1,0:T(8,128)(2,1)}, u32[]{:S(2)}) copy-start(bf16[1536,512]{1,0:T(8,128)(2,1)} %get-tuple-element.88) | copy-start | bytes 4718596
  224.6 19.2 %collective-permute-start.15 = (bf16[768,512]{1,0:T(8,128)(2,1)}, bf16[768,512]{1,0:T(8,128)(2,1)S(1)}, u32[]{:S(2)}, u32[]{:S(2)}) collective-permute-start(bf16[768,512]{1,0:T(8,128)(2,1)} %collective-permute-done.12), channel_id=1, source_target_pairs={{0,8},{4,12},{8,0},{12,4},{16,24},{20,28},{24,16},{28,20},{1,9},{5... | collective-permute-start | bytes 2359304 | tf_op jit(solution)/shard_map/ppermute | solution.py:28
  246.3 32.2 %collective-permute-start.17 = (bf16[768,512]{1,0:T(8,128)(2,1)}, bf16[768,512]{1,0:T(8,128)(2,1)S(1)}, u32[]{:S(2)}, u32[]{:S(2)}) collective-permute-start(bf16[768,512]{1,0:T(8,128)(2,1)} %get-tuple-element.152), channel_id=1, source_target_pairs={{0,8},{4,12},{8,0},{12,4},{16,24},{20,28},{24,16},{28,20},{1,9},{5... | collective-permute-start | bytes 2359304 | tf_op jit(solution)/shard_map/ppermute | solution.py:28
  246.9 34.5 %collective-permute-start.16 = (bf16[768,512]{1,0:T(8,128)(2,1)}, bf16[768,512]{1,0:T(8,128)(2,1)S(1)}, u32[]{:S(2)}, u32[]{:S(2)}) collective-permute-start(bf16[768,512]{1,0:T(8,128)(2,1)} %get-tuple-element.153), channel_id=1, source_target_pairs={{0,8},{4,12},{8,0},{12,4},{16,24},{20,28},{24,16},{28,20},{1,9},{5... | collective-permute-start | bytes 2359304 | tf_op jit(solution)/shard_map/ppermute | solution.py:28
  254.8 28.1 %collective-permute-start.18 = (bf16[768,3072]{1,0:T(8,128)(2,1)}, bf16[768,3072]{1,0:T(8,128)(2,1)}, u32[]{:S(2)}, u32[]{:S(2)}) collective-permute-start(bf16[768,3072]{1,0:T(8,128)(2,1)} %convolution_convert_fusion), channel_id=1, source_target_pairs={{0,4},{4,0},{8,12},{12,8},{16,20},{20,16},{24,28},{28,24},{1,5},{5... | collective-permute-start | bytes 14155784 | tf_op jit(solution)/shard_map/ppermute | solution.py:28
  283.9 45.5 %collective-permute-start.20 = (bf16[768,512]{1,0:T(8,128)(2,1)}, bf16[768,512]{1,0:T(8,128)(2,1)}, u32[]{:S(2)}, u32[]{:S(2)}) collective-permute-start(bf16[768,512]{1,0:T(8,128)(2,1)} %slice.253), channel_id=1, source_target_pairs={{0,8},{4,12},{8,0},{12,4},{16,24},{20,28},{24,16},{28,20},{1,9},{5... | collective-permute-start | bytes 2359304 | tf_op jit(solution)/shard_map/ppermute | solution.py:28
  292.2 51.4 %collective-permute-start.25 = (bf16[768,3072]{1,0:T(8,128)(2,1)}, bf16[768,3072]{1,0:T(8,128)(2,1)}, u32[]{:S(2)}, u32[]{:S(2)}) collective-permute-start(bf16[768,3072]{1,0:T(8,128)(2,1)} %add_convert_fusion.1), channel_id=1, source_target_pairs={{0,4},{4,0},{8,12},{12,8},{16,20},{20,16},{24,28},{28,24},{1,5},{5... | collective-permute-start | bytes 14155784 | tf_op jit(solution)/shard_map/ppermute | solution.py:28
  297.4 28.4 %collective-permute-start.21 = (bf16[384,1536]{1,0:T(8,128)(2,1)S(1)}, bf16[384,1536]{1,0:T(8,128)(2,1)S(1)}, u32[]{:S(2)}, u32[]{:S(2)}) collective-permute-start(bf16[384,1536]{1,0:T(8,128)(2,1)S(1)} %pad_maximum_fusion.10), channel_id=1, source_target_pairs={{0,1},{1,0},{2,3},{3,2},{4,5},{5,4},{6,7},{7,6},{8,9},{9,8},{10,11... | collective-permute-start | bytes 3538952 | tf_op jit(solution)/shard_map/ppermute | solution.py:28
  298.9 28.7 %collective-permute-start.23 = (bf16[384,1536]{1,0:T(8,128)(2,1)S(1)}, bf16[384,1536]{1,0:T(8,128)(2,1)S(1)}, u32[]{:S(2)}, u32[]{:S(2)}) collective-permute-start(bf16[384,1536]{1,0:T(8,128)(2,1)S(1)} %pad_maximum_fusion.11), channel_id=1, source_target_pairs={{0,2},{1,3},{2,0},{3,1},{4,6},{5,7},{6,4},{7,5},{8,10},{9,11},{10,... | collective-permute-start | bytes 3538952 | tf_op jit(solution)/shard_map/ppermute | solution.py:28
  306.4 41.8 %collective-permute-start.19 = (bf16[768,512]{1,0:T(8,128)(2,1)}, bf16[768,512]{1,0:T(8,128)(2,1)}, u32[]{:S(2)}, u32[]{:S(2)}) collective-permute-start(bf16[768,512]{1,0:T(8,128)(2,1)} %get-tuple-element.102), channel_id=1, source_target_pairs={{0,16},{4,20},{8,24},{12,28},{16,0},{20,4},{24,8},{28,12},{1,17},{... | collective-permute-start | bytes 2359304 | tf_op jit(solution)/shard_map/ppermute | solution.py:28
  326.0 15.0 %collective-permute-start.22 = (bf16[384,768]{1,0:T(8,128)(2,1)S(1)}, bf16[384,768]{1,0:T(8,128)(2,1)S(1)}, u32[]{:S(2)}, u32[]{:S(2)}) collective-permute-start(bf16[384,768]{1,0:T(8,128)(2,1)S(1)} %add_convert_fusion.20), channel_id=1, source_target_pairs={{0,2},{1,3},{2,0},{3,1},{4,6},{5,7},{6,4},{7,5},{8,10},{9,11},{10,... | collective-permute-start | bytes 1769480 | tf_op jit(solution)/shard_map/ppermute | solution.py:28
  327.7 14.7 %collective-permute-start.24 = (bf16[384,768]{1,0:T(8,128)(2,1)S(1)}, bf16[384,768]{1,0:T(8,128)(2,1)S(1)}, u32[]{:S(2)}, u32[]{:S(2)}) collective-permute-start(bf16[384,768]{1,0:T(8,128)(2,1)S(1)} %add_convert_fusion.17), channel_id=1, source_target_pairs={{0,1},{1,0},{2,3},{3,2},{4,5},{5,4},{6,7},{7,6},{8,9},{9,8},{10,11... | collective-permute-start | bytes 1769480 | tf_op jit(solution)/shard_map/ppermute | solution.py:28
  348.2 38.3 %collective-permute-start.26 = (bf16[768,512]{1,0:T(8,128)(2,1)}, bf16[768,512]{1,0:T(8,128)(2,1)S(1)}, u32[]{:S(2)}, u32[]{:S(2)}) collective-permute-start(bf16[768,512]{1,0:T(8,128)(2,1)} %add_convert_fusion.6), channel_id=1, source_target_pairs={{0,16},{4,20},{8,24},{12,28},{16,0},{20,4},{24,8},{28,12},{1,17},{... | collective-permute-start | bytes 2359304 | tf_op jit(solution)/shard_map/ppermute | solution.py:28
  350.7 34.3 %collective-permute-start.27 = (bf16[768,512]{1,0:T(8,128)(2,1)S(1)}, bf16[768,512]{1,0:T(8,128)(2,1)S(1)}, u32[]{:S(2)}, u32[]{:S(2)}) collective-permute-start(bf16[768,512]{1,0:T(8,128)(2,1)S(1)} %slice.266), channel_id=1, source_target_pairs={{0,8},{4,12},{8,0},{12,4},{16,24},{20,28},{24,16},{28,20},{1,9},{5... | collective-permute-start | bytes 2359304 | tf_op jit(solution)/shard_map/ppermute | solution.py:28
  352.2 33.1 %collective-permute-start.28 = (bf16[384,1536]{1,0:T(8,128)(2,1)S(1)}, bf16[384,1536]{1,0:T(8,128)(2,1)S(1)}, u32[]{:S(2)}, u32[]{:S(2)}) collective-permute-start(bf16[384,1536]{1,0:T(8,128)(2,1)S(1)} %pad_maximum_fusion.12), channel_id=1, source_target_pairs={{0,1},{1,0},{2,3},{3,2},{4,5},{5,4},{6,7},{7,6},{8,9},{9,8},{10,11... | collective-permute-start | bytes 3538952 | tf_op jit(solution)/shard_map/ppermute | solution.py:28
  355.0 30.3 %collective-permute-start.30 = (bf16[384,1024]{1,0:T(8,128)(2,1)S(1)}, bf16[384,1024]{1,0:T(8,128)(2,1)S(1)}, u32[]{:S(2)}, u32[]{:S(2)}) collective-permute-start(bf16[384,1024]{1,0:T(8,128)(2,1)S(1)} %constant_dynamic-slice_fusion.1), channel_id=1, source_target_pairs={{0,4},{4,0},{8,12},{12,8},{16,20},{20,16},{24,28},{28,24},{1,5},{5... | collective-permute-start | bytes 2359304 | tf_op jit(solution)/shard_map/ppermute | solution.py:28
  355.2 29.8 %copy-start.7 = (bf16[3072,512]{1,0:T(8,128)(2,1)S(1)}, bf16[3072,512]{1,0:T(8,128)(2,1)}, u32[]{:S(2)}) copy-start(bf16[3072,512]{1,0:T(8,128)(2,1)} %convolution_convert_fusion.1) | copy-start | bytes 9437188
  355.3 30.5 %collective-permute-start.29 = (bf16[384,1536]{1,0:T(8,128)(2,1)S(1)}, bf16[384,1536]{1,0:T(8,128)(2,1)S(1)}, u32[]{:S(2)}, u32[]{:S(2)}) collective-permute-start(bf16[384,1536]{1,0:T(8,128)(2,1)S(1)} %pad_maximum_fusion.13), channel_id=1, source_target_pairs={{0,2},{1,3},{2,0},{3,1},{4,6},{5,7},{6,4},{7,5},{8,10},{9,11},{10,... | collective-permute-start | bytes 3538952 | tf_op jit(solution)/shard_map/ppermute | solution.py:28
  386.5 12.7 %collective-permute-start.34 = (bf16[384,768]{1,0:T(8,128)(2,1)S(1)}, bf16[384,768]{1,0:T(8,128)(2,1)S(1)}, u32[]{:S(2)}, u32[]{:S(2)}) collective-permute-start(bf16[384,768]{1,0:T(8,128)(2,1)S(1)} %get-tuple-element.122), channel_id=1, source_target_pairs={{0,2},{1,3},{2,0},{3,1},{4,6},{5,7},{6,4},{7,5},{8,10},{9,11},{10,... | collective-permute-start | bytes 1769480 | tf_op jit(solution)/shard_map/ppermute | solution.py:28
  387.8 12.5 %collective-permute-start.35 = (bf16[384,768]{1,0:T(8,128)(2,1)S(1)}, bf16[384,768]{1,0:T(8,128)(2,1)S(1)}, u32[]{:S(2)}, u32[]{:S(2)}) collective-permute-start(bf16[384,768]{1,0:T(8,128)(2,1)S(1)} %get-tuple-element.124), channel_id=1, source_target_pairs={{0,1},{1,0},{2,3},{3,2},{4,5},{5,4},{6,7},{7,6},{8,9},{9,8},{10,11... | collective-permute-start | bytes 1769480 | tf_op jit(solution)/shard_map/ppermute | solution.py:28
  389.7 31.3 %collective-permute-start.32 = (bf16[768,512]{1,0:T(8,128)(2,1)S(1)}, bf16[768,512]{1,0:T(8,128)(2,1)S(1)}, u32[]{:S(2)}, u32[]{:S(2)}) collective-permute-start(bf16[768,512]{1,0:T(8,128)(2,1)S(1)} %slice.278), channel_id=1, source_target_pairs={{0,8},{4,12},{8,0},{12,4},{16,24},{20,28},{24,16},{28,20},{1,9},{5... | collective-permute-start | bytes 2359304 | tf_op jit(solution)/shard_map/ppermute | solution.py:28
  389.8 46.7 %collective-permute-start.33 = (bf16[384,768]{1,0:T(8,128)(2,1)S(1)}, bf16[384,768]{1,0:T(8,128)(2,1)S(1)}, u32[]{:S(2)}, u32[]{:S(2)}) collective-permute-start(bf16[384,768]{1,0:T(8,128)(2,1)S(1)} %copy-done.25), channel_id=1, source_target_pairs={{0,16},{4,20},{8,24},{12,28},{16,0},{20,4},{24,8},{28,12},{1,17},{... | collective-permute-start | bytes 1769480 | tf_op jit(solution)/shard_map/ppermute | solution.py:28
  390.4 66.9 %collective-permute-start.31 = (bf16[768,512]{1,0:T(8,128)(2,1)S(1)}, bf16[768,512]{1,0:T(8,128)(2,1)S(1)}, u32[]{:S(2)}, u32[]{:S(2)}) collective-permute-start(bf16[768,512]{1,0:T(8,128)(2,1)S(1)} %add_convert_fusion.5), channel_id=1, source_target_pairs={{0,16},{4,20},{8,24},{12,28},{16,0},{20,4},{24,8},{28,12},{1,17},{... | collective-permute-start | bytes 2359304 | tf_op jit(solution)/shard_map/ppermute | solution.py:28
  399.4 57.9 %copy-start.12 = (bf16[384,768]{1,0:T(8,128)(2,1)S(1)}, bf16[384,768]{1,0:T(8,128)(2,1)}, u32[]{:S(2)}) copy-start(bf16[384,768]{1,0:T(8,128)(2,1)} %add_convert_fusion.19) | copy-start | bytes 1769476
  399.4 57.9 %copy-start.28 = (s32[768]{0:T(1024)S(1)}, s32[768]{0:T(1024)}, u32[]{:S(2)}) copy-start(s32[768]{0:T(1024)} %copy-done.27) | copy-start | bytes 9220
  399.4 57.9 %copy-start.31 = (pred[768]{0:T(1024)(128)(4,1)S(1)}, pred[768]{0:T(1024)(128)(4,1)}, u32[]{:S(2)}) copy-start(pred[768]{0:T(1024)(128)(4,1)} %copy-done.30) | copy-start | bytes 2308
  399.4 57.9 %copy-start.34 = (f32[384]{0:T(512)S(1)}, f32[384]{0:T(512)}, u32[]{:S(2)}) copy-start(f32[384]{0:T(512)} %copy-done.33) | copy-start | bytes 4612
  457.3 17.4 %collective-permute-start.36 = (bf16[384,768]{1,0:T(8,128)(2,1)S(1)}, bf16[384,768]{1,0:T(8,128)(2,1)S(1)}, u32[]{:S(2)}, u32[]{:S(2)}) collective-permute-start(bf16[384,768]{1,0:T(8,128)(2,1)S(1)} %add_convert_fusion.10), channel_id=1, source_target_pairs={{0,16},{4,20},{8,24},{12,28},{16,0},{20,4},{24,8},{28,12},{1,17},{... | collective-permute-start | bytes 1769480 | tf_op jit(solution)/shard_map/ppermute | solution.py:28
  460.7 3.6 collective-permute-start.37
  461.1 22.9 %collective-permute-start.40 = (bf16[768,512]{1,0:T(8,128)(2,1)S(1)}, bf16[768,512]{1,0:T(8,128)(2,1)S(1)}, u32[]{:S(2)}, u32[]{:S(2)}) collective-permute-start(bf16[768,512]{1,0:T(8,128)(2,1)S(1)} %slice.284), channel_id=1, source_target_pairs={{0,8},{4,12},{8,0},{12,4},{16,24},{20,28},{24,16},{28,20},{1,9},{5... | collective-permute-start | bytes 2359304 | tf_op jit(solution)/shard_map/ppermute | solution.py:28
  464.3 3.6 collective-permute-start.38
  464.9 19.9 %collective-permute-start.39 = (bf16[384,1024]{1,0:T(8,128)(2,1)S(1)}, bf16[384,1024]{1,0:T(8,128)(2,1)S(1)}, u32[]{:S(2)}, u32[]{:S(2)}) collective-permute-start(bf16[384,1024]{1,0:T(8,128)(2,1)S(1)} %constant_dynamic-slice_fusion), channel_id=1, source_target_pairs={{0,4},{4,0},{8,12},{12,8},{16,20},{20,16},{24,28},{28,24},{1,5},{5... | collective-permute-start | bytes 2359304 | tf_op jit(solution)/shard_map/ppermute | solution.py:28
  484.5 2.4 collective-permute-start.41
  (33 other events, 154.1 us)

commit v4 on v3

v4 whole, which is shorter than its diff:
```python
import jax
import jax.numpy as jnp
from jax import lax
from jax.sharding import PartitionSpec as P

BF16 = jnp.bfloat16
F32 = jnp.float32


def dot(left, right, dims):
    return lax.dot_general(left, right, (dims, ((), ())), preferred_element_type=F32)


def mm(left, right):
    return dot(left, right, ((1,), (0,)))


def mm_last(left, right):
    return dot(left, right, ((1,), (1,)))


def mm_first(left, right):
    return dot(left, right, ((0,), (0,)))


def swap(value, axis, distance):
    size = lax.axis_size(axis)
    return lax.ppermute(value, axis, [(i, i ^ distance) for i in range(size)])


def fence(*values):
    return lax.optimization_barrier(values)


def select_rows(assign_block, combine_block, row_limit):
    expert_hit = assign_block == 0
    routed = jnp.any(expert_hit, axis=1)
    weight = jnp.sum(
        jnp.where(expert_hit, combine_block, jnp.zeros((), combine_block.dtype)), axis=1
    )
    place = jnp.cumsum(routed.astype(jnp.int32)) - 1
    match = routed[None, :] & (place[None, :] == jnp.arange(row_limit, dtype=jnp.int32)[:, None])
    row_weight = jnp.sum(jnp.where(match, weight[None, :], 0.0), axis=1)
    return (match, row_weight)


def cat(*values):
    return jnp.concatenate(values, axis=0)


def beside(*values):
    return jnp.concatenate(values, axis=1)


def by_bits(blocks, index):
    bit = 1
    while bit < len(blocks):
        flag = (index & bit) != 0
        blocks = [jnp.where(flag, blocks[p ^ bit], blocks[p]) for p in range(len(blocks))]
        bit *= 2
    return blocks


def local(tokens, assign, combine, cotangent, w_gate, w_up, w_down_t):
    token_total, depth = tokens.shape
    row_limit = token_total // 2
    n_dp = lax.axis_size("dp")
    n_tensor = lax.axis_size("tensor")
    me = lax.axis_index("dp")
    me_t = lax.axis_index("tensor")
    chip, core = me // 2, me % 2
    far = n_dp // 2
    upper = me // far
    rows_w = w_gate.shape[0]
    pair = 2 * rows_w
    n_chip = n_dp // 2
    hid = w_gate.shape[1] // 4
    width = depth // n_tensor
    mids = [1 << i for i in range(1, far.bit_length() - 1)]
    t_bits = [1 << i for i in range(n_tensor.bit_length() - 1)]

    def z_far(block):
        return swap(block, "dp", far)

    def across(block):
        return swap(block, "dp", 1)

    def grow(block):
        for bit in mids:
            block = cat(block, swap(block, "dp", bit))
        return block

    def whole_panel(own, away):
        full = jnp.zeros((n_chip,) + own.shape[1:], BF16)
        for j in range(n_chip // 2):
            full = lax.dynamic_update_index_in_dim(full, own[j], chip ^ j, 0)
            full = lax.dynamic_update_index_in_dim(full, away[j], chip ^ j ^ (n_chip // 2), 0)
        return full.reshape(depth, hid)

    def block_of(panel, j):
        return lax.dynamic_index_in_dim(panel.reshape(n_chip, pair, hid), chip ^ j, 0, False)

    def blocks_own(panel):
        return {j: block_of(panel, j) for j in range(n_chip // 2)}

    def blocks_far(panel):
        return {j: block_of(panel, j ^ (n_chip // 2)) for j in range(n_chip // 2)}

    def shrink(blocks):
        for bit in mids[::-1]:
            gone = [j for j in blocks if j & (bit // 2)]
            kept = [j for j in blocks if not j & (bit // 2)]
            got = swap(cat(*(blocks[j] for j in gone)), "dp", bit)
            blocks = {
                j: (blocks[j].astype(F32) + got[i * pair : (i + 1) * pair].astype(F32)).astype(BF16)
                for i, j in enumerate(kept)
            }
        return blocks[0]

    def part(w, u, c):
        return lax.dynamic_slice_in_dim(w, (u * 2 + c) * hid, hid, 1)

    def to_sibling(w):
        return beside(part(w, upper, 1 - core), part(w, 1 - upper, 1 - core))

    def by_core(mine, got):
        return jnp.where(core == 0, cat(mine, got), cat(got, mine))

    def pair_rows(w, got):
        mine = by_core(part(w, upper, core), got[:, :hid])
        other = by_core(part(w, 1 - upper, core), got[:, hid:])
        return mine, other

    gate_0 = lax.dynamic_slice_in_dim(w_gate, upper * 2 * hid, 2 * hid, 1)
    gate_4 = z_far(lax.dynamic_slice_in_dim(w_gate, (1 - upper) * 2 * hid, 2 * hid, 1))
    gate_own = grow(gate_0[None])
    match, row_weight = select_rows(assign, combine, row_limit)
    hot = match.astype(BF16)
    rows_in = mm(hot, tokens).astype(BF16)
    rows_grad = mm(hot, cotangent).astype(BF16)
    out_grad = (row_weight[:, None] * rows_grad.astype(F32)).astype(BF16)
    quarter = cat(
        *(lax.dynamic_slice_in_dim(v, me_t * width, width, 1) for v in (rows_in, out_grad))
    )
    send = cat(to_sibling(w_up), to_sibling(w_down_t))
    gate_4, gate_own, quarter, rows_in, out_grad, send = fence(
        gate_4, gate_own, quarter, rows_in, out_grad, send
    )

    quarter = z_far(quarter)
    gate_far = grow(gate_4[None])
    in_sib, out_sib = across(rows_in), across(out_grad)
    got = across(send)
    up_0, up_1 = pair_rows(w_up, got[:rows_w])
    down_0, down_1 = pair_rows(w_down_t, got[rows_w:])
    own = beside(up_0, down_0)[None]
    quarter, gate_far, in_sib, out_sib, own, up_1, down_1 = fence(
        quarter, gate_far, in_sib, out_sib, own, up_1, down_1
    )

    up_4 = z_far(up_1)
    own = grow(own)
    quarters = [quarter] + [swap(quarter, "tensor", k) for k in range(1, n_tensor)]
    gate_all = cat(gate_own, gate_far)
    gate_mine = lax.dynamic_slice_in_dim(gate_all, core * hid, hid, 2)
    gate_send = lax.dynamic_slice_in_dim(gate_all, (1 - core) * hid, hid, 2)
    up_4, own, gate_mine, gate_send, down_1, *quarters = fence(
        up_4, own, gate_mine, gate_send, down_1, *quarters
    )
    up_own, down_own = own[:, :, :hid], own[:, :, hid:]

    up_far = grow(up_4[None])
    down_4 = z_far(down_1)
    gate_got = across(gate_send)
    gate = jnp.zeros((n_chip, 2, rows_w, hid), BF16)
    for j in range(n_chip):
        gate = lax.dynamic_update_slice(gate, gate_mine[j][None, None], (chip ^ j, core, 0, 0))
        gate = lax.dynamic_update_slice(gate, gate_got[j][None, None], (chip ^ j, 1 - core, 0, 0))
    gate = gate.reshape(depth, hid)

    def true_rows(first):
        return beside(*by_bits([q[first : first + row_limit] for q in quarters], me_t))

    in_away, out_away = true_rows(0), true_rows(row_limit)
    in_away_sib, out_away_sib = across(in_away), across(out_away)
    in_all = cat(rows_in, in_away, in_sib, in_away_sib)
    gate_pre = mm(in_all, gate)
    up_far, down_4, in_all, gate_pre, out_away, out_away_sib, gate, up_own, down_own = fence(
        up_far, down_4, in_all, gate_pre, out_away, out_away_sib, gate, up_own, down_own
    )

    down_far = grow(down_4[None])
    up = whole_panel(up_own, up_far)
    out_all = cat(out_grad, out_away, out_sib, out_away_sib)
    up_pre = mm(in_all, up)
    sigmoid_gate = jax.nn.sigmoid(gate_pre)
    hidden = (gate_pre * sigmoid_gate * up_pre).astype(BF16)
    g_down = mm_first(out_all, hidden).astype(BF16)
    g_down, hidden, up_pre, down_far, out_all, up = fence(
        g_down, hidden, up_pre, down_far, out_all, up
    )

    table = 2 * row_limit
    g_down_4 = shrink(blocks_far(g_down))
    g_down_own = shrink(blocks_own(g_down))
    down = whole_panel(down_own, down_far)
    hidden_grad = mm(out_all, down)
    gate_grad = (
        hidden_grad * up_pre * sigmoid_gate * (1.0 + gate_pre * (1.0 - sigmoid_gate))
    ).astype(BF16)
    up_grad = (hidden_grad * gate_pre * sigmoid_gate).astype(BF16)
    g_gate = mm_first(in_all, gate_grad).astype(BF16)
    expert_sib = mm_last(hidden[table:], down).astype(BF16)

    def input_part(rows):
        return mm_last(gate_grad[rows], gate) + mm_last(up_grad[rows], up)

    input_sib = input_part(slice(table, None)).astype(BF16)
    g_down_4, g_down_own, down, gate_grad, up_grad, g_gate, expert_sib, input_sib = fence(
        g_down_4, g_down_own, down, gate_grad, up_grad, g_gate, expert_sib, input_sib
    )

    g_down_far = z_far(g_down_4)
    g_gate_4 = shrink(blocks_far(g_gate))
    expert_got, input_got = across(expert_sib), across(input_sib)
    g_up = mm_first(in_all, up_grad).astype(BF16)
    expert_sum = (mm_last(hidden[:table], down) + expert_got.astype(F32)).astype(BF16)
    input_sum = (input_part(slice(None, table)) + input_got.astype(F32)).astype(BF16)

    def split_parts(value):
        return {
            k: lax.dynamic_slice_in_dim(value, (me_t ^ k) * width, width, 1)
            for k in range(n_tensor)
        }

    def gone(parts, bit):
        return beside(*(parts[k] for k in parts if k & bit))

    def kept(parts, bit, got):
        keep = [k for k in parts if not k & bit]
        return {
            k: (parts[k].astype(F32) + got[:, i * width : (i + 1) * width].astype(F32)).astype(BF16)
            for i, k in enumerate(keep)
        }

    def step(parts, bit):
        return kept(parts, bit, swap(gone(parts, bit), "tensor", bit))

    def split_rows(value):
        return split_parts(value[:row_limit]), split_parts(value[row_limit:])

    def flat(parts):
        return [parts[k] for k in parts]

    expert_mine, expert_other = split_rows(expert_sum)
    g_down_far, g_gate_4, input_sum, g_gate, g_up, expert_mine, expert_other = fence(
        g_down_far, g_gate_4, input_sum, g_gate, g_up, expert_mine, expert_other
    )

    def panel(own, other):
        both = beside(own, other)
        mine = lax.dynamic_slice_in_dim(both, core * rows_w, rows_w, 0)
        got = across(lax.dynamic_slice_in_dim(both, (1 - core) * rows_w, rows_w, 0))
        whole = jnp.zeros((rows_w, 4 * hid), BF16)
        for block, u, c in (
            (mine[:, :hid], upper, core),
            (mine[:, hid:], 1 - upper, core),
            (got[:, :hid], upper, 1 - core),
            (got[:, hid:], 1 - upper, 1 - core),
        ):
            whole = lax.dynamic_update_slice(whole, block, (0, (u * 2 + c) * hid))
        return whole

    g_gate_far = z_far(g_gate_4)
    g_up_4 = shrink(blocks_far(g_up))
    low, high = t_bits[0], t_bits[-1]
    expert_mine = step(expert_mine, low)
    expert_other = step(expert_other, high)
    input_mine, input_other = split_rows(input_sum)
    down_out = panel(g_down_own, g_down_far)
    (g_gate_far, g_up_4, expert_mine, expert_other, input_mine, input_other, g_gate, g_up, down_out) = (
        fence(
            g_gate_far, g_up_4, expert_mine, expert_other, input_mine, input_other, g_gate, g_up, down_out
        )
    )

    g_up_far = z_far(g_up_4)
    g_gate_own = shrink(blocks_own(g_gate))
    for i, bit in enumerate(t_bits[1:]):
        back = t_bits[-2 - i]
        if i == 0:
            cut = len(expert_mine) // 2 * width
            got_high = swap(
                beside(gone(expert_mine, high), gone(input_other, high)), "tensor", high
            ) if bit == high else None
            got_low = swap(
                beside(gone(expert_other, low), gone(input_mine, low)), "tensor", low
            ) if back == low else None
            if got_high is None:
                expert_mine = step(expert_mine, bit)
                input_other = step(input_other, high)
                expert_other = step(expert_other, back)
                input_mine = step(input_mine, low)
            else:
                expert_mine = kept(expert_mine, high, got_high[:, :cut])
                input_other = kept(input_other, high, got_high[:, cut:])
                expert_other = kept(expert_other, low, got_low[:, :cut])
                input_mine = kept(input_mine, low, got_low[:, cut:])
        else:
            expert_mine = step(expert_mine, bit)
            expert_other = step(expert_other, back)
    g_up_far, g_gate_own, expert_mine, expert_other, input_mine, input_other, g_up = fence(
        g_up_far, g_gate_own, expert_mine[0], expert_other[0], input_mine, input_other, g_up
    )

    g_up_own = shrink(blocks_own(g_up))
    expert_got = z_far(expert_other)
    for bit in t_bits[1:]:
        input_mine = step(input_mine, bit)
    for bit in t_bits[:-1][::-1]:
        input_other = step(input_other, bit)
    g_up_own, expert_got, input_mine, input_other = fence(
        g_up_own, expert_got, input_mine[0], input_other[0]
    )

    input_got = z_far(input_other)
    expert_cols = expert_mine.astype(F32) + expert_got.astype(F32)
    grad_cols = lax.dynamic_slice_in_dim(rows_grad, me_t * width, width, 1)
    weight_rows = jnp.sum(grad_cols.astype(F32) * expert_cols, axis=1)
    for bit in t_bits:
        weight_rows = weight_rows + swap(weight_rows, "tensor", bit)
    weight_grad = jnp.sum(jnp.where(match, weight_rows[:, None], 0.0), axis=0)
    mixed = mm_first(hot, (row_weight[:, None] * expert_cols).astype(BF16)).astype(BF16)
    input_cols = (input_mine.astype(F32) + input_got.astype(F32)).astype(BF16)
    input_grad = mm_first(hot, input_cols).astype(BF16)
    return (
        mixed,
        input_grad,
        weight_grad,
        panel(g_gate_own, g_gate_far),
        panel(g_up_own, g_up_far),
        down_out,
    )


def solution(mesh):
    return jax.shard_map(
        local,
        mesh=mesh,
        in_specs=(
            P("dp", None),
            P("dp", None),
            P("dp", None),
            P("dp", None),
            P("dp", "tensor"),
            P("dp", "tensor"),
            P("dp", "tensor"),
        ),
        out_specs=(
            P("dp", "tensor"),
            P("dp", "tensor"),
            P("dp"),
            P("dp", "tensor"),
            P("dp", "tensor"),
            P("dp", "tensor"),
        ),
        check_vma=False,
    )
```

time: 497 us -> 476 us (0.958)
  local copies, waits for them, and re-layouts: 65.1 us -> 38.8 us
  matrix products: 83 us -> 88 us
    dynamic_update_slice x16, local copies, waits for them, and re-layouts: 25.2 us -> 0.74 us  [the longest x4 0.23 us: whole_panel(): full = lax.dynamic_update_index_in_dim(full, own[j], chip ^ j, 0)]
    slice x16 -> x5, local copies, waits for them, and re-layouts: 20.5 us -> 2.52 us  [the longest x1 1.52 us: pair_rows(): other = by_core(part(w, 1 - upper, core), got[:, hid:])]
    unnamed x82 -> x89, local copies, waits for them, and re-layouts: 5.06 us -> 14.9 us
    dot_general x16, matrix products: 83 us -> 88 us  [dot(): lax.dot_general(left, right, (dims, ((), ())), preferred_element_type=F32)]
    convert_element_type x14 -> x11, other arithmetic: 12.9 us -> 7.93 us  [the longest x5 5.85 us: shrink(): (blocks[j].astype(F32) + got[i * pair:(i + 1) * pair].astype(F32)).astype...]
    concatenate x10 -> x8, other arithmetic: 12.4 us -> 14.2 us  [cat(): return jnp.concatenate(values, axis=0)]
  transfers between devices with their start and end apart: 42 -> 42, of which waited for: 22 -> 17; matrix products, arithmetic and copies ran while one was open for 30% -> 32% of each run, Pallas kernels for 0% -> 0%
where the time goes in v4:
time: 476 us; the launch traced here: 468 us
  waiting for transfers between devices  260 us (55%)
  matrix products  88 us (18%)
  starting transfers between devices  41.7 us (9%)
  local copies, waits for them, and re-layouts  38.8 us (8%)
  other arithmetic  37 us (8%)
    ppermute x42, waiting for transfers between devices, swap(): return lax.ppermute(value, axis, [(i, i ^ distance) for i in range(size)])  260 us
    dot_general x16, matrix products, dot(): lax.dot_general(left, right, (dims, ((), ())), preferred_element_type=F32)  88 us
    ppermute x42, starting transfers between devices, swap(): return lax.ppermute(value, axis, [(i, i ^ distance) for i in range(size)])  41.7 us
    unnamed x89, local copies, waits for them, and re-layouts  14.9 us
    concatenate x8, other arithmetic, cat(): return jnp.concatenate(values, axis=0)  14.2 us
  transfers between devices with their start and end apart: 42, of which 17 were waited for; matrix products, arithmetic and copies ran while one was open for 32% of the time, Pallas kernels for 0%

profile of v4, /device:TPU:0, one launch (start us, length us, event | category | flops | bytes accessed | tf_op | source)
XLA Modules:
  0.0 467.8 jit_solution(13399998737816972012)
XLA Ops:
  0.7 2.4 dynamic-slice_bitcast_fusion.6
  3.1 4.0 collective-permute-start
  9.7 5.9 %convolution_convert_fusion.5 = bf16[384,3072]{1,0:T(8,128)(2,1)} fusion(bf16[768,3072]{1,0:T(8,128)(2,1)} %param.7, s32[768]{0:T(1024)S(1)} %add_bitcast_fusion, pred[768]{0:T(1024)(128)(4,1)S(1)} %fusion.35), kind=kOutput, calls=%fused_computation.10 | convolution fusion | flops 1813708800 | bytes 7081728 | tf_op jit(solution)/shard_map/dot_general | solution.py:11
  15.5 4.2 multiply_convert_fusion
  23.1 2.2 constant_dynamic-slice_fusion.21
  27.7 13.3 %collective-permute-done.1 = bf16[1,384,1024]{2,1,0:T(8,128)(2,1)} collective-permute-done((bf16[1,384,1024]{2,1,0:T(8,128)(2,1)S(1)}, bf16[1,384,1024]{2,1,0:T(8,128)(2,1)}, u32[]{:S(2)}, u32[]{:S(2)}) %collective-permute-start.1) | collective-permute-done | bytes 786464 | tf_op jit(solution)/shard_map/ppermute | solution.py:28
  43.0 2.6 collective-permute-start.3
  46.3 32.9 %collective-permute-done.3 = bf16[1,384,1024]{2,1,0:T(8,128)(2,1)} collective-permute-done((bf16[1,384,1024]{2,1,0:T(8,128)(2,1)S(1)}, bf16[1,384,1024]{2,1,0:T(8,128)(2,1)}, u32[]{:S(2)}, u32[]{:S(2)}) %collective-permute-start.3) | collective-permute-done | bytes 786464 | tf_op jit(solution)/shard_map/ppermute | solution.py:28
  87.0 13.1 %collective-permute-done.2 = bf16[768,768]{1,0:T(8,128)(2,1)} collective-permute-done((bf16[768,768]{1,0:T(8,128)(2,1)}, bf16[768,768]{1,0:T(8,128)(2,1)}, u32[]{:S(2)}, u32[]{:S(2)}) %collective-permute-start.2) | collective-permute-done | bytes 1179680 | tf_op jit(solution)/shard_map/ppermute | solution.py:28
  103.7 1.8 collective-permute-start.7
  105.5 3.3 constant_dynamic-update-slice_fusion.5
  109.4 43.5 %collective-permute-done.8 = bf16[1,768,1024]{2,1,0:T(8,128)(2,1)} collective-permute-done((bf16[1,768,1024]{2,1,0:T(8,128)(2,1)}, bf16[1,768,1024]{2,1,0:T(8,128)(2,1)}, u32[]{:S(2)}, u32[]{:S(2)}) %collective-permute-start.8) | collective-permute-done | bytes 1572896 | tf_op jit(solution)/shard_map/ppermute | solution.py:28
  152.9 2.2 pad_maximum_fusion.1
  155.2 2.6 broadcast_select_fusion.11
  157.8 2.6 broadcast_select_fusion.10
  164.3 31.8 %collective-permute-done.12 = bf16[1,768,512]{2,1,0:T(8,128)(2,1)S(1)} collective-permute-done((bf16[1,768,512]{2,1,0:T(8,128)(2,1)S(1)}, bf16[1,768,512]{2,1,0:T(8,128)(2,1)S(1)}, u32[]{:S(2)}, u32[]{:S(2)}) %collective-permute-start.12) | collective-permute-done | bytes 786464 | tf_op jit(solution)/shard_map/ppermute | solution.py:28
  196.5 6.6 %pad_maximum_fusion = bf16[1536,3072]{1,0:T(8,128)(2,1)S(1)} fusion(bf16[384,3072]{1,0:T(8,128)(2,1)S(1)} %collective-permute-done.14, bf16[384,3072]{1,0:T(8,128)(2,1)} %collective-permute-done.4, bf16[384,768]{1,0:T(8,128)(2,1)S(1)} %get-tuple-element.191, bf16[384,768]{1,0:T(8,128)(2,1)S(1)} %get-tuple-element.190, ...), kind=kLoop, calls=%fused_computation | loop fusion | flops 66060288 | bytes 18874368 | tf_op jit(solution)/shard_map/concatenate | solution.py:48
  203.1 5.1 %fusion.40 = f32[1536,512]{1,0:T(8,128)S(1)} fusion(bf16[1536,3072]{1,0:T(8,128)(2,1)S(1)} %pad_maximum_fusion, bf16[3072,512]{1,0:T(8,128)(2,1)S(1)} %bitcast.93), kind=kOutput, calls=%fused_computation.194 | convolution fusion | flops 4831838208 | bytes 15728640 | tf_op jit(solution)/shard_map/dot_general | solution.py:11
  208.8 1.9 constant_dynamic-update-slice_fusion.4
  210.7 3.2 constant_dynamic-update-slice_fusion.3
  215.5 7.3 %multiply_convert_fusion.3 = (bf16[1536,512]{1,0:T(8,128)(2,1)S(1)}, f32[1536,512]{1,0:T(8,128)}) fusion(f32[1536,512]{1,0:T(8,128)S(1)} %fusion.40, bf16[1536,3072]{1,0:T(8,128)(2,1)S(1)} %pad_maximum_fusion, bf16[3072,512]{1,0:T(8,128)(2,1)S(1)} %bitcast.106), kind=kOutput, calls=%fused_computation.14 | convolution fusion | flops 4836556800 | bytes 20447232 | tf_op jit(solution)/shard_map/dot_general | solution.py:11
  222.8 9.9 %convolution_convert_fusion.3 = bf16[3072,512]{1,0:T(8,128)(2,1)S(1)} fusion(bf16[1536,3072]{1,0:T(8,128)(2,1)} %constant_dynamic-update-slice_fusion.2, bf16[1536,512]{1,0:T(8,128)(2,1)S(1)} %get-tuple-element.128), kind=kOutput, calls=%fused_computation.8 | convolution fusion | flops 4833411072 | bytes 14155776 | tf_op jit(solution)/shard_map/dot_general | solution.py:11
  236.7 2.3 copy-done.40
  239.0 11.6 %multiply_convert_fusion.1 = (bf16[1536,512]{1,0:T(8,128)(2,1)}, bf16[1536,512]{1,0:T(8,128)(2,1)S(1)}) fusion(f32[1536,512]{1,0:T(8,128)S(1)} %copy-done.40, f32[1536,512]{1,0:T(8,128)} %get-tuple-element.127, bf16[1536,3072]{1,0:T(8,128)(2,1)} %constant_dynamic-update-slice_fusion.2, bf16[3072,512]{1,0:T(8,128)(2,1)S(1)} %bitcast.109), kind=kOutput, calls=%fused_computation.12 | convolution fusion | flops 4842061824 | bytes 22020096 | tf_op jit(solution)/shard_map/dot_general | solution.py:11
  250.5 6.6 %convolution_convert_fusion.2 = bf16[3072,512]{1,0:T(8,128)(2,1)} fusion(bf16[1536,3072]{1,0:T(8,128)(2,1)S(1)} %pad_maximum_fusion, bf16[1536,512]{1,0:T(8,128)(2,1)S(1)} %get-tuple-element.133), kind=kOutput, calls=%fused_computation.7 | convolution fusion | flops 4833411072 | bytes 14155776 | tf_op jit(solution)/shard_map/dot_general | solution.py:11
  257.2 4.5 convolution_convert_fusion
  261.7 2.6 fusion.11
  264.4 4.4 add_convert_fusion.2
  268.8 2.0 collective-permute-done.18
  270.8 3.0 fusion.4
  273.7 2.4 collective-permute-start.20
  278.3 9.6 %convolution_convert_fusion.1 = bf16[3072,512]{1,0:T(8,128)(2,1)} fusion(bf16[1536,3072]{1,0:T(8,128)(2,1)} %copy-done, bf16[1536,512]{1,0:T(8,128)(2,1)} %get-tuple-element.134), kind=kOutput, calls=%fused_computation.6 | convolution fusion | flops 4833411072 | bytes 14155776 | tf_op jit(solution)/shard_map/dot_general | solution.py:11
  289.0 2.7 fusion.18
  291.6 21.7 %collective-permute-done.21 = bf16[768,512]{1,0:T(8,128)(2,1)S(1)} collective-permute-done((bf16[768,512]{1,0:T(8,128)(2,1)S(1)}, bf16[768,512]{1,0:T(8,128)(2,1)S(1)}, u32[]{:S(2)}, u32[]{:S(2)}) %collective-permute-start.21) | collective-permute-done | bytes 786464 | tf_op jit(solution)/shard_map/ppermute | solution.py:28
  313.3 2.2 fusion.3
  315.5 4.5 add_convert_fusion
  323.3 5.2 %add_convert_fusion.1 = bf16[768,3072]{1,0:T(8,128)(2,1)S(1)} fusion(bf16[768,3072]{1,0:T(8,128)(2,1)} %collective-permute-done.22, f32[768,3072]{1,0:T(8,128)S(1)} %fusion.18, bf16[3072,512]{1,0:T(8,128)(2,1)S(1)} %bitcast.95, bf16[1536,512]{1,0:T(8,128)(2,1)} %copy-done.15), kind=kOutput, calls=%fused_computation.2 | convolution fusion | flops 2425356288 | bytes 22806528 | tf_op jit(solution)/shard_map/dot_general | solution.py:11
  329.9 1.9 collective-permute-start.25
  340.0 25.7 %collective-permute-done.25 = bf16[768,512]{1,0:T(8,128)(2,1)S(1)} collective-permute-done((bf16[768,512]{1,0:T(8,128)(2,1)S(1)}, bf16[768,512]{1,0:T(8,128)(2,1)S(1)}, u32[]{:S(2)}, u32[]{:S(2)}) %collective-permute-start.25) | collective-permute-done | bytes 786464 | tf_op jit(solution)/shard_map/ppermute | solution.py:28
  373.0 30.9 %collective-permute-done.30 = bf16[768,512]{1,0:T(8,128)(2,1)S(1)} collective-permute-done((bf16[768,512]{1,0:T(8,128)(2,1)S(1)}, bf16[768,512]{1,0:T(8,128)(2,1)S(1)}, u32[]{:S(2)}, u32[]{:S(2)}) %collective-permute-start.30) | collective-permute-done | bytes 786464 | tf_op jit(solution)/shard_map/ppermute | solution.py:28
  404.1 1.8 collective-permute-done.31
  412.5 9.9 %collective-permute-done.35 = bf16[384,768]{1,0:T(8,128)(2,1)S(1)} collective-permute-done((bf16[384,768]{1,0:T(8,128)(2,1)S(1)}, bf16[384,768]{1,0:T(8,128)(2,1)S(1)}, u32[]{:S(2)}, u32[]{:S(2)}) %collective-permute-start.35) | collective-permute-done | bytes 589856 | tf_op jit(solution)/shard_map/ppermute | solution.py:28
  423.2 13.5 %collective-permute-done.33 = bf16[768,512]{1,0:T(8,128)(2,1)S(1)} collective-permute-done((bf16[768,512]{1,0:T(8,128)(2,1)S(1)}, bf16[768,512]{1,0:T(8,128)(2,1)S(1)}, u32[]{:S(2)}, u32[]{:S(2)}) %collective-permute-start.33) | collective-permute-done | bytes 786464 | tf_op jit(solution)/shard_map/ppermute | solution.py:28
  437.0 2.4 collective-permute-start.37
  442.7 2.0 convolution_convert_fusion.7
  446.0 2.7 collective-permute-done.39
  449.5 14.7 %collective-permute-done.37 = bf16[384,768]{1,0:T(8,128)(2,1)S(1)} collective-permute-done((bf16[384,768]{1,0:T(8,128)(2,1)S(1)}, bf16[384,768]{1,0:T(8,128)(2,1)S(1)}, u32[]{:S(2)}, u32[]{:S(2)}) %collective-permute-start.37) | collective-permute-done | bytes 589856 | tf_op jit(solution)/shard_map/ppermute | solution.py:28
  464.2 1.9 convolution_convert_fusion.6
  (246 shorter events, 70.5 us)
Async XLA Ops:
  3.1 39.2 %collective-permute-start = (bf16[384,1024]{1,0:T(8,128)(2,1)}, bf16[384,1024]{1,0:T(8,128)(2,1)S(1)}, u32[]{:S(2)}, u32[]{:S(2)}) collective-permute-start(bf16[384,1024]{1,0:T(8,128)(2,1)} %get-tuple-element.239), channel_id=1, source_target_pairs={{0,16},{4,20},{8,24},{12,28},{16,0},{20,4},{24,8},{28,12},{1,17},{... | collective-permute-start | bytes 2359304 | tf_op jit(solution)/shard_map/ppermute | solution.py:28
  7.1 33.9 %collective-permute-start.1 = (bf16[1,384,1024]{2,1,0:T(8,128)(2,1)S(1)}, bf16[1,384,1024]{2,1,0:T(8,128)(2,1)}, u32[]{:S(2)}, u32[]{:S(2)}) collective-permute-start(bf16[1,384,1024]{2,1,0:T(8,128)(2,1)S(1)} %get-tuple-element.238), channel_id=1, source_target_pairs={{0,8},{4,12},{8,0},{12,4},{16,24},{20,28},{24,16},{28,20},{1,9},{5... | collective-permute-start | bytes 2359304 | tf_op jit(solution)/shard_map/ppermute | solution.py:28
  42.3 38.4 %collective-permute-start.6 = (bf16[768,1024]{1,0:T(8,128)(2,1)}, bf16[768,1024]{1,0:T(8,128)(2,1)}, u32[]{:S(2)}, u32[]{:S(2)}) collective-permute-start(bf16[768,1024]{1,0:T(8,128)(2,1)} %maximum_maximum_fusion), channel_id=1, source_target_pairs={{0,4},{4,0},{8,12},{12,8},{16,20},{20,16},{24,28},{28,24},{1,5},{5... | collective-permute-start | bytes 4718600 | tf_op jit(solution)/shard_map/ppermute | solution.py:28
  42.4 57.7 %collective-permute-start.4 = (bf16[384,3072]{1,0:T(8,128)(2,1)}, bf16[384,3072]{1,0:T(8,128)(2,1)}, u32[]{:S(2)}, u32[]{:S(2)}) collective-permute-start(bf16[384,3072]{1,0:T(8,128)(2,1)} %convolution_convert_fusion.5), channel_id=1, source_target_pairs={{0,4},{4,0},{8,12},{12,8},{16,20},{20,16},{24,28},{28,24},{1,5},{5... | collective-permute-start | bytes 7077896 | tf_op jit(solution)/shard_map/ppermute | solution.py:28
  42.9 57.3 %collective-permute-start.5 = (bf16[384,3072]{1,0:T(8,128)(2,1)}, bf16[384,3072]{1,0:T(8,128)(2,1)}, u32[]{:S(2)}, u32[]{:S(2)}) collective-permute-start(bf16[384,3072]{1,0:T(8,128)(2,1)} %get-tuple-element.94), channel_id=1, source_target_pairs={{0,4},{4,0},{8,12},{12,8},{16,20},{20,16},{24,28},{28,24},{1,5},{5... | collective-permute-start | bytes 7077896 | tf_op jit(solution)/shard_map/ppermute | solution.py:28
  43.0 36.2 %collective-permute-start.3 = (bf16[1,384,1024]{2,1,0:T(8,128)(2,1)S(1)}, bf16[1,384,1024]{2,1,0:T(8,128)(2,1)}, u32[]{:S(2)}, u32[]{:S(2)}) collective-permute-start(bf16[1,384,1024]{2,1,0:T(8,128)(2,1)S(1)} %bitcast.112), channel_id=1, source_target_pairs={{0,8},{4,12},{8,0},{12,4},{16,24},{20,28},{24,16},{28,20},{1,9},{5... | collective-permute-start | bytes 2359304 | tf_op jit(solution)/shard_map/ppermute | solution.py:28
  45.5 54.6 %collective-permute-start.2 = (bf16[768,768]{1,0:T(8,128)(2,1)}, bf16[768,768]{1,0:T(8,128)(2,1)}, u32[]{:S(2)}, u32[]{:S(2)}) collective-permute-start(bf16[768,768]{1,0:T(8,128)(2,1)} %pad_maximum_fusion.10), channel_id=1, source_target_pairs={{0,16},{4,20},{8,24},{12,28},{16,0},{20,4},{24,8},{28,12},{1,17},{... | collective-permute-start | bytes 3538952 | tf_op jit(solution)/shard_map/ppermute | solution.py:28
  100.1 52.8 %collective-permute-start.8 = (bf16[1,768,1024]{2,1,0:T(8,128)(2,1)}, bf16[1,768,1024]{2,1,0:T(8,128)(2,1)}, u32[]{:S(2)}, u32[]{:S(2)}) collective-permute-start(bf16[1,768,1024]{2,1,0:T(8,128)(2,1)} %maximum_bitcast_fusion), channel_id=1, source_target_pairs={{0,8},{4,12},{8,0},{12,4},{16,24},{20,28},{24,16},{28,20},{1,9},{5... | collective-permute-start | bytes 4718600 | tf_op jit(solution)/shard_map/ppermute | solution.py:28
  100.1 55.0 %collective-permute-start.9 = (bf16[768,768]{1,0:T(8,128)(2,1)}, bf16[768,768]{1,0:T(8,128)(2,1)}, u32[]{:S(2)}, u32[]{:S(2)}) collective-permute-start(bf16[768,768]{1,0:T(8,128)(2,1)} %collective-permute-done.2), channel_id=1, source_target_pairs={{0,1},{1,0},{2,3},{3,2},{4,5},{5,4},{6,7},{7,6},{8,9},{9,8},{10,11... | collective-permute-start | bytes 3538952 | tf_op jit(solution)/shard_map/ppermute | solution.py:28
  101.7 53.4 %collective-permute-start.10 = (bf16[768,768]{1,0:T(8,128)(2,1)}, bf16[768,768]{1,0:T(8,128)(2,1)}, u32[]{:S(2)}, u32[]{:S(2)}) collective-permute-start(bf16[768,768]{1,0:T(8,128)(2,1)} %collective-permute-done.2), channel_id=1, source_target_pairs={{0,2},{1,3},{2,0},{3,1},{4,6},{5,7},{6,4},{7,5},{8,10},{9,11},{10,... | collective-permute-start | bytes 3538952 | tf_op jit(solution)/shard_map/ppermute | solution.py:28
  103.2 51.9 %collective-permute-start.11 = (bf16[768,768]{1,0:T(8,128)(2,1)}, bf16[768,768]{1,0:T(8,128)(2,1)}, u32[]{:S(2)}, u32[]{:S(2)}) collective-permute-start(bf16[768,768]{1,0:T(8,128)(2,1)} %collective-permute-done.2), channel_id=1, source_target_pairs={{0,3},{1,2},{2,1},{3,0},{4,7},{5,6},{6,5},{7,4},{8,11},{9,10},{10,... | collective-permute-start | bytes 3538952 | tf_op jit(solution)/shard_map/ppermute | solution.py:28
  103.7 51.4 %collective-permute-start.7 = (bf16[768,512]{1,0:T(8,128)(2,1)}, bf16[768,512]{1,0:T(8,128)(2,1)S(1)}, u32[]{:S(2)}, u32[]{:S(2)}) collective-permute-start(bf16[768,512]{1,0:T(8,128)(2,1)} %maximum_select_fusion.2), channel_id=1, source_target_pairs={{0,16},{4,20},{8,24},{12,28},{16,0},{20,4},{24,8},{28,12},{1,17},{... | collective-permute-start | bytes 2359304 | tf_op jit(solution)/shard_map/ppermute | solution.py:28
  155.2 41.1 %collective-permute-start.15 = (bf16[4,384,512]{2,1,0:T(8,128)(2,1)S(1)}, bf16[4,384,512]{2,1,0:T(8,128)(2,1)S(1)}, u32[]{:S(2)}, u32[]{:S(2)}) collective-permute-start(bf16[4,384,512]{2,1,0:T(8,128)(2,1)S(1)} %get-tuple-element.113), channel_id=1, source_target_pairs={{0,4},{4,0},{8,12},{12,8},{16,20},{20,16},{24,28},{28,24},{1,5},{5... | collective-permute-start | bytes 4718600 | tf_op jit(solution)/shard_map/ppermute | solution.py:28
  160.4 35.6 %collective-permute-start.12 = (bf16[1,768,512]{2,1,0:T(8,128)(2,1)S(1)}, bf16[1,768,512]{2,1,0:T(8,128)(2,1)S(1)}, u32[]{:S(2)}, u32[]{:S(2)}) collective-permute-start(bf16[1,768,512]{2,1,0:T(8,128)(2,1)S(1)} %bitcast.116), channel_id=1, source_target_pairs={{0,8},{4,12},{8,0},{12,4},{16,24},{20,28},{24,16},{28,20},{1,9},{5... | collective-permute-start | bytes 2359304 | tf_op jit(solution)/shard_map/ppermute | solution.py:28
  161.2 47.1 %collective-permute-start.13 = (bf16[768,512]{1,0:T(8,128)(2,1)S(1)}, bf16[768,512]{1,0:T(8,128)(2,1)S(1)}, u32[]{:S(2)}, u32[]{:S(2)}) collective-permute-start(bf16[768,512]{1,0:T(8,128)(2,1)S(1)} %copy-done.24), channel_id=1, source_target_pairs={{0,16},{4,20},{8,24},{12,28},{16,0},{20,4},{24,8},{28,12},{1,17},{... | collective-permute-start | bytes 2359304 | tf_op jit(solution)/shard_map/ppermute | solution.py:28
  162.7 33.8 %collective-permute-start.14 = (bf16[384,3072]{1,0:T(8,128)(2,1)S(1)}, bf16[384,3072]{1,0:T(8,128)(2,1)S(1)}, u32[]{:S(2)}, u32[]{:S(2)}) collective-permute-start(bf16[384,3072]{1,0:T(8,128)(2,1)S(1)} %pad_maximum_fusion.2), channel_id=1, source_target_pairs={{0,4},{4,0},{8,12},{12,8},{16,20},{20,16},{24,28},{28,24},{1,5},{5... | collective-permute-start | bytes 7077896 | tf_op jit(solution)/shard_map/ppermute | solution.py:28
  163.1 45.2 %collective-permute-start.16 = (bf16[384,3072]{1,0:T(8,128)(2,1)S(1)}, bf16[384,3072]{1,0:T(8,128)(2,1)S(1)}, u32[]{:S(2)}, u32[]{:S(2)}) collective-permute-start(bf16[384,3072]{1,0:T(8,128)(2,1)S(1)} %pad_maximum_fusion.3), channel_id=1, source_target_pairs={{0,4},{4,0},{8,12},{12,8},{16,20},{20,16},{24,28},{28,24},{1,5},{5... | collective-permute-start | bytes 7077896 | tf_op jit(solution)/shard_map/ppermute | solution.py:28
  203.1 47.4 %copy-start = (bf16[1536,3072]{1,0:T(8,128)(2,1)}, bf16[1536,3072]{1,0:T(8,128)(2,1)S(1)}, u32[]{:S(2)}) copy-start(bf16[1536,3072]{1,0:T(8,128)(2,1)S(1)} %pad_maximum_fusion) | copy-start | bytes 28311556
  208.7 24.3 %collective-permute-start.17 = (bf16[1,768,512]{2,1,0:T(8,128)(2,1)S(1)}, bf16[1,768,512]{2,1,0:T(8,128)(2,1)S(1)}, u32[]{:S(2)}, u32[]{:S(2)}) collective-permute-start(bf16[1,768,512]{2,1,0:T(8,128)(2,1)S(1)} %bitcast.114), channel_id=1, source_target_pairs={{0,8},{4,12},{8,0},{12,4},{16,24},{20,28},{24,16},{28,20},{1,9},{5... | collective-permute-start | bytes 2359304 | tf_op jit(solution)/shard_map/ppermute | solution.py:28
  215.5 46.2 %copy-start.5 = (bf16[4,768,512]{2,1,0:T(8,128)(2,1)}, bf16[4,768,512]{2,1,0:T(8,128)(2,1)S(1)}, u32[]{:S(2)}) copy-start(bf16[4,768,512]{2,1,0:T(8,128)(2,1)S(1)} %slice_dynamic-update-slice_fusion.4) | copy-start | bytes 9437188
  222.8 34.3 %copy-start.37 = (bf16[1536,512]{1,0:T(8,128)(2,1)}, bf16[1536,512]{1,0:T(8,128)(2,1)S(1)}, u32[]{:S(2)}) copy-start(bf16[1536,512]{1,0:T(8,128)(2,1)S(1)} %get-tuple-element.128) | copy-start | bytes 4718596
  234.4 34.4 %collective-permute-start.19 = (bf16[768,512]{1,0:T(8,128)(2,1)}, bf16[768,512]{1,0:T(8,128)(2,1)}, u32[]{:S(2)}, u32[]{:S(2)}) collective-permute-start(bf16[768,512]{1,0:T(8,128)(2,1)} %get-tuple-element.198), channel_id=1, source_target_pairs={{0,8},{4,12},{8,0},{12,4},{16,24},{20,28},{24,16},{28,20},{1,9},{5... | collective-permute-start | bytes 2359304 | tf_op jit(solution)/shard_map/ppermute | solution.py:28
  236.1 34.6 %collective-permute-start.18 = (bf16[768,512]{1,0:T(8,128)(2,1)}, bf16[768,512]{1,0:T(8,128)(2,1)}, u32[]{:S(2)}, u32[]{:S(2)}) collective-permute-start(bf16[768,512]{1,0:T(8,128)(2,1)} %get-tuple-element.199), channel_id=1, source_target_pairs={{0,8},{4,12},{8,0},{12,4},{16,24},{20,28},{24,16},{28,20},{1,9},{5... | collective-permute-start | bytes 2359304 | tf_op jit(solution)/shard_map/ppermute | solution.py:28
  273.7 41.8 %collective-permute-start.23 = (bf16[768,3072]{1,0:T(8,128)(2,1)}, bf16[768,3072]{1,0:T(8,128)(2,1)}, u32[]{:S(2)}, u32[]{:S(2)}) collective-permute-start(bf16[768,3072]{1,0:T(8,128)(2,1)} %convolution_convert_fusion), channel_id=1, source_target_pairs={{0,4},{4,0},{8,12},{12,8},{16,20},{20,16},{24,28},{28,24},{1,5},{5... | collective-permute-start | bytes 14155784 | tf_op jit(solution)/shard_map/ppermute | solution.py:28
  273.7 54.8 %collective-permute-start.20 = (bf16[768,512]{1,0:T(8,128)(2,1)}, bf16[768,512]{1,0:T(8,128)(2,1)}, u32[]{:S(2)}, u32[]{:S(2)}) collective-permute-start(bf16[768,512]{1,0:T(8,128)(2,1)} %get-tuple-element.131), channel_id=1, source_target_pairs={{0,16},{4,20},{8,24},{12,28},{16,0},{20,4},{24,8},{28,12},{1,17},{... | collective-permute-start | bytes 2359304 | tf_op jit(solution)/shard_map/ppermute | solution.py:28
  276.1 47.2 %collective-permute-start.22 = (bf16[768,3072]{1,0:T(8,128)(2,1)}, bf16[768,3072]{1,0:T(8,128)(2,1)}, u32[]{:S(2)}, u32[]{:S(2)}) collective-permute-start(bf16[768,3072]{1,0:T(8,128)(2,1)} %add_convert_fusion.2), channel_id=1, source_target_pairs={{0,4},{4,0},{8,12},{12,8},{16,20},{20,16},{24,28},{28,24},{1,5},{5... | collective-permute-start | bytes 14155784 | tf_op jit(solution)/shard_map/ppermute | solution.py:28
  277.6 35.7 %collective-permute-start.21 = (bf16[768,512]{1,0:T(8,128)(2,1)S(1)}, bf16[768,512]{1,0:T(8,128)(2,1)S(1)}, u32[]{:S(2)}, u32[]{:S(2)}) collective-permute-start(bf16[768,512]{1,0:T(8,128)(2,1)S(1)} %dynamic-slice_bitcast_fusion.3), channel_id=1, source_target_pairs={{0,8},{4,12},{8,0},{12,4},{16,24},{20,28},{24,16},{28,20},{1,9},{5... | collective-permute-start | bytes 2359304 | tf_op jit(solution)/shard_map/ppermute | solution.py:28
  328.6 39.6 %collective-permute-start.24 = (bf16[768,512]{1,0:T(8,128)(2,1)}, bf16[768,512]{1,0:T(8,128)(2,1)S(1)}, u32[]{:S(2)}, u32[]{:S(2)}) collective-permute-start(bf16[768,512]{1,0:T(8,128)(2,1)} %fusion.3), channel_id=1, source_target_pairs={{0,16},{4,20},{8,24},{12,28},{16,0},{20,4},{24,8},{28,12},{1,17},{... | collective-permute-start | bytes 2359304 | tf_op jit(solution)/shard_map/ppermute | solution.py:28
  329.9 35.8 %collective-permute-start.25 = (bf16[768,512]{1,0:T(8,128)(2,1)S(1)}, bf16[768,512]{1,0:T(8,128)(2,1)S(1)}, u32[]{:S(2)}, u32[]{:S(2)}) collective-permute-start(bf16[768,512]{1,0:T(8,128)(2,1)S(1)} %dynamic-slice_bitcast_fusion.2), channel_id=1, source_target_pairs={{0,8},{4,12},{8,0},{12,4},{16,24},{20,28},{24,16},{28,20},{1,9},{5... | collective-permute-start | bytes 2359304 | tf_op jit(solution)/shard_map/ppermute | solution.py:28
  333.1 32.9 %collective-permute-start.26 = (bf16[384,1536]{1,0:T(8,128)(2,1)S(1)}, bf16[384,1536]{1,0:T(8,128)(2,1)S(1)}, u32[]{:S(2)}, u32[]{:S(2)}) collective-permute-start(bf16[384,1536]{1,0:T(8,128)(2,1)S(1)} %pad_maximum_fusion.11), channel_id=1, source_target_pairs={{0,1},{1,0},{2,3},{3,2},{4,5},{5,4},{6,7},{7,6},{8,9},{9,8},{10,11... | collective-permute-start | bytes 3538952 | tf_op jit(solution)/shard_map/ppermute | solution.py:28
  334.8 31.6 %collective-permute-start.27 = (bf16[384,1536]{1,0:T(8,128)(2,1)S(1)}, bf16[384,1536]{1,0:T(8,128)(2,1)S(1)}, u32[]{:S(2)}, u32[]{:S(2)}) collective-permute-start(bf16[384,1536]{1,0:T(8,128)(2,1)S(1)} %pad_maximum_fusion.12), channel_id=1, source_target_pairs={{0,2},{1,3},{2,0},{3,1},{4,6},{5,7},{6,4},{7,5},{8,10},{9,11},{10,... | collective-permute-start | bytes 3538952 | tf_op jit(solution)/shard_map/ppermute | solution.py:28
  337.6 2.4 collective-permute-start.28
  338.6 27.1 %copy-start.3 = (bf16[3072,512]{1,0:T(8,128)(2,1)S(1)}, bf16[3072,512]{1,0:T(8,128)(2,1)}, u32[]{:S(2)}) copy-start(bf16[3072,512]{1,0:T(8,128)(2,1)} %convolution_convert_fusion.1) | copy-start | bytes 9437188
  338.8 27.2 %copy-start.11 = (bf16[384,768]{1,0:T(8,128)(2,1)S(1)}, bf16[384,768]{1,0:T(8,128)(2,1)}, u32[]{:S(2)}) copy-start(bf16[384,768]{1,0:T(8,128)(2,1)} %get-tuple-element.143) | copy-start | bytes 1769476
  338.8 27.2 %copy-start.12 = (bf16[384,768]{1,0:T(8,128)(2,1)S(1)}, bf16[384,768]{1,0:T(8,128)(2,1)}, u32[]{:S(2)}) copy-start(bf16[384,768]{1,0:T(8,128)(2,1)} %get-tuple-element.140) | copy-start | bytes 1769476
  368.3 37.6 %collective-permute-start.31 = (bf16[384,2304]{1,0:T(8,128)(2,1)S(1)}, bf16[384,2304]{1,0:T(8,128)(2,1)S(1)}, u32[]{:S(2)}, u32[]{:S(2)}) collective-permute-start(bf16[384,2304]{1,0:T(8,128)(2,1)S(1)} %pad_maximum_fusion.4), channel_id=1, source_target_pairs={{0,2},{1,3},{2,0},{3,1},{4,6},{5,7},{6,4},{7,5},{8,10},{9,11},{10,... | collective-permute-start | bytes 5308424 | tf_op jit(solution)/shard_map/ppermute | solution.py:28
  370.0 37.3 %collective-permute-start.32 = (bf16[384,2304]{1,0:T(8,128)(2,1)S(1)}, bf16[384,2304]{1,0:T(8,128)(2,1)S(1)}, u32[]{:S(2)}, u32[]{:S(2)}) collective-permute-start(bf16[384,2304]{1,0:T(8,128)(2,1)S(1)} %pad_maximum_fusion.5), channel_id=1, source_target_pairs={{0,1},{1,0},{2,3},{3,2},{4,5},{5,4},{6,7},{7,6},{8,9},{9,8},{10,11... | collective-permute-start | bytes 5308424 | tf_op jit(solution)/shard_map/ppermute | solution.py:28
  371.5 32.4 %collective-permute-start.30 = (bf16[768,512]{1,0:T(8,128)(2,1)S(1)}, bf16[768,512]{1,0:T(8,128)(2,1)S(1)}, u32[]{:S(2)}, u32[]{:S(2)}) collective-permute-start(bf16[768,512]{1,0:T(8,128)(2,1)S(1)} %dynamic-slice_bitcast_fusion.1), channel_id=1, source_target_pairs={{0,8},{4,12},{8,0},{12,4},{16,24},{20,28},{24,16},{28,20},{1,9},{5... | collective-permute-start | bytes 2359304 | tf_op jit(solution)/shard_map/ppermute | solution.py:28
  371.6 36.3 %collective-permute-start.29 = (bf16[768,512]{1,0:T(8,128)(2,1)S(1)}, bf16[768,512]{1,0:T(8,128)(2,1)S(1)}, u32[]{:S(2)}, u32[]{:S(2)}) collective-permute-start(bf16[768,512]{1,0:T(8,128)(2,1)S(1)} %fusion.2), channel_id=1, source_target_pairs={{0,16},{4,20},{8,24},{12,28},{16,0},{20,4},{24,8},{28,12},{1,17},{... | collective-permute-start | bytes 2359304 | tf_op jit(solution)/shard_map/ppermute | solution.py:28
  407.9 28.9 %collective-permute-start.33 = (bf16[768,512]{1,0:T(8,128)(2,1)S(1)}, bf16[768,512]{1,0:T(8,128)(2,1)S(1)}, u32[]{:S(2)}, u32[]{:S(2)}) collective-permute-start(bf16[768,512]{1,0:T(8,128)(2,1)S(1)} %dynamic-slice_bitcast_fusion), channel_id=1, source_target_pairs={{0,8},{4,12},{8,0},{12,4},{16,24},{20,28},{24,16},{28,20},{1,9},{5... | collective-permute-start | bytes 2359304 | tf_op jit(solution)/shard_map/ppermute | solution.py:28
  409.1 27.9 %collective-permute-start.34 = (bf16[384,768]{1,0:T(8,128)(2,1)S(1)}, bf16[384,768]{1,0:T(8,128)(2,1)S(1)}, u32[]{:S(2)}, u32[]{:S(2)}) collective-permute-start(bf16[384,768]{1,0:T(8,128)(2,1)S(1)} %get-tuple-element.169), channel_id=1, source_target_pairs={{0,16},{4,20},{8,24},{12,28},{16,0},{20,4},{24,8},{28,12},{1,17},{... | collective-permute-start | bytes 1769480 | tf_op jit(solution)/shard_map/ppermute | solution.py:28
  409.9 12.6 %collective-permute-start.35 = (bf16[384,768]{1,0:T(8,128)(2,1)S(1)}, bf16[384,768]{1,0:T(8,128)(2,1)S(1)}, u32[]{:S(2)}, u32[]{:S(2)}) collective-permute-start(bf16[384,768]{1,0:T(8,128)(2,1)S(1)} %get-tuple-element.171), channel_id=1, source_target_pairs={{0,2},{1,3},{2,0},{3,1},{4,6},{5,7},{6,4},{7,5},{8,10},{9,11},{10,... | collective-permute-start | bytes 1769480 | tf_op jit(solution)/shard_map/ppermute | solution.py:28
  410.5 12.6 %collective-permute-start.36 = (bf16[384,768]{1,0:T(8,128)(2,1)S(1)}, bf16[384,768]{1,0:T(8,128)(2,1)S(1)}, u32[]{:S(2)}, u32[]{:S(2)}) collective-permute-start(bf16[384,768]{1,0:T(8,128)(2,1)S(1)} %get-tuple-element.173), channel_id=1, source_target_pairs={{0,1},{1,0},{2,3},{3,2},{4,5},{5,4},{6,7},{7,6},{8,9},{9,8},{10,11... | collective-permute-start | bytes 1769480 | tf_op jit(solution)/shard_map/ppermute | solution.py:28
  412.2 32.5 %collective-permute-start.40 = (bf16[384,1024]{1,0:T(8,128)(2,1)S(1)}, bf16[384,1024]{1,0:T(8,128)(2,1)S(1)}, u32[]{:S(2)}, u32[]{:S(2)}) collective-permute-start(bf16[384,1024]{1,0:T(8,128)(2,1)S(1)} %constant_dynamic-slice_fusion.1), channel_id=1, source_target_pairs={{0,4},{4,0},{8,12},{12,8},{16,20},{20,16},{24,28},{28,24},{1,5},{5... | collective-permute-start | bytes 2359304 | tf_op jit(solution)/shard_map/ppermute | solution.py:28
  437.0 27.2 %collective-permute-start.37 = (bf16[384,768]{1,0:T(8,128)(2,1)S(1)}, bf16[384,768]{1,0:T(8,128)(2,1)S(1)}, u32[]{:S(2)}, u32[]{:S(2)}) collective-permute-start(bf16[384,768]{1,0:T(8,128)(2,1)S(1)} %add_convert_fusion.4), channel_id=1, source_target_pairs={{0,16},{4,20},{8,24},{12,28},{16,0},{20,4},{24,8},{28,12},{1,17},{... | collective-permute-start | bytes 1769480 | tf_op jit(solution)/shard_map/ppermute | solution.py:28
  440.9 4.1 collective-permute-start.38
  442.6 23.5 %collective-permute-start.41 = (bf16[384,1024]{1,0:T(8,128)(2,1)S(1)}, bf16[384,1024]{1,0:T(8,128)(2,1)S(1)}, u32[]{:S(2)}, u32[]{:S(2)}) collective-permute-start(bf16[384,1024]{1,0:T(8,128)(2,1)S(1)} %constant_dynamic-slice_fusion), channel_id=1, source_target_pairs={{0,4},{4,0},{8,12},{12,8},{16,20},{20,16},{24,28},{28,24},{1,5},{5... | collective-permute-start | bytes 2359304 | tf_op jit(solution)/shard_map/ppermute | solution.py:28
  445.0 3.7 collective-permute-start.39
  (35 other events, 239.2 us)

commit v5 on v4

--- a/solution.py
+++ b/solution.py
@@ -86,12 +86,15 @@
         return swap(block, "dp", 1)
 
     def grow(block):
+        blocks = [block]
         for bit in mids:
-            block = cat(block, swap(block, "dp", bit))
-        return block
+            count, rows = len(blocks), block.shape[0]
+            got = swap(cat(*blocks) if count > 1 else block, "dp", bit)
+            blocks = blocks + [got[i * rows : (i + 1) * rows] for i in range(count)]
+        return blocks
 
     def whole_panel(own, away):
-        full = jnp.zeros((n_chip,) + own.shape[1:], BF16)
+        full = jnp.zeros((n_chip, pair, hid), BF16)
         for j in range(n_chip // 2):
             full = lax.dynamic_update_index_in_dim(full, own[j], chip ^ j, 0)
             full = lax.dynamic_update_index_in_dim(full, away[j], chip ^ j ^ (n_chip // 2), 0)
@@ -106,16 +109,31 @@
     def blocks_far(panel):
         return {j: block_of(panel, j ^ (n_chip // 2)) for j in range(n_chip // 2)}
 
-    def shrink(blocks):
-        for bit in mids[::-1]:
-            gone = [j for j in blocks if j & (bit // 2)]
-            kept = [j for j in blocks if not j & (bit // 2)]
-            got = swap(cat(*(blocks[j] for j in gone)), "dp", bit)
-            blocks = {
-                j: (blocks[j].astype(F32) + got[i * pair : (i + 1) * pair].astype(F32)).astype(BF16)
-                for i, j in enumerate(kept)
-            }
-        return blocks[0]
+    def add(blocks, got):
+        return {
+            j: (blocks[j].astype(F32) + got[i * pair : (i + 1) * pair].astype(F32)).astype(BF16)
+            for i, j in enumerate(blocks)
+        }
+
+    def first_send(blocks):
+        bit = mids[-1] // 2
+        gone = [blocks[j] for j in blocks if j & bit]
+        return (
+            cat(*gone) if len(gone) > 1 else gone[0],
+            *(blocks[j] for j in blocks if not j & bit),
+        )
+
+    def shrink(send, *kept):
+        got = swap(send, "dp", mids[-1])
+        for bit in mids[:-1][::-1]:
+            blocks = add(dict(enumerate(kept)), got)
+            count = len(blocks) // 2
+            got = swap(cat(*(blocks[j + count] for j in range(count))), "dp", bit)
+            kept = tuple(blocks[j] for j in range(count))
+        return kept[0], got
+
+    def done(kept, got):
+        return (kept.astype(F32) + got.astype(F32)).astype(BF16)
 
     def part(w, u, c):
         return lax.dynamic_slice_in_dim(w, (u * 2 + c) * hid, hid, 1)
@@ -133,7 +151,7 @@
 
     gate_0 = lax.dynamic_slice_in_dim(w_gate, upper * 2 * hid, 2 * hid, 1)
     gate_4 = z_far(lax.dynamic_slice_in_dim(w_gate, (1 - upper) * 2 * hid, 2 * hid, 1))
-    gate_own = grow(gate_0[None])
+    gate_own = grow(gate_0)
     match, row_weight = select_rows(assign, combine, row_limit)
     hot = match.astype(BF16)
     rows_in = mm(hot, tokens).astype(BF16)
@@ -143,35 +161,36 @@
         *(lax.dynamic_slice_in_dim(v, me_t * width, width, 1) for v in (rows_in, out_grad))
     )
     send = cat(to_sibling(w_up), to_sibling(w_down_t))
-    gate_4, gate_own, quarter, rows_in, out_grad, send = fence(
-        gate_4, gate_own, quarter, rows_in, out_grad, send
+    gate_4, quarter, rows_in, out_grad, send, *gate_own = fence(
+        gate_4, quarter, rows_in, out_grad, send, *gate_own
     )
 
     quarter = z_far(quarter)
-    gate_far = grow(gate_4[None])
+    gate_far = grow(gate_4)
     in_sib, out_sib = across(rows_in), across(out_grad)
     got = across(send)
     up_0, up_1 = pair_rows(w_up, got[:rows_w])
     down_0, down_1 = pair_rows(w_down_t, got[rows_w:])
-    own = beside(up_0, down_0)[None]
-    quarter, gate_far, in_sib, out_sib, own, up_1, down_1 = fence(
-        quarter, gate_far, in_sib, out_sib, own, up_1, down_1
+    own = beside(up_0, down_0)
+    quarter, in_sib, out_sib, own, up_1, down_1, *gate_far = fence(
+        quarter, in_sib, out_sib, own, up_1, down_1, *gate_far
     )
 
     up_4 = z_far(up_1)
     own = grow(own)
     quarters = [quarter] + [swap(quarter, "tensor", k) for k in range(1, n_tensor)]
-    gate_all = cat(gate_own, gate_far)
+    gate_all = jnp.stack(gate_own + gate_far)
     gate_mine = lax.dynamic_slice_in_dim(gate_all, core * hid, hid, 2)
     gate_send = lax.dynamic_slice_in_dim(gate_all, (1 - core) * hid, hid, 2)
-    up_4, own, gate_mine, gate_send, down_1, *quarters = fence(
-        up_4, own, gate_mine, gate_send, down_1, *quarters
-    )
-    up_own, down_own = own[:, :, :hid], own[:, :, hid:]
-
-    up_far = grow(up_4[None])
+    up_4, gate_mine, gate_send, down_1, *rest = fence(
+        up_4, gate_mine, gate_send, down_1, *quarters, *own
+    )
+    quarters, own = rest[: len(quarters)], rest[len(quarters) :]
+    up_own, down_own = [b[:, :hid] for b in own], [b[:, hid:] for b in own]
+
+    up_far = grow(up_4)
     down_4 = z_far(down_1)
-    gate_got = across(gate_send)
+    gate_got, *quarters = fence(across(gate_send), *quarters)
     gate = jnp.zeros((n_chip, 2, rows_w, hid), BF16)
     for j in range(n_chip):
         gate = lax.dynamic_update_slice(gate, gate_mine[j][None, None], (chip ^ j, core, 0, 0))
@@ -184,25 +203,25 @@
     in_away, out_away = true_rows(0), true_rows(row_limit)
     in_away_sib, out_away_sib = across(in_away), across(out_away)
     in_all = cat(rows_in, in_away, in_sib, in_away_sib)
+    out_all = cat(out_grad, out_away, out_sib, out_away_sib)
     gate_pre = mm(in_all, gate)
-    up_far, down_4, in_all, gate_pre, out_away, out_away_sib, gate, up_own, down_own = fence(
-        up_far, down_4, in_all, gate_pre, out_away, out_away_sib, gate, up_own, down_own
-    )
-
-    down_far = grow(down_4[None])
+    down_4, in_all, out_all, gate_pre, gate, *up_far = fence(
+        down_4, in_all, out_all, gate_pre, gate, *up_far
+    )
+
+    down_far = grow(down_4)
     up = whole_panel(up_own, up_far)
-    out_all = cat(out_grad, out_away, out_sib, out_away_sib)
     up_pre = mm(in_all, up)
     sigmoid_gate = jax.nn.sigmoid(gate_pre)
     hidden = (gate_pre * sigmoid_gate * up_pre).astype(BF16)
     g_down = mm_first(out_all, hidden).astype(BF16)
-    g_down, hidden, up_pre, down_far, out_all, up = fence(
-        g_down, hidden, up_pre, down_far, out_all, up
-    )
+    g_down, hidden, up_pre, up, *down_far = fence(g_down, hidden, up_pre, up, *down_far)
 
     table = 2 * row_limit
-    g_down_4 = shrink(blocks_far(g_down))
-    g_down_own = shrink(blocks_own(g_down))
+    g_down_4 = first_send(blocks_far(g_down))
+    n_kept = len(g_down_4)
+    g_down_4 = shrink(*g_down_4)
+    g_down_own = shrink(*first_send(blocks_own(g_down)))
     down = whole_panel(down_own, down_far)
     hidden_grad = mm(out_all, down)
     gate_grad = (
@@ -216,12 +235,15 @@
         return mm_last(gate_grad[rows], gate) + mm_last(up_grad[rows], up)
 
     input_sib = input_part(slice(table, None)).astype(BF16)
-    g_down_4, g_down_own, down, gate_grad, up_grad, g_gate, expert_sib, input_sib = fence(
-        g_down_4, g_down_own, down, gate_grad, up_grad, g_gate, expert_sib, input_sib
-    )
+    down, gate_grad, up_grad, g_gate, expert_sib, input_sib, *rest = fence(
+        down, gate_grad, up_grad, g_gate, expert_sib, input_sib, *g_down_4, *g_down_own
+    )
+    g_down_own = rest[2:]
+    g_down_4, expert_sib, input_sib, g_gate = fence(done(*rest[:2]), expert_sib, input_sib, g_gate)
+    g_gate_4, g_gate_own = first_send(blocks_far(g_gate)), first_send(blocks_own(g_gate))
 
     g_down_far = z_far(g_down_4)
-    g_gate_4 = shrink(blocks_far(g_gate))
+    g_gate_4 = shrink(*g_gate_4)
     expert_got, input_got = across(expert_sib), across(input_sib)
     g_up = mm_first(in_all, up_grad).astype(BF16)
     expert_sum = (mm_last(hidden[:table], down) + expert_got.astype(F32)).astype(BF16)
@@ -252,9 +274,16 @@
     def flat(parts):
         return [parts[k] for k in parts]
 
+    low, high = t_bits[0], t_bits[-1]
     expert_mine, expert_other = split_rows(expert_sum)
-    g_down_far, g_gate_4, input_sum, g_gate, g_up, expert_mine, expert_other = fence(
-        g_down_far, g_gate_4, input_sum, g_gate, g_up, expert_mine, expert_other
+    send_low, send_high = gone(expert_mine, low), gone(expert_other, high)
+    g_up_4, g_up_own = first_send(blocks_far(g_up)), first_send(blocks_own(g_up))
+    g_down_far, input_sum, send_low, send_high, *rest = fence(
+        g_down_far, input_sum, send_low, send_high, *g_gate_4, *g_up_4, *g_up_own
+    )
+    g_up_own = rest[2 + n_kept :]
+    g_gate_4, send_low, send_high, input_sum, *g_up_4 = fence(
+        done(*rest[:2]), send_low, send_high, input_sum, *rest[2 : 2 + n_kept]
     )
 
     def panel(own, other):
@@ -272,56 +301,56 @@
         return whole
 
     g_gate_far = z_far(g_gate_4)
-    g_up_4 = shrink(blocks_far(g_up))
-    low, high = t_bits[0], t_bits[-1]
-    expert_mine = step(expert_mine, low)
-    expert_other = step(expert_other, high)
+    g_up_4 = shrink(*g_up_4)
+    expert_mine = kept(expert_mine, low, swap(send_low, "tensor", low))
+    expert_other = kept(expert_other, high, swap(send_high, "tensor", high))
     input_mine, input_other = split_rows(input_sum)
-    down_out = panel(g_down_own, g_down_far)
-    (g_gate_far, g_up_4, expert_mine, expert_other, input_mine, input_other, g_gate, g_up, down_out) = (
+    merged = len(t_bits) == 2
+    if merged:
+        send_high = beside(gone(expert_mine, high), gone(input_other, high))
+        send_low = beside(gone(expert_other, low), gone(input_mine, low))
+    else:
+        send_high, send_low = gone(input_other, high), gone(input_mine, low)
+    g_gate_far, expert_mine, expert_other, input_mine, input_other, send_low, send_high, *rest = (
         fence(
-            g_gate_far, g_up_4, expert_mine, expert_other, input_mine, input_other, g_gate, g_up, down_out
+            g_gate_far, expert_mine, expert_other, input_mine, input_other, send_low, send_high,
+            *g_up_4, *g_gate_own
         )
     )
+    g_up_4, send_low, send_high, *g_gate_own = fence(
+        done(*rest[:2]), send_low, send_high, *rest[2:]
+    )
 
     g_up_far = z_far(g_up_4)
-    g_gate_own = shrink(blocks_own(g_gate))
-    for i, bit in enumerate(t_bits[1:]):
-        back = t_bits[-2 - i]
-        if i == 0:
-            cut = len(expert_mine) // 2 * width
-            got_high = swap(
-                beside(gone(expert_mine, high), gone(input_other, high)), "tensor", high
-            ) if bit == high else None
-            got_low = swap(
-                beside(gone(expert_other, low), gone(input_mine, low)), "tensor", low
-            ) if back == low else None
-            if got_high is None:
-                expert_mine = step(expert_mine, bit)
-                input_other = step(input_other, high)
-                expert_other = step(expert_other, back)
-                input_mine = step(input_mine, low)
-            else:
-                expert_mine = kept(expert_mine, high, got_high[:, :cut])
-                input_other = kept(input_other, high, got_high[:, cut:])
-                expert_other = kept(expert_other, low, got_low[:, :cut])
-                input_mine = kept(input_mine, low, got_low[:, cut:])
-        else:
+    g_gate_own = shrink(*g_gate_own)
+    got_high, got_low = swap(send_high, "tensor", high), swap(send_low, "tensor", low)
+    if merged:
+        expert_mine = kept(expert_mine, high, got_high[:, :width])
+        expert_other = kept(expert_other, low, got_low[:, :width])
+        got_high, got_low = got_high[:, width:], got_low[:, width:]
+    else:
+        for bit in t_bits[1:]:
             expert_mine = step(expert_mine, bit)
-            expert_other = step(expert_other, back)
-    g_up_far, g_gate_own, expert_mine, expert_other, input_mine, input_other, g_up = fence(
-        g_up_far, g_gate_own, expert_mine[0], expert_other[0], input_mine, input_other, g_up
-    )
-
-    g_up_own = shrink(blocks_own(g_up))
+        for bit in t_bits[:-1][::-1]:
+            expert_other = step(expert_other, bit)
+    input_other = kept(input_other, high, got_high)
+    input_mine = kept(input_mine, low, got_low)
+    g_up_far, expert_mine, expert_other, input_mine, input_other, *rest = fence(
+        g_up_far, expert_mine[0], expert_other[0], input_mine, input_other, *g_gate_own, *g_up_own
+    )
+    g_gate_own, g_up_own = rest[:2], rest[2:]
+
+    g_up_own = shrink(*g_up_own)
     expert_got = z_far(expert_other)
     for bit in t_bits[1:]:
         input_mine = step(input_mine, bit)
     for bit in t_bits[:-1][::-1]:
         input_other = step(input_other, bit)
-    g_up_own, expert_got, input_mine, input_other = fence(
-        g_up_own, expert_got, input_mine[0], input_other[0]
-    )
+    expert_got, input_mine, input_other, g_down_far, g_gate_far, *rest = fence(
+        expert_got, input_mine[0], input_other[0], g_down_far, g_gate_far,
+        *g_down_own, *g_gate_own, *g_up_own
+    )
+    g_down_own, g_gate_own, g_up_own = rest[:2], rest[2:4], rest[4:]
 
     input_got = z_far(input_other)
     expert_cols = expert_mine.astype(F32) + expert_got.astype(F32)
@@ -337,9 +366,9 @@
         mixed,
         input_grad,
         weight_grad,
-        panel(g_gate_own, g_gate_far),
-        panel(g_up_own, g_up_far),
-        down_out,
+        panel(done(*g_gate_own), g_gate_far),
+        panel(done(*g_up_own), g_up_far),
+        panel(done(*g_down_own), g_down_far),
     )
 
 

time: 476 us -> 478 us (level)
  other arithmetic: 37 us -> 45.9 us
  waiting for transfers between devices: 260 us -> 254 us
    unnamed x89 -> x100, local copies, waits for them, and re-layouts: 14.9 us -> 8.65 us
    ppermute x42, waiting for transfers between devices: 260 us -> 254 us  [swap(): return lax.ppermute(value, axis, [(i, i ^ distance) for i in range(size)])]
    concatenate x8 -> x4, other arithmetic: 14.2 us -> 14.9 us  [cat(): return jnp.concatenate(values, axis=0)]
  transfers between devices with their start and end apart: 42 -> 42, of which waited for: 17 -> 23; matrix products, arithmetic and copies ran while one was open for 32% -> 28% of each run, Pallas kernels for 0% -> 0%
where the time goes in v5:
time: 478 us; the launch traced here: 471 us
  waiting for transfers between devices  254 us (53%)
  matrix products  88.6 us (19%)
  other arithmetic  45.9 us (10%)
  starting transfers between devices  43 us (9%)
  local copies, waits for them, and re-layouts  37.3 us (8%)
    ppermute x42, waiting for transfers between devices, swap(): return lax.ppermute(value, axis, [(i, i ^ distance) for i in range(size)])  254 us
    dot_general x16, matrix products, dot(): lax.dot_general(left, right, (dims, ((), ())), preferred_element_type=F32)  88.6 us
    ppermute x42, starting transfers between devices, swap(): return lax.ppermute(value, axis, [(i, i ^ distance) for i in range(size)])  43 us
    concatenate x4, other arithmetic, cat(): return jnp.concatenate(values, axis=0)  14.9 us
  transfers between devices with their start and end apart: 42, of which 23 were waited for; matrix products, arithmetic and copies ran while one was open for 28% of the time, Pallas kernels for 0%

profile of v5, /device:TPU:0, one launch (start us, length us, event | category | flops | bytes accessed | tf_op | source)
XLA Modules:
  0.0 470.9 jit_solution(2976154417501992750)
XLA Ops:
  0.7 2.4 constant_dynamic-slice_fusion.18
  3.1 4.0 collective-permute-start
  9.7 5.9 %convolution_convert_fusion.5 = bf16[384,3072]{1,0:T(8,128)(2,1)} fusion(bf16[768,3072]{1,0:T(8,128)(2,1)} %param.7, s32[768]{0:T(1024)S(1)} %add_bitcast_fusion, pred[768]{0:T(1024)(128)(4,1)S(1)} %fusion.28), kind=kOutput, calls=%fused_computation.11 | convolution fusion | flops 1813708800 | bytes 7081728 | tf_op jit(solution)/shard_map/dot_general | solution.py:11
  15.6 4.2 multiply_convert_fusion
  25.6 16.3 %collective-permute-done = bf16[384,1024]{1,0:T(8,128)(2,1)} collective-permute-done((bf16[384,1024]{1,0:T(8,128)(2,1)}, bf16[384,1024]{1,0:T(8,128)(2,1)}, u32[]{:S(2)}, u32[]{:S(2)}) %collective-permute-start) | collective-permute-done | bytes 786464 | tf_op jit(solution)/shard_map/ppermute | solution.py:28
  44.0 2.4 collective-permute-start.6
  52.7 34.4 %collective-permute-done.6 = bf16[384,1024]{1,0:T(8,128)(2,1)S(1)} collective-permute-done((bf16[384,1024]{1,0:T(8,128)(2,1)}, bf16[384,1024]{1,0:T(8,128)(2,1)S(1)}, u32[]{:S(2)}, u32[]{:S(2)}) %collective-permute-start.6) | collective-permute-done | bytes 786464 | tf_op jit(solution)/shard_map/ppermute | solution.py:28
  87.1 10.1 %collective-permute-done.2 = bf16[768,768]{1,0:T(8,128)(2,1)S(1)} collective-permute-done((bf16[768,768]{1,0:T(8,128)(2,1)}, bf16[768,768]{1,0:T(8,128)(2,1)S(1)}, u32[]{:S(2)}, u32[]{:S(2)}) %collective-permute-start.2) | collective-permute-done | bytes 1179680 | tf_op jit(solution)/shard_map/ppermute | solution.py:28
  97.3 2.6 collective-permute-start.10
  100.8 3.0 collective-permute-start.7
  103.8 2.3 pad_maximum_fusion.2
  106.1 2.0 constant_dynamic-slice_fusion.12
  108.1 39.9 %collective-permute-done.7 = bf16[768,512]{1,0:T(8,128)(2,1)} collective-permute-done((bf16[768,512]{1,0:T(8,128)(2,1)}, bf16[768,512]{1,0:T(8,128)(2,1)}, u32[]{:S(2)}, u32[]{:S(2)}) %collective-permute-start.7) | collective-permute-done | bytes 786464 | tf_op jit(solution)/shard_map/ppermute | solution.py:28
  148.0 3.3 collective-permute-done.8
  151.5 3.1 collective-permute-start.12
  156.9 2.3 broadcast_select_fusion.10
  159.2 2.3 broadcast_select_fusion.11
  167.4 6.1 %pad_maximum_fusion = bf16[1536,3072]{1,0:T(8,128)(2,1)S(1)} fusion(bf16[384,3072]{1,0:T(8,128)(2,1)S(1)} %collective-permute-done.14, bf16[384,3072]{1,0:T(8,128)(2,1)} %collective-permute-done.3, bf16[384,768]{1,0:T(8,128)(2,1)S(1)} %get-tuple-element.241, bf16[384,768]{1,0:T(8,128)(2,1)S(1)} %get-tuple-element.240, ...), kind=kLoop, calls=%fused_computation | loop fusion | flops 66060288 | bytes 18874368 | tf_op jit(solution)/shard_map/concatenate | solution.py:48
  173.5 7.5 %pad_maximum_fusion.1 = bf16[1536,3072]{1,0:T(8,128)(2,1)S(1)} fusion(bf16[384,3072]{1,0:T(8,128)(2,1)S(1)} %collective-permute-done.15, bf16[384,3072]{1,0:T(8,128)(2,1)} %collective-permute-done.4, bf16[384,768]{1,0:T(8,128)(2,1)S(1)} %get-tuple-element.244, bf16[384,768]{1,0:T(8,128)(2,1)S(1)} %get-tuple-element.243, ...), kind=kLoop, calls=%fused_computation.1 | loop fusion | flops 66060288 | bytes 18874368 | tf_op jit(solution)/shard_map/concatenate | solution.py:48
  181.0 6.9 %fusion.32 = f32[1536,512]{1,0:T(8,128)} fusion(bf16[1536,3072]{1,0:T(8,128)(2,1)S(1)} %pad_maximum_fusion, bf16[3072,512]{1,0:T(8,128)(2,1)S(1)} %bitcast.90), kind=kOutput, calls=%fused_computation.184 | convolution fusion | flops 4831838208 | bytes 15728640 | tf_op jit(solution)/shard_map/dot_general | solution.py:11
  187.9 1.8 collective-permute-done.12
  193.9 9.2 %multiply_convert_fusion.3 = (bf16[1536,512]{1,0:T(8,128)(2,1)S(1)}, f32[1536,512]{1,0:T(8,128)}) fusion(f32[1536,512]{1,0:T(8,128)} %fusion.32, bf16[1536,3072]{1,0:T(8,128)(2,1)S(1)} %pad_maximum_fusion, bf16[3072,512]{1,0:T(8,128)(2,1)S(1)} %bitcast.100), kind=kOutput, calls=%fused_computation.15 | convolution fusion | flops 4836556800 | bytes 20447232 | tf_op jit(solution)/shard_map/dot_general | solution.py:11
  203.1 5.6 %convolution_convert_fusion.3 = bf16[3072,512]{1,0:T(8,128)(2,1)S(1)} fusion(bf16[1536,3072]{1,0:T(8,128)(2,1)S(1)} %pad_maximum_fusion.1, bf16[1536,512]{1,0:T(8,128)(2,1)S(1)} %get-tuple-element.158), kind=kOutput, calls=%fused_computation.9 | convolution fusion | flops 4833411072 | bytes 14155776 | tf_op jit(solution)/shard_map/dot_general | solution.py:11
  210.3 10.0 %multiply_convert_fusion.1 = (bf16[1536,512]{1,0:T(8,128)(2,1)}, bf16[1536,512]{1,0:T(8,128)(2,1)S(1)}) fusion(f32[1536,512]{1,0:T(8,128)} %fusion.32, f32[1536,512]{1,0:T(8,128)} %get-tuple-element.157, bf16[1536,3072]{1,0:T(8,128)(2,1)S(1)} %pad_maximum_fusion.1, bf16[3072,512]{1,0:T(8,128)(2,1)S(1)} %bitcast.97), kind=kOutput, calls=%fused_computation.13 | convolution fusion | flops 4842061824 | bytes 22020096 | tf_op jit(solution)/shard_map/dot_general | solution.py:11
  220.3 6.2 %convolution_convert_fusion = bf16[768,3072]{1,0:T(8,128)(2,1)} fusion(bf16[3072,512]{1,0:T(8,128)(2,1)S(1)} %bitcast.98, bf16[1536,512]{1,0:T(8,128)(2,1)} %copy-done.48), kind=kOutput, calls=%fused_computation.5 | convolution fusion | flops 2418278400 | bytes 8650752 | tf_op jit(solution)/shard_map/dot_general | solution.py:11
  226.5 6.6 %convolution_convert_fusion.2 = bf16[3072,512]{1,0:T(8,128)(2,1)} fusion(bf16[1536,3072]{1,0:T(8,128)(2,1)S(1)} %pad_maximum_fusion, bf16[1536,512]{1,0:T(8,128)(2,1)S(1)} %get-tuple-element.168), kind=kOutput, calls=%fused_computation.8 | convolution fusion | flops 4833411072 | bytes 14155776 | tf_op jit(solution)/shard_map/dot_general | solution.py:11
  236.5 2.6 fusion.11
  239.2 4.6 add_convert_fusion.2
  243.8 11.4 %collective-permute-done.18 = bf16[768,512]{1,0:T(8,128)(2,1)S(1)} collective-permute-done((bf16[768,512]{1,0:T(8,128)(2,1)}, bf16[768,512]{1,0:T(8,128)(2,1)S(1)}, u32[]{:S(2)}, u32[]{:S(2)}) %collective-permute-start.18) | collective-permute-done | bytes 786464 | tf_op jit(solution)/shard_map/ppermute | solution.py:28
  255.2 14.9 %collective-permute-done.19 = bf16[768,512]{1,0:T(8,128)(2,1)S(1)} collective-permute-done((bf16[768,512]{1,0:T(8,128)(2,1)}, bf16[768,512]{1,0:T(8,128)(2,1)S(1)}, u32[]{:S(2)}, u32[]{:S(2)}) %collective-permute-start.19) | collective-permute-done | bytes 786464 | tf_op jit(solution)/shard_map/ppermute | solution.py:28
  271.7 3.7 dynamic-slice_bitcast_fusion
  277.7 9.3 %convolution_convert_fusion.1 = bf16[3072,512]{1,0:T(8,128)(2,1)S(1)} fusion(bf16[1536,3072]{1,0:T(8,128)(2,1)} %copy-done, bf16[1536,512]{1,0:T(8,128)(2,1)S(1)} %copy-done.47), kind=kOutput, calls=%fused_computation.7 | convolution fusion | flops 4833411072 | bytes 14155776 | tf_op jit(solution)/shard_map/dot_general | solution.py:11
  290.0 2.6 fusion.15
  292.7 4.7 add_convert_fusion
  302.0 5.2 %add_convert_fusion.1 = bf16[768,3072]{1,0:T(8,128)(2,1)S(1)} fusion(bf16[768,3072]{1,0:T(8,128)(2,1)} %collective-permute-done.21, f32[768,3072]{1,0:T(8,128)S(1)} %fusion.15, bf16[3072,512]{1,0:T(8,128)(2,1)S(1)} %bitcast.92, bf16[1536,512]{1,0:T(8,128)(2,1)} %copy-done.19), kind=kOutput, calls=%fused_computation.3 | convolution fusion | flops 2425356288 | bytes 22806528 | tf_op jit(solution)/shard_map/dot_general | solution.py:11
  307.2 3.9 collective-permute-done.23
  311.1 2.7 collective-permute-done.20
  318.9 1.7 collective-permute-start.27
  321.6 18.2 %collective-permute-done.25 = bf16[384,1536]{1,0:T(8,128)(2,1)S(1)} collective-permute-done((bf16[384,1536]{1,0:T(8,128)(2,1)S(1)}, bf16[384,1536]{1,0:T(8,128)(2,1)S(1)}, u32[]{:S(2)}, u32[]{:S(2)}) %collective-permute-start.25) | collective-permute-done | bytes 1179680 | tf_op jit(solution)/shard_map/ppermute | solution.py:28
  341.7 10.4 %collective-permute-done.24 = bf16[768,512]{1,0:T(8,128)(2,1)S(1)} collective-permute-done((bf16[768,512]{1,0:T(8,128)(2,1)S(1)}, bf16[768,512]{1,0:T(8,128)(2,1)S(1)}, u32[]{:S(2)}, u32[]{:S(2)}) %collective-permute-start.24) | collective-permute-done | bytes 786464 | tf_op jit(solution)/shard_map/ppermute | solution.py:28
  355.7 35.8 %collective-permute-done.30 = bf16[384,2304]{1,0:T(8,128)(2,1)S(1)} collective-permute-done((bf16[384,2304]{1,0:T(8,128)(2,1)S(1)}, bf16[384,2304]{1,0:T(8,128)(2,1)S(1)}, u32[]{:S(2)}, u32[]{:S(2)}) %collective-permute-start.30) | collective-permute-done | bytes 1769504 | tf_op jit(solution)/shard_map/ppermute | solution.py:28
  397.5 10.0 %collective-permute-done.34 = bf16[384,768]{1,0:T(8,128)(2,1)} collective-permute-done((bf16[384,768]{1,0:T(8,128)(2,1)}, bf16[384,768]{1,0:T(8,128)(2,1)}, u32[]{:S(2)}, u32[]{:S(2)}) %collective-permute-start.34) | collective-permute-done | bytes 589856 | tf_op jit(solution)/shard_map/ppermute | solution.py:28
  410.0 12.6 %collective-permute-done.32 = bf16[384,768]{1,0:T(8,128)(2,1)} collective-permute-done((bf16[384,768]{1,0:T(8,128)(2,1)}, bf16[384,768]{1,0:T(8,128)(2,1)}, u32[]{:S(2)}, u32[]{:S(2)}) %collective-permute-start.32) | collective-permute-done | bytes 589856 | tf_op jit(solution)/shard_map/ppermute | solution.py:28
  422.6 2.2 collective-permute-done.35
  430.8 3.0 convolution_convert_fusion.7
  441.9 1.8 collective-permute-done.38
  444.6 21.1 %collective-permute-done.36 = bf16[384,768]{1,0:T(8,128)(2,1)S(1)} collective-permute-done((bf16[384,768]{1,0:T(8,128)(2,1)S(1)}, bf16[384,768]{1,0:T(8,128)(2,1)S(1)}, u32[]{:S(2)}, u32[]{:S(2)}) %collective-permute-start.36) | collective-permute-done | bytes 589856 | tf_op jit(solution)/shard_map/ppermute | solution.py:28
  465.7 1.9 convolution_convert_fusion.6
  (247 shorter events, 83.9 us)
Async XLA Ops:
  3.1 38.8 %collective-permute-start = (bf16[384,1024]{1,0:T(8,128)(2,1)}, bf16[384,1024]{1,0:T(8,128)(2,1)}, u32[]{:S(2)}, u32[]{:S(2)}) collective-permute-start(bf16[384,1024]{1,0:T(8,128)(2,1)} %get-tuple-element.301), channel_id=1, source_target_pairs={{0,16},{4,20},{8,24},{12,28},{16,0},{20,4},{24,8},{28,12},{1,17},{... | collective-permute-start | bytes 2359304 | tf_op jit(solution)/shard_map/ppermute | solution.py:28
  7.1 34.8 %collective-permute-start.1 = (bf16[384,1024]{1,0:T(8,128)(2,1)S(1)}, bf16[384,1024]{1,0:T(8,128)(2,1)}, u32[]{:S(2)}, u32[]{:S(2)}) collective-permute-start(bf16[384,1024]{1,0:T(8,128)(2,1)S(1)} %get-tuple-element.125), channel_id=1, source_target_pairs={{0,8},{4,12},{8,0},{12,4},{16,24},{20,28},{24,16},{28,20},{1,9},{5... | collective-permute-start | bytes 2359304 | tf_op jit(solution)/shard_map/ppermute | solution.py:28
  41.9 5.8 %collective-permute-start.5 = (bf16[768,1024]{1,0:T(8,128)(2,1)S(1)}, bf16[768,1024]{1,0:T(8,128)(2,1)}, u32[]{:S(2)}, u32[]{:S(2)}) collective-permute-start(bf16[768,1024]{1,0:T(8,128)(2,1)S(1)} %maximum_maximum_fusion), channel_id=1, source_target_pairs={{0,4},{4,0},{8,12},{12,8},{16,20},{20,16},{24,28},{28,24},{1,5},{5... | collective-permute-start | bytes 4718600 | tf_op jit(solution)/shard_map/ppermute | solution.py:28
  41.9 55.3 %collective-permute-start.3 = (bf16[384,3072]{1,0:T(8,128)(2,1)}, bf16[384,3072]{1,0:T(8,128)(2,1)}, u32[]{:S(2)}, u32[]{:S(2)}) collective-permute-start(bf16[384,3072]{1,0:T(8,128)(2,1)} %convolution_convert_fusion.5), channel_id=1, source_target_pairs={{0,4},{4,0},{8,12},{12,8},{16,20},{20,16},{24,28},{28,24},{1,5},{5... | collective-permute-start | bytes 7077896 | tf_op jit(solution)/shard_map/ppermute | solution.py:28
  42.4 54.8 %collective-permute-start.4 = (bf16[384,3072]{1,0:T(8,128)(2,1)}, bf16[384,3072]{1,0:T(8,128)(2,1)}, u32[]{:S(2)}, u32[]{:S(2)}) collective-permute-start(bf16[384,3072]{1,0:T(8,128)(2,1)} %get-tuple-element.121), channel_id=1, source_target_pairs={{0,4},{4,0},{8,12},{12,8},{16,20},{20,16},{24,28},{28,24},{1,5},{5... | collective-permute-start | bytes 7077896 | tf_op jit(solution)/shard_map/ppermute | solution.py:28
  42.4 54.8 %collective-permute-start.2 = (bf16[768,768]{1,0:T(8,128)(2,1)}, bf16[768,768]{1,0:T(8,128)(2,1)S(1)}, u32[]{:S(2)}, u32[]{:S(2)}) collective-permute-start(bf16[768,768]{1,0:T(8,128)(2,1)} %pad_maximum_fusion.8), channel_id=1, source_target_pairs={{0,16},{4,20},{8,24},{12,28},{16,0},{20,4},{24,8},{28,12},{1,17},{... | collective-permute-start | bytes 3538952 | tf_op jit(solution)/shard_map/ppermute | solution.py:28
  44.0 43.1 %collective-permute-start.6 = (bf16[384,1024]{1,0:T(8,128)(2,1)}, bf16[384,1024]{1,0:T(8,128)(2,1)S(1)}, u32[]{:S(2)}, u32[]{:S(2)}) collective-permute-start(bf16[384,1024]{1,0:T(8,128)(2,1)} %collective-permute-done), channel_id=1, source_target_pairs={{0,8},{4,12},{8,0},{12,4},{16,24},{20,28},{24,16},{28,20},{1,9},{5... | collective-permute-start | bytes 2359304 | tf_op jit(solution)/shard_map/ppermute | solution.py:28
  52.7 53.3 %copy-start.5 = (bf16[768,1024]{1,0:T(8,128)(2,1)}, bf16[768,1024]{1,0:T(8,128)(2,1)S(1)}, u32[]{:S(2)}) copy-start(bf16[768,1024]{1,0:T(8,128)(2,1)S(1)} %pad_maximum_fusion.7) | copy-start | bytes 4718596
  97.2 54.2 %collective-permute-start.11 = (bf16[768,1024]{1,0:T(8,128)(2,1)S(1)}, bf16[768,1024]{1,0:T(8,128)(2,1)}, u32[]{:S(2)}, u32[]{:S(2)}) collective-permute-start(bf16[768,1024]{1,0:T(8,128)(2,1)S(1)} %pad_maximum_fusion.7), channel_id=1, source_target_pairs={{0,8},{4,12},{8,0},{12,4},{16,24},{20,28},{24,16},{28,20},{1,9},{5... | collective-permute-start | bytes 4718600 | tf_op jit(solution)/shard_map/ppermute | solution.py:28
  97.3 50.8 %collective-permute-start.10 = (bf16[768,768]{1,0:T(8,128)(2,1)S(1)}, bf16[768,768]{1,0:T(8,128)(2,1)}, u32[]{:S(2)}, u32[]{:S(2)}) collective-permute-start(bf16[768,768]{1,0:T(8,128)(2,1)S(1)} %collective-permute-done.2), channel_id=1, source_target_pairs={{0,3},{1,2},{2,1},{3,0},{4,7},{5,6},{6,5},{7,4},{8,11},{9,10},{10,... | collective-permute-start | bytes 3538952 | tf_op jit(solution)/shard_map/ppermute | solution.py:28
  99.8 51.5 %collective-permute-start.8 = (bf16[768,768]{1,0:T(8,128)(2,1)S(1)}, bf16[768,768]{1,0:T(8,128)(2,1)}, u32[]{:S(2)}, u32[]{:S(2)}) collective-permute-start(bf16[768,768]{1,0:T(8,128)(2,1)S(1)} %collective-permute-done.2), channel_id=1, source_target_pairs={{0,1},{1,0},{2,3},{3,2},{4,5},{5,4},{6,7},{7,6},{8,9},{9,8},{10,11... | collective-permute-start | bytes 3538952 | tf_op jit(solution)/shard_map/ppermute | solution.py:28
  100.4 51.0 %collective-permute-start.9 = (bf16[768,768]{1,0:T(8,128)(2,1)S(1)}, bf16[768,768]{1,0:T(8,128)(2,1)}, u32[]{:S(2)}, u32[]{:S(2)}) collective-permute-start(bf16[768,768]{1,0:T(8,128)(2,1)S(1)} %collective-permute-done.2), channel_id=1, source_target_pairs={{0,2},{1,3},{2,0},{3,1},{4,6},{5,7},{6,4},{7,5},{8,10},{9,11},{10,... | collective-permute-start | bytes 3538952 | tf_op jit(solution)/shard_map/ppermute | solution.py:28
  100.8 47.2 %collective-permute-start.7 = (bf16[768,512]{1,0:T(8,128)(2,1)}, bf16[768,512]{1,0:T(8,128)(2,1)}, u32[]{:S(2)}, u32[]{:S(2)}) collective-permute-start(bf16[768,512]{1,0:T(8,128)(2,1)} %maximum_select_fusion.2), channel_id=1, source_target_pairs={{0,16},{4,20},{8,24},{12,28},{16,0},{20,4},{24,8},{28,12},{1,17},{... | collective-permute-start | bytes 2359304 | tf_op jit(solution)/shard_map/ppermute | solution.py:28
  151.4 5.3 %collective-permute-start.13 = (bf16[4,384,512]{2,1,0:T(8,128)(2,1)}, bf16[4,384,512]{2,1,0:T(8,128)(2,1)}, u32[]{:S(2)}, u32[]{:S(2)}) collective-permute-start(bf16[4,384,512]{2,1,0:T(8,128)(2,1)} %get-tuple-element.134), channel_id=1, source_target_pairs={{0,4},{4,0},{8,12},{12,8},{16,20},{20,16},{24,28},{28,24},{1,5},{5... | collective-permute-start | bytes 4718600 | tf_op jit(solution)/shard_map/ppermute | solution.py:28
  151.5 38.3 %collective-permute-start.12 = (bf16[768,512]{1,0:T(8,128)(2,1)}, bf16[768,512]{1,0:T(8,128)(2,1)S(1)}, u32[]{:S(2)}, u32[]{:S(2)}) collective-permute-start(bf16[768,512]{1,0:T(8,128)(2,1)} %maximum_select_fusion.3), channel_id=1, source_target_pairs={{0,16},{4,20},{8,24},{12,28},{16,0},{20,4},{24,8},{28,12},{1,17},{... | collective-permute-start | bytes 2359304 | tf_op jit(solution)/shard_map/ppermute | solution.py:28
  154.5 35.7 %collective-permute-start.16 = (bf16[768,512]{1,0:T(8,128)(2,1)}, bf16[768,512]{1,0:T(8,128)(2,1)S(1)}, u32[]{:S(2)}, u32[]{:S(2)}) collective-permute-start(bf16[768,512]{1,0:T(8,128)(2,1)} %collective-permute-done.7), channel_id=1, source_target_pairs={{0,8},{4,12},{8,0},{12,4},{16,24},{20,28},{24,16},{28,20},{1,9},{5... | collective-permute-start | bytes 2359304 | tf_op jit(solution)/shard_map/ppermute | solution.py:28
  161.8 5.5 %collective-permute-start.14 = (bf16[384,3072]{1,0:T(8,128)(2,1)S(1)}, bf16[384,3072]{1,0:T(8,128)(2,1)S(1)}, u32[]{:S(2)}, u32[]{:S(2)}) collective-permute-start(bf16[384,3072]{1,0:T(8,128)(2,1)S(1)} %pad_maximum_fusion.3), channel_id=1, source_target_pairs={{0,4},{4,0},{8,12},{12,8},{16,20},{20,16},{24,28},{28,24},{1,5},{5... | collective-permute-start | bytes 7077896 | tf_op jit(solution)/shard_map/ppermute | solution.py:28
  162.5 11.0 %collective-permute-start.15 = (bf16[384,3072]{1,0:T(8,128)(2,1)S(1)}, bf16[384,3072]{1,0:T(8,128)(2,1)S(1)}, u32[]{:S(2)}, u32[]{:S(2)}) collective-permute-start(bf16[384,3072]{1,0:T(8,128)(2,1)S(1)} %pad_maximum_fusion.4), channel_id=1, source_target_pairs={{0,4},{4,0},{8,12},{12,8},{16,20},{20,16},{24,28},{28,24},{1,5},{5... | collective-permute-start | bytes 7077896 | tf_op jit(solution)/shard_map/ppermute | solution.py:28
  173.5 53.0 %copy-start = (bf16[1536,3072]{1,0:T(8,128)(2,1)}, bf16[1536,3072]{1,0:T(8,128)(2,1)S(1)}, u32[]{:S(2)}) copy-start(bf16[1536,3072]{1,0:T(8,128)(2,1)S(1)} %pad_maximum_fusion) | copy-start | bytes 28311556
  190.2 18.7 %collective-permute-start.17 = (bf16[768,512]{1,0:T(8,128)(2,1)S(1)}, bf16[768,512]{1,0:T(8,128)(2,1)S(1)}, u32[]{:S(2)}, u32[]{:S(2)}) collective-permute-start(bf16[768,512]{1,0:T(8,128)(2,1)S(1)} %collective-permute-done.12), channel_id=1, source_target_pairs={{0,8},{4,12},{8,0},{12,4},{16,24},{20,28},{24,16},{28,20},{1,9},{5... | collective-permute-start | bytes 2359304 | tf_op jit(solution)/shard_map/ppermute | solution.py:28
  234.5 20.7 %collective-permute-start.18 = (bf16[768,512]{1,0:T(8,128)(2,1)}, bf16[768,512]{1,0:T(8,128)(2,1)S(1)}, u32[]{:S(2)}, u32[]{:S(2)}) collective-permute-start(bf16[768,512]{1,0:T(8,128)(2,1)} %get-tuple-element.260), channel_id=1, source_target_pairs={{0,8},{4,12},{8,0},{12,4},{16,24},{20,28},{24,16},{28,20},{1,9},{5... | collective-permute-start | bytes 2359304 | tf_op jit(solution)/shard_map/ppermute | solution.py:28
  236.0 34.1 %collective-permute-start.19 = (bf16[768,512]{1,0:T(8,128)(2,1)}, bf16[768,512]{1,0:T(8,128)(2,1)S(1)}, u32[]{:S(2)}, u32[]{:S(2)}) collective-permute-start(bf16[768,512]{1,0:T(8,128)(2,1)} %get-tuple-element.258), channel_id=1, source_target_pairs={{0,8},{4,12},{8,0},{12,4},{16,24},{20,28},{24,16},{28,20},{1,9},{5... | collective-permute-start | bytes 2359304 | tf_op jit(solution)/shard_map/ppermute | solution.py:28
  271.2 21.4 %collective-permute-start.22 = (bf16[768,3072]{1,0:T(8,128)(2,1)}, bf16[768,3072]{1,0:T(8,128)(2,1)}, u32[]{:S(2)}, u32[]{:S(2)}) collective-permute-start(bf16[768,3072]{1,0:T(8,128)(2,1)} %convolution_convert_fusion), channel_id=1, source_target_pairs={{0,4},{4,0},{8,12},{12,8},{16,20},{20,16},{24,28},{28,24},{1,5},{5... | collective-permute-start | bytes 14155784 | tf_op jit(solution)/shard_map/ppermute | solution.py:28
  271.2 30.8 %collective-permute-start.21 = (bf16[768,3072]{1,0:T(8,128)(2,1)}, bf16[768,3072]{1,0:T(8,128)(2,1)}, u32[]{:S(2)}, u32[]{:S(2)}) collective-permute-start(bf16[768,3072]{1,0:T(8,128)(2,1)} %add_convert_fusion.2), channel_id=1, source_target_pairs={{0,4},{4,0},{8,12},{12,8},{16,20},{20,16},{24,28},{28,24},{1,5},{5... | collective-permute-start | bytes 14155784 | tf_op jit(solution)/shard_map/ppermute | solution.py:28
  275.4 35.7 %collective-permute-start.23 = (bf16[768,512]{1,0:T(8,128)(2,1)}, bf16[768,512]{1,0:T(8,128)(2,1)}, u32[]{:S(2)}, u32[]{:S(2)}) collective-permute-start(bf16[768,512]{1,0:T(8,128)(2,1)} %get-tuple-element.252), channel_id=1, source_target_pairs={{0,8},{4,12},{8,0},{12,4},{16,24},{20,28},{24,16},{28,20},{1,9},{5... | collective-permute-start | bytes 2359304 | tf_op jit(solution)/shard_map/ppermute | solution.py:28
  276.5 37.3 %collective-permute-start.20 = (bf16[768,512]{1,0:T(8,128)(2,1)}, bf16[768,512]{1,0:T(8,128)(2,1)}, u32[]{:S(2)}, u32[]{:S(2)}) collective-permute-start(bf16[768,512]{1,0:T(8,128)(2,1)} %add_convert_fusion.8), channel_id=1, source_target_pairs={{0,16},{4,20},{8,24},{12,28},{16,0},{20,4},{24,8},{28,12},{1,17},{... | collective-permute-start | bytes 2359304 | tf_op jit(solution)/shard_map/ppermute | solution.py:28
  315.4 24.4 %collective-permute-start.25 = (bf16[384,1536]{1,0:T(8,128)(2,1)S(1)}, bf16[384,1536]{1,0:T(8,128)(2,1)S(1)}, u32[]{:S(2)}, u32[]{:S(2)}) collective-permute-start(bf16[384,1536]{1,0:T(8,128)(2,1)S(1)} %copy-done.30), channel_id=1, source_target_pairs={{0,1},{1,0},{2,3},{3,2},{4,5},{5,4},{6,7},{7,6},{8,9},{9,8},{10,11... | collective-permute-start | bytes 3538952 | tf_op jit(solution)/shard_map/ppermute | solution.py:28
  316.9 24.1 %collective-permute-start.26 = (bf16[384,1536]{1,0:T(8,128)(2,1)S(1)}, bf16[384,1536]{1,0:T(8,128)(2,1)S(1)}, u32[]{:S(2)}, u32[]{:S(2)}) collective-permute-start(bf16[384,1536]{1,0:T(8,128)(2,1)S(1)} %copy-done.29), channel_id=1, source_target_pairs={{0,2},{1,3},{2,0},{3,1},{4,6},{5,7},{6,4},{7,5},{8,10},{9,11},{10,... | collective-permute-start | bytes 3538952 | tf_op jit(solution)/shard_map/ppermute | solution.py:28
  318.5 33.5 %collective-permute-start.24 = (bf16[768,512]{1,0:T(8,128)(2,1)S(1)}, bf16[768,512]{1,0:T(8,128)(2,1)S(1)}, u32[]{:S(2)}, u32[]{:S(2)}) collective-permute-start(bf16[768,512]{1,0:T(8,128)(2,1)S(1)} %add_convert_fusion.7), channel_id=1, source_target_pairs={{0,16},{4,20},{8,24},{12,28},{16,0},{20,4},{24,8},{28,12},{1,17},{... | collective-permute-start | bytes 2359304 | tf_op jit(solution)/shard_map/ppermute | solution.py:28
  318.9 33.4 %collective-permute-start.27 = (bf16[768,512]{1,0:T(8,128)(2,1)}, bf16[768,512]{1,0:T(8,128)(2,1)S(1)}, u32[]{:S(2)}, u32[]{:S(2)}) collective-permute-start(bf16[768,512]{1,0:T(8,128)(2,1)} %get-tuple-element.186), channel_id=1, source_target_pairs={{0,8},{4,12},{8,0},{12,4},{16,24},{20,28},{24,16},{28,20},{1,9},{5... | collective-permute-start | bytes 2359304 | tf_op jit(solution)/shard_map/ppermute | solution.py:28
  321.5 19.4 %copy-start.2 = (bf16[384,3072]{1,0:T(8,128)(2,1)S(1)}, bf16[384,3072]{1,0:T(8,128)(2,1)}, u32[]{:S(2)}) copy-start(bf16[384,3072]{1,0:T(8,128)(2,1)} %copy-done.1) | copy-start | bytes 7077892
  352.1 41.0 %copy-start.34 = (bf16[768,512]{1,0:T(8,128)(2,1)}, bf16[768,512]{1,0:T(8,128)(2,1)S(1)}, u32[]{:S(2)}) copy-start(bf16[768,512]{1,0:T(8,128)(2,1)S(1)} %collective-permute-done.24) | copy-start | bytes 2359300
  352.5 39.0 %collective-permute-start.30 = (bf16[384,2304]{1,0:T(8,128)(2,1)S(1)}, bf16[384,2304]{1,0:T(8,128)(2,1)S(1)}, u32[]{:S(2)}, u32[]{:S(2)}) collective-permute-start(bf16[384,2304]{1,0:T(8,128)(2,1)S(1)} %pad_maximum_fusion.5), channel_id=1, source_target_pairs={{0,1},{1,0},{2,3},{3,2},{4,5},{5,4},{6,7},{7,6},{8,9},{9,8},{10,11... | collective-permute-start | bytes 5308424 | tf_op jit(solution)/shard_map/ppermute | solution.py:28
  353.1 40.0 %collective-permute-start.29 = (bf16[384,2304]{1,0:T(8,128)(2,1)S(1)}, bf16[384,2304]{1,0:T(8,128)(2,1)S(1)}, u32[]{:S(2)}, u32[]{:S(2)}) collective-permute-start(bf16[384,2304]{1,0:T(8,128)(2,1)S(1)} %pad_maximum_fusion.6), channel_id=1, source_target_pairs={{0,2},{1,3},{2,0},{3,1},{4,6},{5,7},{6,4},{7,5},{8,10},{9,11},{10,... | collective-permute-start | bytes 5308424 | tf_op jit(solution)/shard_map/ppermute | solution.py:28
  353.4 41.0 %collective-permute-start.28 = (bf16[768,512]{1,0:T(8,128)(2,1)S(1)}, bf16[768,512]{1,0:T(8,128)(2,1)}, u32[]{:S(2)}, u32[]{:S(2)}) collective-permute-start(bf16[768,512]{1,0:T(8,128)(2,1)S(1)} %add_convert_fusion.6), channel_id=1, source_target_pairs={{0,16},{4,20},{8,24},{12,28},{16,0},{20,4},{24,8},{28,12},{1,17},{... | collective-permute-start | bytes 2359304 | tf_op jit(solution)/shard_map/ppermute | solution.py:28
  355.2 39.3 %collective-permute-start.31 = (bf16[768,512]{1,0:T(8,128)(2,1)S(1)}, bf16[768,512]{1,0:T(8,128)(2,1)}, u32[]{:S(2)}, u32[]{:S(2)}) collective-permute-start(bf16[768,512]{1,0:T(8,128)(2,1)S(1)} %copy-done.36), channel_id=1, source_target_pairs={{0,8},{4,12},{8,0},{12,4},{16,24},{20,28},{24,16},{28,20},{1,9},{5... | collective-permute-start | bytes 2359304 | tf_op jit(solution)/shard_map/ppermute | solution.py:28
  394.4 30.4 %copy-start.15 = (bf16[768,512]{1,0:T(8,128)(2,1)S(1)}, bf16[768,512]{1,0:T(8,128)(2,1)}, u32[]{:S(2)}) copy-start(bf16[768,512]{1,0:T(8,128)(2,1)} %get-tuple-element.229) | copy-start | bytes 2359300
  394.4 30.4 %copy-start.33 = (bf16[768,512]{1,0:T(8,128)(2,1)S(1)}, bf16[768,512]{1,0:T(8,128)(2,1)}, u32[]{:S(2)}) copy-start(bf16[768,512]{1,0:T(8,128)(2,1)} %copy-done.32) | copy-start | bytes 2359300
  394.4 13.1 %collective-permute-start.34 = (bf16[384,768]{1,0:T(8,128)(2,1)}, bf16[384,768]{1,0:T(8,128)(2,1)}, u32[]{:S(2)}, u32[]{:S(2)}) collective-permute-start(bf16[384,768]{1,0:T(8,128)(2,1)} %get-tuple-element.211), channel_id=1, source_target_pairs={{0,1},{1,0},{2,3},{3,2},{4,5},{5,4},{6,7},{7,6},{8,9},{9,8},{10,11... | collective-permute-start | bytes 1769480 | tf_op jit(solution)/shard_map/ppermute | solution.py:28
  395.0 13.7 %collective-permute-start.33 = (bf16[384,768]{1,0:T(8,128)(2,1)}, bf16[384,768]{1,0:T(8,128)(2,1)}, u32[]{:S(2)}, u32[]{:S(2)}) collective-permute-start(bf16[384,768]{1,0:T(8,128)(2,1)} %get-tuple-element.209), channel_id=1, source_target_pairs={{0,2},{1,3},{2,0},{3,1},{4,6},{5,7},{6,4},{7,5},{8,10},{9,11},{10,... | collective-permute-start | bytes 1769480 | tf_op jit(solution)/shard_map/ppermute | solution.py:28
  395.3 29.5 %collective-permute-start.35 = (bf16[768,512]{1,0:T(8,128)(2,1)}, bf16[768,512]{1,0:T(8,128)(2,1)}, u32[]{:S(2)}, u32[]{:S(2)}) collective-permute-start(bf16[768,512]{1,0:T(8,128)(2,1)} %get-tuple-element.219), channel_id=1, source_target_pairs={{0,8},{4,12},{8,0},{12,4},{16,24},{20,28},{24,16},{28,20},{1,9},{5... | collective-permute-start | bytes 2359304 | tf_op jit(solution)/shard_map/ppermute | solution.py:28
  396.1 26.5 %collective-permute-start.32 = (bf16[384,768]{1,0:T(8,128)(2,1)}, bf16[384,768]{1,0:T(8,128)(2,1)}, u32[]{:S(2)}, u32[]{:S(2)}) collective-permute-start(bf16[384,768]{1,0:T(8,128)(2,1)} %get-tuple-element.207), channel_id=1, source_target_pairs={{0,16},{4,20},{8,24},{12,28},{16,0},{20,4},{24,8},{28,12},{1,17},{... | collective-permute-start | bytes 1769480 | tf_op jit(solution)/shard_map/ppermute | solution.py:28
  426.6 40.9 %collective-permute-start.41 = (bf16[384,1024]{1,0:T(8,128)(2,1)S(1)}, bf16[384,1024]{1,0:T(8,128)(2,1)S(1)}, u32[]{:S(2)}, u32[]{:S(2)}) collective-permute-start(bf16[384,1024]{1,0:T(8,128)(2,1)S(1)} %get-tuple-element.282), channel_id=1, source_target_pairs={{0,4},{4,0},{8,12},{12,8},{16,20},{20,16},{24,28},{28,24},{1,5},{5... | collective-permute-start | bytes 2359304 | tf_op jit(solution)/shard_map/ppermute | solution.py:28
  430.4 37.2 %collective-permute-start.40 = (bf16[384,1024]{1,0:T(8,128)(2,1)S(1)}, bf16[384,1024]{1,0:T(8,128)(2,1)S(1)}, u32[]{:S(2)}, u32[]{:S(2)}) collective-permute-start(bf16[384,1024]{1,0:T(8,128)(2,1)S(1)} %get-tuple-element.284), channel_id=1, source_target_pairs={{0,4},{4,0},{8,12},{12,8},{16,20},{20,16},{24,28},{28,24},{1,5},{5... | collective-permute-start | bytes 2359304 | tf_op jit(solution)/shard_map/ppermute | solution.py:28
  435.5 4.6 collective-permute-start.37
  437.0 28.7 %collective-permute-start.36 = (bf16[384,768]{1,0:T(8,128)(2,1)S(1)}, bf16[384,768]{1,0:T(8,128)(2,1)S(1)}, u32[]{:S(2)}, u32[]{:S(2)}) collective-permute-start(bf16[384,768]{1,0:T(8,128)(2,1)S(1)} %add_convert_fusion.10), channel_id=1, source_target_pairs={{0,16},{4,20},{8,24},{12,28},{16,0},{20,4},{24,8},{28,12},{1,17},{... | collective-permute-start | bytes 1769480 | tf_op jit(solution)/shard_map/ppermute | solution.py:28
  440.0 3.7 collective-permute-start.38
  441.8 26.0 %collective-permute-start.39 = (bf16[384,1024]{1,0:T(8,128)(2,1)S(1)}, bf16[384,1024]{1,0:T(8,128)(2,1)S(1)}, u32[]{:S(2)}, u32[]{:S(2)}) collective-permute-start(bf16[384,1024]{1,0:T(8,128)(2,1)S(1)} %get-tuple-element.286), channel_id=1, source_target_pairs={{0,4},{4,0},{8,12},{12,8},{16,20},{20,16},{24,28},{28,24},{1,5},{5... | collective-permute-start | bytes 2359304 | tf_op jit(solution)/shard_map/ppermute | solution.py:28
  (44 other events, 240.7 us)

commit v6 on v5

--- a/solution.py
+++ b/solution.py
@@ -100,40 +100,16 @@
             full = lax.dynamic_update_index_in_dim(full, away[j], chip ^ j ^ (n_chip // 2), 0)
         return full.reshape(depth, hid)
 
-    def block_of(panel, j):
-        return lax.dynamic_index_in_dim(panel.reshape(n_chip, pair, hid), chip ^ j, 0, False)
-
-    def blocks_own(panel):
-        return {j: block_of(panel, j) for j in range(n_chip // 2)}
-
-    def blocks_far(panel):
-        return {j: block_of(panel, j ^ (n_chip // 2)) for j in range(n_chip // 2)}
-
-    def add(blocks, got):
-        return {
-            j: (blocks[j].astype(F32) + got[i * pair : (i + 1) * pair].astype(F32)).astype(BF16)
-            for i, j in enumerate(blocks)
-        }
-
-    def first_send(blocks):
-        bit = mids[-1] // 2
-        gone = [blocks[j] for j in blocks if j & bit]
-        return (
-            cat(*gone) if len(gone) > 1 else gone[0],
-            *(blocks[j] for j in blocks if not j & bit),
+    half_rows = depth // 2
+    same_core = [[u * far + 2 * i + c for i in range(n_chip // 2)] for u in range(2) for c in range(2)]
+
+    def side(value, u):
+        return lax.dynamic_slice_in_dim(value, u * half_rows, half_rows, 0)
+
+    def scatter(value):
+        return lax.psum_scatter(
+            value, "dp", scatter_dimension=0, tiled=True, axis_index_groups=same_core
         )
-
-    def shrink(send, *kept):
-        got = swap(send, "dp", mids[-1])
-        for bit in mids[:-1][::-1]:
-            blocks = add(dict(enumerate(kept)), got)
-            count = len(blocks) // 2
-            got = swap(cat(*(blocks[j + count] for j in range(count))), "dp", bit)
-            kept = tuple(blocks[j] for j in range(count))
-        return kept[0], got
-
-    def done(kept, got):
-        return (kept.astype(F32) + got.astype(F32)).astype(BF16)
 
     def part(w, u, c):
         return lax.dynamic_slice_in_dim(w, (u * 2 + c) * hid, hid, 1)
@@ -218,10 +194,8 @@
     g_down, hidden, up_pre, up, *down_far = fence(g_down, hidden, up_pre, up, *down_far)
 
     table = 2 * row_limit
-    g_down_4 = first_send(blocks_far(g_down))
-    n_kept = len(g_down_4)
-    g_down_4 = shrink(*g_down_4)
-    g_down_own = shrink(*first_send(blocks_own(g_down)))
+    g_down_4 = scatter(side(g_down, 1 - upper))
+    g_down_own = scatter(side(g_down, upper))
     down = whole_panel(down_own, down_far)
     hidden_grad = mm(out_all, down)
     gate_grad = (
@@ -235,15 +209,13 @@
         return mm_last(gate_grad[rows], gate) + mm_last(up_grad[rows], up)
 
     input_sib = input_part(slice(table, None)).astype(BF16)
-    down, gate_grad, up_grad, g_gate, expert_sib, input_sib, *rest = fence(
-        down, gate_grad, up_grad, g_gate, expert_sib, input_sib, *g_down_4, *g_down_own
-    )
-    g_down_own = rest[2:]
-    g_down_4, expert_sib, input_sib, g_gate = fence(done(*rest[:2]), expert_sib, input_sib, g_gate)
-    g_gate_4, g_gate_own = first_send(blocks_far(g_gate)), first_send(blocks_own(g_gate))
+    g_gate_4, g_gate_own = side(g_gate, 1 - upper), side(g_gate, upper)
+    down, gate_grad, up_grad, expert_sib, input_sib, g_down_4, g_down_own, g_gate_4, g_gate_own = fence(
+        down, gate_grad, up_grad, expert_sib, input_sib, g_down_4, g_down_own, g_gate_4, g_gate_own
+    )
 
     g_down_far = z_far(g_down_4)
-    g_gate_4 = shrink(*g_gate_4)
+    g_gate_4 = scatter(g_gate_4)
     expert_got, input_got = across(expert_sib), across(input_sib)
     g_up = mm_first(in_all, up_grad).astype(BF16)
     expert_sum = (mm_last(hidden[:table], down) + expert_got.astype(F32)).astype(BF16)
@@ -277,13 +249,9 @@
     low, high = t_bits[0], t_bits[-1]
     expert_mine, expert_other = split_rows(expert_sum)
     send_low, send_high = gone(expert_mine, low), gone(expert_other, high)
-    g_up_4, g_up_own = first_send(blocks_far(g_up)), first_send(blocks_own(g_up))
-    g_down_far, input_sum, send_low, send_high, *rest = fence(
-        g_down_far, input_sum, send_low, send_high, *g_gate_4, *g_up_4, *g_up_own
-    )
-    g_up_own = rest[2 + n_kept :]
-    g_gate_4, send_low, send_high, input_sum, *g_up_4 = fence(
-        done(*rest[:2]), send_low, send_high, input_sum, *rest[2 : 2 + n_kept]
+    g_up_4, g_up_own = side(g_up, 1 - upper), side(g_up, upper)
+    g_down_far, input_sum, send_low, send_high, g_gate_4, g_up_4, g_up_own = fence(
+        g_down_far, input_sum, send_low, send_high, g_gate_4, g_up_4, g_up_own
     )
 
     def panel(own, other):
@@ -301,7 +269,7 @@
         return whole
 
     g_gate_far = z_far(g_gate_4)
-    g_up_4 = shrink(*g_up_4)
+    g_up_4 = scatter(g_up_4)
     expert_mine = kept(expert_mine, low, swap(send_low, "tensor", low))
     expert_other = kept(expert_other, high, swap(send_high, "tensor", high))
     input_mine, input_other = split_rows(input_sum)
@@ -311,18 +279,16 @@
         send_low = beside(gone(expert_other, low), gone(input_mine, low))
     else:
         send_high, send_low = gone(input_other, high), gone(input_mine, low)
-    g_gate_far, expert_mine, expert_other, input_mine, input_other, send_low, send_high, *rest = (
-        fence(
-            g_gate_far, expert_mine, expert_other, input_mine, input_other, send_low, send_high,
-            *g_up_4, *g_gate_own
-        )
-    )
-    g_up_4, send_low, send_high, *g_gate_own = fence(
-        done(*rest[:2]), send_low, send_high, *rest[2:]
+    (
+        g_gate_far, expert_mine, expert_other, input_mine, input_other,
+        send_low, send_high, g_up_4, g_gate_own,
+    ) = fence(
+        g_gate_far, expert_mine, expert_other, input_mine, input_other,
+        send_low, send_high, g_up_4, g_gate_own,
     )
 
     g_up_far = z_far(g_up_4)
-    g_gate_own = shrink(*g_gate_own)
+    g_gate_own = scatter(g_gate_own)
     got_high, got_low = swap(send_high, "tensor", high), swap(send_low, "tensor", low)
     if merged:
         expert_mine = kept(expert_mine, high, got_high[:, :width])
@@ -335,24 +301,21 @@
             expert_other = step(expert_other, bit)
     input_other = kept(input_other, high, got_high)
     input_mine = kept(input_mine, low, got_low)
-    g_up_far, expert_mine, expert_other, input_mine, input_other, *rest = fence(
-        g_up_far, expert_mine[0], expert_other[0], input_mine, input_other, *g_gate_own, *g_up_own
-    )
-    g_gate_own, g_up_own = rest[:2], rest[2:]
-
-    g_up_own = shrink(*g_up_own)
+    (
+        g_up_far, expert_mine, expert_other, input_mine, input_other,
+        g_gate_own, g_up_own, g_down_own, g_down_far, g_gate_far,
+    ) = fence(
+        g_up_far, expert_mine[0], expert_other[0], input_mine, input_other,
+        g_gate_own, g_up_own, g_down_own, g_down_far, g_gate_far,
+    )
+
+    g_up_own = scatter(g_up_own)
     expert_got = z_far(expert_other)
     for bit in t_bits[1:]:
         input_mine = step(input_mine, bit)
     for bit in t_bits[:-1][::-1]:
         input_other = step(input_other, bit)
-    expert_got, input_mine, input_other, g_down_far, g_gate_far, *rest = fence(
-        expert_got, input_mine[0], input_other[0], g_down_far, g_gate_far,
-        *g_down_own, *g_gate_own, *g_up_own
-    )
-    g_down_own, g_gate_own, g_up_own = rest[:2], rest[2:4], rest[4:]
-
-    input_got = z_far(input_other)
+    input_got = z_far(input_other[0])
     expert_cols = expert_mine.astype(F32) + expert_got.astype(F32)
     grad_cols = lax.dynamic_slice_in_dim(rows_grad, me_t * width, width, 1)
     weight_rows = jnp.sum(grad_cols.astype(F32) * expert_cols, axis=1)
@@ -360,15 +323,15 @@
         weight_rows = weight_rows + swap(weight_rows, "tensor", bit)
     weight_grad = jnp.sum(jnp.where(match, weight_rows[:, None], 0.0), axis=0)
     mixed = mm_first(hot, (row_weight[:, None] * expert_cols).astype(BF16)).astype(BF16)
-    input_cols = (input_mine.astype(F32) + input_got.astype(F32)).astype(BF16)
+    input_cols = (input_mine[0].astype(F32) + input_got.astype(F32)).astype(BF16)
     input_grad = mm_first(hot, input_cols).astype(BF16)
     return (
         mixed,
         input_grad,
         weight_grad,
-        panel(done(*g_gate_own), g_gate_far),
-        panel(done(*g_up_own), g_up_far),
-        panel(done(*g_down_own), g_down_far),
+        panel(g_gate_own, g_gate_far),
+        panel(g_up_own, g_up_far),
+        panel(g_down_own, g_down_far),
     )
 
 

time: 478 us -> 487 us (1.019)
  local copies, waits for them, and re-layouts: 37.3 us -> 59.6 us
  between operations: 2.21 us -> 15.5 us
  waiting for transfers between devices: 254 us -> 243 us
  other arithmetic: 45.9 us -> 37.1 us
  starting transfers between devices: 43 us -> 38.1 us
    ppermute x42 -> x36, waiting for transfers between devices: 254 us -> 215 us  [swap(): return lax.ppermute(value, axis, [(i, i ^ distance) for i in range(size)])]
    reduce_scatter x0 -> x6, waiting for transfers between devices: none -> 27.2 us  [scatter(): lax.psum_scatter(value, 'dp', scatter_dimension=0, tiled=True, axis_index...]
    squeeze x3 -> x0, local copies, waits for them, and re-layouts: 6.85 us -> none  [block_of(): lax.dynamic_index_in_dim(panel.reshape(n_chip, pair, hid), chip ^ j, 0, F...]
    dynamic_update_slice x12, local copies, waits for them, and re-layouts: 0.42 us -> 6.32 us  [panel(): whole = lax.dynamic_update_slice(whole, block, (0, (u * 2 + c) * hid))]
    convert_element_type x6 -> x0, other arithmetic: 5.83 us -> none  [done(): return (kept.astype(F32) + got.astype(F32)).astype(BF16)]
    dynamic_slice x0 -> x6, local copies, waits for them, and re-layouts: none -> 5.8 us  [the longest x3 5.62 us: side(): return lax.dynamic_slice_in_dim(value, u * half_rows, half_rows, 0)]
    ppermute x42 -> x36, starting transfers between devices: 43 us -> 37.6 us  [swap(): return lax.ppermute(value, axis, [(i, i ^ distance) for i in range(size)])]
    unnamed x100 -> x105, local copies, waits for them, and re-layouts: 8.65 us -> 12.5 us
  transfers between devices with their start and end apart: 42 -> 42, of which waited for: 23 -> 22; matrix products, arithmetic and copies ran while one was open for 28% -> 35% of each run, Pallas kernels for 0% -> 0%
where the time goes in v6:
time: 487 us; the launch traced here: 480 us
  waiting for transfers between devices  243 us (50%)
  matrix products  87.1 us (18%)
  local copies, waits for them, and re-layouts  59.6 us (12%)
  starting transfers between devices  38.1 us (8%)
  other arithmetic  37.1 us (8%)
  between operations  15.5 us (3%)
    ppermute x36, waiting for transfers between devices, swap(): return lax.ppermute(value, axis, [(i, i ^ distance) for i in range(size)])  215 us
    dot_general x16, matrix products, dot(): lax.dot_general(left, right, (dims, ((), ())), preferred_element_type=F32)  87.1 us
    ppermute x36, starting transfers between devices, swap(): return lax.ppermute(value, axis, [(i, i ^ distance) for i in range(size)])  37.6 us
    reduce_scatter x6, waiting for transfers between devices, scatter(): lax.psum_scatter(value, 'dp', scatter_dimension=0, tiled=True, axis_index...  27.2 us
    concatenate x4, other arithmetic, cat(): return jnp.concatenate(values, axis=0)  14.9 us
    unnamed x105, local copies, waits for them, and re-layouts  12.5 us
  transfers between devices with their start and end apart: 42, of which 22 were waited for; matrix products, arithmetic and copies ran while one was open for 35% of the time, Pallas kernels for 0%

profile of v6, /device:TPU:0, one launch (start us, length us, event | category | flops | bytes accessed | tf_op | source)
XLA Modules:
  0.0 480.0 jit_solution(5904486133703575738)
XLA Ops:
  7.3 2.4 constant_dynamic-slice_fusion.27
  9.6 4.0 collective-permute-start
  16.2 6.0 %convolution_convert_fusion.5 = bf16[384,3072]{1,0:T(8,128)(2,1)} fusion(bf16[768,3072]{1,0:T(8,128)(2,1)} %param.7, s32[768]{0:T(1024)S(1)} %add_bitcast_fusion, pred[768]{0:T(1024)(128)(4,1)S(1)} %fusion.22), kind=kOutput, calls=%fused_computation.11 | convolution fusion | flops 1813708800 | bytes 7081728 | tf_op jit(solution)/shard_map/dot_general | solution.py:11
  22.2 4.2 multiply_convert_fusion
  32.2 16.3 %collective-permute-done = bf16[384,1024]{1,0:T(8,128)(2,1)} collective-permute-done((bf16[384,1024]{1,0:T(8,128)(2,1)}, bf16[384,1024]{1,0:T(8,128)(2,1)}, u32[]{:S(2)}, u32[]{:S(2)}) %collective-permute-start) | collective-permute-done | bytes 786464 | tf_op jit(solution)/shard_map/ppermute | solution.py:28
  50.6 2.4 collective-permute-start.6
  59.3 34.4 %collective-permute-done.6 = bf16[384,1024]{1,0:T(8,128)(2,1)S(1)} collective-permute-done((bf16[384,1024]{1,0:T(8,128)(2,1)}, bf16[384,1024]{1,0:T(8,128)(2,1)S(1)}, u32[]{:S(2)}, u32[]{:S(2)}) %collective-permute-start.6) | collective-permute-done | bytes 786464 | tf_op jit(solution)/shard_map/ppermute | solution.py:28
  93.7 10.1 %collective-permute-done.2 = bf16[768,768]{1,0:T(8,128)(2,1)S(1)} collective-permute-done((bf16[768,768]{1,0:T(8,128)(2,1)}, bf16[768,768]{1,0:T(8,128)(2,1)S(1)}, u32[]{:S(2)}, u32[]{:S(2)}) %collective-permute-start.2) | collective-permute-done | bytes 1179680 | tf_op jit(solution)/shard_map/ppermute | solution.py:28
  103.8 2.6 collective-permute-start.10
  107.4 3.0 collective-permute-start.7
  110.4 2.3 pad_maximum_fusion.2
  112.7 2.0 constant_dynamic-slice_fusion.21
  114.7 39.9 %collective-permute-done.7 = bf16[768,512]{1,0:T(8,128)(2,1)} collective-permute-done((bf16[768,512]{1,0:T(8,128)(2,1)}, bf16[768,512]{1,0:T(8,128)(2,1)}, u32[]{:S(2)}, u32[]{:S(2)}) %collective-permute-start.7) | collective-permute-done | bytes 786464 | tf_op jit(solution)/shard_map/ppermute | solution.py:28
  154.6 3.3 collective-permute-done.8
  158.1 3.0 collective-permute-start.12
  163.5 2.3 broadcast_select_fusion.10
  165.8 2.3 broadcast_select_fusion.11
  175.6 6.1 %pad_maximum_fusion = bf16[1536,3072]{1,0:T(8,128)(2,1)S(1)} fusion(bf16[384,3072]{1,0:T(8,128)(2,1)S(1)} %collective-permute-done.14, bf16[384,3072]{1,0:T(8,128)(2,1)} %collective-permute-done.3, bf16[384,768]{1,0:T(8,128)(2,1)S(1)} %get-tuple-element.179, bf16[384,768]{1,0:T(8,128)(2,1)S(1)} %get-tuple-element.178, ...), kind=kLoop, calls=%fused_computation | loop fusion | flops 66060288 | bytes 18874368 | tf_op jit(solution)/shard_map/concatenate | solution.py:48
  181.8 7.5 %pad_maximum_fusion.1 = bf16[1536,3072]{1,0:T(8,128)(2,1)S(1)} fusion(bf16[384,3072]{1,0:T(8,128)(2,1)S(1)} %collective-permute-done.15, bf16[384,3072]{1,0:T(8,128)(2,1)} %collective-permute-done.4, bf16[384,768]{1,0:T(8,128)(2,1)S(1)} %get-tuple-element.182, bf16[384,768]{1,0:T(8,128)(2,1)S(1)} %get-tuple-element.181, ...), kind=kLoop, calls=%fused_computation.1 | loop fusion | flops 66060288 | bytes 18874368 | tf_op jit(solution)/shard_map/concatenate | solution.py:48
  189.3 5.2 %fusion.26 = f32[1536,512]{1,0:T(8,128)S(1)} fusion(bf16[1536,3072]{1,0:T(8,128)(2,1)S(1)} %pad_maximum_fusion, bf16[3072,512]{1,0:T(8,128)(2,1)S(1)} %bitcast.63), kind=kOutput, calls=%fused_computation.163 | convolution fusion | flops 4831838208 | bytes 15728640 | tf_op jit(solution)/shard_map/dot_general | solution.py:11
  201.7 7.3 %multiply_convert_fusion.3 = (bf16[1536,512]{1,0:T(8,128)(2,1)S(1)}, f32[1536,512]{1,0:T(8,128)}) fusion(f32[1536,512]{1,0:T(8,128)S(1)} %fusion.26, bf16[1536,3072]{1,0:T(8,128)(2,1)S(1)} %pad_maximum_fusion, bf16[3072,512]{1,0:T(8,128)(2,1)S(1)} %bitcast.70), kind=kOutput, calls=%fused_computation.15 | convolution fusion | flops 4836556800 | bytes 20447232 | tf_op jit(solution)/shard_map/dot_general | solution.py:11
  209.1 5.5 %convolution_convert_fusion.3 = bf16[3072,512]{1,0:T(8,128)(2,1)S(1)} fusion(bf16[1536,3072]{1,0:T(8,128)(2,1)S(1)} %pad_maximum_fusion.1, bf16[1536,512]{1,0:T(8,128)(2,1)S(1)} %get-tuple-element.127), kind=kOutput, calls=%fused_computation.9 | convolution fusion | flops 4833411072 | bytes 14155776 | tf_op jit(solution)/shard_map/dot_general | solution.py:11
  215.5 1.9 constant_dynamic-slice_fusion.19
  217.5 2.2 bitcast_dynamic-update-slice_fusion.2
  219.7 2.1 bitcast_dynamic-update-slice_fusion.1
  222.8 12.7 %multiply_convert_fusion.1 = (bf16[1536,512]{1,0:T(8,128)(2,1)}, bf16[1536,512]{1,0:T(8,128)(2,1)}) fusion(f32[1536,512]{1,0:T(8,128)S(1)} %copy-done.50, f32[1536,512]{1,0:T(8,128)} %get-tuple-element.126, bf16[1536,3072]{1,0:T(8,128)(2,1)} %copy-done.1, bf16[3072,512]{1,0:T(8,128)(2,1)} %bitcast.67), kind=kOutput, calls=%fused_computation.13 | convolution fusion | flops 4842061824 | bytes 22020096 | tf_op jit(solution)/shard_map/dot_general | solution.py:11
  235.5 8.2 %convolution_convert_fusion.2 = bf16[3072,512]{1,0:T(8,128)(2,1)S(1)} fusion(bf16[1536,3072]{1,0:T(8,128)(2,1)} %copy-done, bf16[1536,512]{1,0:T(8,128)(2,1)} %get-tuple-element.132), kind=kOutput, calls=%fused_computation.8 | convolution fusion | flops 4833411072 | bytes 14155776 | tf_op jit(solution)/shard_map/dot_general | solution.py:11
  243.7 1.9 constant_dynamic-slice_fusion.17
  247.2 4.3 convolution_convert_fusion
  251.5 2.6 fusion.5
  254.1 4.4 add_convert_fusion.2
  258.5 13.4 %reduce-scatter.9.cloned.1.call-done = bf16[768,512]{1,0:T(8,128)(2,1)} async-done(((bf16[1536,512]{1,0:T(8,128)(2,1)}), bf16[768,512]{1,0:T(8,128)(2,1)}) %reduce-scatter.9.cloned.1.call-update) | async-done | bytes 786448 | tf_op jit(solution)/shard_map/reduce_scatter | solution.py:110
  272.4 2.4 collective-permute-start.18
  274.9 8.4 %convolution_convert_fusion.1 = bf16[3072,512]{1,0:T(8,128)(2,1)S(1)} fusion(bf16[1536,3072]{1,0:T(8,128)(2,1)} %copy-done, bf16[1536,512]{1,0:T(8,128)(2,1)} %get-tuple-element.133), kind=kOutput, calls=%fused_computation.7 | convolution fusion | flops 4833411072 | bytes 14155776 | tf_op jit(solution)/shard_map/dot_general | solution.py:11
  286.8 2.6 fusion.9
  289.5 4.7 add_convert_fusion
  298.9 6.2 %add_convert_fusion.1 = bf16[768,3072]{1,0:T(8,128)(2,1)} fusion(bf16[768,3072]{1,0:T(8,128)(2,1)} %collective-permute-done.19, f32[768,3072]{1,0:T(8,128)S(1)} %fusion.9, bf16[3072,512]{1,0:T(8,128)(2,1)S(1)} %bitcast.65, bf16[1536,512]{1,0:T(8,128)(2,1)S(1)} %copy-done.18), kind=kOutput, calls=%fused_computation.3 | convolution fusion | flops 2425356288 | bytes 22806528 | tf_op jit(solution)/shard_map/dot_general | solution.py:11
  305.1 4.7 collective-permute-done.18
  309.7 7.3 %reduce-scatter.11.cloned.1.call-done = bf16[768,512]{1,0:T(8,128)(2,1)} async-done(((bf16[1536,512]{1,0:T(8,128)(2,1)}), bf16[768,512]{1,0:T(8,128)(2,1)}) %reduce-scatter.11.cloned.1.call-update) | async-done | bytes 786448 | tf_op jit(solution)/shard_map/reduce_scatter | solution.py:110
  320.1 2.7 fusion.23
  323.4 21.7 %collective-permute-done.22 = bf16[384,1536]{1,0:T(8,128)(2,1)S(1)} collective-permute-done((bf16[384,1536]{1,0:T(8,128)(2,1)}, bf16[384,1536]{1,0:T(8,128)(2,1)S(1)}, u32[]{:S(2)}, u32[]{:S(2)}) %collective-permute-start.22) | collective-permute-done | bytes 1179680 | tf_op jit(solution)/shard_map/ppermute | solution.py:28
  349.4 6.4 %collective-permute-done.21 = bf16[768,512]{1,0:T(8,128)(2,1)} collective-permute-done((bf16[768,512]{1,0:T(8,128)(2,1)}, bf16[768,512]{1,0:T(8,128)(2,1)}, u32[]{:S(2)}, u32[]{:S(2)}) %collective-permute-start.21) | collective-permute-done | bytes 786464 | tf_op jit(solution)/shard_map/ppermute | solution.py:28
  355.8 5.3 %reduce-scatter.13.cloned.1.call-done = bf16[768,512]{1,0:T(8,128)(2,1)} async-done(((bf16[1536,512]{1,0:T(8,128)(2,1)}), bf16[768,512]{1,0:T(8,128)(2,1)}) %reduce-scatter.13.cloned.1.call-update) | async-done | bytes 786448 | tf_op jit(solution)/shard_map/reduce_scatter | solution.py:110
  364.5 37.6 %collective-permute-done.26 = bf16[384,2304]{1,0:T(8,128)(2,1)S(1)} collective-permute-done((bf16[384,2304]{1,0:T(8,128)(2,1)}, bf16[384,2304]{1,0:T(8,128)(2,1)S(1)}, u32[]{:S(2)}, u32[]{:S(2)}) %collective-permute-start.26) | collective-permute-done | bytes 1769504 | tf_op jit(solution)/shard_map/ppermute | solution.py:28
  419.6 18.4 %collective-permute-done.27 = bf16[384,768]{1,0:T(8,128)(2,1)S(1)} collective-permute-done((bf16[384,768]{1,0:T(8,128)(2,1)S(1)}, bf16[384,768]{1,0:T(8,128)(2,1)S(1)}, u32[]{:S(2)}, u32[]{:S(2)}) %collective-permute-start.27) | collective-permute-done | bytes 589856 | tf_op jit(solution)/shard_map/ppermute | solution.py:28
  444.5 2.0 convolution_convert_fusion.7
  453.2 15.2 %collective-permute-done.30 = bf16[384,768]{1,0:T(8,128)(2,1)S(1)} collective-permute-done((bf16[384,768]{1,0:T(8,128)(2,1)S(1)}, bf16[384,768]{1,0:T(8,128)(2,1)S(1)}, u32[]{:S(2)}, u32[]{:S(2)}) %collective-permute-start.30) | collective-permute-done | bytes 589856 | tf_op jit(solution)/shard_map/ppermute | solution.py:28
  468.4 3.0 convolution_convert_fusion.6
  (254 shorter events, 90.5 us)
Async XLA Ops:
  7.2 251.3 %reduce-scatter.7.cloned.1.call-start = ((), (), s32[]{:S(2)}) async-start(), calls=%async_computation.6 | async-start | bytes 2359296 | tf_op jit(solution)/shard_map/reduce_scatter | solution.py:110
  9.6 38.8 %collective-permute-start = (bf16[384,1024]{1,0:T(8,128)(2,1)}, bf16[384,1024]{1,0:T(8,128)(2,1)}, u32[]{:S(2)}, u32[]{:S(2)}) collective-permute-start(bf16[384,1024]{1,0:T(8,128)(2,1)} %get-tuple-element.227), channel_id=1, source_target_pairs={{0,16},{4,20},{8,24},{12,28},{16,0},{20,4},{24,8},{28,12},{1,17},{... | collective-permute-start | bytes 2359304 | tf_op jit(solution)/shard_map/ppermute | solution.py:28
  13.7 34.8 %collective-permute-start.1 = (bf16[384,1024]{1,0:T(8,128)(2,1)S(1)}, bf16[384,1024]{1,0:T(8,128)(2,1)}, u32[]{:S(2)}, u32[]{:S(2)}) collective-permute-start(bf16[384,1024]{1,0:T(8,128)(2,1)S(1)} %get-tuple-element.94), channel_id=1, source_target_pairs={{0,8},{4,12},{8,0},{12,4},{16,24},{20,28},{24,16},{28,20},{1,9},{5... | collective-permute-start | bytes 2359304 | tf_op jit(solution)/shard_map/ppermute | solution.py:28
  48.5 5.8 %collective-permute-start.5 = (bf16[768,1024]{1,0:T(8,128)(2,1)S(1)}, bf16[768,1024]{1,0:T(8,128)(2,1)}, u32[]{:S(2)}, u32[]{:S(2)}) collective-permute-start(bf16[768,1024]{1,0:T(8,128)(2,1)S(1)} %maximum_maximum_fusion), channel_id=1, source_target_pairs={{0,4},{4,0},{8,12},{12,8},{16,20},{20,16},{24,28},{28,24},{1,5},{5... | collective-permute-start | bytes 4718600 | tf_op jit(solution)/shard_map/ppermute | solution.py:28
  48.5 55.3 %collective-permute-start.3 = (bf16[384,3072]{1,0:T(8,128)(2,1)}, bf16[384,3072]{1,0:T(8,128)(2,1)}, u32[]{:S(2)}, u32[]{:S(2)}) collective-permute-start(bf16[384,3072]{1,0:T(8,128)(2,1)} %convolution_convert_fusion.5), channel_id=1, source_target_pairs={{0,4},{4,0},{8,12},{12,8},{16,20},{20,16},{24,28},{28,24},{1,5},{5... | collective-permute-start | bytes 7077896 | tf_op jit(solution)/shard_map/ppermute | solution.py:28
  49.0 54.8 %collective-permute-start.4 = (bf16[384,3072]{1,0:T(8,128)(2,1)}, bf16[384,3072]{1,0:T(8,128)(2,1)}, u32[]{:S(2)}, u32[]{:S(2)}) collective-permute-start(bf16[384,3072]{1,0:T(8,128)(2,1)} %get-tuple-element.90), channel_id=1, source_target_pairs={{0,4},{4,0},{8,12},{12,8},{16,20},{20,16},{24,28},{28,24},{1,5},{5... | collective-permute-start | bytes 7077896 | tf_op jit(solution)/shard_map/ppermute | solution.py:28
  49.0 54.8 %collective-permute-start.2 = (bf16[768,768]{1,0:T(8,128)(2,1)}, bf16[768,768]{1,0:T(8,128)(2,1)S(1)}, u32[]{:S(2)}, u32[]{:S(2)}) collective-permute-start(bf16[768,768]{1,0:T(8,128)(2,1)} %pad_maximum_fusion.8), channel_id=1, source_target_pairs={{0,16},{4,20},{8,24},{12,28},{16,0},{20,4},{24,8},{28,12},{1,17},{... | collective-permute-start | bytes 3538952 | tf_op jit(solution)/shard_map/ppermute | solution.py:28
  50.6 43.1 %collective-permute-start.6 = (bf16[384,1024]{1,0:T(8,128)(2,1)}, bf16[384,1024]{1,0:T(8,128)(2,1)S(1)}, u32[]{:S(2)}, u32[]{:S(2)}) collective-permute-start(bf16[384,1024]{1,0:T(8,128)(2,1)} %collective-permute-done), channel_id=1, source_target_pairs={{0,8},{4,12},{8,0},{12,4},{16,24},{20,28},{24,16},{28,20},{1,9},{5... | collective-permute-start | bytes 2359304 | tf_op jit(solution)/shard_map/ppermute | solution.py:28
  59.3 53.3 %copy-start.6 = (bf16[768,1024]{1,0:T(8,128)(2,1)}, bf16[768,1024]{1,0:T(8,128)(2,1)S(1)}, u32[]{:S(2)}) copy-start(bf16[768,1024]{1,0:T(8,128)(2,1)S(1)} %pad_maximum_fusion.7) | copy-start | bytes 4718596
  103.8 54.2 %collective-permute-start.11 = (bf16[768,1024]{1,0:T(8,128)(2,1)S(1)}, bf16[768,1024]{1,0:T(8,128)(2,1)}, u32[]{:S(2)}, u32[]{:S(2)}) collective-permute-start(bf16[768,1024]{1,0:T(8,128)(2,1)S(1)} %pad_maximum_fusion.7), channel_id=1, source_target_pairs={{0,8},{4,12},{8,0},{12,4},{16,24},{20,28},{24,16},{28,20},{1,9},{5... | collective-permute-start | bytes 4718600 | tf_op jit(solution)/shard_map/ppermute | solution.py:28
  103.8 50.8 %collective-permute-start.10 = (bf16[768,768]{1,0:T(8,128)(2,1)S(1)}, bf16[768,768]{1,0:T(8,128)(2,1)}, u32[]{:S(2)}, u32[]{:S(2)}) collective-permute-start(bf16[768,768]{1,0:T(8,128)(2,1)S(1)} %collective-permute-done.2), channel_id=1, source_target_pairs={{0,3},{1,2},{2,1},{3,0},{4,7},{5,6},{6,5},{7,4},{8,11},{9,10},{10,... | collective-permute-start | bytes 3538952 | tf_op jit(solution)/shard_map/ppermute | solution.py:28
  106.4 51.5 %collective-permute-start.8 = (bf16[768,768]{1,0:T(8,128)(2,1)S(1)}, bf16[768,768]{1,0:T(8,128)(2,1)}, u32[]{:S(2)}, u32[]{:S(2)}) collective-permute-start(bf16[768,768]{1,0:T(8,128)(2,1)S(1)} %collective-permute-done.2), channel_id=1, source_target_pairs={{0,1},{1,0},{2,3},{3,2},{4,5},{5,4},{6,7},{7,6},{8,9},{9,8},{10,11... | collective-permute-start | bytes 3538952 | tf_op jit(solution)/shard_map/ppermute | solution.py:28
  107.0 51.0 %collective-permute-start.9 = (bf16[768,768]{1,0:T(8,128)(2,1)S(1)}, bf16[768,768]{1,0:T(8,128)(2,1)}, u32[]{:S(2)}, u32[]{:S(2)}) collective-permute-start(bf16[768,768]{1,0:T(8,128)(2,1)S(1)} %collective-permute-done.2), channel_id=1, source_target_pairs={{0,2},{1,3},{2,0},{3,1},{4,6},{5,7},{6,4},{7,5},{8,10},{9,11},{10,... | collective-permute-start | bytes 3538952 | tf_op jit(solution)/shard_map/ppermute | solution.py:28
  107.4 47.2 %collective-permute-start.7 = (bf16[768,512]{1,0:T(8,128)(2,1)}, bf16[768,512]{1,0:T(8,128)(2,1)}, u32[]{:S(2)}, u32[]{:S(2)}) collective-permute-start(bf16[768,512]{1,0:T(8,128)(2,1)} %maximum_select_fusion.2), channel_id=1, source_target_pairs={{0,16},{4,20},{8,24},{12,28},{16,0},{20,4},{24,8},{28,12},{1,17},{... | collective-permute-start | bytes 2359304 | tf_op jit(solution)/shard_map/ppermute | solution.py:28
  158.0 5.3 %collective-permute-start.13 = (bf16[4,384,512]{2,1,0:T(8,128)(2,1)}, bf16[4,384,512]{2,1,0:T(8,128)(2,1)}, u32[]{:S(2)}, u32[]{:S(2)}) collective-permute-start(bf16[4,384,512]{2,1,0:T(8,128)(2,1)} %get-tuple-element.103), channel_id=1, source_target_pairs={{0,4},{4,0},{8,12},{12,8},{16,20},{20,16},{24,28},{28,24},{1,5},{5... | collective-permute-start | bytes 4718600 | tf_op jit(solution)/shard_map/ppermute | solution.py:28
  158.1 38.3 %collective-permute-start.12 = (bf16[768,512]{1,0:T(8,128)(2,1)}, bf16[768,512]{1,0:T(8,128)(2,1)S(1)}, u32[]{:S(2)}, u32[]{:S(2)}) collective-permute-start(bf16[768,512]{1,0:T(8,128)(2,1)} %maximum_select_fusion.3), channel_id=1, source_target_pairs={{0,16},{4,20},{8,24},{12,28},{16,0},{20,4},{24,8},{28,12},{1,17},{... | collective-permute-start | bytes 2359304 | tf_op jit(solution)/shard_map/ppermute | solution.py:28
  161.1 35.8 %collective-permute-start.16 = (bf16[768,512]{1,0:T(8,128)(2,1)}, bf16[768,512]{1,0:T(8,128)(2,1)}, u32[]{:S(2)}, u32[]{:S(2)}) collective-permute-start(bf16[768,512]{1,0:T(8,128)(2,1)} %collective-permute-done.7), channel_id=1, source_target_pairs={{0,8},{4,12},{8,0},{12,4},{16,24},{20,28},{24,16},{28,20},{1,9},{5... | collective-permute-start | bytes 2359304 | tf_op jit(solution)/shard_map/ppermute | solution.py:28
  168.4 7.2 %collective-permute-start.14 = (bf16[384,3072]{1,0:T(8,128)(2,1)S(1)}, bf16[384,3072]{1,0:T(8,128)(2,1)S(1)}, u32[]{:S(2)}, u32[]{:S(2)}) collective-permute-start(bf16[384,3072]{1,0:T(8,128)(2,1)S(1)} %pad_maximum_fusion.3), channel_id=1, source_target_pairs={{0,4},{4,0},{8,12},{12,8},{16,20},{20,16},{24,28},{28,24},{1,5},{5... | collective-permute-start | bytes 7077896 | tf_op jit(solution)/shard_map/ppermute | solution.py:28
  170.8 11.0 %collective-permute-start.15 = (bf16[384,3072]{1,0:T(8,128)(2,1)S(1)}, bf16[384,3072]{1,0:T(8,128)(2,1)S(1)}, u32[]{:S(2)}, u32[]{:S(2)}) collective-permute-start(bf16[384,3072]{1,0:T(8,128)(2,1)S(1)} %pad_maximum_fusion.4), channel_id=1, source_target_pairs={{0,4},{4,0},{8,12},{12,8},{16,20},{20,16},{24,28},{28,24},{1,5},{5... | collective-permute-start | bytes 7077896 | tf_op jit(solution)/shard_map/ppermute | solution.py:28
  196.9 18.6 %collective-permute-start.17 = (bf16[768,512]{1,0:T(8,128)(2,1)S(1)}, bf16[768,512]{1,0:T(8,128)(2,1)S(1)}, u32[]{:S(2)}, u32[]{:S(2)}) collective-permute-start(bf16[768,512]{1,0:T(8,128)(2,1)S(1)} %collective-permute-done.12), channel_id=1, source_target_pairs={{0,8},{4,12},{8,0},{12,4},{16,24},{20,28},{24,16},{28,20},{1,9},{5... | collective-permute-start | bytes 2359304 | tf_op jit(solution)/shard_map/ppermute | solution.py:28
  217.4 54.5 %reduce-scatter.9.cloned.1.call-start = ((), (), s32[]{:S(2)}) async-start(), calls=%async_computation.7 | async-start | bytes 2359296 | tf_op jit(solution)/shard_map/reduce_scatter | solution.py:110
  235.5 81.6 %reduce-scatter.11.cloned.1.call-start = ((), (), s32[]{:S(2)}) async-start(), calls=%async_computation.8 | async-start | bytes 2359296 | tf_op jit(solution)/shard_map/reduce_scatter | solution.py:110
  271.9 17.5 %collective-permute-start.20 = (bf16[768,3072]{1,0:T(8,128)(2,1)}, bf16[768,3072]{1,0:T(8,128)(2,1)}, u32[]{:S(2)}, u32[]{:S(2)}) collective-permute-start(bf16[768,3072]{1,0:T(8,128)(2,1)} %convolution_convert_fusion), channel_id=1, source_target_pairs={{0,4},{4,0},{8,12},{12,8},{16,20},{20,16},{24,28},{28,24},{1,5},{5... | collective-permute-start | bytes 14155784 | tf_op jit(solution)/shard_map/ppermute | solution.py:28
  271.9 27.0 %collective-permute-start.19 = (bf16[768,3072]{1,0:T(8,128)(2,1)}, bf16[768,3072]{1,0:T(8,128)(2,1)}, u32[]{:S(2)}, u32[]{:S(2)}) collective-permute-start(bf16[768,3072]{1,0:T(8,128)(2,1)} %add_convert_fusion.2), channel_id=1, source_target_pairs={{0,4},{4,0},{8,12},{12,8},{16,20},{20,16},{24,28},{28,24},{1,5},{5... | collective-permute-start | bytes 14155784 | tf_op jit(solution)/shard_map/ppermute | solution.py:28
  272.4 37.3 %collective-permute-start.18 = (bf16[768,512]{1,0:T(8,128)(2,1)}, bf16[768,512]{1,0:T(8,128)(2,1)}, u32[]{:S(2)}, u32[]{:S(2)}) collective-permute-start(bf16[768,512]{1,0:T(8,128)(2,1)} %reduce-scatter.7.cloned.1.call-done), channel_id=1, source_target_pairs={{0,16},{4,20},{8,24},{12,28},{16,0},{20,4},{24,8},{28,12},{1,17},{... | collective-permute-start | bytes 2359304 | tf_op jit(solution)/shard_map/ppermute | solution.py:28
  274.9 86.3 %reduce-scatter.13.cloned.1.call-start = ((), (), s32[]{:S(2)}) async-start(), calls=%async_computation.9 | async-start | bytes 2359296 | tf_op jit(solution)/shard_map/reduce_scatter | solution.py:110
  317.0 89.0 %reduce-scatter.15.cloned.1.call-start = ((), (), s32[]{:S(2)}) async-start(), calls=%async_computation.10 | async-start | bytes 2359296 | tf_op jit(solution)/shard_map/reduce_scatter | solution.py:110
  317.1 28.0 %collective-permute-start.22 = (bf16[384,1536]{1,0:T(8,128)(2,1)}, bf16[384,1536]{1,0:T(8,128)(2,1)S(1)}, u32[]{:S(2)}, u32[]{:S(2)}) collective-permute-start(bf16[384,1536]{1,0:T(8,128)(2,1)} %pad_maximum_fusion.9), channel_id=1, source_target_pairs={{0,1},{1,0},{2,3},{3,2},{4,5},{5,4},{6,7},{7,6},{8,9},{9,8},{10,11... | collective-permute-start | bytes 3538952 | tf_op jit(solution)/shard_map/ppermute | solution.py:28
  318.7 27.6 %collective-permute-start.23 = (bf16[384,1536]{1,0:T(8,128)(2,1)}, bf16[384,1536]{1,0:T(8,128)(2,1)S(1)}, u32[]{:S(2)}, u32[]{:S(2)}) collective-permute-start(bf16[384,1536]{1,0:T(8,128)(2,1)} %pad_maximum_fusion.10), channel_id=1, source_target_pairs={{0,2},{1,3},{2,0},{3,1},{4,6},{5,7},{6,4},{7,5},{8,10},{9,11},{10,... | collective-permute-start | bytes 3538952 | tf_op jit(solution)/shard_map/ppermute | solution.py:28
  320.1 35.7 %collective-permute-start.21 = (bf16[768,512]{1,0:T(8,128)(2,1)}, bf16[768,512]{1,0:T(8,128)(2,1)}, u32[]{:S(2)}, u32[]{:S(2)}) collective-permute-start(bf16[768,512]{1,0:T(8,128)(2,1)} %reduce-scatter.11.cloned.1.call-done), channel_id=1, source_target_pairs={{0,16},{4,20},{8,24},{12,28},{16,0},{20,4},{24,8},{28,12},{1,17},{... | collective-permute-start | bytes 2359304 | tf_op jit(solution)/shard_map/ppermute | solution.py:28
  322.8 22.3 %copy-start.5 = (bf16[384,3072]{1,0:T(8,128)(2,1)S(1)}, bf16[384,3072]{1,0:T(8,128)(2,1)}, u32[]{:S(2)}) copy-start(bf16[384,3072]{1,0:T(8,128)(2,1)} %copy-done.4) | copy-start | bytes 7077892
  323.4 22.9 %copy-start.3 = (bf16[384,3072]{1,0:T(8,128)(2,1)S(1)}, bf16[384,3072]{1,0:T(8,128)(2,1)}, u32[]{:S(2)}) copy-start(bf16[384,3072]{1,0:T(8,128)(2,1)} %copy-done.2) | copy-start | bytes 7077892
  361.2 88.6 %reduce-scatter.17.cloned.1.call-start = ((), (), s32[]{:S(2)}) async-start(), calls=%async_computation.11 | async-start | bytes 2359296 | tf_op jit(solution)/shard_map/reduce_scatter | solution.py:110
  361.5 40.6 %collective-permute-start.26 = (bf16[384,2304]{1,0:T(8,128)(2,1)}, bf16[384,2304]{1,0:T(8,128)(2,1)S(1)}, u32[]{:S(2)}, u32[]{:S(2)}) collective-permute-start(bf16[384,2304]{1,0:T(8,128)(2,1)} %pad_maximum_fusion.5), channel_id=1, source_target_pairs={{0,1},{1,0},{2,3},{3,2},{4,5},{5,4},{6,7},{7,6},{8,9},{9,8},{10,11... | collective-permute-start | bytes 5308424 | tf_op jit(solution)/shard_map/ppermute | solution.py:28
  363.0 40.6 %collective-permute-start.25 = (bf16[384,2304]{1,0:T(8,128)(2,1)}, bf16[384,2304]{1,0:T(8,128)(2,1)S(1)}, u32[]{:S(2)}, u32[]{:S(2)}) collective-permute-start(bf16[384,2304]{1,0:T(8,128)(2,1)} %pad_maximum_fusion.6), channel_id=1, source_target_pairs={{0,2},{1,3},{2,0},{3,1},{4,6},{5,7},{6,4},{7,5},{8,10},{9,11},{10,... | collective-permute-start | bytes 5308424 | tf_op jit(solution)/shard_map/ppermute | solution.py:28
  364.5 40.4 %collective-permute-start.24 = (bf16[768,512]{1,0:T(8,128)(2,1)}, bf16[768,512]{1,0:T(8,128)(2,1)}, u32[]{:S(2)}, u32[]{:S(2)}) collective-permute-start(bf16[768,512]{1,0:T(8,128)(2,1)} %reduce-scatter.13.cloned.1.call-done), channel_id=1, source_target_pairs={{0,16},{4,20},{8,24},{12,28},{16,0},{20,4},{24,8},{28,12},{1,17},{... | collective-permute-start | bytes 2359304 | tf_op jit(solution)/shard_map/ppermute | solution.py:28
  408.8 38.6 %collective-permute-start.35 = (bf16[384,1024]{1,0:T(8,128)(2,1)S(1)}, bf16[384,1024]{1,0:T(8,128)(2,1)S(1)}, u32[]{:S(2)}, u32[]{:S(2)}) collective-permute-start(bf16[384,1024]{1,0:T(8,128)(2,1)S(1)} %constant_dynamic-slice_fusion), channel_id=1, source_target_pairs={{0,4},{4,0},{8,12},{12,8},{16,20},{20,16},{24,28},{28,24},{1,5},{5... | collective-permute-start | bytes 2359304 | tf_op jit(solution)/shard_map/ppermute | solution.py:28
  408.9 29.0 %collective-permute-start.27 = (bf16[384,768]{1,0:T(8,128)(2,1)S(1)}, bf16[384,768]{1,0:T(8,128)(2,1)S(1)}, u32[]{:S(2)}, u32[]{:S(2)}) collective-permute-start(bf16[384,768]{1,0:T(8,128)(2,1)S(1)} %copy-done.33), channel_id=1, source_target_pairs={{0,16},{4,20},{8,24},{12,28},{16,0},{20,4},{24,8},{28,12},{1,17},{... | collective-permute-start | bytes 1769480 | tf_op jit(solution)/shard_map/ppermute | solution.py:28
  410.5 38.5 %collective-permute-start.33 = (bf16[384,1024]{1,0:T(8,128)(2,1)S(1)}, bf16[384,1024]{1,0:T(8,128)(2,1)S(1)}, u32[]{:S(2)}, u32[]{:S(2)}) collective-permute-start(bf16[384,1024]{1,0:T(8,128)(2,1)S(1)} %constant_dynamic-slice_fusion.2), channel_id=1, source_target_pairs={{0,4},{4,0},{8,12},{12,8},{16,20},{20,16},{24,28},{28,24},{1,5},{5... | collective-permute-start | bytes 2359304 | tf_op jit(solution)/shard_map/ppermute | solution.py:28
  410.9 30.0 %collective-permute-start.29 = (bf16[384,768]{1,0:T(8,128)(2,1)S(1)}, bf16[384,768]{1,0:T(8,128)(2,1)S(1)}, u32[]{:S(2)}, u32[]{:S(2)}) collective-permute-start(bf16[384,768]{1,0:T(8,128)(2,1)S(1)} %copy-done.34), channel_id=1, source_target_pairs={{0,1},{1,0},{2,3},{3,2},{4,5},{5,4},{6,7},{7,6},{8,9},{9,8},{10,11... | collective-permute-start | bytes 1769480 | tf_op jit(solution)/shard_map/ppermute | solution.py:28
  412.4 40.8 %collective-permute-start.28 = (bf16[384,768]{1,0:T(8,128)(2,1)S(1)}, bf16[384,768]{1,0:T(8,128)(2,1)}, u32[]{:S(2)}, u32[]{:S(2)}) collective-permute-start(bf16[384,768]{1,0:T(8,128)(2,1)S(1)} %copy-done.32), channel_id=1, source_target_pairs={{0,2},{1,3},{2,0},{3,1},{4,6},{5,7},{6,4},{7,5},{8,10},{9,11},{10,... | collective-permute-start | bytes 1769480 | tf_op jit(solution)/shard_map/ppermute | solution.py:28
  418.8 25.6 %copy-start.36 = (s32[768]{0:T(1024)S(1)}, s32[768]{0:T(1024)}, u32[]{:S(2)}) copy-start(s32[768]{0:T(1024)} %copy-done.35) | copy-start | bytes 9220
  418.8 25.6 %copy-start.39 = (pred[768]{0:T(1024)(128)(4,1)S(1)}, pred[768]{0:T(1024)(128)(4,1)}, u32[]{:S(2)}) copy-start(pred[768]{0:T(1024)(128)(4,1)} %copy-done.38) | copy-start | bytes 2308
  418.8 25.6 %copy-start.42 = (f32[384]{0:T(512)S(1)}, f32[384]{0:T(512)}, u32[]{:S(2)}) copy-start(f32[384]{0:T(512)} %copy-done.41) | copy-start | bytes 4612
  439.3 3.6 collective-permute-start.31
  441.0 27.4 %collective-permute-start.30 = (bf16[384,768]{1,0:T(8,128)(2,1)S(1)}, bf16[384,768]{1,0:T(8,128)(2,1)S(1)}, u32[]{:S(2)}, u32[]{:S(2)}) collective-permute-start(bf16[384,768]{1,0:T(8,128)(2,1)S(1)} %add_convert_fusion.4), channel_id=1, source_target_pairs={{0,16},{4,20},{8,24},{12,28},{16,0},{20,4},{24,8},{28,12},{1,17},{... | collective-permute-start | bytes 1769480 | tf_op jit(solution)/shard_map/ppermute | solution.py:28
  443.0 3.6 collective-permute-start.32
  452.4 19.3 %collective-permute-start.34 = (bf16[384,1024]{1,0:T(8,128)(2,1)S(1)}, bf16[384,1024]{1,0:T(8,128)(2,1)S(1)}, u32[]{:S(2)}, u32[]{:S(2)}) collective-permute-start(bf16[384,1024]{1,0:T(8,128)(2,1)S(1)} %constant_dynamic-slice_fusion.1), channel_id=1, source_target_pairs={{0,4},{4,0},{8,12},{12,8},{16,20},{20,16},{24,28},{28,24},{1,5},{5... | collective-permute-start | bytes 2359304 | tf_op jit(solution)/shard_map/ppermute | solution.py:28
  (45 other events, 233.6 us)
Sparse Core Ops, SparseCore 0:
  217.5 25.8 reduce-scatter.6
  245.8 26.0 reduce-scatter.8
  275.0 42.0 reduce-scatter.10
  319.2 41.8 reduce-scatter.12
  363.2 42.7 reduce-scatter.14
  408.3 38.6 reduce-scatter.16

commit v7 on v5

--- a/solution.py
+++ b/solution.py
@@ -135,6 +135,15 @@
     def done(kept, got):
         return (kept.astype(F32) + got.astype(F32)).astype(BF16)
 
+    half_rows = depth // 2
+    same_core = [[u * far + 2 * i + c for i in range(n_chip // 2)] for u in range(2) for c in range(2)]
+
+    def scatter_far(panel):
+        rows = lax.dynamic_slice_in_dim(panel, (1 - upper) * half_rows, half_rows, 0)
+        return lax.psum_scatter(
+            rows, "dp", scatter_dimension=0, tiled=True, axis_index_groups=same_core
+        )
+
     def part(w, u, c):
         return lax.dynamic_slice_in_dim(w, (u * 2 + c) * hid, hid, 1)
 
@@ -218,10 +227,7 @@
     g_down, hidden, up_pre, up, *down_far = fence(g_down, hidden, up_pre, up, *down_far)
 
     table = 2 * row_limit
-    g_down_4 = first_send(blocks_far(g_down))
-    n_kept = len(g_down_4)
-    g_down_4 = shrink(*g_down_4)
-    g_down_own = shrink(*first_send(blocks_own(g_down)))
+    g_down_4 = scatter_far(g_down)
     down = whole_panel(down_own, down_far)
     hidden_grad = mm(out_all, down)
     gate_grad = (
@@ -234,20 +240,23 @@
     def input_part(rows):
         return mm_last(gate_grad[rows], gate) + mm_last(up_grad[rows], up)
 
-    input_sib = input_part(slice(table, None)).astype(BF16)
-    down, gate_grad, up_grad, g_gate, expert_sib, input_sib, *rest = fence(
-        down, gate_grad, up_grad, g_gate, expert_sib, input_sib, *g_down_4, *g_down_own
-    )
-    g_down_own = rest[2:]
-    g_down_4, expert_sib, input_sib, g_gate = fence(done(*rest[:2]), expert_sib, input_sib, g_gate)
     g_gate_4, g_gate_own = first_send(blocks_far(g_gate)), first_send(blocks_own(g_gate))
+    n_kept = len(g_gate_4)
+    down, gate_grad, up_grad, expert_sib, g_down_4, g_down, *rest = fence(
+        down, gate_grad, up_grad, expert_sib, g_down_4, g_down, *g_gate_4, *g_gate_own
+    )
+    g_gate_4, g_gate_own = rest[:n_kept], rest[n_kept:]
 
     g_down_far = z_far(g_down_4)
     g_gate_4 = shrink(*g_gate_4)
-    expert_got, input_got = across(expert_sib), across(input_sib)
+    expert_got, in_all, gate_grad, up_grad, hidden = fence(
+        across(expert_sib[:row_limit]), in_all, gate_grad, up_grad, hidden
+    )
+    expert_got = cat(expert_got, across(expert_sib[row_limit:]))
     g_up = mm_first(in_all, up_grad).astype(BF16)
     expert_sum = (mm_last(hidden[:table], down) + expert_got.astype(F32)).astype(BF16)
-    input_sum = (input_part(slice(None, table)) + input_got.astype(F32)).astype(BF16)
+    input_sib = input_part(slice(table, None)).astype(BF16)
+    input_sum = input_part(slice(None, table)).astype(BF16)
 
     def split_parts(value):
         return {
@@ -278,12 +287,12 @@
     expert_mine, expert_other = split_rows(expert_sum)
     send_low, send_high = gone(expert_mine, low), gone(expert_other, high)
     g_up_4, g_up_own = first_send(blocks_far(g_up)), first_send(blocks_own(g_up))
-    g_down_far, input_sum, send_low, send_high, *rest = fence(
-        g_down_far, input_sum, send_low, send_high, *g_gate_4, *g_up_4, *g_up_own
+    g_down_far, input_sum, input_sib, send_low, send_high, *rest = fence(
+        g_down_far, input_sum, input_sib, send_low, send_high, *g_gate_4, *g_up_4, *g_up_own
     )
     g_up_own = rest[2 + n_kept :]
-    g_gate_4, send_low, send_high, input_sum, *g_up_4 = fence(
-        done(*rest[:2]), send_low, send_high, input_sum, *rest[2 : 2 + n_kept]
+    g_gate_4, send_low, send_high, input_sib, *g_up_4 = fence(
+        done(*rest[:2]), send_low, send_high, input_sib, *rest[2 : 2 + n_kept]
     )
 
     def panel(own, other):
@@ -304,6 +313,7 @@
     g_up_4 = shrink(*g_up_4)
     expert_mine = kept(expert_mine, low, swap(send_low, "tensor", low))
     expert_other = kept(expert_other, high, swap(send_high, "tensor", high))
+    input_sum = (input_sum.astype(F32) + across(input_sib).astype(F32)).astype(BF16)
     input_mine, input_other = split_rows(input_sum)
     merged = len(t_bits) == 2
     if merged:
@@ -335,24 +345,21 @@
             expert_other = step(expert_other, bit)
     input_other = kept(input_other, high, got_high)
     input_mine = kept(input_mine, low, got_low)
-    g_up_far, expert_mine, expert_other, input_mine, input_other, *rest = fence(
-        g_up_far, expert_mine[0], expert_other[0], input_mine, input_other, *g_gate_own, *g_up_own
-    )
-    g_gate_own, g_up_own = rest[:2], rest[2:]
-
-    g_up_own = shrink(*g_up_own)
+    last_own = tuple(beside(*both) for both in zip(g_up_own, first_send(blocks_own(g_down))))
+    g_up_far, expert_mine, expert_other, input_mine, input_other, g_down_far, g_gate_far, *rest = fence(
+        g_up_far, expert_mine[0], expert_other[0], input_mine, input_other, g_down_far, g_gate_far,
+        *g_gate_own, *last_own
+    )
+    g_gate_own, last_own = rest[:2], rest[2:]
+
+    last_own = done(*shrink(*last_own))
+    g_up_own, g_down_own = last_own[:, :hid], last_own[:, hid:]
     expert_got = z_far(expert_other)
     for bit in t_bits[1:]:
         input_mine = step(input_mine, bit)
     for bit in t_bits[:-1][::-1]:
         input_other = step(input_other, bit)
-    expert_got, input_mine, input_other, g_down_far, g_gate_far, *rest = fence(
-        expert_got, input_mine[0], input_other[0], g_down_far, g_gate_far,
-        *g_down_own, *g_gate_own, *g_up_own
-    )
-    g_down_own, g_gate_own, g_up_own = rest[:2], rest[2:4], rest[4:]
-
-    input_got = z_far(input_other)
+    input_got = z_far(input_other[0])
     expert_cols = expert_mine.astype(F32) + expert_got.astype(F32)
     grad_cols = lax.dynamic_slice_in_dim(rows_grad, me_t * width, width, 1)
     weight_rows = jnp.sum(grad_cols.astype(F32) * expert_cols, axis=1)
@@ -360,16 +367,15 @@
         weight_rows = weight_rows + swap(weight_rows, "tensor", bit)
     weight_grad = jnp.sum(jnp.where(match, weight_rows[:, None], 0.0), axis=0)
     mixed = mm_first(hot, (row_weight[:, None] * expert_cols).astype(BF16)).astype(BF16)
-    input_cols = (input_mine.astype(F32) + input_got.astype(F32)).astype(BF16)
+    gate_out, up_out, down_out, input_got = fence(
+        panel(done(*g_gate_own), g_gate_far),
+        panel(g_up_own, g_up_far),
+        panel(g_down_own, g_down_far),
+        input_got,
+    )
+    input_cols = (input_mine[0].astype(F32) + input_got.astype(F32)).astype(BF16)
     input_grad = mm_first(hot, input_cols).astype(BF16)
-    return (
-        mixed,
-        input_grad,
-        weight_grad,
-        panel(done(*g_gate_own), g_gate_far),
-        panel(done(*g_up_own), g_up_far),
-        panel(done(*g_down_own), g_down_far),
-    )
+    return (mixed, input_grad, weight_grad, gate_out, up_out, down_out)
 
 
 def solution(mesh):

time: 478 us -> 477 us (level)
  waiting for transfers between devices: 254 us -> 218 us
  local copies, waits for them, and re-layouts: 37.3 us -> 52.4 us
  between operations: 2.21 us -> 15.8 us
    ppermute x42 -> x41, waiting for transfers between devices: 254 us -> 218 us  [swap(): return lax.ppermute(value, axis, [(i, i ^ distance) for i in range(size)])]
    slice x1 -> x3, local copies, waits for them, and re-layouts: 0.07 us -> 5.03 us  [the longest x1 4.85 us: local(): expert_got = cat(expert_got, across(expert_sib[row_limit:]))]
    unnamed x100 -> x136, local copies, waits for them, and re-layouts: 8.65 us -> 10.2 us
    ppermute x42 -> x41, starting transfers between devices: 43 us -> 43.4 us  [swap(): return lax.ppermute(value, axis, [(i, i ^ distance) for i in range(size)])]
  transfers between devices with their start and end apart: 42 -> 42, of which waited for: 23 -> 19; matrix products, arithmetic and copies ran while one was open for 28% -> 35% of each run, Pallas kernels for 0% -> 0%
where the time goes in v7:
time: 477 us; the launch traced here: 470 us
  waiting for transfers between devices  218 us (46%)
  matrix products  91.4 us (19%)
  local copies, waits for them, and re-layouts  52.4 us (11%)
  other arithmetic  49.1 us (10%)
  starting transfers between devices  43.5 us (9%)
  between operations  15.8 us (3%)
    ppermute x41, waiting for transfers between devices, swap(): return lax.ppermute(value, axis, [(i, i ^ distance) for i in range(size)])  218 us
    dot_general x16, matrix products, dot(): lax.dot_general(left, right, (dims, ((), ())), preferred_element_type=F32)  91.4 us
    ppermute x41, starting transfers between devices, swap(): return lax.ppermute(value, axis, [(i, i ^ distance) for i in range(size)])  43.4 us
    concatenate x4, other arithmetic, cat(): return jnp.concatenate(values, axis=0)  14.9 us
    unnamed x136, local copies, waits for them, and re-layouts  10.2 us
  transfers between devices with their start and end apart: 42, of which 19 were waited for; matrix products, arithmetic and copies ran while one was open for 35% of the time, Pallas kernels for 0%

profile of v7, /device:TPU:0, one launch (start us, length us, event | category | flops | bytes accessed | tf_op | source)
XLA Modules:
  0.0 469.8 jit_solution(5671289250942120401)
XLA Ops:
  7.3 2.4 constant_dynamic-slice_fusion.19
  9.6 4.0 collective-permute-start
  16.2 5.9 %convolution_convert_fusion.5 = bf16[384,3072]{1,0:T(8,128)(2,1)} fusion(bf16[768,3072]{1,0:T(8,128)(2,1)} %param.7, s32[768]{0:T(1024)S(1)} %add_bitcast_fusion, pred[768]{0:T(1024)(128)(4,1)S(1)} %fusion.28), kind=kOutput, calls=%fused_computation.12 | convolution fusion | flops 1813708800 | bytes 7081728 | tf_op jit(solution)/shard_map/dot_general | solution.py:11
  22.1 4.3 multiply_convert_fusion
  32.3 16.2 %collective-permute-done = bf16[384,1024]{1,0:T(8,128)(2,1)} collective-permute-done((bf16[384,1024]{1,0:T(8,128)(2,1)}, bf16[384,1024]{1,0:T(8,128)(2,1)}, u32[]{:S(2)}, u32[]{:S(2)}) %collective-permute-start) | collective-permute-done | bytes 786464 | tf_op jit(solution)/shard_map/ppermute | solution.py:28
  50.6 2.4 collective-permute-start.6
  59.3 34.4 %collective-permute-done.6 = bf16[384,1024]{1,0:T(8,128)(2,1)S(1)} collective-permute-done((bf16[384,1024]{1,0:T(8,128)(2,1)}, bf16[384,1024]{1,0:T(8,128)(2,1)S(1)}, u32[]{:S(2)}, u32[]{:S(2)}) %collective-permute-start.6) | collective-permute-done | bytes 786464 | tf_op jit(solution)/shard_map/ppermute | solution.py:28
  93.7 10.1 %collective-permute-done.2 = bf16[768,768]{1,0:T(8,128)(2,1)S(1)} collective-permute-done((bf16[768,768]{1,0:T(8,128)(2,1)}, bf16[768,768]{1,0:T(8,128)(2,1)S(1)}, u32[]{:S(2)}, u32[]{:S(2)}) %collective-permute-start.2) | collective-permute-done | bytes 1179680 | tf_op jit(solution)/shard_map/ppermute | solution.py:28
  103.8 2.6 collective-permute-start.10
  107.4 3.0 collective-permute-start.7
  110.4 2.3 pad_maximum_fusion.2
  112.7 2.0 constant_dynamic-slice_fusion.13
  114.7 39.9 %collective-permute-done.7 = bf16[768,512]{1,0:T(8,128)(2,1)} collective-permute-done((bf16[768,512]{1,0:T(8,128)(2,1)}, bf16[768,512]{1,0:T(8,128)(2,1)}, u32[]{:S(2)}, u32[]{:S(2)}) %collective-permute-start.7) | collective-permute-done | bytes 786464 | tf_op jit(solution)/shard_map/ppermute | solution.py:28
  154.6 3.3 collective-permute-done.8
  158.0 3.1 collective-permute-start.12
  163.5 2.3 broadcast_select_fusion.10
  165.8 2.3 broadcast_select_fusion.11
  176.5 6.1 %pad_maximum_fusion = bf16[1536,3072]{1,0:T(8,128)(2,1)S(1)} fusion(bf16[384,3072]{1,0:T(8,128)(2,1)S(1)} %collective-permute-done.14, bf16[384,3072]{1,0:T(8,128)(2,1)} %collective-permute-done.3, bf16[384,768]{1,0:T(8,128)(2,1)S(1)} %get-tuple-element.237, bf16[384,768]{1,0:T(8,128)(2,1)S(1)} %get-tuple-element.236, ...), kind=kLoop, calls=%fused_computation | loop fusion | flops 66060288 | bytes 18874368 | tf_op jit(solution)/shard_map/concatenate | solution.py:48
  182.6 7.5 %pad_maximum_fusion.1 = bf16[1536,3072]{1,0:T(8,128)(2,1)S(1)} fusion(bf16[384,3072]{1,0:T(8,128)(2,1)S(1)} %collective-permute-done.15, bf16[384,3072]{1,0:T(8,128)(2,1)} %collective-permute-done.4, bf16[384,768]{1,0:T(8,128)(2,1)S(1)} %get-tuple-element.240, bf16[384,768]{1,0:T(8,128)(2,1)S(1)} %get-tuple-element.239, ...), kind=kLoop, calls=%fused_computation.1 | loop fusion | flops 66060288 | bytes 18874368 | tf_op jit(solution)/shard_map/concatenate | solution.py:48
  190.1 5.2 %fusion.34 = f32[1536,512]{1,0:T(8,128)S(1)} fusion(bf16[1536,3072]{1,0:T(8,128)(2,1)S(1)} %pad_maximum_fusion, bf16[3072,512]{1,0:T(8,128)(2,1)S(1)} %bitcast.86), kind=kOutput, calls=%fused_computation.186 | convolution fusion | flops 4831838208 | bytes 15728640 | tf_op jit(solution)/shard_map/dot_general | solution.py:11
  201.7 7.3 %multiply_convert_fusion.3 = (bf16[1536,512]{1,0:T(8,128)(2,1)S(1)}, f32[1536,512]{1,0:T(8,128)}) fusion(f32[1536,512]{1,0:T(8,128)S(1)} %fusion.34, bf16[1536,3072]{1,0:T(8,128)(2,1)S(1)} %pad_maximum_fusion, bf16[3072,512]{1,0:T(8,128)(2,1)S(1)} %bitcast.99), kind=kOutput, calls=%fused_computation.17 | convolution fusion | flops 4836556800 | bytes 20447232 | tf_op jit(solution)/shard_map/dot_general | solution.py:11
  209.0 5.5 %convolution_convert_fusion.3 = bf16[3072,512]{1,0:T(8,128)(2,1)S(1)} fusion(bf16[1536,3072]{1,0:T(8,128)(2,1)S(1)} %pad_maximum_fusion.1, bf16[1536,512]{1,0:T(8,128)(2,1)S(1)} %get-tuple-element.165), kind=kOutput, calls=%fused_computation.10 | convolution fusion | flops 4833411072 | bytes 14155776 | tf_op jit(solution)/shard_map/dot_general | solution.py:11
  216.7 2.1 bitcast_dynamic-update-slice_fusion.1
  220.1 2.2 bitcast_dynamic-update-slice_fusion
  222.3 13.6 %multiply_convert_fusion.1 = (bf16[1536,512]{1,0:T(8,128)(2,1)}, bf16[1536,512]{1,0:T(8,128)(2,1)S(1)}) fusion(f32[1536,512]{1,0:T(8,128)} %copy-done.58, f32[1536,512]{1,0:T(8,128)} %get-tuple-element.154, bf16[1536,3072]{1,0:T(8,128)(2,1)} %copy-done.1, bf16[3072,512]{1,0:T(8,128)(2,1)} %bitcast.24), kind=kOutput, calls=%fused_computation.15 | convolution fusion | flops 4842061824 | bytes 22020096 | tf_op jit(solution)/shard_map/dot_general | solution.py:11
  236.0 5.5 %convolution_convert_fusion.2 = bf16[3072,512]{1,0:T(8,128)(2,1)S(1)} fusion(bf16[1536,3072]{1,0:T(8,128)(2,1)S(1)} %bitcast.90, bf16[1536,512]{1,0:T(8,128)(2,1)S(1)} %get-tuple-element.161), kind=kOutput, calls=%fused_computation.9 | convolution fusion | flops 4833411072 | bytes 14155776 | tf_op jit(solution)/shard_map/dot_general | solution.py:11
  243.9 6.1 %convolution_convert_fusion = bf16[768,3072]{1,0:T(8,128)(2,1)} fusion(bf16[3072,512]{1,0:T(8,128)(2,1)} %bitcast.24, bf16[1536,512]{1,0:T(8,128)(2,1)S(1)} %copy-done.56), kind=kOutput, calls=%fused_computation.6 | convolution fusion | flops 2418278400 | bytes 8650752 | tf_op jit(solution)/shard_map/dot_general | solution.py:11
  250.0 4.9 %fusion.31 = (bf16[384,3072]{1,0:T(8,128)(2,1)}, bf16[384,3072]{1,0:T(8,128)(2,1)}) fusion(bf16[768,3072]{1,0:T(8,128)(2,1)} %convolution_convert_fusion), kind=kLoop, calls=%fused_computation.183 | loop fusion | bytes 9437184 | tf_op jit(solution)/shard_map/slice | solution.py:255
  259.8 8.4 %fusion.12 = f32[768,3072]{1,0:T(8,128)} fusion(bf16[3072,512]{1,0:T(8,128)(2,1)} %bitcast.100, bf16[1536,512]{1,0:T(8,128)(2,1)} %get-tuple-element.163), kind=kOutput, calls=%fused_computation.92 | convolution fusion | flops 2415919104 | bytes 13369344 | tf_op jit(solution)/shard_map/dot_general | solution.py:11
  268.2 2.6 fusion.15
  270.9 6.9 %convolution_convert_fusion.1 = bf16[3072,512]{1,0:T(8,128)(2,1)} fusion(bf16[1536,3072]{1,0:T(8,128)(2,1)S(1)} %bitcast.92, bf16[1536,512]{1,0:T(8,128)(2,1)S(1)} %copy-done.54), kind=kOutput, calls=%fused_computation.8 | convolution fusion | flops 4833411072 | bytes 14155776 | tf_op jit(solution)/shard_map/dot_general | solution.py:11
  277.8 6.1 %add_convert_fusion.1 = bf16[768,3072]{1,0:T(8,128)(2,1)S(1)} fusion(bf16[3072,512]{1,0:T(8,128)(2,1)} %bitcast.24, bf16[384,3072]{1,0:T(8,128)(2,1)} %collective-permute-done.20, bf16[384,3072]{1,0:T(8,128)(2,1)} %collective-permute-done.19, bf16[1536,512]{1,0:T(8,128)(2,1)S(1)} %copy-done.57), kind=kOutput, calls=%fused_computation.3 | convolution fusion | flops 2430074880 | bytes 13369344 | tf_op jit(solution)/shard_map/dot_general | solution.py:11
  284.2 3.0 copy-done.12
  288.4 2.5 dynamic-slice_bitcast_fusion
  294.8 5.7 %add_convert_fusion.2 = bf16[768,3072]{1,0:T(8,128)(2,1)} fusion(f32[768,3072]{1,0:T(8,128)S(1)} %bitcast.94, bf16[3072,512]{1,0:T(8,128)(2,1)S(1)} %bitcast.87, bf16[1536,512]{1,0:T(8,128)(2,1)} %copy-done.29), kind=kOutput, calls=%fused_computation.4 | convolution fusion | flops 2420637696 | bytes 18087936 | tf_op jit(solution)/shard_map/dot_general | solution.py:11
  300.5 4.5 add_convert_fusion.3
  312.7 22.8 %collective-permute-done.23 = bf16[384,1536]{1,0:T(8,128)(2,1)S(1)} collective-permute-done((bf16[384,1536]{1,0:T(8,128)(2,1)}, bf16[384,1536]{1,0:T(8,128)(2,1)S(1)}, u32[]{:S(2)}, u32[]{:S(2)}) %collective-permute-start.23) | collective-permute-done | bytes 1179680 | tf_op jit(solution)/shard_map/ppermute | solution.py:28
  337.9 2.0 add_convert_fusion
  347.8 2.3 add_convert_fusion.6
  355.9 34.0 %collective-permute-done.29 = bf16[384,2304]{1,0:T(8,128)(2,1)} collective-permute-done((bf16[384,2304]{1,0:T(8,128)(2,1)}, bf16[384,2304]{1,0:T(8,128)(2,1)}, u32[]{:S(2)}, u32[]{:S(2)}) %collective-permute-start.29) | collective-permute-done | bytes 1769504 | tf_op jit(solution)/shard_map/ppermute | solution.py:28
  389.9 1.9 add_convert_fusion.13
  391.9 2.0 add_convert_fusion.11
  395.9 2.4 collective-permute-start.34
  399.9 20.9 %collective-permute-done.31 = bf16[384,768]{1,0:T(8,128)(2,1)S(1)} collective-permute-done((bf16[384,768]{1,0:T(8,128)(2,1)S(1)}, bf16[384,768]{1,0:T(8,128)(2,1)S(1)}, u32[]{:S(2)}, u32[]{:S(2)}) %collective-permute-start.31) | collective-permute-done | bytes 589856 | tf_op jit(solution)/shard_map/ppermute | solution.py:28
  423.4 2.5 collective-permute-done.39
  427.0 2.0 convolution_convert_fusion.7
  430.4 24.4 %collective-permute-done.34 = bf16[768,1024]{1,0:T(8,128)(2,1)S(1)} collective-permute-done((bf16[768,1024]{1,0:T(8,128)(2,1)S(1)}, bf16[768,1024]{1,0:T(8,128)(2,1)S(1)}, u32[]{:S(2)}, u32[]{:S(2)}) %collective-permute-start.34) | collective-permute-done | bytes 1572896 | tf_op jit(solution)/shard_map/ppermute | solution.py:28
  460.6 1.9 convolution_convert_fusion.6
  (289 shorter events, 89.1 us)
Async XLA Ops:
  7.2 242.8 %reduce-scatter.2.cloned.1.call-start = ((), (), s32[]{:S(2)}) async-start(), calls=%async_computation.1 | async-start | bytes 2359296 | tf_op jit(solution)/shard_map/reduce_scatter | solution.py:143
  9.6 38.8 %collective-permute-start = (bf16[384,1024]{1,0:T(8,128)(2,1)}, bf16[384,1024]{1,0:T(8,128)(2,1)}, u32[]{:S(2)}, u32[]{:S(2)}) collective-permute-start(bf16[384,1024]{1,0:T(8,128)(2,1)} %get-tuple-element.297), channel_id=1, source_target_pairs={{0,16},{4,20},{8,24},{12,28},{16,0},{20,4},{24,8},{28,12},{1,17},{... | collective-permute-start | bytes 2359304 | tf_op jit(solution)/shard_map/ppermute | solution.py:28
  13.7 34.8 %collective-permute-start.1 = (bf16[384,1024]{1,0:T(8,128)(2,1)S(1)}, bf16[384,1024]{1,0:T(8,128)(2,1)}, u32[]{:S(2)}, u32[]{:S(2)}) collective-permute-start(bf16[384,1024]{1,0:T(8,128)(2,1)S(1)} %get-tuple-element.122), channel_id=1, source_target_pairs={{0,8},{4,12},{8,0},{12,4},{16,24},{20,28},{24,16},{28,20},{1,9},{5... | collective-permute-start | bytes 2359304 | tf_op jit(solution)/shard_map/ppermute | solution.py:28
  48.5 5.8 %collective-permute-start.5 = (bf16[768,1024]{1,0:T(8,128)(2,1)S(1)}, bf16[768,1024]{1,0:T(8,128)(2,1)}, u32[]{:S(2)}, u32[]{:S(2)}) collective-permute-start(bf16[768,1024]{1,0:T(8,128)(2,1)S(1)} %maximum_maximum_fusion), channel_id=1, source_target_pairs={{0,4},{4,0},{8,12},{12,8},{16,20},{20,16},{24,28},{28,24},{1,5},{5... | collective-permute-start | bytes 4718600 | tf_op jit(solution)/shard_map/ppermute | solution.py:28
  48.5 55.3 %collective-permute-start.3 = (bf16[384,3072]{1,0:T(8,128)(2,1)}, bf16[384,3072]{1,0:T(8,128)(2,1)}, u32[]{:S(2)}, u32[]{:S(2)}) collective-permute-start(bf16[384,3072]{1,0:T(8,128)(2,1)} %convolution_convert_fusion.5), channel_id=1, source_target_pairs={{0,4},{4,0},{8,12},{12,8},{16,20},{20,16},{24,28},{28,24},{1,5},{5... | collective-permute-start | bytes 7077896 | tf_op jit(solution)/shard_map/ppermute | solution.py:28
  49.0 54.8 %collective-permute-start.4 = (bf16[384,3072]{1,0:T(8,128)(2,1)}, bf16[384,3072]{1,0:T(8,128)(2,1)}, u32[]{:S(2)}, u32[]{:S(2)}) collective-permute-start(bf16[384,3072]{1,0:T(8,128)(2,1)} %get-tuple-element.118), channel_id=1, source_target_pairs={{0,4},{4,0},{8,12},{12,8},{16,20},{20,16},{24,28},{28,24},{1,5},{5... | collective-permute-start | bytes 7077896 | tf_op jit(solution)/shard_map/ppermute | solution.py:28
  49.0 54.8 %collective-permute-start.2 = (bf16[768,768]{1,0:T(8,128)(2,1)}, bf16[768,768]{1,0:T(8,128)(2,1)S(1)}, u32[]{:S(2)}, u32[]{:S(2)}) collective-permute-start(bf16[768,768]{1,0:T(8,128)(2,1)} %pad_maximum_fusion.10), channel_id=1, source_target_pairs={{0,16},{4,20},{8,24},{12,28},{16,0},{20,4},{24,8},{28,12},{1,17},{... | collective-permute-start | bytes 3538952 | tf_op jit(solution)/shard_map/ppermute | solution.py:28
  50.6 43.1 %collective-permute-start.6 = (bf16[384,1024]{1,0:T(8,128)(2,1)}, bf16[384,1024]{1,0:T(8,128)(2,1)S(1)}, u32[]{:S(2)}, u32[]{:S(2)}) collective-permute-start(bf16[384,1024]{1,0:T(8,128)(2,1)} %collective-permute-done), channel_id=1, source_target_pairs={{0,8},{4,12},{8,0},{12,4},{16,24},{20,28},{24,16},{28,20},{1,9},{5... | collective-permute-start | bytes 2359304 | tf_op jit(solution)/shard_map/ppermute | solution.py:28
  59.3 53.3 %copy-start.6 = (bf16[768,1024]{1,0:T(8,128)(2,1)}, bf16[768,1024]{1,0:T(8,128)(2,1)S(1)}, u32[]{:S(2)}) copy-start(bf16[768,1024]{1,0:T(8,128)(2,1)S(1)} %pad_maximum_fusion.7) | copy-start | bytes 4718596
  103.8 54.2 %collective-permute-start.11 = (bf16[768,1024]{1,0:T(8,128)(2,1)S(1)}, bf16[768,1024]{1,0:T(8,128)(2,1)}, u32[]{:S(2)}, u32[]{:S(2)}) collective-permute-start(bf16[768,1024]{1,0:T(8,128)(2,1)S(1)} %pad_maximum_fusion.7), channel_id=1, source_target_pairs={{0,8},{4,12},{8,0},{12,4},{16,24},{20,28},{24,16},{28,20},{1,9},{5... | collective-permute-start | bytes 4718600 | tf_op jit(solution)/shard_map/ppermute | solution.py:28
  103.8 50.8 %collective-permute-start.10 = (bf16[768,768]{1,0:T(8,128)(2,1)S(1)}, bf16[768,768]{1,0:T(8,128)(2,1)}, u32[]{:S(2)}, u32[]{:S(2)}) collective-permute-start(bf16[768,768]{1,0:T(8,128)(2,1)S(1)} %collective-permute-done.2), channel_id=1, source_target_pairs={{0,3},{1,2},{2,1},{3,0},{4,7},{5,6},{6,5},{7,4},{8,11},{9,10},{10,... | collective-permute-start | bytes 3538952 | tf_op jit(solution)/shard_map/ppermute | solution.py:28
  106.4 51.5 %collective-permute-start.8 = (bf16[768,768]{1,0:T(8,128)(2,1)S(1)}, bf16[768,768]{1,0:T(8,128)(2,1)}, u32[]{:S(2)}, u32[]{:S(2)}) collective-permute-start(bf16[768,768]{1,0:T(8,128)(2,1)S(1)} %collective-permute-done.2), channel_id=1, source_target_pairs={{0,1},{1,0},{2,3},{3,2},{4,5},{5,4},{6,7},{7,6},{8,9},{9,8},{10,11... | collective-permute-start | bytes 3538952 | tf_op jit(solution)/shard_map/ppermute | solution.py:28
  107.0 51.0 %collective-permute-start.9 = (bf16[768,768]{1,0:T(8,128)(2,1)S(1)}, bf16[768,768]{1,0:T(8,128)(2,1)}, u32[]{:S(2)}, u32[]{:S(2)}) collective-permute-start(bf16[768,768]{1,0:T(8,128)(2,1)S(1)} %collective-permute-done.2), channel_id=1, source_target_pairs={{0,2},{1,3},{2,0},{3,1},{4,6},{5,7},{6,4},{7,5},{8,10},{9,11},{10,... | collective-permute-start | bytes 3538952 | tf_op jit(solution)/shard_map/ppermute | solution.py:28
  107.4 47.2 %collective-permute-start.7 = (bf16[768,512]{1,0:T(8,128)(2,1)}, bf16[768,512]{1,0:T(8,128)(2,1)}, u32[]{:S(2)}, u32[]{:S(2)}) collective-permute-start(bf16[768,512]{1,0:T(8,128)(2,1)} %maximum_select_fusion.2), channel_id=1, source_target_pairs={{0,16},{4,20},{8,24},{12,28},{16,0},{20,4},{24,8},{28,12},{1,17},{... | collective-permute-start | bytes 2359304 | tf_op jit(solution)/shard_map/ppermute | solution.py:28
  158.0 5.3 %collective-permute-start.13 = (bf16[4,384,512]{2,1,0:T(8,128)(2,1)}, bf16[4,384,512]{2,1,0:T(8,128)(2,1)}, u32[]{:S(2)}, u32[]{:S(2)}) collective-permute-start(bf16[4,384,512]{2,1,0:T(8,128)(2,1)} %get-tuple-element.131), channel_id=1, source_target_pairs={{0,4},{4,0},{8,12},{12,8},{16,20},{20,16},{24,28},{28,24},{1,5},{5... | collective-permute-start | bytes 4718600 | tf_op jit(solution)/shard_map/ppermute | solution.py:28
  158.0 38.3 %collective-permute-start.12 = (bf16[768,512]{1,0:T(8,128)(2,1)}, bf16[768,512]{1,0:T(8,128)(2,1)S(1)}, u32[]{:S(2)}, u32[]{:S(2)}) collective-permute-start(bf16[768,512]{1,0:T(8,128)(2,1)} %maximum_select_fusion.3), channel_id=1, source_target_pairs={{0,16},{4,20},{8,24},{12,28},{16,0},{20,4},{24,8},{28,12},{1,17},{... | collective-permute-start | bytes 2359304 | tf_op jit(solution)/shard_map/ppermute | solution.py:28
  161.1 35.8 %collective-permute-start.16 = (bf16[768,512]{1,0:T(8,128)(2,1)}, bf16[768,512]{1,0:T(8,128)(2,1)}, u32[]{:S(2)}, u32[]{:S(2)}) collective-permute-start(bf16[768,512]{1,0:T(8,128)(2,1)} %collective-permute-done.7), channel_id=1, source_target_pairs={{0,8},{4,12},{8,0},{12,4},{16,24},{20,28},{24,16},{28,20},{1,9},{5... | collective-permute-start | bytes 2359304 | tf_op jit(solution)/shard_map/ppermute | solution.py:28
  168.4 8.1 %collective-permute-start.14 = (bf16[384,3072]{1,0:T(8,128)(2,1)S(1)}, bf16[384,3072]{1,0:T(8,128)(2,1)S(1)}, u32[]{:S(2)}, u32[]{:S(2)}) collective-permute-start(bf16[384,3072]{1,0:T(8,128)(2,1)S(1)} %pad_maximum_fusion.3), channel_id=1, source_target_pairs={{0,4},{4,0},{8,12},{12,8},{16,20},{20,16},{24,28},{28,24},{1,5},{5... | collective-permute-start | bytes 7077896 | tf_op jit(solution)/shard_map/ppermute | solution.py:28
  171.7 11.0 %collective-permute-start.15 = (bf16[384,3072]{1,0:T(8,128)(2,1)S(1)}, bf16[384,3072]{1,0:T(8,128)(2,1)S(1)}, u32[]{:S(2)}, u32[]{:S(2)}) collective-permute-start(bf16[384,3072]{1,0:T(8,128)(2,1)S(1)} %pad_maximum_fusion.4), channel_id=1, source_target_pairs={{0,4},{4,0},{8,12},{12,8},{16,20},{20,16},{24,28},{28,24},{1,5},{5... | collective-permute-start | bytes 7077896 | tf_op jit(solution)/shard_map/ppermute | solution.py:28
  196.9 18.6 %collective-permute-start.17 = (bf16[768,512]{1,0:T(8,128)(2,1)S(1)}, bf16[768,512]{1,0:T(8,128)(2,1)S(1)}, u32[]{:S(2)}, u32[]{:S(2)}) collective-permute-start(bf16[768,512]{1,0:T(8,128)(2,1)S(1)} %collective-permute-done.12), channel_id=1, source_target_pairs={{0,8},{4,12},{8,0},{12,4},{16,24},{20,28},{24,16},{28,20},{1,9},{5... | collective-permute-start | bytes 2359304 | tf_op jit(solution)/shard_map/ppermute | solution.py:28
  254.9 4.9 %collective-permute-start.19 = (bf16[384,3072]{1,0:T(8,128)(2,1)}, bf16[384,3072]{1,0:T(8,128)(2,1)}, u32[]{:S(2)}, u32[]{:S(2)}) collective-permute-start(bf16[384,3072]{1,0:T(8,128)(2,1)} %get-tuple-element.233), channel_id=1, source_target_pairs={{0,4},{4,0},{8,12},{12,8},{16,20},{20,16},{24,28},{28,24},{1,5},{5... | collective-permute-start | bytes 7077896 | tf_op jit(solution)/shard_map/ppermute | solution.py:28
  254.9 22.9 %collective-permute-start.20 = (bf16[384,3072]{1,0:T(8,128)(2,1)}, bf16[384,3072]{1,0:T(8,128)(2,1)}, u32[]{:S(2)}, u32[]{:S(2)}) collective-permute-start(bf16[384,3072]{1,0:T(8,128)(2,1)} %get-tuple-element.232), channel_id=1, source_target_pairs={{0,4},{4,0},{8,12},{12,8},{16,20},{20,16},{24,28},{28,24},{1,5},{5... | collective-permute-start | bytes 7077896 | tf_op jit(solution)/shard_map/ppermute | solution.py:28
  255.4 49.6 %collective-permute-start.18 = (bf16[768,512]{1,0:T(8,128)(2,1)}, bf16[768,512]{1,0:T(8,128)(2,1)}, u32[]{:S(2)}, u32[]{:S(2)}) collective-permute-start(bf16[768,512]{1,0:T(8,128)(2,1)} %reduce-scatter.2.cloned.1.call-done), channel_id=1, source_target_pairs={{0,16},{4,20},{8,24},{12,28},{16,0},{20,4},{24,8},{28,12},{1,17},{... | collective-permute-start | bytes 2359304 | tf_op jit(solution)/shard_map/ppermute | solution.py:28
  256.4 48.6 %collective-permute-start.21 = (bf16[768,512]{1,0:T(8,128)(2,1)}, bf16[768,512]{1,0:T(8,128)(2,1)}, u32[]{:S(2)}, u32[]{:S(2)}) collective-permute-start(bf16[768,512]{1,0:T(8,128)(2,1)} %get-tuple-element.169), channel_id=1, source_target_pairs={{0,8},{4,12},{8,0},{12,4},{16,24},{20,28},{24,16},{28,20},{1,9},{5... | collective-permute-start | bytes 2359304 | tf_op jit(solution)/shard_map/ppermute | solution.py:28
  306.8 31.1 %collective-permute-start.25 = (bf16[768,3072]{1,0:T(8,128)(2,1)S(1)}, bf16[768,3072]{1,0:T(8,128)(2,1)S(1)}, u32[]{:S(2)}, u32[]{:S(2)}) collective-permute-start(bf16[768,3072]{1,0:T(8,128)(2,1)S(1)} %copy-done.9), channel_id=1, source_target_pairs={{0,4},{4,0},{8,12},{12,8},{16,20},{20,16},{24,28},{28,24},{1,5},{5... | collective-permute-start | bytes 14155784 | tf_op jit(solution)/shard_map/ppermute | solution.py:28
  307.0 28.5 %collective-permute-start.23 = (bf16[384,1536]{1,0:T(8,128)(2,1)}, bf16[384,1536]{1,0:T(8,128)(2,1)S(1)}, u32[]{:S(2)}, u32[]{:S(2)}) collective-permute-start(bf16[384,1536]{1,0:T(8,128)(2,1)} %pad_maximum_fusion.11), channel_id=1, source_target_pairs={{0,1},{1,0},{2,3},{3,2},{4,5},{5,4},{6,7},{7,6},{8,9},{9,8},{10,11... | collective-permute-start | bytes 3538952 | tf_op jit(solution)/shard_map/ppermute | solution.py:28
  308.5 28.2 %collective-permute-start.24 = (bf16[384,1536]{1,0:T(8,128)(2,1)}, bf16[384,1536]{1,0:T(8,128)(2,1)S(1)}, u32[]{:S(2)}, u32[]{:S(2)}) collective-permute-start(bf16[384,1536]{1,0:T(8,128)(2,1)} %pad_maximum_fusion.12), channel_id=1, source_target_pairs={{0,2},{1,3},{2,0},{3,1},{4,6},{5,7},{6,4},{7,5},{8,10},{9,11},{10,... | collective-permute-start | bytes 3538952 | tf_op jit(solution)/shard_map/ppermute | solution.py:28
  309.9 37.0 %collective-permute-start.22 = (bf16[768,512]{1,0:T(8,128)(2,1)S(1)}, bf16[768,512]{1,0:T(8,128)(2,1)S(1)}, u32[]{:S(2)}, u32[]{:S(2)}) collective-permute-start(bf16[768,512]{1,0:T(8,128)(2,1)S(1)} %add_convert_fusion.7), channel_id=1, source_target_pairs={{0,16},{4,20},{8,24},{12,28},{16,0},{20,4},{24,8},{28,12},{1,17},{... | collective-permute-start | bytes 2359304 | tf_op jit(solution)/shard_map/ppermute | solution.py:28
  311.1 35.8 %collective-permute-start.26 = (bf16[768,512]{1,0:T(8,128)(2,1)}, bf16[768,512]{1,0:T(8,128)(2,1)}, u32[]{:S(2)}, u32[]{:S(2)}) collective-permute-start(bf16[768,512]{1,0:T(8,128)(2,1)} %get-tuple-element.184), channel_id=1, source_target_pairs={{0,8},{4,12},{8,0},{12,4},{16,24},{20,28},{24,16},{28,20},{1,9},{5... | collective-permute-start | bytes 2359304 | tf_op jit(solution)/shard_map/ppermute | solution.py:28
  350.2 39.8 %collective-permute-start.29 = (bf16[384,2304]{1,0:T(8,128)(2,1)}, bf16[384,2304]{1,0:T(8,128)(2,1)}, u32[]{:S(2)}, u32[]{:S(2)}) collective-permute-start(bf16[384,2304]{1,0:T(8,128)(2,1)} %pad_maximum_fusion.5), channel_id=1, source_target_pairs={{0,1},{1,0},{2,3},{3,2},{4,5},{5,4},{6,7},{7,6},{8,9},{9,8},{10,11... | collective-permute-start | bytes 5308424 | tf_op jit(solution)/shard_map/ppermute | solution.py:28
  350.7 41.1 %collective-permute-start.28 = (bf16[384,2304]{1,0:T(8,128)(2,1)}, bf16[384,2304]{1,0:T(8,128)(2,1)}, u32[]{:S(2)}, u32[]{:S(2)}) collective-permute-start(bf16[384,2304]{1,0:T(8,128)(2,1)} %pad_maximum_fusion.6), channel_id=1, source_target_pairs={{0,2},{1,3},{2,0},{3,1},{4,6},{5,7},{6,4},{7,5},{8,10},{9,11},{10,... | collective-permute-start | bytes 5308424 | tf_op jit(solution)/shard_map/ppermute | solution.py:28
  352.8 37.1 %copy-start.24 = (bf16[384,768]{1,0:T(8,128)(2,1)S(1)}, bf16[384,768]{1,0:T(8,128)(2,1)}, u32[]{:S(2)}) copy-start(bf16[384,768]{1,0:T(8,128)(2,1)} %get-tuple-element.196) | copy-start | bytes 1769476
  352.8 37.1 %copy-start.27 = (bf16[384,768]{1,0:T(8,128)(2,1)S(1)}, bf16[384,768]{1,0:T(8,128)(2,1)}, u32[]{:S(2)}) copy-start(bf16[384,768]{1,0:T(8,128)(2,1)} %get-tuple-element.199) | copy-start | bytes 1769476
  352.8 37.1 %copy-start.28 = (bf16[384,768]{1,0:T(8,128)(2,1)S(1)}, bf16[384,768]{1,0:T(8,128)(2,1)}, u32[]{:S(2)}) copy-start(bf16[384,768]{1,0:T(8,128)(2,1)} %get-tuple-element.198) | copy-start | bytes 1769476
  352.8 41.0 %collective-permute-start.27 = (bf16[768,512]{1,0:T(8,128)(2,1)S(1)}, bf16[768,512]{1,0:T(8,128)(2,1)S(1)}, u32[]{:S(2)}, u32[]{:S(2)}) collective-permute-start(bf16[768,512]{1,0:T(8,128)(2,1)S(1)} %copy-done.43), channel_id=1, source_target_pairs={{0,16},{4,20},{8,24},{12,28},{16,0},{20,4},{24,8},{28,12},{1,17},{... | collective-permute-start | bytes 2359304 | tf_op jit(solution)/shard_map/ppermute | solution.py:28
  354.0 39.9 %collective-permute-start.30 = (bf16[768,512]{1,0:T(8,128)(2,1)S(1)}, bf16[768,512]{1,0:T(8,128)(2,1)S(1)}, u32[]{:S(2)}, u32[]{:S(2)}) collective-permute-start(bf16[768,512]{1,0:T(8,128)(2,1)S(1)} %copy-done.44), channel_id=1, source_target_pairs={{0,8},{4,12},{8,0},{12,4},{16,24},{20,28},{24,16},{28,20},{1,9},{5... | collective-permute-start | bytes 2359304 | tf_op jit(solution)/shard_map/ppermute | solution.py:28
  355.9 36.0 %copy-start.23 = (bf16[384,768]{1,0:T(8,128)(2,1)S(1)}, bf16[384,768]{1,0:T(8,128)(2,1)}, u32[]{:S(2)}) copy-start(bf16[384,768]{1,0:T(8,128)(2,1)} %get-tuple-element.194) | copy-start | bytes 1769476
  355.9 36.0 %copy-start.25 = (bf16[384,768]{1,0:T(8,128)(2,1)S(1)}, bf16[384,768]{1,0:T(8,128)(2,1)}, u32[]{:S(2)}) copy-start(bf16[384,768]{1,0:T(8,128)(2,1)} %get-tuple-element.201) | copy-start | bytes 1769476
  393.9 27.0 %collective-permute-start.31 = (bf16[384,768]{1,0:T(8,128)(2,1)S(1)}, bf16[384,768]{1,0:T(8,128)(2,1)S(1)}, u32[]{:S(2)}, u32[]{:S(2)}) collective-permute-start(bf16[384,768]{1,0:T(8,128)(2,1)S(1)} %get-tuple-element.210), channel_id=1, source_target_pairs={{0,16},{4,20},{8,24},{12,28},{16,0},{20,4},{24,8},{28,12},{1,17},{... | collective-permute-start | bytes 1769480 | tf_op jit(solution)/shard_map/ppermute | solution.py:28
  395.0 28.2 %collective-permute-start.37 = (bf16[384,768]{1,0:T(8,128)(2,1)S(1)}, bf16[384,768]{1,0:T(8,128)(2,1)S(1)}, u32[]{:S(2)}, u32[]{:S(2)}) collective-permute-start(bf16[384,768]{1,0:T(8,128)(2,1)S(1)} %get-tuple-element.221), channel_id=1, source_target_pairs={{0,1},{1,0},{2,3},{3,2},{4,5},{5,4},{6,7},{7,6},{8,9},{9,8},{10,11... | collective-permute-start | bytes 1769480 | tf_op jit(solution)/shard_map/ppermute | solution.py:28
  395.9 59.0 %collective-permute-start.34 = (bf16[768,1024]{1,0:T(8,128)(2,1)S(1)}, bf16[768,1024]{1,0:T(8,128)(2,1)S(1)}, u32[]{:S(2)}, u32[]{:S(2)}) collective-permute-start(bf16[768,1024]{1,0:T(8,128)(2,1)S(1)} %pad_maximum_fusion.8), channel_id=1, source_target_pairs={{0,8},{4,12},{8,0},{12,4},{16,24},{20,28},{24,16},{28,20},{1,9},{5... | collective-permute-start | bytes 4718600 | tf_op jit(solution)/shard_map/ppermute | solution.py:28
  398.7 31.7 %collective-permute-start.33 = (bf16[384,1024]{1,0:T(8,128)(2,1)S(1)}, bf16[384,1024]{1,0:T(8,128)(2,1)S(1)}, u32[]{:S(2)}, u32[]{:S(2)}) collective-permute-start(bf16[384,1024]{1,0:T(8,128)(2,1)S(1)} %get-tuple-element.282), channel_id=1, source_target_pairs={{0,4},{4,0},{8,12},{12,8},{16,20},{20,16},{24,28},{28,24},{1,5},{5... | collective-permute-start | bytes 2359304 | tf_op jit(solution)/shard_map/ppermute | solution.py:28
  398.8 61.8 %collective-permute-start.32 = (bf16[384,768]{1,0:T(8,128)(2,1)S(1)}, bf16[384,768]{1,0:T(8,128)(2,1)S(1)}, u32[]{:S(2)}, u32[]{:S(2)}) collective-permute-start(bf16[384,768]{1,0:T(8,128)(2,1)S(1)} %get-tuple-element.212), channel_id=1, source_target_pairs={{0,2},{1,3},{2,0},{3,1},{4,6},{5,7},{6,4},{7,5},{8,10},{9,11},{10,... | collective-permute-start | bytes 1769480 | tf_op jit(solution)/shard_map/ppermute | solution.py:28
  422.2 3.6 collective-permute-start.39
  423.3 37.2 %collective-permute-start.38 = (bf16[384,768]{1,0:T(8,128)(2,1)S(1)}, bf16[384,768]{1,0:T(8,128)(2,1)S(1)}, u32[]{:S(2)}, u32[]{:S(2)}) collective-permute-start(bf16[384,768]{1,0:T(8,128)(2,1)S(1)} %add_convert_fusion.9), channel_id=1, source_target_pairs={{0,16},{4,20},{8,24},{12,28},{16,0},{20,4},{24,8},{28,12},{1,17},{... | collective-permute-start | bytes 1769480 | tf_op jit(solution)/shard_map/ppermute | solution.py:28
  425.9 3.6 collective-permute-start.40
  457.0 2.4 collective-permute-start.36
  457.3 3.2 collective-permute-start.35
  (62 other events, 561.4 us)
Sparse Core Ops, SparseCore 0:
  220.2 25.8 reduce-scatter.1

commit v8 on v5

--- a/solution.py
+++ b/solution.py
@@ -229,22 +229,25 @@
     ).astype(BF16)
     up_grad = (hidden_grad * gate_pre * sigmoid_gate).astype(BF16)
     g_gate = mm_first(in_all, gate_grad).astype(BF16)
-    expert_sib = mm_last(hidden[table:], down).astype(BF16)
+    expert_got = across(mm_last(hidden[table:], down).astype(BF16))
 
     def input_part(rows):
         return mm_last(gate_grad[rows], gate) + mm_last(up_grad[rows], up)
 
     input_sib = input_part(slice(table, None)).astype(BF16)
-    down, gate_grad, up_grad, g_gate, expert_sib, input_sib, *rest = fence(
-        down, gate_grad, up_grad, g_gate, expert_sib, input_sib, *g_down_4, *g_down_own
+    down, gate_grad, up_grad, g_gate, expert_got, input_sib, *rest = fence(
+        down, gate_grad, up_grad, g_gate, expert_got, input_sib, *g_down_4, *g_down_own
     )
     g_down_own = rest[2:]
-    g_down_4, expert_sib, input_sib, g_gate = fence(done(*rest[:2]), expert_sib, input_sib, g_gate)
+    g_down_4, input_sib, g_gate = fence(done(*rest[:2]), input_sib, g_gate)
     g_gate_4, g_gate_own = first_send(blocks_far(g_gate)), first_send(blocks_own(g_gate))
 
     g_down_far = z_far(g_down_4)
     g_gate_4 = shrink(*g_gate_4)
-    expert_got, input_got = across(expert_sib), across(input_sib)
+    input_got, in_all, gate_grad, up_grad, hidden = fence(
+        across(input_sib[:row_limit]), in_all, gate_grad, up_grad, hidden
+    )
+    input_got = cat(input_got, across(input_sib[row_limit:]))
     g_up = mm_first(in_all, up_grad).astype(BF16)
     expert_sum = (mm_last(hidden[:table], down) + expert_got.astype(F32)).astype(BF16)
     input_sum = (input_part(slice(None, table)) + input_got.astype(F32)).astype(BF16)
@@ -335,10 +338,11 @@
             expert_other = step(expert_other, bit)
     input_other = kept(input_other, high, got_high)
     input_mine = kept(input_mine, low, got_low)
-    g_up_far, expert_mine, expert_other, input_mine, input_other, *rest = fence(
-        g_up_far, expert_mine[0], expert_other[0], input_mine, input_other, *g_gate_own, *g_up_own
-    )
-    g_gate_own, g_up_own = rest[:2], rest[2:]
+    g_up_far, expert_mine, expert_other, input_mine, input_other, g_down_far, g_gate_far, *rest = fence(
+        g_up_far, expert_mine[0], expert_other[0], input_mine, input_other, g_down_far, g_gate_far,
+        *g_gate_own, *g_down_own, *g_up_own
+    )
+    g_gate_own, g_down_own, g_up_own = rest[:2], rest[2:4], rest[4:]
 
     g_up_own = shrink(*g_up_own)
     expert_got = z_far(expert_other)
@@ -346,12 +350,10 @@
         input_mine = step(input_mine, bit)
     for bit in t_bits[:-1][::-1]:
         input_other = step(input_other, bit)
-    expert_got, input_mine, input_other, g_down_far, g_gate_far, *rest = fence(
-        expert_got, input_mine[0], input_other[0], g_down_far, g_gate_far,
-        *g_down_own, *g_gate_own, *g_up_own
-    )
-    g_down_own, g_gate_own, g_up_own = rest[:2], rest[2:4], rest[4:]
-
+    input_other, g_down_far, g_gate_far, *rest = fence(
+        input_other[0], g_down_far, g_gate_far, *g_down_own, *g_gate_own
+    )
+    g_down_own, g_gate_own = rest[:2], rest[2:]
     input_got = z_far(input_other)
     expert_cols = expert_mine.astype(F32) + expert_got.astype(F32)
     grad_cols = lax.dynamic_slice_in_dim(rows_grad, me_t * width, width, 1)
@@ -360,7 +362,7 @@
         weight_rows = weight_rows + swap(weight_rows, "tensor", bit)
     weight_grad = jnp.sum(jnp.where(match, weight_rows[:, None], 0.0), axis=0)
     mixed = mm_first(hot, (row_weight[:, None] * expert_cols).astype(BF16)).astype(BF16)
-    input_cols = (input_mine.astype(F32) + input_got.astype(F32)).astype(BF16)
+    input_cols = (input_mine[0].astype(F32) + input_got.astype(F32)).astype(BF16)
     input_grad = mm_first(hot, input_cols).astype(BF16)
     return (
         mixed,

time: 478 us -> 458 us (0.958)
  waiting for transfers between devices: 254 us -> 241 us
    ppermute x42 -> x43, waiting for transfers between devices: 254 us -> 241 us  [swap(): return lax.ppermute(value, axis, [(i, i ^ distance) for i in range(size)])]
    ppermute x42 -> x43, starting transfers between devices: 43 us -> 41.4 us  [swap(): return lax.ppermute(value, axis, [(i, i ^ distance) for i in range(size)])]
  transfers between devices with their start and end apart: 42 -> 43, of which waited for: 23 -> 20; matrix products, arithmetic and copies ran while one was open for 28% -> 32% of each run, Pallas kernels for 0% -> 0%
where the time goes in v8:
time: 458 us; the launch traced here: 451 us
  waiting for transfers between devices  241 us (53%)
  matrix products  86.5 us (19%)
  other arithmetic  44.1 us (10%)
  starting transfers between devices  41.4 us (9%)
  local copies, waits for them, and re-layouts  36.7 us (8%)
    ppermute x43, waiting for transfers between devices, swap(): return lax.ppermute(value, axis, [(i, i ^ distance) for i in range(size)])  241 us
    dot_general x16, matrix products, dot(): lax.dot_general(left, right, (dims, ((), ())), preferred_element_type=F32)  86.5 us
    ppermute x43, starting transfers between devices, swap(): return lax.ppermute(value, axis, [(i, i ^ distance) for i in range(size)])  41.4 us
    concatenate x4, other arithmetic, cat(): return jnp.concatenate(values, axis=0)  14.9 us
  transfers between devices with their start and end apart: 43, of which 20 were waited for; matrix products, arithmetic and copies ran while one was open for 32% of the time, Pallas kernels for 0%

profile of v8, /device:TPU:0, one launch (start us, length us, event | category | flops | bytes accessed | tf_op | source)
XLA Modules:
  0.0 451.2 jit_solution(2012213368992107369)
XLA Ops:
  0.7 2.4 constant_dynamic-slice_fusion.18
  3.1 4.0 collective-permute-start
  9.7 5.9 %convolution_convert_fusion.5 = bf16[384,3072]{1,0:T(8,128)(2,1)} fusion(bf16[768,3072]{1,0:T(8,128)(2,1)} %param.7, s32[768]{0:T(1024)S(1)} %add_bitcast_fusion, pred[768]{0:T(1024)(128)(4,1)S(1)} %fusion.31), kind=kOutput, calls=%fused_computation.11 | convolution fusion | flops 1813708800 | bytes 7081728 | tf_op jit(solution)/shard_map/dot_general | solution.py:11
  15.6 4.2 multiply_convert_fusion
  25.6 16.3 %collective-permute-done = bf16[384,1024]{1,0:T(8,128)(2,1)} collective-permute-done((bf16[384,1024]{1,0:T(8,128)(2,1)}, bf16[384,1024]{1,0:T(8,128)(2,1)}, u32[]{:S(2)}, u32[]{:S(2)}) %collective-permute-start) | collective-permute-done | bytes 786464 | tf_op jit(solution)/shard_map/ppermute | solution.py:28
  44.0 2.4 collective-permute-start.6
  52.8 34.3 %collective-permute-done.6 = bf16[384,1024]{1,0:T(8,128)(2,1)S(1)} collective-permute-done((bf16[384,1024]{1,0:T(8,128)(2,1)}, bf16[384,1024]{1,0:T(8,128)(2,1)S(1)}, u32[]{:S(2)}, u32[]{:S(2)}) %collective-permute-start.6) | collective-permute-done | bytes 786464 | tf_op jit(solution)/shard_map/ppermute | solution.py:28
  87.1 10.1 %collective-permute-done.2 = bf16[768,768]{1,0:T(8,128)(2,1)S(1)} collective-permute-done((bf16[768,768]{1,0:T(8,128)(2,1)}, bf16[768,768]{1,0:T(8,128)(2,1)S(1)}, u32[]{:S(2)}, u32[]{:S(2)}) %collective-permute-start.2) | collective-permute-done | bytes 1179680 | tf_op jit(solution)/shard_map/ppermute | solution.py:28
  97.3 2.6 collective-permute-start.10
  100.8 3.0 collective-permute-start.7
  103.8 2.0 pad_maximum_fusion.2
  105.8 2.0 constant_dynamic-slice_fusion.12
  107.9 40.2 %collective-permute-done.7 = bf16[768,512]{1,0:T(8,128)(2,1)} collective-permute-done((bf16[768,512]{1,0:T(8,128)(2,1)}, bf16[768,512]{1,0:T(8,128)(2,1)}, u32[]{:S(2)}, u32[]{:S(2)}) %collective-permute-start.7) | collective-permute-done | bytes 786464 | tf_op jit(solution)/shard_map/ppermute | solution.py:28
  148.0 3.3 collective-permute-done.8
  151.5 3.1 collective-permute-start.12
  156.9 2.3 broadcast_select_fusion.10
  159.2 2.2 broadcast_select_fusion.11
  167.2 6.1 %pad_maximum_fusion = bf16[1536,3072]{1,0:T(8,128)(2,1)S(1)} fusion(bf16[384,3072]{1,0:T(8,128)(2,1)S(1)} %collective-permute-done.14, bf16[384,3072]{1,0:T(8,128)(2,1)} %collective-permute-done.3, bf16[384,768]{1,0:T(8,128)(2,1)S(1)} %get-tuple-element.251, bf16[384,768]{1,0:T(8,128)(2,1)S(1)} %get-tuple-element.250, ...), kind=kLoop, calls=%fused_computation | loop fusion | flops 66060288 | bytes 18874368 | tf_op jit(solution)/shard_map/concatenate | solution.py:48
  173.4 7.5 %pad_maximum_fusion.1 = bf16[1536,3072]{1,0:T(8,128)(2,1)S(1)} fusion(bf16[384,3072]{1,0:T(8,128)(2,1)S(1)} %collective-permute-done.15, bf16[384,3072]{1,0:T(8,128)(2,1)} %collective-permute-done.4, bf16[384,768]{1,0:T(8,128)(2,1)S(1)} %get-tuple-element.254, bf16[384,768]{1,0:T(8,128)(2,1)S(1)} %get-tuple-element.253, ...), kind=kLoop, calls=%fused_computation.1 | loop fusion | flops 66060288 | bytes 18874368 | tf_op jit(solution)/shard_map/concatenate | solution.py:48
  180.9 6.9 %fusion.36 = f32[1536,512]{1,0:T(8,128)} fusion(bf16[1536,3072]{1,0:T(8,128)(2,1)S(1)} %pad_maximum_fusion, bf16[3072,512]{1,0:T(8,128)(2,1)S(1)} %bitcast.90), kind=kOutput, calls=%fused_computation.186 | convolution fusion | flops 4831838208 | bytes 15728640 | tf_op jit(solution)/shard_map/dot_general | solution.py:11
  187.7 2.0 collective-permute-done.12
  193.9 9.2 %multiply_convert_fusion.3 = (bf16[1536,512]{1,0:T(8,128)(2,1)S(1)}, f32[1536,512]{1,0:T(8,128)}) fusion(f32[1536,512]{1,0:T(8,128)} %fusion.36, bf16[1536,3072]{1,0:T(8,128)(2,1)S(1)} %pad_maximum_fusion, bf16[3072,512]{1,0:T(8,128)(2,1)S(1)} %bitcast.102), kind=kOutput, calls=%fused_computation.15 | convolution fusion | flops 4836556800 | bytes 20447232 | tf_op jit(solution)/shard_map/dot_general | solution.py:11
  203.1 5.9 %convolution_convert_fusion.3 = bf16[3072,512]{1,0:T(8,128)(2,1)S(1)} fusion(bf16[1536,3072]{1,0:T(8,128)(2,1)S(1)} %pad_maximum_fusion.1, bf16[1536,512]{1,0:T(8,128)(2,1)S(1)} %get-tuple-element.177), kind=kOutput, calls=%fused_computation.9 | convolution fusion | flops 4833411072 | bytes 14155776 | tf_op jit(solution)/shard_map/dot_general | solution.py:11
  210.3 4.4 convolution_convert_fusion
  218.2 9.4 %multiply_convert_fusion.1 = (bf16[1536,512]{1,0:T(8,128)(2,1)}, bf16[1536,512]{1,0:T(8,128)(2,1)}) fusion(f32[1536,512]{1,0:T(8,128)} %fusion.36, f32[1536,512]{1,0:T(8,128)} %get-tuple-element.161, bf16[1536,3072]{1,0:T(8,128)(2,1)S(1)} %pad_maximum_fusion.1, bf16[3072,512]{1,0:T(8,128)(2,1)S(1)} %bitcast.100), kind=kOutput, calls=%fused_computation.13 | convolution fusion | flops 4842061824 | bytes 22020096 | tf_op jit(solution)/shard_map/dot_general | solution.py:11
  227.7 3.9 fusion.11
  231.6 6.7 %convolution_convert_fusion.2 = bf16[3072,512]{1,0:T(8,128)(2,1)} fusion(bf16[1536,3072]{1,0:T(8,128)(2,1)S(1)} %pad_maximum_fusion, bf16[1536,512]{1,0:T(8,128)(2,1)S(1)} %copy-done.13), kind=kOutput, calls=%fused_computation.8 | convolution fusion | flops 4833411072 | bytes 14155776 | tf_op jit(solution)/shard_map/dot_general | solution.py:11
  238.3 3.1 add_convert_fusion.2
  241.4 11.8 %collective-permute-done.20 = bf16[768,512]{1,0:T(8,128)(2,1)S(1)} collective-permute-done((bf16[768,512]{1,0:T(8,128)(2,1)}, bf16[768,512]{1,0:T(8,128)(2,1)S(1)}, u32[]{:S(2)}, u32[]{:S(2)}) %collective-permute-start.20) | collective-permute-done | bytes 786464 | tf_op jit(solution)/shard_map/ppermute | solution.py:28
  253.2 2.5 add_convert_fusion.8
  255.7 2.5 fusion.34
  258.7 3.4 dynamic-slice_bitcast_fusion
  264.8 5.5 %add_convert_fusion = bf16[768,3072]{1,0:T(8,128)(2,1)S(1)} fusion(bf16[768,3072]{1,0:T(8,128)(2,1)} %collective-permute-done.18, bf16[3072,512]{1,0:T(8,128)(2,1)} %bitcast.101, bf16[1536,512]{1,0:T(8,128)(2,1)S(1)} %copy-done.42), kind=kOutput, calls=%fused_computation.2 | convolution fusion | flops 2422996992 | bytes 13369344 | tf_op jit(solution)/shard_map/dot_general | solution.py:11
  272.0 5.4 %convolution_convert_fusion.1 = bf16[3072,512]{1,0:T(8,128)(2,1)S(1)} fusion(bf16[1536,3072]{1,0:T(8,128)(2,1)S(1)} %bitcast.94, bf16[1536,512]{1,0:T(8,128)(2,1)S(1)} %copy-done.40), kind=kOutput, calls=%fused_computation.7 | convolution fusion | flops 4833411072 | bytes 14155776 | tf_op jit(solution)/shard_map/dot_general | solution.py:11
  281.7 5.2 %fusion.15 = f32[768,3072]{1,0:T(8,128)} fusion(bf16[3072,512]{1,0:T(8,128)(2,1)S(1)} %bitcast.104, bf16[1536,512]{1,0:T(8,128)(2,1)S(1)} %copy-done.40), kind=kOutput, calls=%fused_computation.96 | convolution fusion | flops 2415919104 | bytes 13369344 | tf_op jit(solution)/shard_map/dot_general | solution.py:11
  286.8 6.9 %add_convert_fusion.1 = bf16[768,3072]{1,0:T(8,128)(2,1)S(1)} fusion(f32[768,3072]{1,0:T(8,128)} %fusion.15, bf16[384,3072]{1,0:T(8,128)(2,1)} %collective-permute-done.23, bf16[384,3072]{1,0:T(8,128)(2,1)} %collective-permute-done.22, bf16[3072,512]{1,0:T(8,128)(2,1)S(1)} %bitcast.92, bf16[1536,512]{1,0:T(8,128)(2,1)} %get-tuple-element.174), kind=kOutput, calls=%fused_computation.3 | convolution fusion | flops 2432434176 | bytes 22806528 | tf_op jit(solution)/shard_map/dot_general | solution.py:11
  293.8 3.6 collective-permute-done.24
  297.4 3.4 collective-permute-done.21
  306.7 22.3 %collective-permute-done.26 = bf16[384,1536]{1,0:T(8,128)(2,1)S(1)} collective-permute-done((bf16[384,1536]{1,0:T(8,128)(2,1)S(1)}, bf16[384,1536]{1,0:T(8,128)(2,1)S(1)}, u32[]{:S(2)}, u32[]{:S(2)}) %collective-permute-start.26) | collective-permute-done | bytes 1179680 | tf_op jit(solution)/shard_map/ppermute | solution.py:28
  330.9 8.8 %collective-permute-done.25 = bf16[768,512]{1,0:T(8,128)(2,1)S(1)} collective-permute-done((bf16[768,512]{1,0:T(8,128)(2,1)S(1)}, bf16[768,512]{1,0:T(8,128)(2,1)S(1)}, u32[]{:S(2)}, u32[]{:S(2)}) %collective-permute-start.25) | collective-permute-done | bytes 786464 | tf_op jit(solution)/shard_map/ppermute | solution.py:28
  343.0 37.4 %collective-permute-done.31 = bf16[384,2304]{1,0:T(8,128)(2,1)S(1)} collective-permute-done((bf16[384,2304]{1,0:T(8,128)(2,1)S(1)}, bf16[384,2304]{1,0:T(8,128)(2,1)S(1)}, u32[]{:S(2)}, u32[]{:S(2)}) %collective-permute-start.31) | collective-permute-done | bytes 1769504 | tf_op jit(solution)/shard_map/ppermute | solution.py:28
  385.0 12.1 %collective-permute-done.35 = bf16[384,768]{1,0:T(8,128)(2,1)} collective-permute-done((bf16[384,768]{1,0:T(8,128)(2,1)}, bf16[384,768]{1,0:T(8,128)(2,1)}, u32[]{:S(2)}, u32[]{:S(2)}) %collective-permute-start.35) | collective-permute-done | bytes 589856 | tf_op jit(solution)/shard_map/ppermute | solution.py:28
  402.2 9.9 %collective-permute-done.33 = bf16[384,768]{1,0:T(8,128)(2,1)S(1)} collective-permute-done((bf16[384,768]{1,0:T(8,128)(2,1)}, bf16[384,768]{1,0:T(8,128)(2,1)S(1)}, u32[]{:S(2)}, u32[]{:S(2)}) %collective-permute-start.33) | collective-permute-done | bytes 589856 | tf_op jit(solution)/shard_map/ppermute | solution.py:28
  415.2 2.0 convolution_convert_fusion.7
  418.3 2.9 collective-permute-done.38
  421.2 3.3 collective-permute-start.36
  427.2 18.9 %collective-permute-done.36 = bf16[384,768]{1,0:T(8,128)(2,1)S(1)} collective-permute-done((bf16[384,768]{1,0:T(8,128)(2,1)S(1)}, bf16[384,768]{1,0:T(8,128)(2,1)S(1)}, u32[]{:S(2)}, u32[]{:S(2)}) %collective-permute-start.36) | collective-permute-done | bytes 589856 | tf_op jit(solution)/shard_map/ppermute | solution.py:28
  446.1 1.9 convolution_convert_fusion.6
  (242 shorter events, 74.1 us)
Async XLA Ops:
  3.1 38.8 %collective-permute-start = (bf16[384,1024]{1,0:T(8,128)(2,1)}, bf16[384,1024]{1,0:T(8,128)(2,1)}, u32[]{:S(2)}, u32[]{:S(2)}) collective-permute-start(bf16[384,1024]{1,0:T(8,128)(2,1)} %get-tuple-element.311), channel_id=1, source_target_pairs={{0,16},{4,20},{8,24},{12,28},{16,0},{20,4},{24,8},{28,12},{1,17},{... | collective-permute-start | bytes 2359304 | tf_op jit(solution)/shard_map/ppermute | solution.py:28
  7.1 34.8 %collective-permute-start.1 = (bf16[384,1024]{1,0:T(8,128)(2,1)S(1)}, bf16[384,1024]{1,0:T(8,128)(2,1)}, u32[]{:S(2)}, u32[]{:S(2)}) collective-permute-start(bf16[384,1024]{1,0:T(8,128)(2,1)S(1)} %get-tuple-element.129), channel_id=1, source_target_pairs={{0,8},{4,12},{8,0},{12,4},{16,24},{20,28},{24,16},{28,20},{1,9},{5... | collective-permute-start | bytes 2359304 | tf_op jit(solution)/shard_map/ppermute | solution.py:28
  41.9 5.8 %collective-permute-start.5 = (bf16[768,1024]{1,0:T(8,128)(2,1)S(1)}, bf16[768,1024]{1,0:T(8,128)(2,1)}, u32[]{:S(2)}, u32[]{:S(2)}) collective-permute-start(bf16[768,1024]{1,0:T(8,128)(2,1)S(1)} %maximum_maximum_fusion), channel_id=1, source_target_pairs={{0,4},{4,0},{8,12},{12,8},{16,20},{20,16},{24,28},{28,24},{1,5},{5... | collective-permute-start | bytes 4718600 | tf_op jit(solution)/shard_map/ppermute | solution.py:28
  41.9 55.3 %collective-permute-start.3 = (bf16[384,3072]{1,0:T(8,128)(2,1)}, bf16[384,3072]{1,0:T(8,128)(2,1)}, u32[]{:S(2)}, u32[]{:S(2)}) collective-permute-start(bf16[384,3072]{1,0:T(8,128)(2,1)} %convolution_convert_fusion.5), channel_id=1, source_target_pairs={{0,4},{4,0},{8,12},{12,8},{16,20},{20,16},{24,28},{28,24},{1,5},{5... | collective-permute-start | bytes 7077896 | tf_op jit(solution)/shard_map/ppermute | solution.py:28
  42.4 54.8 %collective-permute-start.4 = (bf16[384,3072]{1,0:T(8,128)(2,1)}, bf16[384,3072]{1,0:T(8,128)(2,1)}, u32[]{:S(2)}, u32[]{:S(2)}) collective-permute-start(bf16[384,3072]{1,0:T(8,128)(2,1)} %get-tuple-element.125), channel_id=1, source_target_pairs={{0,4},{4,0},{8,12},{12,8},{16,20},{20,16},{24,28},{28,24},{1,5},{5... | collective-permute-start | bytes 7077896 | tf_op jit(solution)/shard_map/ppermute | solution.py:28
  42.4 54.8 %collective-permute-start.2 = (bf16[768,768]{1,0:T(8,128)(2,1)}, bf16[768,768]{1,0:T(8,128)(2,1)S(1)}, u32[]{:S(2)}, u32[]{:S(2)}) collective-permute-start(bf16[768,768]{1,0:T(8,128)(2,1)} %pad_maximum_fusion.8), channel_id=1, source_target_pairs={{0,16},{4,20},{8,24},{12,28},{16,0},{20,4},{24,8},{28,12},{1,17},{... | collective-permute-start | bytes 3538952 | tf_op jit(solution)/shard_map/ppermute | solution.py:28
  44.0 43.1 %collective-permute-start.6 = (bf16[384,1024]{1,0:T(8,128)(2,1)}, bf16[384,1024]{1,0:T(8,128)(2,1)S(1)}, u32[]{:S(2)}, u32[]{:S(2)}) collective-permute-start(bf16[384,1024]{1,0:T(8,128)(2,1)} %collective-permute-done), channel_id=1, source_target_pairs={{0,8},{4,12},{8,0},{12,4},{16,24},{20,28},{24,16},{28,20},{1,9},{5... | collective-permute-start | bytes 2359304 | tf_op jit(solution)/shard_map/ppermute | solution.py:28
  52.8 53.1 %copy-start.1 = (bf16[768,1024]{1,0:T(8,128)(2,1)}, bf16[768,1024]{1,0:T(8,128)(2,1)S(1)}, u32[]{:S(2)}) copy-start(bf16[768,1024]{1,0:T(8,128)(2,1)S(1)} %pad_maximum_fusion.7) | copy-start | bytes 4718596
  97.2 54.2 %collective-permute-start.11 = (bf16[768,1024]{1,0:T(8,128)(2,1)S(1)}, bf16[768,1024]{1,0:T(8,128)(2,1)}, u32[]{:S(2)}, u32[]{:S(2)}) collective-permute-start(bf16[768,1024]{1,0:T(8,128)(2,1)S(1)} %pad_maximum_fusion.7), channel_id=1, source_target_pairs={{0,8},{4,12},{8,0},{12,4},{16,24},{20,28},{24,16},{28,20},{1,9},{5... | collective-permute-start | bytes 4718600 | tf_op jit(solution)/shard_map/ppermute | solution.py:28
  97.3 50.8 %collective-permute-start.10 = (bf16[768,768]{1,0:T(8,128)(2,1)S(1)}, bf16[768,768]{1,0:T(8,128)(2,1)}, u32[]{:S(2)}, u32[]{:S(2)}) collective-permute-start(bf16[768,768]{1,0:T(8,128)(2,1)S(1)} %collective-permute-done.2), channel_id=1, source_target_pairs={{0,3},{1,2},{2,1},{3,0},{4,7},{5,6},{6,5},{7,4},{8,11},{9,10},{10,... | collective-permute-start | bytes 3538952 | tf_op jit(solution)/shard_map/ppermute | solution.py:28
  99.8 51.5 %collective-permute-start.8 = (bf16[768,768]{1,0:T(8,128)(2,1)S(1)}, bf16[768,768]{1,0:T(8,128)(2,1)}, u32[]{:S(2)}, u32[]{:S(2)}) collective-permute-start(bf16[768,768]{1,0:T(8,128)(2,1)S(1)} %collective-permute-done.2), channel_id=1, source_target_pairs={{0,1},{1,0},{2,3},{3,2},{4,5},{5,4},{6,7},{7,6},{8,9},{9,8},{10,11... | collective-permute-start | bytes 3538952 | tf_op jit(solution)/shard_map/ppermute | solution.py:28
  100.4 51.0 %collective-permute-start.9 = (bf16[768,768]{1,0:T(8,128)(2,1)S(1)}, bf16[768,768]{1,0:T(8,128)(2,1)}, u32[]{:S(2)}, u32[]{:S(2)}) collective-permute-start(bf16[768,768]{1,0:T(8,128)(2,1)S(1)} %collective-permute-done.2), channel_id=1, source_target_pairs={{0,2},{1,3},{2,0},{3,1},{4,6},{5,7},{6,4},{7,5},{8,10},{9,11},{10,... | collective-permute-start | bytes 3538952 | tf_op jit(solution)/shard_map/ppermute | solution.py:28
  100.8 47.2 %collective-permute-start.7 = (bf16[768,512]{1,0:T(8,128)(2,1)}, bf16[768,512]{1,0:T(8,128)(2,1)}, u32[]{:S(2)}, u32[]{:S(2)}) collective-permute-start(bf16[768,512]{1,0:T(8,128)(2,1)} %maximum_select_fusion.2), channel_id=1, source_target_pairs={{0,16},{4,20},{8,24},{12,28},{16,0},{20,4},{24,8},{28,12},{1,17},{... | collective-permute-start | bytes 2359304 | tf_op jit(solution)/shard_map/ppermute | solution.py:28
  151.4 5.3 %collective-permute-start.13 = (bf16[4,384,512]{2,1,0:T(8,128)(2,1)}, bf16[4,384,512]{2,1,0:T(8,128)(2,1)}, u32[]{:S(2)}, u32[]{:S(2)}) collective-permute-start(bf16[4,384,512]{2,1,0:T(8,128)(2,1)} %get-tuple-element.138), channel_id=1, source_target_pairs={{0,4},{4,0},{8,12},{12,8},{16,20},{20,16},{24,28},{28,24},{1,5},{5... | collective-permute-start | bytes 4718600 | tf_op jit(solution)/shard_map/ppermute | solution.py:28
  151.5 38.3 %collective-permute-start.12 = (bf16[768,512]{1,0:T(8,128)(2,1)}, bf16[768,512]{1,0:T(8,128)(2,1)S(1)}, u32[]{:S(2)}, u32[]{:S(2)}) collective-permute-start(bf16[768,512]{1,0:T(8,128)(2,1)} %maximum_select_fusion.3), channel_id=1, source_target_pairs={{0,16},{4,20},{8,24},{12,28},{16,0},{20,4},{24,8},{28,12},{1,17},{... | collective-permute-start | bytes 2359304 | tf_op jit(solution)/shard_map/ppermute | solution.py:28
  154.5 35.7 %collective-permute-start.16 = (bf16[768,512]{1,0:T(8,128)(2,1)}, bf16[768,512]{1,0:T(8,128)(2,1)S(1)}, u32[]{:S(2)}, u32[]{:S(2)}) collective-permute-start(bf16[768,512]{1,0:T(8,128)(2,1)} %collective-permute-done.7), channel_id=1, source_target_pairs={{0,8},{4,12},{8,0},{12,4},{16,24},{20,28},{24,16},{28,20},{1,9},{5... | collective-permute-start | bytes 2359304 | tf_op jit(solution)/shard_map/ppermute | solution.py:28
  161.7 5.5 %collective-permute-start.14 = (bf16[384,3072]{1,0:T(8,128)(2,1)S(1)}, bf16[384,3072]{1,0:T(8,128)(2,1)S(1)}, u32[]{:S(2)}, u32[]{:S(2)}) collective-permute-start(bf16[384,3072]{1,0:T(8,128)(2,1)S(1)} %pad_maximum_fusion.3), channel_id=1, source_target_pairs={{0,4},{4,0},{8,12},{12,8},{16,20},{20,16},{24,28},{28,24},{1,5},{5... | collective-permute-start | bytes 7077896 | tf_op jit(solution)/shard_map/ppermute | solution.py:28
  162.4 11.0 %collective-permute-start.15 = (bf16[384,3072]{1,0:T(8,128)(2,1)S(1)}, bf16[384,3072]{1,0:T(8,128)(2,1)S(1)}, u32[]{:S(2)}, u32[]{:S(2)}) collective-permute-start(bf16[384,3072]{1,0:T(8,128)(2,1)S(1)} %pad_maximum_fusion.4), channel_id=1, source_target_pairs={{0,4},{4,0},{8,12},{12,8},{16,20},{20,16},{24,28},{28,24},{1,5},{5... | collective-permute-start | bytes 7077896 | tf_op jit(solution)/shard_map/ppermute | solution.py:28
  173.4 58.2 %copy-start = (bf16[1536,3072]{1,0:T(8,128)(2,1)}, bf16[1536,3072]{1,0:T(8,128)(2,1)S(1)}, u32[]{:S(2)}) copy-start(bf16[1536,3072]{1,0:T(8,128)(2,1)S(1)} %pad_maximum_fusion) | copy-start | bytes 28311556
  190.2 18.8 %collective-permute-start.17 = (bf16[768,512]{1,0:T(8,128)(2,1)S(1)}, bf16[768,512]{1,0:T(8,128)(2,1)S(1)}, u32[]{:S(2)}, u32[]{:S(2)}) collective-permute-start(bf16[768,512]{1,0:T(8,128)(2,1)S(1)} %collective-permute-done.12), channel_id=1, source_target_pairs={{0,8},{4,12},{8,0},{12,4},{16,24},{20,28},{24,16},{28,20},{1,9},{5... | collective-permute-start | bytes 2359304 | tf_op jit(solution)/shard_map/ppermute | solution.py:28
  214.7 38.5 %collective-permute-start.18 = (bf16[768,3072]{1,0:T(8,128)(2,1)}, bf16[768,3072]{1,0:T(8,128)(2,1)}, u32[]{:S(2)}, u32[]{:S(2)}) collective-permute-start(bf16[768,3072]{1,0:T(8,128)(2,1)} %convolution_convert_fusion), channel_id=1, source_target_pairs={{0,4},{4,0},{8,12},{12,8},{16,20},{20,16},{24,28},{28,24},{1,5},{5... | collective-permute-start | bytes 14155784 | tf_op jit(solution)/shard_map/ppermute | solution.py:28
  216.2 25.2 %collective-permute-start.19 = (bf16[768,512]{1,0:T(8,128)(2,1)}, bf16[768,512]{1,0:T(8,128)(2,1)}, u32[]{:S(2)}, u32[]{:S(2)}) collective-permute-start(bf16[768,512]{1,0:T(8,128)(2,1)} %get-tuple-element.270), channel_id=1, source_target_pairs={{0,8},{4,12},{8,0},{12,4},{16,24},{20,28},{24,16},{28,20},{1,9},{5... | collective-permute-start | bytes 2359304 | tf_op jit(solution)/shard_map/ppermute | solution.py:28
  217.6 35.6 %collective-permute-start.20 = (bf16[768,512]{1,0:T(8,128)(2,1)}, bf16[768,512]{1,0:T(8,128)(2,1)S(1)}, u32[]{:S(2)}, u32[]{:S(2)}) collective-permute-start(bf16[768,512]{1,0:T(8,128)(2,1)} %get-tuple-element.268), channel_id=1, source_target_pairs={{0,8},{4,12},{8,0},{12,4},{16,24},{20,28},{24,16},{28,20},{1,9},{5... | collective-permute-start | bytes 2359304 | tf_op jit(solution)/shard_map/ppermute | solution.py:28
  258.2 6.6 %collective-permute-start.22 = (bf16[384,3072]{1,0:T(8,128)(2,1)}, bf16[384,3072]{1,0:T(8,128)(2,1)}, u32[]{:S(2)}, u32[]{:S(2)}) collective-permute-start(bf16[384,3072]{1,0:T(8,128)(2,1)} %get-tuple-element.247), channel_id=1, source_target_pairs={{0,4},{4,0},{8,12},{12,8},{16,20},{20,16},{24,28},{28,24},{1,5},{5... | collective-permute-start | bytes 7077896 | tf_op jit(solution)/shard_map/ppermute | solution.py:28
  258.2 28.7 %collective-permute-start.23 = (bf16[384,3072]{1,0:T(8,128)(2,1)}, bf16[384,3072]{1,0:T(8,128)(2,1)}, u32[]{:S(2)}, u32[]{:S(2)}) collective-permute-start(bf16[384,3072]{1,0:T(8,128)(2,1)} %get-tuple-element.246), channel_id=1, source_target_pairs={{0,4},{4,0},{8,12},{12,8},{16,20},{20,16},{24,28},{28,24},{1,5},{5... | collective-permute-start | bytes 7077896 | tf_op jit(solution)/shard_map/ppermute | solution.py:28
  262.1 35.3 %collective-permute-start.24 = (bf16[768,512]{1,0:T(8,128)(2,1)}, bf16[768,512]{1,0:T(8,128)(2,1)}, u32[]{:S(2)}, u32[]{:S(2)}) collective-permute-start(bf16[768,512]{1,0:T(8,128)(2,1)} %get-tuple-element.262), channel_id=1, source_target_pairs={{0,8},{4,12},{8,0},{12,4},{16,24},{20,28},{24,16},{28,20},{1,9},{5... | collective-permute-start | bytes 2359304 | tf_op jit(solution)/shard_map/ppermute | solution.py:28
  263.6 37.3 %collective-permute-start.21 = (bf16[768,512]{1,0:T(8,128)(2,1)}, bf16[768,512]{1,0:T(8,128)(2,1)}, u32[]{:S(2)}, u32[]{:S(2)}) collective-permute-start(bf16[768,512]{1,0:T(8,128)(2,1)} %add_convert_fusion.8), channel_id=1, source_target_pairs={{0,16},{4,20},{8,24},{12,28},{16,0},{20,4},{24,8},{28,12},{1,17},{... | collective-permute-start | bytes 2359304 | tf_op jit(solution)/shard_map/ppermute | solution.py:28
  302.2 26.8 %collective-permute-start.26 = (bf16[384,1536]{1,0:T(8,128)(2,1)S(1)}, bf16[384,1536]{1,0:T(8,128)(2,1)S(1)}, u32[]{:S(2)}, u32[]{:S(2)}) collective-permute-start(bf16[384,1536]{1,0:T(8,128)(2,1)S(1)} %copy-done.25), channel_id=1, source_target_pairs={{0,1},{1,0},{2,3},{3,2},{4,5},{5,4},{6,7},{7,6},{8,9},{9,8},{10,11... | collective-permute-start | bytes 3538952 | tf_op jit(solution)/shard_map/ppermute | solution.py:28
  303.8 26.5 %collective-permute-start.27 = (bf16[384,1536]{1,0:T(8,128)(2,1)S(1)}, bf16[384,1536]{1,0:T(8,128)(2,1)S(1)}, u32[]{:S(2)}, u32[]{:S(2)}) collective-permute-start(bf16[384,1536]{1,0:T(8,128)(2,1)S(1)} %copy-done.24), channel_id=1, source_target_pairs={{0,2},{1,3},{2,0},{3,1},{4,6},{5,7},{6,4},{7,5},{8,10},{9,11},{10,... | collective-permute-start | bytes 3538952 | tf_op jit(solution)/shard_map/ppermute | solution.py:28
  305.3 34.4 %collective-permute-start.25 = (bf16[768,512]{1,0:T(8,128)(2,1)S(1)}, bf16[768,512]{1,0:T(8,128)(2,1)S(1)}, u32[]{:S(2)}, u32[]{:S(2)}) collective-permute-start(bf16[768,512]{1,0:T(8,128)(2,1)S(1)} %add_convert_fusion.7), channel_id=1, source_target_pairs={{0,16},{4,20},{8,24},{12,28},{16,0},{20,4},{24,8},{28,12},{1,17},{... | collective-permute-start | bytes 2359304 | tf_op jit(solution)/shard_map/ppermute | solution.py:28
  305.5 34.8 %collective-permute-start.28 = (bf16[768,512]{1,0:T(8,128)(2,1)}, bf16[768,512]{1,0:T(8,128)(2,1)S(1)}, u32[]{:S(2)}, u32[]{:S(2)}) collective-permute-start(bf16[768,512]{1,0:T(8,128)(2,1)} %get-tuple-element.194), channel_id=1, source_target_pairs={{0,8},{4,12},{8,0},{12,4},{16,24},{20,28},{24,16},{28,20},{1,9},{5... | collective-permute-start | bytes 2359304 | tf_op jit(solution)/shard_map/ppermute | solution.py:28
  340.5 39.9 %collective-permute-start.31 = (bf16[384,2304]{1,0:T(8,128)(2,1)S(1)}, bf16[384,2304]{1,0:T(8,128)(2,1)S(1)}, u32[]{:S(2)}, u32[]{:S(2)}) collective-permute-start(bf16[384,2304]{1,0:T(8,128)(2,1)S(1)} %pad_maximum_fusion.5), channel_id=1, source_target_pairs={{0,1},{1,0},{2,3},{3,2},{4,5},{5,4},{6,7},{7,6},{8,9},{9,8},{10,11... | collective-permute-start | bytes 5308424 | tf_op jit(solution)/shard_map/ppermute | solution.py:28
  341.1 40.8 %collective-permute-start.30 = (bf16[384,2304]{1,0:T(8,128)(2,1)S(1)}, bf16[384,2304]{1,0:T(8,128)(2,1)S(1)}, u32[]{:S(2)}, u32[]{:S(2)}) collective-permute-start(bf16[384,2304]{1,0:T(8,128)(2,1)S(1)} %pad_maximum_fusion.6), channel_id=1, source_target_pairs={{0,2},{1,3},{2,0},{3,1},{4,6},{5,7},{6,4},{7,5},{8,10},{9,11},{10,... | collective-permute-start | bytes 5308424 | tf_op jit(solution)/shard_map/ppermute | solution.py:28
  341.7 41.5 %collective-permute-start.29 = (bf16[768,512]{1,0:T(8,128)(2,1)S(1)}, bf16[768,512]{1,0:T(8,128)(2,1)}, u32[]{:S(2)}, u32[]{:S(2)}) collective-permute-start(bf16[768,512]{1,0:T(8,128)(2,1)S(1)} %add_convert_fusion.6), channel_id=1, source_target_pairs={{0,16},{4,20},{8,24},{12,28},{16,0},{20,4},{24,8},{28,12},{1,17},{... | collective-permute-start | bytes 2359304 | tf_op jit(solution)/shard_map/ppermute | solution.py:28
  341.7 41.5 %collective-permute-start.32 = (bf16[768,512]{1,0:T(8,128)(2,1)S(1)}, bf16[768,512]{1,0:T(8,128)(2,1)}, u32[]{:S(2)}, u32[]{:S(2)}) collective-permute-start(bf16[768,512]{1,0:T(8,128)(2,1)S(1)} %copy-done.29), channel_id=1, source_target_pairs={{0,8},{4,12},{8,0},{12,4},{16,24},{20,28},{24,16},{28,20},{1,9},{5... | collective-permute-start | bytes 2359304 | tf_op jit(solution)/shard_map/ppermute | solution.py:28
  381.9 16.5 %copy-start.10 = (bf16[768,512]{1,0:T(8,128)(2,1)S(1)}, bf16[768,512]{1,0:T(8,128)(2,1)}, u32[]{:S(2)}) copy-start(bf16[768,512]{1,0:T(8,128)(2,1)} %get-tuple-element.237) | copy-start | bytes 2359300
  381.9 16.5 %copy-start.28 = (bf16[768,512]{1,0:T(8,128)(2,1)S(1)}, bf16[768,512]{1,0:T(8,128)(2,1)}, u32[]{:S(2)}) copy-start(bf16[768,512]{1,0:T(8,128)(2,1)} %copy-done.27) | copy-start | bytes 2359300
  383.2 13.9 %collective-permute-start.35 = (bf16[384,768]{1,0:T(8,128)(2,1)}, bf16[384,768]{1,0:T(8,128)(2,1)}, u32[]{:S(2)}, u32[]{:S(2)}) collective-permute-start(bf16[384,768]{1,0:T(8,128)(2,1)} %get-tuple-element.223), channel_id=1, source_target_pairs={{0,1},{1,0},{2,3},{3,2},{4,5},{5,4},{6,7},{7,6},{8,9},{9,8},{10,11... | collective-permute-start | bytes 1769480 | tf_op jit(solution)/shard_map/ppermute | solution.py:28
  383.8 41.6 %collective-permute-start.40 = (bf16[768,512]{1,0:T(8,128)(2,1)}, bf16[768,512]{1,0:T(8,128)(2,1)S(1)}, u32[]{:S(2)}, u32[]{:S(2)}) collective-permute-start(bf16[768,512]{1,0:T(8,128)(2,1)} %get-tuple-element.235), channel_id=1, source_target_pairs={{0,8},{4,12},{8,0},{12,4},{16,24},{20,28},{24,16},{28,20},{1,9},{5... | collective-permute-start | bytes 2359304 | tf_op jit(solution)/shard_map/ppermute | solution.py:28
  383.8 28.3 %collective-permute-start.33 = (bf16[384,768]{1,0:T(8,128)(2,1)}, bf16[384,768]{1,0:T(8,128)(2,1)S(1)}, u32[]{:S(2)}, u32[]{:S(2)}) collective-permute-start(bf16[384,768]{1,0:T(8,128)(2,1)} %get-tuple-element.219), channel_id=1, source_target_pairs={{0,16},{4,20},{8,24},{12,28},{16,0},{20,4},{24,8},{28,12},{1,17},{... | collective-permute-start | bytes 1769480 | tf_op jit(solution)/shard_map/ppermute | solution.py:28
  384.6 42.7 %collective-permute-start.34 = (bf16[384,768]{1,0:T(8,128)(2,1)}, bf16[384,768]{1,0:T(8,128)(2,1)S(1)}, u32[]{:S(2)}, u32[]{:S(2)}) collective-permute-start(bf16[384,768]{1,0:T(8,128)(2,1)} %get-tuple-element.221), channel_id=1, source_target_pairs={{0,2},{1,3},{2,0},{3,1},{4,6},{5,7},{6,4},{7,5},{8,10},{9,11},{10,... | collective-permute-start | bytes 1769480 | tf_op jit(solution)/shard_map/ppermute | solution.py:28
  399.9 48.1 %collective-permute-start.42 = (bf16[384,1024]{1,0:T(8,128)(2,1)S(1)}, bf16[384,1024]{1,0:T(8,128)(2,1)S(1)}, u32[]{:S(2)}, u32[]{:S(2)}) collective-permute-start(bf16[384,1024]{1,0:T(8,128)(2,1)S(1)} %get-tuple-element.292), channel_id=1, source_target_pairs={{0,4},{4,0},{8,12},{12,8},{16,20},{20,16},{24,28},{28,24},{1,5},{5... | collective-permute-start | bytes 2359304 | tf_op jit(solution)/shard_map/ppermute | solution.py:28
  401.6 46.6 %collective-permute-start.39 = (bf16[384,1024]{1,0:T(8,128)(2,1)S(1)}, bf16[384,1024]{1,0:T(8,128)(2,1)S(1)}, u32[]{:S(2)}, u32[]{:S(2)}) collective-permute-start(bf16[384,1024]{1,0:T(8,128)(2,1)S(1)} %get-tuple-element.296), channel_id=1, source_target_pairs={{0,4},{4,0},{8,12},{12,8},{16,20},{20,16},{24,28},{28,24},{1,5},{5... | collective-permute-start | bytes 2359304 | tf_op jit(solution)/shard_map/ppermute | solution.py:28
  413.4 4.0 collective-permute-start.37
  417.5 3.7 collective-permute-start.38
  421.2 25.0 %collective-permute-start.36 = (bf16[384,768]{1,0:T(8,128)(2,1)S(1)}, bf16[384,768]{1,0:T(8,128)(2,1)S(1)}, u32[]{:S(2)}, u32[]{:S(2)}) collective-permute-start(bf16[384,768]{1,0:T(8,128)(2,1)S(1)} %add_convert_fusion.10), channel_id=1, source_target_pairs={{0,16},{4,20},{8,24},{12,28},{16,0},{20,4},{24,8},{28,12},{1,17},{... | collective-permute-start | bytes 1769480 | tf_op jit(solution)/shard_map/ppermute | solution.py:28
  426.9 19.3 %copy-start.30 = (bf16[384,768]{1,0:T(8,128)(2,1)S(1)}, bf16[384,768]{1,0:T(8,128)(2,1)}, u32[]{:S(2)}) copy-start(bf16[384,768]{1,0:T(8,128)(2,1)} %get-tuple-element.220) | copy-start | bytes 1769476
  426.9 21.4 %collective-permute-start.41 = (bf16[384,1024]{1,0:T(8,128)(2,1)S(1)}, bf16[384,1024]{1,0:T(8,128)(2,1)S(1)}, u32[]{:S(2)}, u32[]{:S(2)}) collective-permute-start(bf16[384,1024]{1,0:T(8,128)(2,1)S(1)} %get-tuple-element.294), channel_id=1, source_target_pairs={{0,4},{4,0},{8,12},{12,8},{16,20},{20,16},{24,28},{28,24},{1,5},{5... | collective-permute-start | bytes 2359304 | tf_op jit(solution)/shard_map/ppermute | solution.py:28
  (41 other events, 262.9 us)

commit v9 on v8

--- a/solution.py
+++ b/solution.py
@@ -235,19 +235,20 @@
         return mm_last(gate_grad[rows], gate) + mm_last(up_grad[rows], up)
 
     input_sib = input_part(slice(table, None)).astype(BF16)
-    down, gate_grad, up_grad, g_gate, expert_got, input_sib, *rest = fence(
-        down, gate_grad, up_grad, g_gate, expert_got, input_sib, *g_down_4, *g_down_own
+    input_a, input_b = input_sib[:row_limit], input_sib[row_limit:]
+    down, gate_grad, up_grad, g_gate, expert_got, input_a, input_b, *rest = fence(
+        down, gate_grad, up_grad, g_gate, expert_got, input_a, input_b, *g_down_4, *g_down_own
     )
     g_down_own = rest[2:]
-    g_down_4, input_sib, g_gate = fence(done(*rest[:2]), input_sib, g_gate)
+    g_down_4, input_a, input_b, g_gate = fence(done(*rest[:2]), input_a, input_b, g_gate)
     g_gate_4, g_gate_own = first_send(blocks_far(g_gate)), first_send(blocks_own(g_gate))
 
     g_down_far = z_far(g_down_4)
     g_gate_4 = shrink(*g_gate_4)
     input_got, in_all, gate_grad, up_grad, hidden = fence(
-        across(input_sib[:row_limit]), in_all, gate_grad, up_grad, hidden
-    )
-    input_got = cat(input_got, across(input_sib[row_limit:]))
+        across(input_a), in_all, gate_grad, up_grad, hidden
+    )
+    input_got = cat(input_got, across(input_b))
     g_up = mm_first(in_all, up_grad).astype(BF16)
     expert_sum = (mm_last(hidden[:table], down) + expert_got.astype(F32)).astype(BF16)
     input_sum = (input_part(slice(None, table)) + input_got.astype(F32)).astype(BF16)
@@ -289,10 +290,12 @@
         done(*rest[:2]), send_low, send_high, input_sum, *rest[2 : 2 + n_kept]
     )
 
-    def panel(own, other):
+    def halves_of(own, other):
         both = beside(own, other)
         mine = lax.dynamic_slice_in_dim(both, core * rows_w, rows_w, 0)
-        got = across(lax.dynamic_slice_in_dim(both, (1 - core) * rows_w, rows_w, 0))
+        return mine, lax.dynamic_slice_in_dim(both, (1 - core) * rows_w, rows_w, 0)
+
+    def panel(mine, got):
         whole = jnp.zeros((rows_w, 4 * hid), BF16)
         for block, u, c in (
             (mine[:, :hid], upper, core),
@@ -350,10 +353,15 @@
         input_mine = step(input_mine, bit)
     for bit in t_bits[:-1][::-1]:
         input_other = step(input_other, bit)
-    input_other, g_down_far, g_gate_far, *rest = fence(
-        input_other[0], g_down_far, g_gate_far, *g_down_own, *g_gate_own
-    )
-    g_down_own, g_gate_own = rest[:2], rest[2:]
+    input_mine, input_other, g_down_far, g_gate_far, *rest = fence(
+        input_mine[0], input_other[0], g_down_far, g_gate_far, *g_down_own, *g_gate_own
+    )
+    down_mine, down_send = halves_of(done(*rest[:2]), g_down_far)
+    gate_mine, gate_send = halves_of(done(*rest[2:]), g_gate_far)
+    got = across(cat(down_send, gate_send))
+    down_out, gate_out = panel(down_mine, got[:rows_w]), panel(gate_mine, got[rows_w:])
+    up_mine, up_send = halves_of(done(*g_up_own), g_up_far)
+    up_out = panel(up_mine, across(up_send))
     input_got = z_far(input_other)
     expert_cols = expert_mine.astype(F32) + expert_got.astype(F32)
     grad_cols = lax.dynamic_slice_in_dim(rows_grad, me_t * width, width, 1)
@@ -362,16 +370,9 @@
         weight_rows = weight_rows + swap(weight_rows, "tensor", bit)
     weight_grad = jnp.sum(jnp.where(match, weight_rows[:, None], 0.0), axis=0)
     mixed = mm_first(hot, (row_weight[:, None] * expert_cols).astype(BF16)).astype(BF16)
-    input_cols = (input_mine[0].astype(F32) + input_got.astype(F32)).astype(BF16)
+    input_cols = (input_mine.astype(F32) + input_got.astype(F32)).astype(BF16)
     input_grad = mm_first(hot, input_cols).astype(BF16)
-    return (
-        mixed,
-        input_grad,
-        weight_grad,
-        panel(done(*g_gate_own), g_gate_far),
-        panel(done(*g_up_own), g_up_far),
-        panel(done(*g_down_own), g_down_far),
-    )
+    return (mixed, input_grad, weight_grad, gate_out, up_out, down_out)
 
 
 def solution(mesh):

time: 458 us -> 459 us (level)
    ppermute x43 -> x42, waiting for transfers between devices: 241 us -> 238 us  [swap(): return lax.ppermute(value, axis, [(i, i ^ distance) for i in range(size)])]
    ppermute x43 -> x42, starting transfers between devices: 41.4 us -> 42 us  [swap(): return lax.ppermute(value, axis, [(i, i ^ distance) for i in range(size)])]
    concatenate x4 -> x5, other arithmetic: 14.9 us -> 15 us  [cat(): return jnp.concatenate(values, axis=0)]
  transfers between devices with their start and end apart: 43 -> 42, of which waited for: 20 -> 21; matrix products, arithmetic and copies ran while one was open for 32% -> 33% of each run, Pallas kernels for 0% -> 0%
where the time goes in v9:
time: 459 us; the launch traced here: 452 us
  waiting for transfers between devices  238 us (52%)
  matrix products  86.7 us (19%)
  other arithmetic  44.3 us (10%)
  starting transfers between devices  42 us (9%)
  local copies, waits for them, and re-layouts  38.8 us (8%)
    ppermute x42, waiting for transfers between devices, swap(): return lax.ppermute(value, axis, [(i, i ^ distance) for i in range(size)])  238 us
    dot_general x16, matrix products, dot(): lax.dot_general(left, right, (dims, ((), ())), preferred_element_type=F32)  86.7 us
    ppermute x42, starting transfers between devices, swap(): return lax.ppermute(value, axis, [(i, i ^ distance) for i in range(size)])  42 us
    concatenate x5, other arithmetic, cat(): return jnp.concatenate(values, axis=0)  15 us
  transfers between devices with their start and end apart: 42, of which 21 were waited for; matrix products, arithmetic and copies ran while one was open for 33% of the time, Pallas kernels for 0%

profile of v9, /device:TPU:0, one launch (start us, length us, event | category | flops | bytes accessed | tf_op | source)
XLA Modules:
  0.0 451.7 jit_solution(13368102051273062243)
XLA Ops:
  0.7 2.4 constant_dynamic-slice_fusion.18
  3.1 4.0 collective-permute-start
  9.7 5.9 %convolution_convert_fusion.5 = bf16[384,3072]{1,0:T(8,128)(2,1)} fusion(bf16[768,3072]{1,0:T(8,128)(2,1)} %param.7, s32[768]{0:T(1024)S(1)} %add_bitcast_fusion, pred[768]{0:T(1024)(128)(4,1)S(1)} %fusion.31), kind=kOutput, calls=%fused_computation.11 | convolution fusion | flops 1813708800 | bytes 7081728 | tf_op jit(solution)/shard_map/dot_general | solution.py:11
  15.5 4.2 multiply_convert_fusion
  25.5 16.3 %collective-permute-done = bf16[384,1024]{1,0:T(8,128)(2,1)} collective-permute-done((bf16[384,1024]{1,0:T(8,128)(2,1)}, bf16[384,1024]{1,0:T(8,128)(2,1)}, u32[]{:S(2)}, u32[]{:S(2)}) %collective-permute-start) | collective-permute-done | bytes 786464 | tf_op jit(solution)/shard_map/ppermute | solution.py:28
  44.0 2.4 collective-permute-start.6
  52.8 34.3 %collective-permute-done.6 = bf16[384,1024]{1,0:T(8,128)(2,1)S(1)} collective-permute-done((bf16[384,1024]{1,0:T(8,128)(2,1)}, bf16[384,1024]{1,0:T(8,128)(2,1)S(1)}, u32[]{:S(2)}, u32[]{:S(2)}) %collective-permute-start.6) | collective-permute-done | bytes 786464 | tf_op jit(solution)/shard_map/ppermute | solution.py:28
  87.1 10.1 %collective-permute-done.2 = bf16[768,768]{1,0:T(8,128)(2,1)S(1)} collective-permute-done((bf16[768,768]{1,0:T(8,128)(2,1)}, bf16[768,768]{1,0:T(8,128)(2,1)S(1)}, u32[]{:S(2)}, u32[]{:S(2)}) %collective-permute-start.2) | collective-permute-done | bytes 1179680 | tf_op jit(solution)/shard_map/ppermute | solution.py:28
  97.3 2.6 collective-permute-start.10
  100.8 3.0 collective-permute-start.7
  103.8 2.0 pad_maximum_fusion.2
  105.8 2.0 constant_dynamic-slice_fusion.12
  107.8 40.2 %collective-permute-done.7 = bf16[768,512]{1,0:T(8,128)(2,1)} collective-permute-done((bf16[768,512]{1,0:T(8,128)(2,1)}, bf16[768,512]{1,0:T(8,128)(2,1)}, u32[]{:S(2)}, u32[]{:S(2)}) %collective-permute-start.7) | collective-permute-done | bytes 786464 | tf_op jit(solution)/shard_map/ppermute | solution.py:28
  148.0 3.3 collective-permute-done.8
  151.5 3.1 collective-permute-start.12
  156.7 1.8 copy-done.7
  158.4 2.3 broadcast_select_fusion.10
  160.8 2.3 broadcast_select_fusion.11
  168.9 6.1 %pad_maximum_fusion = bf16[1536,3072]{1,0:T(8,128)(2,1)S(1)} fusion(bf16[384,3072]{1,0:T(8,128)(2,1)S(1)} %collective-permute-done.14, bf16[384,3072]{1,0:T(8,128)(2,1)} %collective-permute-done.3, bf16[384,768]{1,0:T(8,128)(2,1)S(1)} %get-tuple-element.257, bf16[384,768]{1,0:T(8,128)(2,1)S(1)} %get-tuple-element.256, ...), kind=kLoop, calls=%fused_computation | loop fusion | flops 66060288 | bytes 18874368 | tf_op jit(solution)/shard_map/concatenate | solution.py:48
  175.0 7.5 %pad_maximum_fusion.1 = bf16[1536,3072]{1,0:T(8,128)(2,1)S(1)} fusion(bf16[384,3072]{1,0:T(8,128)(2,1)S(1)} %collective-permute-done.15, bf16[384,3072]{1,0:T(8,128)(2,1)} %collective-permute-done.4, bf16[384,768]{1,0:T(8,128)(2,1)S(1)} %get-tuple-element.260, bf16[384,768]{1,0:T(8,128)(2,1)S(1)} %get-tuple-element.259, ...), kind=kLoop, calls=%fused_computation.1 | loop fusion | flops 66060288 | bytes 18874368 | tf_op jit(solution)/shard_map/concatenate | solution.py:48
  182.5 5.2 %fusion.36 = f32[1536,512]{1,0:T(8,128)S(1)} fusion(bf16[1536,3072]{1,0:T(8,128)(2,1)S(1)} %pad_maximum_fusion, bf16[3072,512]{1,0:T(8,128)(2,1)S(1)} %bitcast.90), kind=kOutput, calls=%fused_computation.187 | convolution fusion | flops 4831838208 | bytes 15728640 | tf_op jit(solution)/shard_map/dot_general | solution.py:11
  187.7 2.1 collective-permute-done.12
  193.9 7.0 %multiply_convert_fusion.3 = (bf16[1536,512]{1,0:T(8,128)(2,1)}, f32[1536,512]{1,0:T(8,128)}) fusion(f32[1536,512]{1,0:T(8,128)S(1)} %fusion.36, bf16[1536,3072]{1,0:T(8,128)(2,1)S(1)} %pad_maximum_fusion, bf16[3072,512]{1,0:T(8,128)(2,1)S(1)} %bitcast.102), kind=kOutput, calls=%fused_computation.15 | convolution fusion | flops 4836556800 | bytes 20447232 | tf_op jit(solution)/shard_map/dot_general | solution.py:11
  200.9 7.1 %convolution_convert_fusion.3 = bf16[3072,512]{1,0:T(8,128)(2,1)S(1)} fusion(bf16[1536,3072]{1,0:T(8,128)(2,1)S(1)} %pad_maximum_fusion.1, bf16[1536,512]{1,0:T(8,128)(2,1)} %get-tuple-element.182), kind=kOutput, calls=%fused_computation.9 | convolution fusion | flops 4833411072 | bytes 14155776 | tf_op jit(solution)/shard_map/dot_general | solution.py:11
  211.6 4.3 convolution_convert_fusion
  215.9 8.9 %multiply_convert_fusion.1 = (bf16[1536,512]{1,0:T(8,128)(2,1)S(1)}, bf16[1536,512]{1,0:T(8,128)(2,1)}) fusion(f32[1536,512]{1,0:T(8,128)} %copy-done.44, f32[1536,512]{1,0:T(8,128)} %get-tuple-element.164, bf16[1536,3072]{1,0:T(8,128)(2,1)S(1)} %pad_maximum_fusion.1, bf16[3072,512]{1,0:T(8,128)(2,1)S(1)} %bitcast.100), kind=kOutput, calls=%fused_computation.13 | convolution fusion | flops 4842061824 | bytes 22020096 | tf_op jit(solution)/shard_map/dot_general | solution.py:11
  228.2 5.2 %fusion.11 = f32[768,3072]{1,0:T(8,128)} fusion(bf16[3072,512]{1,0:T(8,128)(2,1)S(1)} %bitcast.103, bf16[1536,512]{1,0:T(8,128)(2,1)S(1)} %get-tuple-element.179), kind=kOutput, calls=%fused_computation.73 | convolution fusion | flops 2415919104 | bytes 13369344 | tf_op jit(solution)/shard_map/dot_general | solution.py:11
  233.3 5.3 %add_convert_fusion.2 = bf16[768,3072]{1,0:T(8,128)(2,1)S(1)} fusion(f32[768,3072]{1,0:T(8,128)} %fusion.11, bf16[3072,512]{1,0:T(8,128)(2,1)S(1)} %bitcast.91, bf16[1536,512]{1,0:T(8,128)(2,1)S(1)} %copy-done.15), kind=kOutput, calls=%fused_computation.4 | convolution fusion | flops 2420637696 | bytes 18087936 | tf_op jit(solution)/shard_map/dot_general | solution.py:11
  238.6 6.7 %convolution_convert_fusion.2 = bf16[3072,512]{1,0:T(8,128)(2,1)} fusion(bf16[1536,3072]{1,0:T(8,128)(2,1)S(1)} %pad_maximum_fusion, bf16[1536,512]{1,0:T(8,128)(2,1)S(1)} %copy-done.15), kind=kOutput, calls=%fused_computation.8 | convolution fusion | flops 4833411072 | bytes 14155776 | tf_op jit(solution)/shard_map/dot_general | solution.py:11
  245.3 2.4 fusion.34
  247.8 15.4 %collective-permute-done.20 = bf16[768,512]{1,0:T(8,128)(2,1)S(1)} collective-permute-done((bf16[768,512]{1,0:T(8,128)(2,1)S(1)}, bf16[768,512]{1,0:T(8,128)(2,1)S(1)}, u32[]{:S(2)}, u32[]{:S(2)}) %collective-permute-start.20) | collective-permute-done | bytes 786464 | tf_op jit(solution)/shard_map/ppermute | solution.py:28
  264.8 3.5 dynamic-slice_bitcast_fusion
  271.1 5.9 %add_convert_fusion = bf16[768,3072]{1,0:T(8,128)(2,1)S(1)} fusion(bf16[768,3072]{1,0:T(8,128)(2,1)} %collective-permute-done.18, bf16[3072,512]{1,0:T(8,128)(2,1)} %bitcast.101, bf16[1536,512]{1,0:T(8,128)(2,1)S(1)} %copy-done.43), kind=kOutput, calls=%fused_computation.2 | convolution fusion | flops 2422996992 | bytes 13369344 | tf_op jit(solution)/shard_map/dot_general | solution.py:11
  278.7 5.4 %convolution_convert_fusion.1 = bf16[3072,512]{1,0:T(8,128)(2,1)S(1)} fusion(bf16[1536,3072]{1,0:T(8,128)(2,1)S(1)} %bitcast.94, bf16[1536,512]{1,0:T(8,128)(2,1)S(1)} %copy-done.41), kind=kOutput, calls=%fused_computation.7 | convolution fusion | flops 4833411072 | bytes 14155776 | tf_op jit(solution)/shard_map/dot_general | solution.py:11
  288.3 5.1 %fusion.15 = f32[768,3072]{1,0:T(8,128)} fusion(bf16[3072,512]{1,0:T(8,128)(2,1)S(1)} %bitcast.104, bf16[1536,512]{1,0:T(8,128)(2,1)S(1)} %copy-done.41), kind=kOutput, calls=%fused_computation.97 | convolution fusion | flops 2415919104 | bytes 13369344 | tf_op jit(solution)/shard_map/dot_general | solution.py:11
  293.4 6.9 %add_convert_fusion.1 = bf16[768,3072]{1,0:T(8,128)(2,1)S(1)} fusion(f32[768,3072]{1,0:T(8,128)} %fusion.15, bf16[384,3072]{1,0:T(8,128)(2,1)} %collective-permute-done.23, bf16[384,3072]{1,0:T(8,128)(2,1)} %collective-permute-done.22, bf16[3072,512]{1,0:T(8,128)(2,1)S(1)} %bitcast.92, bf16[1536,512]{1,0:T(8,128)(2,1)} %get-tuple-element.178), kind=kOutput, calls=%fused_computation.3 | convolution fusion | flops 2432434176 | bytes 22806528 | tf_op jit(solution)/shard_map/dot_general | solution.py:11
  300.3 3.1 collective-permute-done.24
  303.4 3.7 collective-permute-done.21
  313.0 22.3 %collective-permute-done.26 = bf16[384,1536]{1,0:T(8,128)(2,1)S(1)} collective-permute-done((bf16[384,1536]{1,0:T(8,128)(2,1)S(1)}, bf16[384,1536]{1,0:T(8,128)(2,1)S(1)}, u32[]{:S(2)}, u32[]{:S(2)}) %collective-permute-start.26) | collective-permute-done | bytes 1179680 | tf_op jit(solution)/shard_map/ppermute | solution.py:28
  337.2 8.7 %collective-permute-done.25 = bf16[768,512]{1,0:T(8,128)(2,1)S(1)} collective-permute-done((bf16[768,512]{1,0:T(8,128)(2,1)S(1)}, bf16[768,512]{1,0:T(8,128)(2,1)S(1)}, u32[]{:S(2)}, u32[]{:S(2)}) %collective-permute-start.25) | collective-permute-done | bytes 786464 | tf_op jit(solution)/shard_map/ppermute | solution.py:28
  349.4 37.2 %collective-permute-done.31 = bf16[384,2304]{1,0:T(8,128)(2,1)S(1)} collective-permute-done((bf16[384,2304]{1,0:T(8,128)(2,1)S(1)}, bf16[384,2304]{1,0:T(8,128)(2,1)S(1)}, u32[]{:S(2)}, u32[]{:S(2)}) %collective-permute-start.31) | collective-permute-done | bytes 1769504 | tf_op jit(solution)/shard_map/ppermute | solution.py:28
  391.5 11.8 %collective-permute-done.35 = bf16[384,768]{1,0:T(8,128)(2,1)} collective-permute-done((bf16[384,768]{1,0:T(8,128)(2,1)}, bf16[384,768]{1,0:T(8,128)(2,1)}, u32[]{:S(2)}, u32[]{:S(2)}) %collective-permute-start.35) | collective-permute-done | bytes 589856 | tf_op jit(solution)/shard_map/ppermute | solution.py:28
  409.5 9.1 %collective-permute-done.33 = bf16[384,768]{1,0:T(8,128)(2,1)S(1)} collective-permute-done((bf16[384,768]{1,0:T(8,128)(2,1)}, bf16[384,768]{1,0:T(8,128)(2,1)S(1)}, u32[]{:S(2)}, u32[]{:S(2)}) %collective-permute-start.33) | collective-permute-done | bytes 589856 | tf_op jit(solution)/shard_map/ppermute | solution.py:28
  421.5 3.4 collective-permute-start.36
  424.8 2.0 convolution_convert_fusion.7
  428.7 2.0 collective-permute-done.38
  433.5 13.9 %collective-permute-done.36 = bf16[384,768]{1,0:T(8,128)(2,1)S(1)} collective-permute-done((bf16[384,768]{1,0:T(8,128)(2,1)S(1)}, bf16[384,768]{1,0:T(8,128)(2,1)S(1)}, u32[]{:S(2)}, u32[]{:S(2)}) %collective-permute-start.36) | collective-permute-done | bytes 589856 | tf_op jit(solution)/shard_map/ppermute | solution.py:28
  447.4 1.9 convolution_convert_fusion.6
  (245 shorter events, 78.8 us)
Async XLA Ops:
  3.1 38.8 %collective-permute-start = (bf16[384,1024]{1,0:T(8,128)(2,1)}, bf16[384,1024]{1,0:T(8,128)(2,1)}, u32[]{:S(2)}, u32[]{:S(2)}) collective-permute-start(bf16[384,1024]{1,0:T(8,128)(2,1)} %get-tuple-element.319), channel_id=1, source_target_pairs={{0,16},{4,20},{8,24},{12,28},{16,0},{20,4},{24,8},{28,12},{1,17},{... | collective-permute-start | bytes 2359304 | tf_op jit(solution)/shard_map/ppermute | solution.py:28
  7.1 34.8 %collective-permute-start.1 = (bf16[384,1024]{1,0:T(8,128)(2,1)S(1)}, bf16[384,1024]{1,0:T(8,128)(2,1)}, u32[]{:S(2)}, u32[]{:S(2)}) collective-permute-start(bf16[384,1024]{1,0:T(8,128)(2,1)S(1)} %get-tuple-element.132), channel_id=1, source_target_pairs={{0,8},{4,12},{8,0},{12,4},{16,24},{20,28},{24,16},{28,20},{1,9},{5... | collective-permute-start | bytes 2359304 | tf_op jit(solution)/shard_map/ppermute | solution.py:28
  41.9 5.8 %collective-permute-start.5 = (bf16[768,1024]{1,0:T(8,128)(2,1)S(1)}, bf16[768,1024]{1,0:T(8,128)(2,1)}, u32[]{:S(2)}, u32[]{:S(2)}) collective-permute-start(bf16[768,1024]{1,0:T(8,128)(2,1)S(1)} %maximum_maximum_fusion), channel_id=1, source_target_pairs={{0,4},{4,0},{8,12},{12,8},{16,20},{20,16},{24,28},{28,24},{1,5},{5... | collective-permute-start | bytes 4718600 | tf_op jit(solution)/shard_map/ppermute | solution.py:28
  41.9 55.3 %collective-permute-start.3 = (bf16[384,3072]{1,0:T(8,128)(2,1)}, bf16[384,3072]{1,0:T(8,128)(2,1)}, u32[]{:S(2)}, u32[]{:S(2)}) collective-permute-start(bf16[384,3072]{1,0:T(8,128)(2,1)} %convolution_convert_fusion.5), channel_id=1, source_target_pairs={{0,4},{4,0},{8,12},{12,8},{16,20},{20,16},{24,28},{28,24},{1,5},{5... | collective-permute-start | bytes 7077896 | tf_op jit(solution)/shard_map/ppermute | solution.py:28
  42.4 54.8 %collective-permute-start.4 = (bf16[384,3072]{1,0:T(8,128)(2,1)}, bf16[384,3072]{1,0:T(8,128)(2,1)}, u32[]{:S(2)}, u32[]{:S(2)}) collective-permute-start(bf16[384,3072]{1,0:T(8,128)(2,1)} %get-tuple-element.128), channel_id=1, source_target_pairs={{0,4},{4,0},{8,12},{12,8},{16,20},{20,16},{24,28},{28,24},{1,5},{5... | collective-permute-start | bytes 7077896 | tf_op jit(solution)/shard_map/ppermute | solution.py:28
  42.4 54.8 %collective-permute-start.2 = (bf16[768,768]{1,0:T(8,128)(2,1)}, bf16[768,768]{1,0:T(8,128)(2,1)S(1)}, u32[]{:S(2)}, u32[]{:S(2)}) collective-permute-start(bf16[768,768]{1,0:T(8,128)(2,1)} %pad_maximum_fusion.9), channel_id=1, source_target_pairs={{0,16},{4,20},{8,24},{12,28},{16,0},{20,4},{24,8},{28,12},{1,17},{... | collective-permute-start | bytes 3538952 | tf_op jit(solution)/shard_map/ppermute | solution.py:28
  44.0 43.1 %collective-permute-start.6 = (bf16[384,1024]{1,0:T(8,128)(2,1)}, bf16[384,1024]{1,0:T(8,128)(2,1)S(1)}, u32[]{:S(2)}, u32[]{:S(2)}) collective-permute-start(bf16[384,1024]{1,0:T(8,128)(2,1)} %collective-permute-done), channel_id=1, source_target_pairs={{0,8},{4,12},{8,0},{12,4},{16,24},{20,28},{24,16},{28,20},{1,9},{5... | collective-permute-start | bytes 2359304 | tf_op jit(solution)/shard_map/ppermute | solution.py:28
  52.8 53.0 %copy-start.1 = (bf16[768,1024]{1,0:T(8,128)(2,1)}, bf16[768,1024]{1,0:T(8,128)(2,1)S(1)}, u32[]{:S(2)}) copy-start(bf16[768,1024]{1,0:T(8,128)(2,1)S(1)} %pad_maximum_fusion.7) | copy-start | bytes 4718596
  97.2 54.2 %collective-permute-start.11 = (bf16[768,1024]{1,0:T(8,128)(2,1)S(1)}, bf16[768,1024]{1,0:T(8,128)(2,1)}, u32[]{:S(2)}, u32[]{:S(2)}) collective-permute-start(bf16[768,1024]{1,0:T(8,128)(2,1)S(1)} %pad_maximum_fusion.7), channel_id=1, source_target_pairs={{0,8},{4,12},{8,0},{12,4},{16,24},{20,28},{24,16},{28,20},{1,9},{5... | collective-permute-start | bytes 4718600 | tf_op jit(solution)/shard_map/ppermute | solution.py:28
  97.3 50.8 %collective-permute-start.10 = (bf16[768,768]{1,0:T(8,128)(2,1)S(1)}, bf16[768,768]{1,0:T(8,128)(2,1)}, u32[]{:S(2)}, u32[]{:S(2)}) collective-permute-start(bf16[768,768]{1,0:T(8,128)(2,1)S(1)} %collective-permute-done.2), channel_id=1, source_target_pairs={{0,3},{1,2},{2,1},{3,0},{4,7},{5,6},{6,5},{7,4},{8,11},{9,10},{10,... | collective-permute-start | bytes 3538952 | tf_op jit(solution)/shard_map/ppermute | solution.py:28
  99.8 51.5 %collective-permute-start.8 = (bf16[768,768]{1,0:T(8,128)(2,1)S(1)}, bf16[768,768]{1,0:T(8,128)(2,1)}, u32[]{:S(2)}, u32[]{:S(2)}) collective-permute-start(bf16[768,768]{1,0:T(8,128)(2,1)S(1)} %collective-permute-done.2), channel_id=1, source_target_pairs={{0,1},{1,0},{2,3},{3,2},{4,5},{5,4},{6,7},{7,6},{8,9},{9,8},{10,11... | collective-permute-start | bytes 3538952 | tf_op jit(solution)/shard_map/ppermute | solution.py:28
  100.4 51.0 %collective-permute-start.9 = (bf16[768,768]{1,0:T(8,128)(2,1)S(1)}, bf16[768,768]{1,0:T(8,128)(2,1)}, u32[]{:S(2)}, u32[]{:S(2)}) collective-permute-start(bf16[768,768]{1,0:T(8,128)(2,1)S(1)} %collective-permute-done.2), channel_id=1, source_target_pairs={{0,2},{1,3},{2,0},{3,1},{4,6},{5,7},{6,4},{7,5},{8,10},{9,11},{10,... | collective-permute-start | bytes 3538952 | tf_op jit(solution)/shard_map/ppermute | solution.py:28
  100.8 47.2 %collective-permute-start.7 = (bf16[768,512]{1,0:T(8,128)(2,1)}, bf16[768,512]{1,0:T(8,128)(2,1)}, u32[]{:S(2)}, u32[]{:S(2)}) collective-permute-start(bf16[768,512]{1,0:T(8,128)(2,1)} %maximum_select_fusion.2), channel_id=1, source_target_pairs={{0,16},{4,20},{8,24},{12,28},{16,0},{20,4},{24,8},{28,12},{1,17},{... | collective-permute-start | bytes 2359304 | tf_op jit(solution)/shard_map/ppermute | solution.py:28
  151.4 7.0 %collective-permute-start.13 = (bf16[4,384,512]{2,1,0:T(8,128)(2,1)}, bf16[4,384,512]{2,1,0:T(8,128)(2,1)}, u32[]{:S(2)}, u32[]{:S(2)}) collective-permute-start(bf16[4,384,512]{2,1,0:T(8,128)(2,1)} %get-tuple-element.141), channel_id=1, source_target_pairs={{0,4},{4,0},{8,12},{12,8},{16,20},{20,16},{24,28},{28,24},{1,5},{5... | collective-permute-start | bytes 4718600 | tf_op jit(solution)/shard_map/ppermute | solution.py:28
  151.5 38.3 %collective-permute-start.12 = (bf16[768,512]{1,0:T(8,128)(2,1)}, bf16[768,512]{1,0:T(8,128)(2,1)S(1)}, u32[]{:S(2)}, u32[]{:S(2)}) collective-permute-start(bf16[768,512]{1,0:T(8,128)(2,1)} %maximum_select_fusion.3), channel_id=1, source_target_pairs={{0,16},{4,20},{8,24},{12,28},{16,0},{20,4},{24,8},{28,12},{1,17},{... | collective-permute-start | bytes 2359304 | tf_op jit(solution)/shard_map/ppermute | solution.py:28
  154.5 35.7 %collective-permute-start.16 = (bf16[768,512]{1,0:T(8,128)(2,1)}, bf16[768,512]{1,0:T(8,128)(2,1)S(1)}, u32[]{:S(2)}, u32[]{:S(2)}) collective-permute-start(bf16[768,512]{1,0:T(8,128)(2,1)} %collective-permute-done.7), channel_id=1, source_target_pairs={{0,8},{4,12},{8,0},{12,4},{16,24},{20,28},{24,16},{28,20},{1,9},{5... | collective-permute-start | bytes 2359304 | tf_op jit(solution)/shard_map/ppermute | solution.py:28
  163.3 5.5 %collective-permute-start.14 = (bf16[384,3072]{1,0:T(8,128)(2,1)S(1)}, bf16[384,3072]{1,0:T(8,128)(2,1)S(1)}, u32[]{:S(2)}, u32[]{:S(2)}) collective-permute-start(bf16[384,3072]{1,0:T(8,128)(2,1)S(1)} %pad_maximum_fusion.3), channel_id=1, source_target_pairs={{0,4},{4,0},{8,12},{12,8},{16,20},{20,16},{24,28},{28,24},{1,5},{5... | collective-permute-start | bytes 7077896 | tf_op jit(solution)/shard_map/ppermute | solution.py:28
  164.0 11.0 %collective-permute-start.15 = (bf16[384,3072]{1,0:T(8,128)(2,1)S(1)}, bf16[384,3072]{1,0:T(8,128)(2,1)S(1)}, u32[]{:S(2)}, u32[]{:S(2)}) collective-permute-start(bf16[384,3072]{1,0:T(8,128)(2,1)S(1)} %pad_maximum_fusion.4), channel_id=1, source_target_pairs={{0,4},{4,0},{8,12},{12,8},{16,20},{20,16},{24,28},{28,24},{1,5},{5... | collective-permute-start | bytes 7077896 | tf_op jit(solution)/shard_map/ppermute | solution.py:28
  175.0 63.6 %copy-start = (bf16[1536,3072]{1,0:T(8,128)(2,1)}, bf16[1536,3072]{1,0:T(8,128)(2,1)S(1)}, u32[]{:S(2)}) copy-start(bf16[1536,3072]{1,0:T(8,128)(2,1)S(1)} %pad_maximum_fusion) | copy-start | bytes 28311556
  190.2 18.8 %collective-permute-start.17 = (bf16[768,512]{1,0:T(8,128)(2,1)S(1)}, bf16[768,512]{1,0:T(8,128)(2,1)}, u32[]{:S(2)}, u32[]{:S(2)}) collective-permute-start(bf16[768,512]{1,0:T(8,128)(2,1)S(1)} %collective-permute-done.12), channel_id=1, source_target_pairs={{0,8},{4,12},{8,0},{12,4},{16,24},{20,28},{24,16},{28,20},{1,9},{5... | collective-permute-start | bytes 2359304 | tf_op jit(solution)/shard_map/ppermute | solution.py:28
  215.9 47.2 %collective-permute-start.18 = (bf16[768,3072]{1,0:T(8,128)(2,1)}, bf16[768,3072]{1,0:T(8,128)(2,1)}, u32[]{:S(2)}, u32[]{:S(2)}) collective-permute-start(bf16[768,3072]{1,0:T(8,128)(2,1)} %convolution_convert_fusion), channel_id=1, source_target_pairs={{0,4},{4,0},{8,12},{12,8},{16,20},{20,16},{24,28},{28,24},{1,5},{5... | collective-permute-start | bytes 14155784 | tf_op jit(solution)/shard_map/ppermute | solution.py:28
  226.1 21.6 %collective-permute-start.19 = (bf16[768,512]{1,0:T(8,128)(2,1)}, bf16[768,512]{1,0:T(8,128)(2,1)S(1)}, u32[]{:S(2)}, u32[]{:S(2)}) collective-permute-start(bf16[768,512]{1,0:T(8,128)(2,1)} %get-tuple-element.276), channel_id=1, source_target_pairs={{0,8},{4,12},{8,0},{12,4},{16,24},{20,28},{24,16},{28,20},{1,9},{5... | collective-permute-start | bytes 2359304 | tf_op jit(solution)/shard_map/ppermute | solution.py:28
  227.6 35.5 %collective-permute-start.20 = (bf16[768,512]{1,0:T(8,128)(2,1)S(1)}, bf16[768,512]{1,0:T(8,128)(2,1)S(1)}, u32[]{:S(2)}, u32[]{:S(2)}) collective-permute-start(bf16[768,512]{1,0:T(8,128)(2,1)S(1)} %get-tuple-element.274), channel_id=1, source_target_pairs={{0,8},{4,12},{8,0},{12,4},{16,24},{20,28},{24,16},{28,20},{1,9},{5... | collective-permute-start | bytes 2359304 | tf_op jit(solution)/shard_map/ppermute | solution.py:28
  264.3 6.7 %collective-permute-start.22 = (bf16[384,3072]{1,0:T(8,128)(2,1)}, bf16[384,3072]{1,0:T(8,128)(2,1)}, u32[]{:S(2)}, u32[]{:S(2)}) collective-permute-start(bf16[384,3072]{1,0:T(8,128)(2,1)} %get-tuple-element.175), channel_id=1, source_target_pairs={{0,4},{4,0},{8,12},{12,8},{16,20},{20,16},{24,28},{28,24},{1,5},{5... | collective-permute-start | bytes 7077896 | tf_op jit(solution)/shard_map/ppermute | solution.py:28
  264.3 29.1 %collective-permute-start.23 = (bf16[384,3072]{1,0:T(8,128)(2,1)}, bf16[384,3072]{1,0:T(8,128)(2,1)}, u32[]{:S(2)}, u32[]{:S(2)}) collective-permute-start(bf16[384,3072]{1,0:T(8,128)(2,1)} %get-tuple-element.181), channel_id=1, source_target_pairs={{0,4},{4,0},{8,12},{12,8},{16,20},{20,16},{24,28},{28,24},{1,5},{5... | collective-permute-start | bytes 7077896 | tf_op jit(solution)/shard_map/ppermute | solution.py:28
  268.4 35.1 %collective-permute-start.24 = (bf16[768,512]{1,0:T(8,128)(2,1)}, bf16[768,512]{1,0:T(8,128)(2,1)}, u32[]{:S(2)}, u32[]{:S(2)}) collective-permute-start(bf16[768,512]{1,0:T(8,128)(2,1)} %get-tuple-element.268), channel_id=1, source_target_pairs={{0,8},{4,12},{8,0},{12,4},{16,24},{20,28},{24,16},{28,20},{1,9},{5... | collective-permute-start | bytes 2359304 | tf_op jit(solution)/shard_map/ppermute | solution.py:28
  269.8 37.3 %collective-permute-start.21 = (bf16[768,512]{1,0:T(8,128)(2,1)}, bf16[768,512]{1,0:T(8,128)(2,1)}, u32[]{:S(2)}, u32[]{:S(2)}) collective-permute-start(bf16[768,512]{1,0:T(8,128)(2,1)} %add_convert_fusion.8), channel_id=1, source_target_pairs={{0,16},{4,20},{8,24},{12,28},{16,0},{20,4},{24,8},{28,12},{1,17},{... | collective-permute-start | bytes 2359304 | tf_op jit(solution)/shard_map/ppermute | solution.py:28
  308.5 26.8 %collective-permute-start.26 = (bf16[384,1536]{1,0:T(8,128)(2,1)S(1)}, bf16[384,1536]{1,0:T(8,128)(2,1)S(1)}, u32[]{:S(2)}, u32[]{:S(2)}) collective-permute-start(bf16[384,1536]{1,0:T(8,128)(2,1)S(1)} %copy-done.26), channel_id=1, source_target_pairs={{0,1},{1,0},{2,3},{3,2},{4,5},{5,4},{6,7},{7,6},{8,9},{9,8},{10,11... | collective-permute-start | bytes 3538952 | tf_op jit(solution)/shard_map/ppermute | solution.py:28
  310.0 26.5 %collective-permute-start.27 = (bf16[384,1536]{1,0:T(8,128)(2,1)S(1)}, bf16[384,1536]{1,0:T(8,128)(2,1)S(1)}, u32[]{:S(2)}, u32[]{:S(2)}) collective-permute-start(bf16[384,1536]{1,0:T(8,128)(2,1)S(1)} %copy-done.25), channel_id=1, source_target_pairs={{0,2},{1,3},{2,0},{3,1},{4,6},{5,7},{6,4},{7,5},{8,10},{9,11},{10,... | collective-permute-start | bytes 3538952 | tf_op jit(solution)/shard_map/ppermute | solution.py:28
  311.6 34.3 %collective-permute-start.25 = (bf16[768,512]{1,0:T(8,128)(2,1)S(1)}, bf16[768,512]{1,0:T(8,128)(2,1)S(1)}, u32[]{:S(2)}, u32[]{:S(2)}) collective-permute-start(bf16[768,512]{1,0:T(8,128)(2,1)S(1)} %add_convert_fusion.7), channel_id=1, source_target_pairs={{0,16},{4,20},{8,24},{12,28},{16,0},{20,4},{24,8},{28,12},{1,17},{... | collective-permute-start | bytes 2359304 | tf_op jit(solution)/shard_map/ppermute | solution.py:28
  311.8 34.8 %collective-permute-start.28 = (bf16[768,512]{1,0:T(8,128)(2,1)}, bf16[768,512]{1,0:T(8,128)(2,1)S(1)}, u32[]{:S(2)}, u32[]{:S(2)}) collective-permute-start(bf16[768,512]{1,0:T(8,128)(2,1)} %get-tuple-element.199), channel_id=1, source_target_pairs={{0,8},{4,12},{8,0},{12,4},{16,24},{20,28},{24,16},{28,20},{1,9},{5... | collective-permute-start | bytes 2359304 | tf_op jit(solution)/shard_map/ppermute | solution.py:28
  346.8 39.8 %collective-permute-start.31 = (bf16[384,2304]{1,0:T(8,128)(2,1)S(1)}, bf16[384,2304]{1,0:T(8,128)(2,1)S(1)}, u32[]{:S(2)}, u32[]{:S(2)}) collective-permute-start(bf16[384,2304]{1,0:T(8,128)(2,1)S(1)} %pad_maximum_fusion.5), channel_id=1, source_target_pairs={{0,1},{1,0},{2,3},{3,2},{4,5},{5,4},{6,7},{7,6},{8,9},{9,8},{10,11... | collective-permute-start | bytes 5308424 | tf_op jit(solution)/shard_map/ppermute | solution.py:28
  347.5 40.7 %collective-permute-start.30 = (bf16[384,2304]{1,0:T(8,128)(2,1)S(1)}, bf16[384,2304]{1,0:T(8,128)(2,1)S(1)}, u32[]{:S(2)}, u32[]{:S(2)}) collective-permute-start(bf16[384,2304]{1,0:T(8,128)(2,1)S(1)} %pad_maximum_fusion.6), channel_id=1, source_target_pairs={{0,2},{1,3},{2,0},{3,1},{4,6},{5,7},{6,4},{7,5},{8,10},{9,11},{10,... | collective-permute-start | bytes 5308424 | tf_op jit(solution)/shard_map/ppermute | solution.py:28
  347.9 41.5 %collective-permute-start.29 = (bf16[768,512]{1,0:T(8,128)(2,1)S(1)}, bf16[768,512]{1,0:T(8,128)(2,1)}, u32[]{:S(2)}, u32[]{:S(2)}) collective-permute-start(bf16[768,512]{1,0:T(8,128)(2,1)S(1)} %add_convert_fusion.6), channel_id=1, source_target_pairs={{0,16},{4,20},{8,24},{12,28},{16,0},{20,4},{24,8},{28,12},{1,17},{... | collective-permute-start | bytes 2359304 | tf_op jit(solution)/shard_map/ppermute | solution.py:28
  347.9 41.5 %collective-permute-start.32 = (bf16[768,512]{1,0:T(8,128)(2,1)S(1)}, bf16[768,512]{1,0:T(8,128)(2,1)}, u32[]{:S(2)}, u32[]{:S(2)}) collective-permute-start(bf16[768,512]{1,0:T(8,128)(2,1)S(1)} %copy-done.30), channel_id=1, source_target_pairs={{0,8},{4,12},{8,0},{12,4},{16,24},{20,28},{24,16},{28,20},{1,9},{5... | collective-permute-start | bytes 2359304 | tf_op jit(solution)/shard_map/ppermute | solution.py:28
  389.5 16.5 %copy-start.14 = (bf16[768,512]{1,0:T(8,128)(2,1)S(1)}, bf16[768,512]{1,0:T(8,128)(2,1)}, u32[]{:S(2)}) copy-start(bf16[768,512]{1,0:T(8,128)(2,1)} %get-tuple-element.237) | copy-start | bytes 2359300
  389.5 13.9 %collective-permute-start.35 = (bf16[384,768]{1,0:T(8,128)(2,1)}, bf16[384,768]{1,0:T(8,128)(2,1)}, u32[]{:S(2)}, u32[]{:S(2)}) collective-permute-start(bf16[384,768]{1,0:T(8,128)(2,1)} %get-tuple-element.228), channel_id=1, source_target_pairs={{0,1},{1,0},{2,3},{3,2},{4,5},{5,4},{6,7},{7,6},{8,9},{9,8},{10,11... | collective-permute-start | bytes 1769480 | tf_op jit(solution)/shard_map/ppermute | solution.py:28
  390.1 14.5 %collective-permute-start.34 = (bf16[384,768]{1,0:T(8,128)(2,1)}, bf16[384,768]{1,0:T(8,128)(2,1)}, u32[]{:S(2)}, u32[]{:S(2)}) collective-permute-start(bf16[384,768]{1,0:T(8,128)(2,1)} %get-tuple-element.226), channel_id=1, source_target_pairs={{0,2},{1,3},{2,0},{3,1},{4,6},{5,7},{6,4},{7,5},{8,10},{9,11},{10,... | collective-permute-start | bytes 1769480 | tf_op jit(solution)/shard_map/ppermute | solution.py:28
  390.6 40.1 %collective-permute-start.40 = (bf16[768,512]{1,0:T(8,128)(2,1)}, bf16[768,512]{1,0:T(8,128)(2,1)S(1)}, u32[]{:S(2)}, u32[]{:S(2)}) collective-permute-start(bf16[768,512]{1,0:T(8,128)(2,1)} %get-tuple-element.244), channel_id=1, source_target_pairs={{0,8},{4,12},{8,0},{12,4},{16,24},{20,28},{24,16},{28,20},{1,9},{5... | collective-permute-start | bytes 2359304 | tf_op jit(solution)/shard_map/ppermute | solution.py:28
  390.6 28.0 %collective-permute-start.33 = (bf16[384,768]{1,0:T(8,128)(2,1)}, bf16[384,768]{1,0:T(8,128)(2,1)S(1)}, u32[]{:S(2)}, u32[]{:S(2)}) collective-permute-start(bf16[384,768]{1,0:T(8,128)(2,1)} %get-tuple-element.224), channel_id=1, source_target_pairs={{0,16},{4,20},{8,24},{12,28},{16,0},{20,4},{24,8},{28,12},{1,17},{... | collective-permute-start | bytes 1769480 | tf_op jit(solution)/shard_map/ppermute | solution.py:28
  409.2 40.2 %collective-permute-start.39 = (bf16[768,1024]{1,0:T(8,128)(2,1)S(1)}, bf16[768,1024]{1,0:T(8,128)(2,1)S(1)}, u32[]{:S(2)}, u32[]{:S(2)}) collective-permute-start(bf16[768,1024]{1,0:T(8,128)(2,1)S(1)} %pad_maximum_fusion.8), channel_id=1, source_target_pairs={{0,4},{4,0},{8,12},{12,8},{16,20},{20,16},{24,28},{28,24},{1,5},{5... | collective-permute-start | bytes 4718600 | tf_op jit(solution)/shard_map/ppermute | solution.py:28
  409.2 15.6 %copy-start.32 = (s32[768]{0:T(1024)S(1)}, s32[768]{0:T(1024)}, u32[]{:S(2)}) copy-start(s32[768]{0:T(1024)} %copy-done.31) | copy-start | bytes 9220
  409.3 15.6 %copy-start.35 = (pred[768]{0:T(1024)(128)(4,1)S(1)}, pred[768]{0:T(1024)(128)(4,1)}, u32[]{:S(2)}) copy-start(pred[768]{0:T(1024)(128)(4,1)} %copy-done.34) | copy-start | bytes 2308
  409.3 15.6 %copy-start.38 = (f32[384]{0:T(512)S(1)}, f32[384]{0:T(512)}, u32[]{:S(2)}) copy-start(f32[384]{0:T(512)} %copy-done.37) | copy-start | bytes 4612
  420.0 7.0 %collective-permute-start.37 = (f32[384]{0:T(512)S(1)}, f32[384]{0:T(512)S(1)}, u32[]{:S(2)}, u32[]{:S(2)}) collective-permute-start(f32[384]{0:T(512)S(1)} %multiply_reduce_fusion), channel_id=1, source_target_pairs={{0,1},{1,0},{2,3},{3,2},{4,5},{5,4},{6,7},{7,6},{8,9},{9,8},{10,11... | collective-permute-start | bytes 4616 | tf_op jit(solution)/shard_map/ppermute | solution.py:28
  421.5 26.0 %collective-permute-start.36 = (bf16[384,768]{1,0:T(8,128)(2,1)S(1)}, bf16[384,768]{1,0:T(8,128)(2,1)S(1)}, u32[]{:S(2)}, u32[]{:S(2)}) collective-permute-start(bf16[384,768]{1,0:T(8,128)(2,1)S(1)} %add_convert_fusion.10), channel_id=1, source_target_pairs={{0,16},{4,20},{8,24},{12,28},{16,0},{20,4},{24,8},{28,12},{1,17},{... | collective-permute-start | bytes 1769480 | tf_op jit(solution)/shard_map/ppermute | solution.py:28
  427.1 3.7 collective-permute-start.38
  432.3 17.0 %collective-permute-start.41 = (bf16[384,1024]{1,0:T(8,128)(2,1)S(1)}, bf16[384,1024]{1,0:T(8,128)(2,1)S(1)}, u32[]{:S(2)}, u32[]{:S(2)}) collective-permute-start(bf16[384,1024]{1,0:T(8,128)(2,1)S(1)} %get-tuple-element.302), channel_id=1, source_target_pairs={{0,4},{4,0},{8,12},{12,8},{16,20},{20,16},{24,28},{28,24},{1,5},{5... | collective-permute-start | bytes 2359304 | tf_op jit(solution)/shard_map/ppermute | solution.py:28
  (42 other events, 225.5 us)

commit v10 on v9

--- a/solution.py
+++ b/solution.py
@@ -235,20 +235,19 @@
         return mm_last(gate_grad[rows], gate) + mm_last(up_grad[rows], up)
 
     input_sib = input_part(slice(table, None)).astype(BF16)
-    input_a, input_b = input_sib[:row_limit], input_sib[row_limit:]
-    down, gate_grad, up_grad, g_gate, expert_got, input_a, input_b, *rest = fence(
-        down, gate_grad, up_grad, g_gate, expert_got, input_a, input_b, *g_down_4, *g_down_own
+    down, gate_grad, up_grad, g_gate, expert_got, input_sib, *rest = fence(
+        down, gate_grad, up_grad, g_gate, expert_got, input_sib, *g_down_4, *g_down_own
     )
     g_down_own = rest[2:]
-    g_down_4, input_a, input_b, g_gate = fence(done(*rest[:2]), input_a, input_b, g_gate)
+    g_down_4, input_sib, g_gate = fence(done(*rest[:2]), input_sib, g_gate)
     g_gate_4, g_gate_own = first_send(blocks_far(g_gate)), first_send(blocks_own(g_gate))
 
     g_down_far = z_far(g_down_4)
     g_gate_4 = shrink(*g_gate_4)
     input_got, in_all, gate_grad, up_grad, hidden = fence(
-        across(input_a), in_all, gate_grad, up_grad, hidden
-    )
-    input_got = cat(input_got, across(input_b))
+        across(input_sib[:row_limit]), in_all, gate_grad, up_grad, hidden
+    )
+    input_got = cat(input_got, across(input_sib[row_limit:]))
     g_up = mm_first(in_all, up_grad).astype(BF16)
     expert_sum = (mm_last(hidden[:table], down) + expert_got.astype(F32)).astype(BF16)
     input_sum = (input_part(slice(None, table)) + input_got.astype(F32)).astype(BF16)

time: 459 us -> 453 us (0.987)
  transfers between devices with their start and end apart: 42 -> 42, of which waited for: 21 -> 20; matrix products, arithmetic and copies ran while one was open for 33% -> 33% of each run, Pallas kernels for 0% -> 0%
where the time goes in v10:
time: 453 us; the launch traced here: 446 us
  waiting for transfers between devices  234 us (52%)
  matrix products  86.4 us (19%)
  other arithmetic  45.5 us (10%)
  starting transfers between devices  41.8 us (9%)
  local copies, waits for them, and re-layouts  36.1 us (8%)
    ppermute x42, waiting for transfers between devices, swap(): return lax.ppermute(value, axis, [(i, i ^ distance) for i in range(size)])  234 us
    dot_general x16, matrix products, dot(): lax.dot_general(left, right, (dims, ((), ())), preferred_element_type=F32)  86.4 us
    ppermute x42, starting transfers between devices, swap(): return lax.ppermute(value, axis, [(i, i ^ distance) for i in range(size)])  41.8 us
    concatenate x5, other arithmetic, cat(): return jnp.concatenate(values, axis=0)  15 us
  transfers between devices with their start and end apart: 42, of which 20 were waited for; matrix products, arithmetic and copies ran while one was open for 33% of the time, Pallas kernels for 0%

profile of v10, /device:TPU:0, one launch (start us, length us, event | category | flops | bytes accessed | tf_op | source)
XLA Modules:
  0.0 445.7 jit_solution(6010090945288095417)
XLA Ops:
  0.7 2.4 constant_dynamic-slice_fusion.18
  3.1 4.0 collective-permute-start
  9.7 5.9 %convolution_convert_fusion.5 = bf16[384,3072]{1,0:T(8,128)(2,1)} fusion(bf16[768,3072]{1,0:T(8,128)(2,1)} %param.7, s32[768]{0:T(1024)S(1)} %add_bitcast_fusion, pred[768]{0:T(1024)(128)(4,1)S(1)} %fusion.31), kind=kOutput, calls=%fused_computation.11 | convolution fusion | flops 1813708800 | bytes 7081728 | tf_op jit(solution)/shard_map/dot_general | solution.py:11
  15.6 4.2 multiply_convert_fusion
  25.6 16.3 %collective-permute-done = bf16[384,1024]{1,0:T(8,128)(2,1)} collective-permute-done((bf16[384,1024]{1,0:T(8,128)(2,1)}, bf16[384,1024]{1,0:T(8,128)(2,1)}, u32[]{:S(2)}, u32[]{:S(2)}) %collective-permute-start) | collective-permute-done | bytes 786464 | tf_op jit(solution)/shard_map/ppermute | solution.py:28
  44.0 2.4 collective-permute-start.6
  52.8 34.3 %collective-permute-done.6 = bf16[384,1024]{1,0:T(8,128)(2,1)S(1)} collective-permute-done((bf16[384,1024]{1,0:T(8,128)(2,1)}, bf16[384,1024]{1,0:T(8,128)(2,1)S(1)}, u32[]{:S(2)}, u32[]{:S(2)}) %collective-permute-start.6) | collective-permute-done | bytes 786464 | tf_op jit(solution)/shard_map/ppermute | solution.py:28
  87.1 10.1 %collective-permute-done.2 = bf16[768,768]{1,0:T(8,128)(2,1)S(1)} collective-permute-done((bf16[768,768]{1,0:T(8,128)(2,1)}, bf16[768,768]{1,0:T(8,128)(2,1)S(1)}, u32[]{:S(2)}, u32[]{:S(2)}) %collective-permute-start.2) | collective-permute-done | bytes 1179680 | tf_op jit(solution)/shard_map/ppermute | solution.py:28
  97.3 2.6 collective-permute-start.10
  100.8 3.0 collective-permute-start.7
  103.8 2.0 pad_maximum_fusion.2
  105.8 2.0 constant_dynamic-slice_fusion.12
  107.9 40.2 %collective-permute-done.7 = bf16[768,512]{1,0:T(8,128)(2,1)} collective-permute-done((bf16[768,512]{1,0:T(8,128)(2,1)}, bf16[768,512]{1,0:T(8,128)(2,1)}, u32[]{:S(2)}, u32[]{:S(2)}) %collective-permute-start.7) | collective-permute-done | bytes 786464 | tf_op jit(solution)/shard_map/ppermute | solution.py:28
  148.0 3.3 collective-permute-done.8
  151.5 3.1 collective-permute-start.12
  156.9 2.3 broadcast_select_fusion.10
  159.2 2.2 broadcast_select_fusion.11
  167.2 6.1 %pad_maximum_fusion = bf16[1536,3072]{1,0:T(8,128)(2,1)S(1)} fusion(bf16[384,3072]{1,0:T(8,128)(2,1)S(1)} %collective-permute-done.14, bf16[384,3072]{1,0:T(8,128)(2,1)} %collective-permute-done.3, bf16[384,768]{1,0:T(8,128)(2,1)S(1)} %get-tuple-element.253, bf16[384,768]{1,0:T(8,128)(2,1)S(1)} %get-tuple-element.252, ...), kind=kLoop, calls=%fused_computation | loop fusion | flops 66060288 | bytes 18874368 | tf_op jit(solution)/shard_map/concatenate | solution.py:48
  173.4 7.5 %pad_maximum_fusion.1 = bf16[1536,3072]{1,0:T(8,128)(2,1)S(1)} fusion(bf16[384,3072]{1,0:T(8,128)(2,1)S(1)} %collective-permute-done.15, bf16[384,3072]{1,0:T(8,128)(2,1)} %collective-permute-done.4, bf16[384,768]{1,0:T(8,128)(2,1)S(1)} %get-tuple-element.256, bf16[384,768]{1,0:T(8,128)(2,1)S(1)} %get-tuple-element.255, ...), kind=kLoop, calls=%fused_computation.1 | loop fusion | flops 66060288 | bytes 18874368 | tf_op jit(solution)/shard_map/concatenate | solution.py:48
  180.9 6.8 %fusion.36 = f32[1536,512]{1,0:T(8,128)} fusion(bf16[1536,3072]{1,0:T(8,128)(2,1)S(1)} %pad_maximum_fusion, bf16[3072,512]{1,0:T(8,128)(2,1)S(1)} %bitcast.90), kind=kOutput, calls=%fused_computation.187 | convolution fusion | flops 4831838208 | bytes 15728640 | tf_op jit(solution)/shard_map/dot_general | solution.py:11
  187.7 2.0 collective-permute-done.12
  193.9 9.2 %multiply_convert_fusion.3 = (bf16[1536,512]{1,0:T(8,128)(2,1)S(1)}, f32[1536,512]{1,0:T(8,128)}) fusion(f32[1536,512]{1,0:T(8,128)} %fusion.36, bf16[1536,3072]{1,0:T(8,128)(2,1)S(1)} %pad_maximum_fusion, bf16[3072,512]{1,0:T(8,128)(2,1)S(1)} %bitcast.102), kind=kOutput, calls=%fused_computation.15 | convolution fusion | flops 4836556800 | bytes 20447232 | tf_op jit(solution)/shard_map/dot_general | solution.py:11
  203.1 5.9 %convolution_convert_fusion.3 = bf16[3072,512]{1,0:T(8,128)(2,1)S(1)} fusion(bf16[1536,3072]{1,0:T(8,128)(2,1)S(1)} %pad_maximum_fusion.1, bf16[1536,512]{1,0:T(8,128)(2,1)S(1)} %get-tuple-element.178), kind=kOutput, calls=%fused_computation.9 | convolution fusion | flops 4833411072 | bytes 14155776 | tf_op jit(solution)/shard_map/dot_general | solution.py:11
  210.3 4.5 %convolution_convert_fusion = bf16[768,3072]{1,0:T(8,128)(2,1)} fusion(bf16[3072,512]{1,0:T(8,128)(2,1)S(1)} %bitcast.99, bf16[1536,512]{1,0:T(8,128)(2,1)S(1)} %get-tuple-element.178), kind=kOutput, calls=%fused_computation.5 | convolution fusion | flops 2418278400 | bytes 8650752 | tf_op jit(solution)/shard_map/dot_general | solution.py:11
  218.3 9.4 %multiply_convert_fusion.1 = (bf16[1536,512]{1,0:T(8,128)(2,1)}, bf16[1536,512]{1,0:T(8,128)(2,1)}) fusion(f32[1536,512]{1,0:T(8,128)} %fusion.36, f32[1536,512]{1,0:T(8,128)} %get-tuple-element.162, bf16[1536,3072]{1,0:T(8,128)(2,1)S(1)} %pad_maximum_fusion.1, bf16[3072,512]{1,0:T(8,128)(2,1)S(1)} %bitcast.100), kind=kOutput, calls=%fused_computation.13 | convolution fusion | flops 4842061824 | bytes 22020096 | tf_op jit(solution)/shard_map/dot_general | solution.py:11
  227.7 3.9 fusion.11
  231.7 6.7 %convolution_convert_fusion.2 = bf16[3072,512]{1,0:T(8,128)(2,1)} fusion(bf16[1536,3072]{1,0:T(8,128)(2,1)S(1)} %pad_maximum_fusion, bf16[1536,512]{1,0:T(8,128)(2,1)S(1)} %copy-done.13), kind=kOutput, calls=%fused_computation.8 | convolution fusion | flops 4833411072 | bytes 14155776 | tf_op jit(solution)/shard_map/dot_general | solution.py:11
  238.3 3.1 add_convert_fusion.2
  241.4 11.9 %collective-permute-done.20 = bf16[768,512]{1,0:T(8,128)(2,1)S(1)} collective-permute-done((bf16[768,512]{1,0:T(8,128)(2,1)}, bf16[768,512]{1,0:T(8,128)(2,1)S(1)}, u32[]{:S(2)}, u32[]{:S(2)}) %collective-permute-start.20) | collective-permute-done | bytes 786464 | tf_op jit(solution)/shard_map/ppermute | solution.py:28
  253.3 2.5 add_convert_fusion.8
  255.8 2.5 fusion.34
  258.8 3.4 dynamic-slice_bitcast_fusion
  264.9 5.5 %add_convert_fusion = bf16[768,3072]{1,0:T(8,128)(2,1)S(1)} fusion(bf16[768,3072]{1,0:T(8,128)(2,1)} %collective-permute-done.18, bf16[3072,512]{1,0:T(8,128)(2,1)} %bitcast.101, bf16[1536,512]{1,0:T(8,128)(2,1)S(1)} %copy-done.41), kind=kOutput, calls=%fused_computation.2 | convolution fusion | flops 2422996992 | bytes 13369344 | tf_op jit(solution)/shard_map/dot_general | solution.py:11
  272.1 5.4 %convolution_convert_fusion.1 = bf16[3072,512]{1,0:T(8,128)(2,1)S(1)} fusion(bf16[1536,3072]{1,0:T(8,128)(2,1)S(1)} %bitcast.94, bf16[1536,512]{1,0:T(8,128)(2,1)S(1)} %copy-done.39), kind=kOutput, calls=%fused_computation.7 | convolution fusion | flops 4833411072 | bytes 14155776 | tf_op jit(solution)/shard_map/dot_general | solution.py:11
  281.7 5.1 %fusion.15 = f32[768,3072]{1,0:T(8,128)} fusion(bf16[3072,512]{1,0:T(8,128)(2,1)S(1)} %bitcast.104, bf16[1536,512]{1,0:T(8,128)(2,1)S(1)} %copy-done.39), kind=kOutput, calls=%fused_computation.97 | convolution fusion | flops 2415919104 | bytes 13369344 | tf_op jit(solution)/shard_map/dot_general | solution.py:11
  286.9 6.9 %add_convert_fusion.1 = bf16[768,3072]{1,0:T(8,128)(2,1)S(1)} fusion(f32[768,3072]{1,0:T(8,128)} %fusion.15, bf16[384,3072]{1,0:T(8,128)(2,1)} %collective-permute-done.23, bf16[384,3072]{1,0:T(8,128)(2,1)} %collective-permute-done.22, bf16[3072,512]{1,0:T(8,128)(2,1)S(1)} %bitcast.92, bf16[1536,512]{1,0:T(8,128)(2,1)} %get-tuple-element.175), kind=kOutput, calls=%fused_computation.3 | convolution fusion | flops 2432434176 | bytes 22806528 | tf_op jit(solution)/shard_map/dot_general | solution.py:11
  293.9 3.6 collective-permute-done.24
  297.5 3.5 collective-permute-done.21
  306.8 22.3 %collective-permute-done.26 = bf16[384,1536]{1,0:T(8,128)(2,1)S(1)} collective-permute-done((bf16[384,1536]{1,0:T(8,128)(2,1)S(1)}, bf16[384,1536]{1,0:T(8,128)(2,1)S(1)}, u32[]{:S(2)}, u32[]{:S(2)}) %collective-permute-start.26) | collective-permute-done | bytes 1179680 | tf_op jit(solution)/shard_map/ppermute | solution.py:28
  331.0 8.8 %collective-permute-done.25 = bf16[768,512]{1,0:T(8,128)(2,1)S(1)} collective-permute-done((bf16[768,512]{1,0:T(8,128)(2,1)S(1)}, bf16[768,512]{1,0:T(8,128)(2,1)S(1)}, u32[]{:S(2)}, u32[]{:S(2)}) %collective-permute-start.25) | collective-permute-done | bytes 786464 | tf_op jit(solution)/shard_map/ppermute | solution.py:28
  343.2 37.3 %collective-permute-done.31 = bf16[384,2304]{1,0:T(8,128)(2,1)S(1)} collective-permute-done((bf16[384,2304]{1,0:T(8,128)(2,1)S(1)}, bf16[384,2304]{1,0:T(8,128)(2,1)S(1)}, u32[]{:S(2)}, u32[]{:S(2)}) %collective-permute-start.31) | collective-permute-done | bytes 1769504 | tf_op jit(solution)/shard_map/ppermute | solution.py:28
  385.2 12.1 %collective-permute-done.35 = bf16[384,768]{1,0:T(8,128)(2,1)} collective-permute-done((bf16[384,768]{1,0:T(8,128)(2,1)}, bf16[384,768]{1,0:T(8,128)(2,1)}, u32[]{:S(2)}, u32[]{:S(2)}) %collective-permute-start.35) | collective-permute-done | bytes 589856 | tf_op jit(solution)/shard_map/ppermute | solution.py:28
  403.4 9.1 %collective-permute-done.33 = bf16[384,768]{1,0:T(8,128)(2,1)S(1)} collective-permute-done((bf16[384,768]{1,0:T(8,128)(2,1)}, bf16[384,768]{1,0:T(8,128)(2,1)S(1)}, u32[]{:S(2)}, u32[]{:S(2)}) %collective-permute-start.33) | collective-permute-done | bytes 589856 | tf_op jit(solution)/shard_map/ppermute | solution.py:28
  415.5 3.4 collective-permute-start.36
  418.9 2.0 convolution_convert_fusion.7
  422.6 2.2 collective-permute-done.38
  427.6 13.8 %collective-permute-done.36 = bf16[384,768]{1,0:T(8,128)(2,1)S(1)} collective-permute-done((bf16[384,768]{1,0:T(8,128)(2,1)S(1)}, bf16[384,768]{1,0:T(8,128)(2,1)S(1)}, u32[]{:S(2)}, u32[]{:S(2)}) %collective-permute-start.36) | collective-permute-done | bytes 589856 | tf_op jit(solution)/shard_map/ppermute | solution.py:28
  441.4 1.9 convolution_convert_fusion.6
  (239 shorter events, 75.2 us)
Async XLA Ops:
  3.1 38.8 %collective-permute-start = (bf16[384,1024]{1,0:T(8,128)(2,1)}, bf16[384,1024]{1,0:T(8,128)(2,1)}, u32[]{:S(2)}, u32[]{:S(2)}) collective-permute-start(bf16[384,1024]{1,0:T(8,128)(2,1)} %get-tuple-element.315), channel_id=1, source_target_pairs={{0,16},{4,20},{8,24},{12,28},{16,0},{20,4},{24,8},{28,12},{1,17},{... | collective-permute-start | bytes 2359304 | tf_op jit(solution)/shard_map/ppermute | solution.py:28
  7.1 34.8 %collective-permute-start.1 = (bf16[384,1024]{1,0:T(8,128)(2,1)S(1)}, bf16[384,1024]{1,0:T(8,128)(2,1)}, u32[]{:S(2)}, u32[]{:S(2)}) collective-permute-start(bf16[384,1024]{1,0:T(8,128)(2,1)S(1)} %get-tuple-element.130), channel_id=1, source_target_pairs={{0,8},{4,12},{8,0},{12,4},{16,24},{20,28},{24,16},{28,20},{1,9},{5... | collective-permute-start | bytes 2359304 | tf_op jit(solution)/shard_map/ppermute | solution.py:28
  41.9 5.8 %collective-permute-start.5 = (bf16[768,1024]{1,0:T(8,128)(2,1)S(1)}, bf16[768,1024]{1,0:T(8,128)(2,1)}, u32[]{:S(2)}, u32[]{:S(2)}) collective-permute-start(bf16[768,1024]{1,0:T(8,128)(2,1)S(1)} %maximum_maximum_fusion), channel_id=1, source_target_pairs={{0,4},{4,0},{8,12},{12,8},{16,20},{20,16},{24,28},{28,24},{1,5},{5... | collective-permute-start | bytes 4718600 | tf_op jit(solution)/shard_map/ppermute | solution.py:28
  41.9 55.3 %collective-permute-start.3 = (bf16[384,3072]{1,0:T(8,128)(2,1)}, bf16[384,3072]{1,0:T(8,128)(2,1)}, u32[]{:S(2)}, u32[]{:S(2)}) collective-permute-start(bf16[384,3072]{1,0:T(8,128)(2,1)} %convolution_convert_fusion.5), channel_id=1, source_target_pairs={{0,4},{4,0},{8,12},{12,8},{16,20},{20,16},{24,28},{28,24},{1,5},{5... | collective-permute-start | bytes 7077896 | tf_op jit(solution)/shard_map/ppermute | solution.py:28
  42.4 54.8 %collective-permute-start.4 = (bf16[384,3072]{1,0:T(8,128)(2,1)}, bf16[384,3072]{1,0:T(8,128)(2,1)}, u32[]{:S(2)}, u32[]{:S(2)}) collective-permute-start(bf16[384,3072]{1,0:T(8,128)(2,1)} %get-tuple-element.126), channel_id=1, source_target_pairs={{0,4},{4,0},{8,12},{12,8},{16,20},{20,16},{24,28},{28,24},{1,5},{5... | collective-permute-start | bytes 7077896 | tf_op jit(solution)/shard_map/ppermute | solution.py:28
  42.4 54.8 %collective-permute-start.2 = (bf16[768,768]{1,0:T(8,128)(2,1)}, bf16[768,768]{1,0:T(8,128)(2,1)S(1)}, u32[]{:S(2)}, u32[]{:S(2)}) collective-permute-start(bf16[768,768]{1,0:T(8,128)(2,1)} %pad_maximum_fusion.9), channel_id=1, source_target_pairs={{0,16},{4,20},{8,24},{12,28},{16,0},{20,4},{24,8},{28,12},{1,17},{... | collective-permute-start | bytes 3538952 | tf_op jit(solution)/shard_map/ppermute | solution.py:28
  44.0 43.1 %collective-permute-start.6 = (bf16[384,1024]{1,0:T(8,128)(2,1)}, bf16[384,1024]{1,0:T(8,128)(2,1)S(1)}, u32[]{:S(2)}, u32[]{:S(2)}) collective-permute-start(bf16[384,1024]{1,0:T(8,128)(2,1)} %collective-permute-done), channel_id=1, source_target_pairs={{0,8},{4,12},{8,0},{12,4},{16,24},{20,28},{24,16},{28,20},{1,9},{5... | collective-permute-start | bytes 2359304 | tf_op jit(solution)/shard_map/ppermute | solution.py:28
  52.8 53.0 %copy-start.1 = (bf16[768,1024]{1,0:T(8,128)(2,1)}, bf16[768,1024]{1,0:T(8,128)(2,1)S(1)}, u32[]{:S(2)}) copy-start(bf16[768,1024]{1,0:T(8,128)(2,1)S(1)} %pad_maximum_fusion.7) | copy-start | bytes 4718596
  97.2 54.2 %collective-permute-start.11 = (bf16[768,1024]{1,0:T(8,128)(2,1)S(1)}, bf16[768,1024]{1,0:T(8,128)(2,1)}, u32[]{:S(2)}, u32[]{:S(2)}) collective-permute-start(bf16[768,1024]{1,0:T(8,128)(2,1)S(1)} %pad_maximum_fusion.7), channel_id=1, source_target_pairs={{0,8},{4,12},{8,0},{12,4},{16,24},{20,28},{24,16},{28,20},{1,9},{5... | collective-permute-start | bytes 4718600 | tf_op jit(solution)/shard_map/ppermute | solution.py:28
  97.3 50.8 %collective-permute-start.10 = (bf16[768,768]{1,0:T(8,128)(2,1)S(1)}, bf16[768,768]{1,0:T(8,128)(2,1)}, u32[]{:S(2)}, u32[]{:S(2)}) collective-permute-start(bf16[768,768]{1,0:T(8,128)(2,1)S(1)} %collective-permute-done.2), channel_id=1, source_target_pairs={{0,3},{1,2},{2,1},{3,0},{4,7},{5,6},{6,5},{7,4},{8,11},{9,10},{10,... | collective-permute-start | bytes 3538952 | tf_op jit(solution)/shard_map/ppermute | solution.py:28
  99.8 51.5 %collective-permute-start.8 = (bf16[768,768]{1,0:T(8,128)(2,1)S(1)}, bf16[768,768]{1,0:T(8,128)(2,1)}, u32[]{:S(2)}, u32[]{:S(2)}) collective-permute-start(bf16[768,768]{1,0:T(8,128)(2,1)S(1)} %collective-permute-done.2), channel_id=1, source_target_pairs={{0,1},{1,0},{2,3},{3,2},{4,5},{5,4},{6,7},{7,6},{8,9},{9,8},{10,11... | collective-permute-start | bytes 3538952 | tf_op jit(solution)/shard_map/ppermute | solution.py:28
  100.4 51.0 %collective-permute-start.9 = (bf16[768,768]{1,0:T(8,128)(2,1)S(1)}, bf16[768,768]{1,0:T(8,128)(2,1)}, u32[]{:S(2)}, u32[]{:S(2)}) collective-permute-start(bf16[768,768]{1,0:T(8,128)(2,1)S(1)} %collective-permute-done.2), channel_id=1, source_target_pairs={{0,2},{1,3},{2,0},{3,1},{4,6},{5,7},{6,4},{7,5},{8,10},{9,11},{10,... | collective-permute-start | bytes 3538952 | tf_op jit(solution)/shard_map/ppermute | solution.py:28
  100.8 47.2 %collective-permute-start.7 = (bf16[768,512]{1,0:T(8,128)(2,1)}, bf16[768,512]{1,0:T(8,128)(2,1)}, u32[]{:S(2)}, u32[]{:S(2)}) collective-permute-start(bf16[768,512]{1,0:T(8,128)(2,1)} %maximum_select_fusion.2), channel_id=1, source_target_pairs={{0,16},{4,20},{8,24},{12,28},{16,0},{20,4},{24,8},{28,12},{1,17},{... | collective-permute-start | bytes 2359304 | tf_op jit(solution)/shard_map/ppermute | solution.py:28
  151.4 5.3 %collective-permute-start.13 = (bf16[4,384,512]{2,1,0:T(8,128)(2,1)}, bf16[4,384,512]{2,1,0:T(8,128)(2,1)}, u32[]{:S(2)}, u32[]{:S(2)}) collective-permute-start(bf16[4,384,512]{2,1,0:T(8,128)(2,1)} %get-tuple-element.139), channel_id=1, source_target_pairs={{0,4},{4,0},{8,12},{12,8},{16,20},{20,16},{24,28},{28,24},{1,5},{5... | collective-permute-start | bytes 4718600 | tf_op jit(solution)/shard_map/ppermute | solution.py:28
  151.5 38.3 %collective-permute-start.12 = (bf16[768,512]{1,0:T(8,128)(2,1)}, bf16[768,512]{1,0:T(8,128)(2,1)S(1)}, u32[]{:S(2)}, u32[]{:S(2)}) collective-permute-start(bf16[768,512]{1,0:T(8,128)(2,1)} %maximum_select_fusion.3), channel_id=1, source_target_pairs={{0,16},{4,20},{8,24},{12,28},{16,0},{20,4},{24,8},{28,12},{1,17},{... | collective-permute-start | bytes 2359304 | tf_op jit(solution)/shard_map/ppermute | solution.py:28
  154.5 35.7 %collective-permute-start.16 = (bf16[768,512]{1,0:T(8,128)(2,1)}, bf16[768,512]{1,0:T(8,128)(2,1)S(1)}, u32[]{:S(2)}, u32[]{:S(2)}) collective-permute-start(bf16[768,512]{1,0:T(8,128)(2,1)} %collective-permute-done.7), channel_id=1, source_target_pairs={{0,8},{4,12},{8,0},{12,4},{16,24},{20,28},{24,16},{28,20},{1,9},{5... | collective-permute-start | bytes 2359304 | tf_op jit(solution)/shard_map/ppermute | solution.py:28
  161.7 5.5 %collective-permute-start.14 = (bf16[384,3072]{1,0:T(8,128)(2,1)S(1)}, bf16[384,3072]{1,0:T(8,128)(2,1)S(1)}, u32[]{:S(2)}, u32[]{:S(2)}) collective-permute-start(bf16[384,3072]{1,0:T(8,128)(2,1)S(1)} %pad_maximum_fusion.3), channel_id=1, source_target_pairs={{0,4},{4,0},{8,12},{12,8},{16,20},{20,16},{24,28},{28,24},{1,5},{5... | collective-permute-start | bytes 7077896 | tf_op jit(solution)/shard_map/ppermute | solution.py:28
  162.4 11.0 %collective-permute-start.15 = (bf16[384,3072]{1,0:T(8,128)(2,1)S(1)}, bf16[384,3072]{1,0:T(8,128)(2,1)S(1)}, u32[]{:S(2)}, u32[]{:S(2)}) collective-permute-start(bf16[384,3072]{1,0:T(8,128)(2,1)S(1)} %pad_maximum_fusion.4), channel_id=1, source_target_pairs={{0,4},{4,0},{8,12},{12,8},{16,20},{20,16},{24,28},{28,24},{1,5},{5... | collective-permute-start | bytes 7077896 | tf_op jit(solution)/shard_map/ppermute | solution.py:28
  173.4 58.3 %copy-start = (bf16[1536,3072]{1,0:T(8,128)(2,1)}, bf16[1536,3072]{1,0:T(8,128)(2,1)S(1)}, u32[]{:S(2)}) copy-start(bf16[1536,3072]{1,0:T(8,128)(2,1)S(1)} %pad_maximum_fusion) | copy-start | bytes 28311556
  190.2 18.7 %collective-permute-start.17 = (bf16[768,512]{1,0:T(8,128)(2,1)S(1)}, bf16[768,512]{1,0:T(8,128)(2,1)S(1)}, u32[]{:S(2)}, u32[]{:S(2)}) collective-permute-start(bf16[768,512]{1,0:T(8,128)(2,1)S(1)} %collective-permute-done.12), channel_id=1, source_target_pairs={{0,8},{4,12},{8,0},{12,4},{16,24},{20,28},{24,16},{28,20},{1,9},{5... | collective-permute-start | bytes 2359304 | tf_op jit(solution)/shard_map/ppermute | solution.py:28
  214.8 38.5 %collective-permute-start.18 = (bf16[768,3072]{1,0:T(8,128)(2,1)}, bf16[768,3072]{1,0:T(8,128)(2,1)}, u32[]{:S(2)}, u32[]{:S(2)}) collective-permute-start(bf16[768,3072]{1,0:T(8,128)(2,1)} %convolution_convert_fusion), channel_id=1, source_target_pairs={{0,4},{4,0},{8,12},{12,8},{16,20},{20,16},{24,28},{28,24},{1,5},{5... | collective-permute-start | bytes 14155784 | tf_op jit(solution)/shard_map/ppermute | solution.py:28
  216.3 25.1 %collective-permute-start.19 = (bf16[768,512]{1,0:T(8,128)(2,1)}, bf16[768,512]{1,0:T(8,128)(2,1)}, u32[]{:S(2)}, u32[]{:S(2)}) collective-permute-start(bf16[768,512]{1,0:T(8,128)(2,1)} %get-tuple-element.272), channel_id=1, source_target_pairs={{0,8},{4,12},{8,0},{12,4},{16,24},{20,28},{24,16},{28,20},{1,9},{5... | collective-permute-start | bytes 2359304 | tf_op jit(solution)/shard_map/ppermute | solution.py:28
  217.7 35.6 %collective-permute-start.20 = (bf16[768,512]{1,0:T(8,128)(2,1)}, bf16[768,512]{1,0:T(8,128)(2,1)S(1)}, u32[]{:S(2)}, u32[]{:S(2)}) collective-permute-start(bf16[768,512]{1,0:T(8,128)(2,1)} %get-tuple-element.270), channel_id=1, source_target_pairs={{0,8},{4,12},{8,0},{12,4},{16,24},{20,28},{24,16},{28,20},{1,9},{5... | collective-permute-start | bytes 2359304 | tf_op jit(solution)/shard_map/ppermute | solution.py:28
  258.2 6.6 %collective-permute-start.22 = (bf16[384,3072]{1,0:T(8,128)(2,1)}, bf16[384,3072]{1,0:T(8,128)(2,1)}, u32[]{:S(2)}, u32[]{:S(2)}) collective-permute-start(bf16[384,3072]{1,0:T(8,128)(2,1)} %get-tuple-element.249), channel_id=1, source_target_pairs={{0,4},{4,0},{8,12},{12,8},{16,20},{20,16},{24,28},{28,24},{1,5},{5... | collective-permute-start | bytes 7077896 | tf_op jit(solution)/shard_map/ppermute | solution.py:28
  258.3 28.6 %collective-permute-start.23 = (bf16[384,3072]{1,0:T(8,128)(2,1)}, bf16[384,3072]{1,0:T(8,128)(2,1)}, u32[]{:S(2)}, u32[]{:S(2)}) collective-permute-start(bf16[384,3072]{1,0:T(8,128)(2,1)} %get-tuple-element.248), channel_id=1, source_target_pairs={{0,4},{4,0},{8,12},{12,8},{16,20},{20,16},{24,28},{28,24},{1,5},{5... | collective-permute-start | bytes 7077896 | tf_op jit(solution)/shard_map/ppermute | solution.py:28
  262.2 35.3 %collective-permute-start.24 = (bf16[768,512]{1,0:T(8,128)(2,1)}, bf16[768,512]{1,0:T(8,128)(2,1)}, u32[]{:S(2)}, u32[]{:S(2)}) collective-permute-start(bf16[768,512]{1,0:T(8,128)(2,1)} %get-tuple-element.264), channel_id=1, source_target_pairs={{0,8},{4,12},{8,0},{12,4},{16,24},{20,28},{24,16},{28,20},{1,9},{5... | collective-permute-start | bytes 2359304 | tf_op jit(solution)/shard_map/ppermute | solution.py:28
  263.7 37.3 %collective-permute-start.21 = (bf16[768,512]{1,0:T(8,128)(2,1)}, bf16[768,512]{1,0:T(8,128)(2,1)}, u32[]{:S(2)}, u32[]{:S(2)}) collective-permute-start(bf16[768,512]{1,0:T(8,128)(2,1)} %add_convert_fusion.8), channel_id=1, source_target_pairs={{0,16},{4,20},{8,24},{12,28},{16,0},{20,4},{24,8},{28,12},{1,17},{... | collective-permute-start | bytes 2359304 | tf_op jit(solution)/shard_map/ppermute | solution.py:28
  302.3 26.8 %collective-permute-start.26 = (bf16[384,1536]{1,0:T(8,128)(2,1)S(1)}, bf16[384,1536]{1,0:T(8,128)(2,1)S(1)}, u32[]{:S(2)}, u32[]{:S(2)}) collective-permute-start(bf16[384,1536]{1,0:T(8,128)(2,1)S(1)} %copy-done.25), channel_id=1, source_target_pairs={{0,1},{1,0},{2,3},{3,2},{4,5},{5,4},{6,7},{7,6},{8,9},{9,8},{10,11... | collective-permute-start | bytes 3538952 | tf_op jit(solution)/shard_map/ppermute | solution.py:28
  303.8 26.5 %collective-permute-start.27 = (bf16[384,1536]{1,0:T(8,128)(2,1)S(1)}, bf16[384,1536]{1,0:T(8,128)(2,1)S(1)}, u32[]{:S(2)}, u32[]{:S(2)}) collective-permute-start(bf16[384,1536]{1,0:T(8,128)(2,1)S(1)} %copy-done.24), channel_id=1, source_target_pairs={{0,2},{1,3},{2,0},{3,1},{4,6},{5,7},{6,4},{7,5},{8,10},{9,11},{10,... | collective-permute-start | bytes 3538952 | tf_op jit(solution)/shard_map/ppermute | solution.py:28
  305.4 34.4 %collective-permute-start.25 = (bf16[768,512]{1,0:T(8,128)(2,1)S(1)}, bf16[768,512]{1,0:T(8,128)(2,1)S(1)}, u32[]{:S(2)}, u32[]{:S(2)}) collective-permute-start(bf16[768,512]{1,0:T(8,128)(2,1)S(1)} %add_convert_fusion.7), channel_id=1, source_target_pairs={{0,16},{4,20},{8,24},{12,28},{16,0},{20,4},{24,8},{28,12},{1,17},{... | collective-permute-start | bytes 2359304 | tf_op jit(solution)/shard_map/ppermute | solution.py:28
  305.6 34.8 %collective-permute-start.28 = (bf16[768,512]{1,0:T(8,128)(2,1)}, bf16[768,512]{1,0:T(8,128)(2,1)S(1)}, u32[]{:S(2)}, u32[]{:S(2)}) collective-permute-start(bf16[768,512]{1,0:T(8,128)(2,1)} %get-tuple-element.195), channel_id=1, source_target_pairs={{0,8},{4,12},{8,0},{12,4},{16,24},{20,28},{24,16},{28,20},{1,9},{5... | collective-permute-start | bytes 2359304 | tf_op jit(solution)/shard_map/ppermute | solution.py:28
  340.6 39.9 %collective-permute-start.31 = (bf16[384,2304]{1,0:T(8,128)(2,1)S(1)}, bf16[384,2304]{1,0:T(8,128)(2,1)S(1)}, u32[]{:S(2)}, u32[]{:S(2)}) collective-permute-start(bf16[384,2304]{1,0:T(8,128)(2,1)S(1)} %pad_maximum_fusion.5), channel_id=1, source_target_pairs={{0,1},{1,0},{2,3},{3,2},{4,5},{5,4},{6,7},{7,6},{8,9},{9,8},{10,11... | collective-permute-start | bytes 5308424 | tf_op jit(solution)/shard_map/ppermute | solution.py:28
  341.2 40.8 %collective-permute-start.30 = (bf16[384,2304]{1,0:T(8,128)(2,1)S(1)}, bf16[384,2304]{1,0:T(8,128)(2,1)S(1)}, u32[]{:S(2)}, u32[]{:S(2)}) collective-permute-start(bf16[384,2304]{1,0:T(8,128)(2,1)S(1)} %pad_maximum_fusion.6), channel_id=1, source_target_pairs={{0,2},{1,3},{2,0},{3,1},{4,6},{5,7},{6,4},{7,5},{8,10},{9,11},{10,... | collective-permute-start | bytes 5308424 | tf_op jit(solution)/shard_map/ppermute | solution.py:28
  341.8 41.5 %collective-permute-start.29 = (bf16[768,512]{1,0:T(8,128)(2,1)S(1)}, bf16[768,512]{1,0:T(8,128)(2,1)}, u32[]{:S(2)}, u32[]{:S(2)}) collective-permute-start(bf16[768,512]{1,0:T(8,128)(2,1)S(1)} %add_convert_fusion.6), channel_id=1, source_target_pairs={{0,16},{4,20},{8,24},{12,28},{16,0},{20,4},{24,8},{28,12},{1,17},{... | collective-permute-start | bytes 2359304 | tf_op jit(solution)/shard_map/ppermute | solution.py:28
  341.8 41.5 %collective-permute-start.32 = (bf16[768,512]{1,0:T(8,128)(2,1)S(1)}, bf16[768,512]{1,0:T(8,128)(2,1)}, u32[]{:S(2)}, u32[]{:S(2)}) collective-permute-start(bf16[768,512]{1,0:T(8,128)(2,1)S(1)} %copy-done.29), channel_id=1, source_target_pairs={{0,8},{4,12},{8,0},{12,4},{16,24},{20,28},{24,16},{28,20},{1,9},{5... | collective-permute-start | bytes 2359304 | tf_op jit(solution)/shard_map/ppermute | solution.py:28
  383.3 16.6 %copy-start.12 = (bf16[768,512]{1,0:T(8,128)(2,1)S(1)}, bf16[768,512]{1,0:T(8,128)(2,1)}, u32[]{:S(2)}) copy-start(bf16[768,512]{1,0:T(8,128)(2,1)} %get-tuple-element.233) | copy-start | bytes 2359300
  383.3 14.0 %collective-permute-start.35 = (bf16[384,768]{1,0:T(8,128)(2,1)}, bf16[384,768]{1,0:T(8,128)(2,1)}, u32[]{:S(2)}, u32[]{:S(2)}) collective-permute-start(bf16[384,768]{1,0:T(8,128)(2,1)} %get-tuple-element.224), channel_id=1, source_target_pairs={{0,1},{1,0},{2,3},{3,2},{4,5},{5,4},{6,7},{7,6},{8,9},{9,8},{10,11... | collective-permute-start | bytes 1769480 | tf_op jit(solution)/shard_map/ppermute | solution.py:28
  383.9 14.6 %collective-permute-start.34 = (bf16[384,768]{1,0:T(8,128)(2,1)}, bf16[384,768]{1,0:T(8,128)(2,1)}, u32[]{:S(2)}, u32[]{:S(2)}) collective-permute-start(bf16[384,768]{1,0:T(8,128)(2,1)} %get-tuple-element.222), channel_id=1, source_target_pairs={{0,2},{1,3},{2,0},{3,1},{4,6},{5,7},{6,4},{7,5},{8,10},{9,11},{10,... | collective-permute-start | bytes 1769480 | tf_op jit(solution)/shard_map/ppermute | solution.py:28
  384.5 40.3 %collective-permute-start.40 = (bf16[768,512]{1,0:T(8,128)(2,1)}, bf16[768,512]{1,0:T(8,128)(2,1)S(1)}, u32[]{:S(2)}, u32[]{:S(2)}) collective-permute-start(bf16[768,512]{1,0:T(8,128)(2,1)} %get-tuple-element.240), channel_id=1, source_target_pairs={{0,8},{4,12},{8,0},{12,4},{16,24},{20,28},{24,16},{28,20},{1,9},{5... | collective-permute-start | bytes 2359304 | tf_op jit(solution)/shard_map/ppermute | solution.py:28
  384.5 28.1 %collective-permute-start.33 = (bf16[384,768]{1,0:T(8,128)(2,1)}, bf16[384,768]{1,0:T(8,128)(2,1)S(1)}, u32[]{:S(2)}, u32[]{:S(2)}) collective-permute-start(bf16[384,768]{1,0:T(8,128)(2,1)} %get-tuple-element.220), channel_id=1, source_target_pairs={{0,16},{4,20},{8,24},{12,28},{16,0},{20,4},{24,8},{28,12},{1,17},{... | collective-permute-start | bytes 1769480 | tf_op jit(solution)/shard_map/ppermute | solution.py:28
  403.1 40.3 %collective-permute-start.39 = (bf16[768,1024]{1,0:T(8,128)(2,1)S(1)}, bf16[768,1024]{1,0:T(8,128)(2,1)S(1)}, u32[]{:S(2)}, u32[]{:S(2)}) collective-permute-start(bf16[768,1024]{1,0:T(8,128)(2,1)S(1)} %pad_maximum_fusion.8), channel_id=1, source_target_pairs={{0,4},{4,0},{8,12},{12,8},{16,20},{20,16},{24,28},{28,24},{1,5},{5... | collective-permute-start | bytes 4718600 | tf_op jit(solution)/shard_map/ppermute | solution.py:28
  403.1 15.8 %copy-start.31 = (s32[768]{0:T(1024)S(1)}, s32[768]{0:T(1024)}, u32[]{:S(2)}) copy-start(s32[768]{0:T(1024)} %copy-done.30) | copy-start | bytes 9220
  403.1 15.8 %copy-start.34 = (pred[768]{0:T(1024)(128)(4,1)S(1)}, pred[768]{0:T(1024)(128)(4,1)}, u32[]{:S(2)}) copy-start(pred[768]{0:T(1024)(128)(4,1)} %copy-done.33) | copy-start | bytes 2308
  403.2 15.8 %copy-start.37 = (f32[384]{0:T(512)S(1)}, f32[384]{0:T(512)}, u32[]{:S(2)}) copy-start(f32[384]{0:T(512)} %copy-done.36) | copy-start | bytes 4612
  413.9 7.2 %collective-permute-start.37 = (f32[384]{0:T(512)S(1)}, f32[384]{0:T(512)S(1)}, u32[]{:S(2)}, u32[]{:S(2)}) collective-permute-start(f32[384]{0:T(512)S(1)} %multiply_reduce_fusion), channel_id=1, source_target_pairs={{0,1},{1,0},{2,3},{3,2},{4,5},{5,4},{6,7},{7,6},{8,9},{9,8},{10,11... | collective-permute-start | bytes 4616 | tf_op jit(solution)/shard_map/ppermute | solution.py:28
  415.5 25.8 %collective-permute-start.36 = (bf16[384,768]{1,0:T(8,128)(2,1)S(1)}, bf16[384,768]{1,0:T(8,128)(2,1)S(1)}, u32[]{:S(2)}, u32[]{:S(2)}) collective-permute-start(bf16[384,768]{1,0:T(8,128)(2,1)S(1)} %add_convert_fusion.10), channel_id=1, source_target_pairs={{0,16},{4,20},{8,24},{12,28},{16,0},{20,4},{24,8},{28,12},{1,17},{... | collective-permute-start | bytes 1769480 | tf_op jit(solution)/shard_map/ppermute | solution.py:28
  421.1 3.7 collective-permute-start.38
  426.3 16.9 %collective-permute-start.41 = (bf16[384,1024]{1,0:T(8,128)(2,1)S(1)}, bf16[384,1024]{1,0:T(8,128)(2,1)S(1)}, u32[]{:S(2)}, u32[]{:S(2)}) collective-permute-start(bf16[384,1024]{1,0:T(8,128)(2,1)S(1)} %get-tuple-element.298), channel_id=1, source_target_pairs={{0,4},{4,0},{8,12},{12,8},{16,20},{20,16},{24,28},{28,24},{1,5},{5... | collective-permute-start | bytes 2359304 | tf_op jit(solution)/shard_map/ppermute | solution.py:28
  (39 other events, 229.4 us)

commit v11 on v10

--- a/solution.py
+++ b/solution.py
@@ -1,6 +1,10 @@
+import functools
+
 import jax
 import jax.numpy as jnp
 from jax import lax
+from jax.experimental import pallas as pl
+from jax.experimental.pallas import tpu as pltpu
 from jax.sharding import PartitionSpec as P
 
 BF16 = jnp.bfloat16
@@ -59,6 +63,95 @@
         blocks = [jnp.where(flag, blocks[p ^ bit], blocks[p]) for p in range(len(blocks))]
         bit *= 2
     return blocks
+
+
+def backward_kernel(
+    tiles, step, out_ref, hidden_ref, gate_pre_ref, up_pre_ref, down_ref, gate_ref, up_ref, in_ref,
+    expert_ref, expert_sib_ref, input_ref, input_sib_ref, g_gate_ref, g_up_ref, grads,
+):
+    i = pl.program_id(0)
+    rows, depth = out_ref.shape
+    hid = hidden_ref.shape[1]
+
+    def outputs(expert, inputs, gate_grad, up_grad):
+        for c in range(0, depth, step):
+            part = slice(c, c + step)
+            expert[:, part] = mm_last(hidden_ref[...], down_ref[part, :]).astype(BF16)
+            inputs[:, part] = (
+                mm_last(gate_grad, gate_ref[part, :]) + mm_last(up_grad, up_ref[part, :])
+            ).astype(BF16)
+
+    @pl.when(i < tiles)
+    def _():
+        hidden_grad = mm(out_ref[...], down_ref[...])
+        gate_pre, up_pre = gate_pre_ref[...], up_pre_ref[...]
+        sigmoid_gate = jax.nn.sigmoid(gate_pre)
+        gate_grad = (
+            hidden_grad * up_pre * sigmoid_gate * (1.0 + gate_pre * (1.0 - sigmoid_gate))
+        ).astype(BF16)
+        up_grad = (hidden_grad * gate_pre * sigmoid_gate).astype(BF16)
+        place = pl.ds(pl.multiple_of(i * rows, rows), rows)
+        grads[place, :hid] = gate_grad
+        grads[place, hid:] = up_grad
+
+        @pl.when(i < tiles // 2)
+        def _():
+            outputs(expert_ref, input_ref, gate_grad, up_grad)
+
+        @pl.when(i >= tiles // 2)
+        def _():
+            outputs(expert_sib_ref, input_sib_ref, gate_grad, up_grad)
+
+    @pl.when(i >= tiles)
+    def _():
+        both = mm_first(in_ref[...], grads[...])
+        g_gate_ref[...] = both[:, :hid].astype(BF16)
+        g_up_ref[...] = both[:, hid:].astype(BF16)
+
+
+def backward(out_all, hidden, gate_pre, up_pre, down, gate, up, in_all):
+    total, depth = out_all.shape
+    hid = hidden.shape[1]
+    rows, block = total // 6, depth // 8
+    tiles, blocks = 6, 8
+    half = tiles // 2
+
+    def row(width):
+        return pl.BlockSpec((rows, width), lambda i: (jnp.minimum(i, tiles - 1), 0))
+
+    def first_rows():
+        return pl.BlockSpec((rows, depth), lambda i: (jnp.minimum(i, half - 1), 0))
+
+    def last_rows():
+        return pl.BlockSpec((rows, depth), lambda i: (jnp.clip(i - half, 0, half - 1), 0))
+
+    def weights():
+        return pl.BlockSpec((depth, hid), lambda i: (0, 0), pipeline_mode=pl.Buffered(1))
+
+    def width_rows():
+        return pl.BlockSpec((block, hid), lambda i: (jnp.maximum(i - tiles, 0), 0))
+
+    half_out = jax.ShapeDtypeStruct((total // 2, depth), BF16)
+    panel_out = jax.ShapeDtypeStruct((depth, hid), BF16)
+    return pl.pallas_call(
+        functools.partial(backward_kernel, tiles, depth // 4),
+        grid=(tiles + blocks,),
+        in_specs=[
+            row(depth), row(hid), row(hid), row(hid), weights(), weights(), weights(),
+            pl.BlockSpec((total, block), lambda i: (0, jnp.maximum(i - tiles, 0))),
+        ],
+        out_specs=[first_rows(), last_rows(), first_rows(), last_rows(), width_rows(), width_rows()],
+        out_shape=[half_out, half_out, half_out, half_out, panel_out, panel_out],
+        scratch_shapes=[pltpu.VMEM((total, 2 * hid), BF16)],
+        compiler_params=pltpu.CompilerParams(
+            dimension_semantics=("arbitrary",), vmem_limit_bytes=52 * 1024 * 1024
+        ),
+        cost_estimate=pl.CostEstimate(
+            flops=12 * total * depth * hid,
+            bytes_accessed=2 * (4 * total * depth + 5 * depth * hid + 5 * total * hid),
+            transcendentals=total * hid,
+        ),
+    )(out_all, hidden, gate_pre, up_pre, down, gate, up, in_all)
 
 
 def local(tokens, assign, combine, cotangent, w_gate, w_up, w_down_t):
@@ -217,40 +310,28 @@
     g_down = mm_first(out_all, hidden).astype(BF16)
     g_down, hidden, up_pre, up, *down_far = fence(g_down, hidden, up_pre, up, *down_far)
 
-    table = 2 * row_limit
     g_down_4 = first_send(blocks_far(g_down))
     n_kept = len(g_down_4)
     g_down_4 = shrink(*g_down_4)
     g_down_own = shrink(*first_send(blocks_own(g_down)))
     down = whole_panel(down_own, down_far)
-    hidden_grad = mm(out_all, down)
-    gate_grad = (
-        hidden_grad * up_pre * sigmoid_gate * (1.0 + gate_pre * (1.0 - sigmoid_gate))
-    ).astype(BF16)
-    up_grad = (hidden_grad * gate_pre * sigmoid_gate).astype(BF16)
-    g_gate = mm_first(in_all, gate_grad).astype(BF16)
-    expert_got = across(mm_last(hidden[table:], down).astype(BF16))
-
-    def input_part(rows):
-        return mm_last(gate_grad[rows], gate) + mm_last(up_grad[rows], up)
-
-    input_sib = input_part(slice(table, None)).astype(BF16)
-    down, gate_grad, up_grad, g_gate, expert_got, input_sib, *rest = fence(
-        down, gate_grad, up_grad, g_gate, expert_got, input_sib, *g_down_4, *g_down_own
+    expert_part, expert_sib, input_part, input_sib, g_gate, g_up = backward(
+        out_all, hidden, gate_pre, up_pre, down, gate, up, in_all
+    )
+    expert_part, expert_sib, input_part, input_sib, g_gate, g_up, *rest = fence(
+        expert_part, expert_sib, input_part, input_sib, g_gate, g_up, *g_down_4, *g_down_own
     )
     g_down_own = rest[2:]
-    g_down_4, input_sib, g_gate = fence(done(*rest[:2]), input_sib, g_gate)
+    g_down_4, expert_sib, input_sib, g_gate, g_up = fence(
+        done(*rest[:2]), expert_sib, input_sib, g_gate, g_up
+    )
     g_gate_4, g_gate_own = first_send(blocks_far(g_gate)), first_send(blocks_own(g_gate))
 
     g_down_far = z_far(g_down_4)
     g_gate_4 = shrink(*g_gate_4)
-    input_got, in_all, gate_grad, up_grad, hidden = fence(
-        across(input_sib[:row_limit]), in_all, gate_grad, up_grad, hidden
-    )
-    input_got = cat(input_got, across(input_sib[row_limit:]))
-    g_up = mm_first(in_all, up_grad).astype(BF16)
-    expert_sum = (mm_last(hidden[:table], down) + expert_got.astype(F32)).astype(BF16)
-    input_sum = (input_part(slice(None, table)) + input_got.astype(F32)).astype(BF16)
+    expert_got, input_got = across(expert_sib), across(input_sib)
+    expert_sum = (expert_part.astype(F32) + expert_got.astype(F32)).astype(BF16)
+    input_sum = (input_part.astype(F32) + input_got.astype(F32)).astype(BF16)
 
     def split_parts(value):
         return {

time: 453 us -> 461 us (1.018); the launches traced: 446 us -> 461 us
  Pallas kernels: 0 us -> 55.9 us
  matrix products: 86.4 us -> 33.9 us
  other arithmetic: 45.5 us -> 55.9 us
    pallas_call x0 -> x1, Pallas kernels: none -> 55.9 us  [backward(): pl.pallas_call(functools.partial(backward_kernel, tiles, depth // 4), gri...]
    dot_general x16 -> x7, matrix products: 86.4 us -> 33.9 us  [dot(): lax.dot_general(left, right, (dims, ((), ())), preferred_element_type=F32)]
    convert_element_type x0 -> x2, other arithmetic: none -> 8.64 us  [the longest x1 4.37 us: local(): input_sum = (input_part.astype(F32) + input_got.astype(F32)).astype(BF16)]
    ppermute x42 -> x41, waiting for transfers between devices: 234 us -> 238 us  [swap(): return lax.ppermute(value, axis, [(i, i ^ distance) for i in range(size)])]
    ppermute x42 -> x41, starting transfers between devices: 41.8 us -> 41.9 us  [swap(): return lax.ppermute(value, axis, [(i, i ^ distance) for i in range(size)])]
  transfers between devices with their start and end apart: 42 -> 41, of which waited for: 20 -> 21; matrix products, arithmetic and copies ran while one was open for 33% -> 24% of each run, Pallas kernels for 0% -> 12%
where the time goes in v11:
time: 461 us
  waiting for transfers between devices  238 us (52%)
  other arithmetic  55.9 us (12%)
  Pallas kernels  55.9 us (12%)
  starting transfers between devices  41.9 us (9%)
  matrix products  33.9 us (7%)
  local copies, waits for them, and re-layouts  33.1 us (7%)
    ppermute x41, waiting for transfers between devices, swap(): return lax.ppermute(value, axis, [(i, i ^ distance) for i in range(size)])  238 us
    pallas_call x1, Pallas kernels, backward(): pl.pallas_call(functools.partial(backward_kernel, tiles, depth // 4), gri...  55.9 us
    ppermute x41, starting transfers between devices, swap(): return lax.ppermute(value, axis, [(i, i ^ distance) for i in range(size)])  41.9 us
    dot_general x7, matrix products, dot(): lax.dot_general(left, right, (dims, ((), ())), preferred_element_type=F32)  33.9 us
    concatenate x5, other arithmetic, cat(): return jnp.concatenate(values, axis=0)  15.7 us
  transfers between devices with their start and end apart: 41, of which 21 were waited for; matrix products, arithmetic and copies ran while one was open for 24% of the time, Pallas kernels for 12%

profile of v11, /device:TPU:0, one launch (start us, length us, event | category | flops | bytes accessed | tf_op | source)
XLA Modules:
  0.0 460.6 jit_solution(155152517386310211)
XLA Ops:
  0.7 2.4 constant_dynamic-slice_fusion.18
  3.1 4.0 collective-permute-start
  7.2 1.6 collective-permute-start.1
  9.7 5.9 %convolution_convert_fusion.2 = bf16[384,3072]{1,0:T(8,128)(2,1)} fusion(bf16[768,3072]{1,0:T(8,128)(2,1)} %param.7, s32[768]{0:T(1024)S(1)} %add_bitcast_fusion, pred[768]{0:T(1024)(128)(4,1)S(1)} %fusion.20), kind=kOutput, calls=%fused_computation.7 | convolution fusion | flops 1813708800 | bytes 7081728 | tf_op jit(solution)/shard_map/dot_general | solution.py:15
  15.6 4.4 multiply_convert_fusion
  26.0 16.0 %collective-permute-done = bf16[384,1024]{1,0:T(8,128)(2,1)} collective-permute-done((bf16[384,1024]{1,0:T(8,128)(2,1)}, bf16[384,1024]{1,0:T(8,128)(2,1)}, u32[]{:S(2)}, u32[]{:S(2)}) %collective-permute-start) | collective-permute-done | bytes 786464 | tf_op jit(solution)/shard_map/ppermute | solution.py:32
  42.5 1.6 collective-permute-start.2
  44.1 2.4 collective-permute-start.6
  52.4 34.8 %collective-permute-done.6 = bf16[384,1024]{1,0:T(8,128)(2,1)} collective-permute-done((bf16[384,1024]{1,0:T(8,128)(2,1)}, bf16[384,1024]{1,0:T(8,128)(2,1)}, u32[]{:S(2)}, u32[]{:S(2)}) %collective-permute-start.6) | collective-permute-done | bytes 786464 | tf_op jit(solution)/shard_map/ppermute | solution.py:32
  87.2 10.2 %collective-permute-done.2 = bf16[768,768]{1,0:T(8,128)(2,1)} collective-permute-done((bf16[768,768]{1,0:T(8,128)(2,1)}, bf16[768,768]{1,0:T(8,128)(2,1)}, u32[]{:S(2)}, u32[]{:S(2)}) %collective-permute-start.2) | collective-permute-done | bytes 1179680 | tf_op jit(solution)/shard_map/ppermute | solution.py:32
  97.4 2.6 collective-permute-start.10
  100.9 3.0 collective-permute-start.7
  103.9 2.2 pad_maximum_fusion.2
  106.1 1.5 constant_dynamic-slice_fusion.12
  107.6 40.5 %collective-permute-done.7 = bf16[768,512]{1,0:T(8,128)(2,1)} collective-permute-done((bf16[768,512]{1,0:T(8,128)(2,1)}, bf16[768,512]{1,0:T(8,128)(2,1)}, u32[]{:S(2)}, u32[]{:S(2)}) %collective-permute-start.7) | collective-permute-done | bytes 786464 | tf_op jit(solution)/shard_map/ppermute | solution.py:32
  148.1 3.5 collective-permute-done.8
  151.8 3.1 collective-permute-start.12
  155.8 3.7 broadcast_select_fusion.10
  159.6 2.6 broadcast_select_fusion.11
  168.0 6.8 %pad_maximum_fusion.in_ref = bf16[1536,3072]{1,0:T(8,128)(2,1)S(1)} fusion(bf16[384,3072]{1,0:T(8,128)(2,1)S(1)} %collective-permute-done.14, bf16[384,3072]{1,0:T(8,128)(2,1)} %collective-permute-done.3, bf16[384,768]{1,0:T(8,128)(2,1)S(1)} %get-tuple-element.255, bf16[384,768]{1,0:T(8,128)(2,1)S(1)} %get-tuple-element.254, ...), kind=kLoop, calls=%fused_computation | loop fusion | flops 66060288 | bytes 18874368 | tf_op jit(solution)/shard_map/concatenate | solution.py:52
  174.8 7.5 %pad_maximum_fusion.1.out_ref = bf16[1536,3072]{1,0:T(8,128)(2,1)S(1)} fusion(bf16[384,3072]{1,0:T(8,128)(2,1)S(1)} %collective-permute-done.15, bf16[384,3072]{1,0:T(8,128)(2,1)} %collective-permute-done.4, bf16[384,768]{1,0:T(8,128)(2,1)S(1)} %get-tuple-element.258, bf16[384,768]{1,0:T(8,128)(2,1)S(1)} %get-tuple-element.257, ...), kind=kLoop, calls=%fused_computation.1 | loop fusion | flops 66060288 | bytes 18874368 | tf_op jit(solution)/shard_map/concatenate | solution.py:52
  182.3 6.9 %fusion.24.gate_pre_ref = f32[1536,512]{1,0:T(8,128)} fusion(bf16[1536,3072]{1,0:T(8,128)(2,1)S(1)} %pad_maximum_fusion.in_ref, bf16[3072,512]{1,0:T(8,128)(2,1)S(1)} %bitcast.87), kind=kOutput, calls=%fused_computation.170 | convolution fusion | flops 4831838208 | bytes 15728640 | tf_op jit(solution)/shard_map/dot_general | solution.py:15
  195.6 7.3 %multiply_convert_fusion.1 = (bf16[1536,512]{1,0:T(8,128)(2,1)S(1)}, f32[1536,512]{1,0:T(8,128)}) fusion(f32[1536,512]{1,0:T(8,128)S(1)} %copy-done.25, bf16[1536,3072]{1,0:T(8,128)(2,1)S(1)} %pad_maximum_fusion.in_ref, bf16[3072,512]{1,0:T(8,128)(2,1)S(1)} %bitcast.89), kind=kOutput, calls=%fused_computation.9 | convolution fusion | flops 4836556800 | bytes 20447232 | tf_op jit(solution)/shard_map/dot_general | solution.py:15
  203.0 5.4 %convolution_convert_fusion = bf16[3072,512]{1,0:T(8,128)(2,1)S(1)} fusion(bf16[1536,3072]{1,0:T(8,128)(2,1)S(1)} %pad_maximum_fusion.1.out_ref, bf16[1536,512]{1,0:T(8,128)(2,1)S(1)} %get-tuple-element.163.hidden_ref), kind=kOutput, calls=%fused_computation.5 | convolution fusion | flops 4833411072 | bytes 14155776 | tf_op jit(solution)/shard_map/dot_general | solution.py:15
  212.3 1.6 collective-permute-start.18
  214.4 1.7 copy-done.3
  216.1 55.9 %shard_map.118 = (bf16[768,3072]{1,0:T(8,128)(2,1)}, bf16[768,3072]{1,0:T(8,128)(2,1)}, bf16[768,3072]{1,0:T(8,128)(2,1)}, bf16[768,3072]{1,0:T(8,128)(2,1)}, bf...) custom-call(bf16[1536,3072]{1,0:T(8,128)(2,1)} %copy-done.1, bf16[1536,512]{1,0:T(8,128)(2,1)S(1)} %get-tuple-element.163.hidden_ref, ...), custom_call_target="tpu_custom_call" | custom-call | flops 28991029248 | bytes 61341696 | tf_op jit(solution)/shard_map/pallas_call | solution.py:136
  273.6 3.4 dynamic-slice_bitcast_fusion
  277.1 1.5 collective-permute-start.23
  281.4 4.3 add_convert_fusion
  288.6 4.4 add_convert_fusion.1
  293.0 19.2 %collective-permute-done.23 = bf16[768,512]{1,0:T(8,128)(2,1)} collective-permute-done((bf16[768,512]{1,0:T(8,128)(2,1)}, bf16[768,512]{1,0:T(8,128)(2,1)}, u32[]{:S(2)}, u32[]{:S(2)}) %collective-permute-start.23) | collective-permute-done | bytes 786464 | tf_op jit(solution)/shard_map/ppermute | solution.py:32
  312.2 3.7 collective-permute-done.20
  317.2 1.6 collective-permute-start.25
  318.8 1.6 collective-permute-start.26
  321.8 22.2 %collective-permute-done.25 = bf16[384,1536]{1,0:T(8,128)(2,1)S(1)} collective-permute-done((bf16[384,1536]{1,0:T(8,128)(2,1)S(1)}, bf16[384,1536]{1,0:T(8,128)(2,1)S(1)}, u32[]{:S(2)}, u32[]{:S(2)}) %collective-permute-start.25) | collective-permute-done | bytes 1179680 | tf_op jit(solution)/shard_map/ppermute | solution.py:32
  345.9 8.7 %collective-permute-done.24 = bf16[768,512]{1,0:T(8,128)(2,1)S(1)} collective-permute-done((bf16[768,512]{1,0:T(8,128)(2,1)S(1)}, bf16[768,512]{1,0:T(8,128)(2,1)S(1)}, u32[]{:S(2)}, u32[]{:S(2)}) %collective-permute-start.24) | collective-permute-done | bytes 786464 | tf_op jit(solution)/shard_map/ppermute | solution.py:32
  358.1 37.3 %collective-permute-done.30 = bf16[384,2304]{1,0:T(8,128)(2,1)S(1)} collective-permute-done((bf16[384,2304]{1,0:T(8,128)(2,1)S(1)}, bf16[384,2304]{1,0:T(8,128)(2,1)S(1)}, u32[]{:S(2)}, u32[]{:S(2)}) %collective-permute-start.30) | collective-permute-done | bytes 1769504 | tf_op jit(solution)/shard_map/ppermute | solution.py:32
  395.4 1.5 add_convert_fusion.13
  396.9 1.6 add_convert_fusion.11
  400.4 11.9 %collective-permute-done.34 = bf16[384,768]{1,0:T(8,128)(2,1)} collective-permute-done((bf16[384,768]{1,0:T(8,128)(2,1)}, bf16[384,768]{1,0:T(8,128)(2,1)}, u32[]{:S(2)}, u32[]{:S(2)}) %collective-permute-start.34) | collective-permute-done | bytes 589856 | tf_op jit(solution)/shard_map/ppermute | solution.py:32
  418.8 8.7 %collective-permute-done.32 = bf16[384,768]{1,0:T(8,128)(2,1)S(1)} collective-permute-done((bf16[384,768]{1,0:T(8,128)(2,1)}, bf16[384,768]{1,0:T(8,128)(2,1)S(1)}, u32[]{:S(2)}, u32[]{:S(2)}) %collective-permute-start.32) | collective-permute-done | bytes 589856 | tf_op jit(solution)/shard_map/ppermute | solution.py:32
  430.3 3.4 collective-permute-start.35
  433.7 2.1 convolution_convert_fusion.4
  436.1 1.6 collective-permute-start.37
  437.8 2.0 collective-permute-done.37
  442.5 13.8 %collective-permute-done.35 = bf16[384,768]{1,0:T(8,128)(2,1)S(1)} collective-permute-done((bf16[384,768]{1,0:T(8,128)(2,1)S(1)}, bf16[384,768]{1,0:T(8,128)(2,1)S(1)}, u32[]{:S(2)}, u32[]{:S(2)}) %collective-permute-start.35) | collective-permute-done | bytes 589856 | tf_op jit(solution)/shard_map/ppermute | solution.py:32
  456.3 1.9 convolution_convert_fusion.3
  (206 shorter events, 63.6 us)
Async XLA Ops:
  0.7 14.9 %slice-start.4 = ((s8[4718592]{0:T(1024)(128)(4,1)}), s8[524288]{0:T(1024)(128)(4,1)S(1)}, s32[]{:S(2)}) async-start(s8[4718592]{0:T(1024)(128)(4,1)} %bitcast.91), calls=%async_computation.4 | async-start | bytes 1048576
  3.1 38.8 %collective-permute-start = (bf16[384,1024]{1,0:T(8,128)(2,1)}, bf16[384,1024]{1,0:T(8,128)(2,1)}, u32[]{:S(2)}, u32[]{:S(2)}) collective-permute-start(bf16[384,1024]{1,0:T(8,128)(2,1)} %get-tuple-element.317), channel_id=1, source_target_pairs={{0,16},{4,20},{8,24},{12,28},{16,0},{20,4},{24,8},{28,12},{1,17},{... | collective-permute-start | bytes 2359304 | tf_op jit(solution)/shard_map/ppermute | solution.py:32
  7.2 34.8 %collective-permute-start.1 = (bf16[384,1024]{1,0:T(8,128)(2,1)S(1)}, bf16[384,1024]{1,0:T(8,128)(2,1)}, u32[]{:S(2)}, u32[]{:S(2)}) collective-permute-start(bf16[384,1024]{1,0:T(8,128)(2,1)S(1)} %get-tuple-element.133), channel_id=1, source_target_pairs={{0,8},{4,12},{8,0},{12,4},{16,24},{20,28},{24,16},{28,20},{1,9},{5... | collective-permute-start | bytes 2359304 | tf_op jit(solution)/shard_map/ppermute | solution.py:32
  42.0 5.8 %collective-permute-start.5 = (bf16[768,1024]{1,0:T(8,128)(2,1)S(1)}, bf16[768,1024]{1,0:T(8,128)(2,1)}, u32[]{:S(2)}, u32[]{:S(2)}) collective-permute-start(bf16[768,1024]{1,0:T(8,128)(2,1)S(1)} %maximum_maximum_fusion), channel_id=1, source_target_pairs={{0,4},{4,0},{8,12},{12,8},{16,20},{20,16},{24,28},{28,24},{1,5},{5... | collective-permute-start | bytes 4718600 | tf_op jit(solution)/shard_map/ppermute | solution.py:32
  42.0 55.4 %collective-permute-start.3 = (bf16[384,3072]{1,0:T(8,128)(2,1)}, bf16[384,3072]{1,0:T(8,128)(2,1)}, u32[]{:S(2)}, u32[]{:S(2)}) collective-permute-start(bf16[384,3072]{1,0:T(8,128)(2,1)} %convolution_convert_fusion.2), channel_id=1, source_target_pairs={{0,4},{4,0},{8,12},{12,8},{16,20},{20,16},{24,28},{28,24},{1,5},{5... | collective-permute-start | bytes 7077896 | tf_op jit(solution)/shard_map/ppermute | solution.py:32
  42.5 54.9 %collective-permute-start.4 = (bf16[384,3072]{1,0:T(8,128)(2,1)}, bf16[384,3072]{1,0:T(8,128)(2,1)}, u32[]{:S(2)}, u32[]{:S(2)}) collective-permute-start(bf16[384,3072]{1,0:T(8,128)(2,1)} %get-tuple-element.129), channel_id=1, source_target_pairs={{0,4},{4,0},{8,12},{12,8},{16,20},{20,16},{24,28},{28,24},{1,5},{5... | collective-permute-start | bytes 7077896 | tf_op jit(solution)/shard_map/ppermute | solution.py:32
  42.5 54.9 %collective-permute-start.2 = (bf16[768,768]{1,0:T(8,128)(2,1)}, bf16[768,768]{1,0:T(8,128)(2,1)}, u32[]{:S(2)}, u32[]{:S(2)}) collective-permute-start(bf16[768,768]{1,0:T(8,128)(2,1)} %pad_maximum_fusion.9), channel_id=1, source_target_pairs={{0,16},{4,20},{8,24},{12,28},{16,0},{20,4},{24,8},{28,12},{1,17},{... | collective-permute-start | bytes 3538952 | tf_op jit(solution)/shard_map/ppermute | solution.py:32
  44.1 43.1 %collective-permute-start.6 = (bf16[384,1024]{1,0:T(8,128)(2,1)}, bf16[384,1024]{1,0:T(8,128)(2,1)}, u32[]{:S(2)}, u32[]{:S(2)}) collective-permute-start(bf16[384,1024]{1,0:T(8,128)(2,1)} %collective-permute-done), channel_id=1, source_target_pairs={{0,8},{4,12},{8,0},{12,4},{16,24},{20,28},{24,16},{28,20},{1,9},{5... | collective-permute-start | bytes 2359304 | tf_op jit(solution)/shard_map/ppermute | solution.py:32
  97.4 54.3 %collective-permute-start.11 = (bf16[768,1024]{1,0:T(8,128)(2,1)S(1)}, bf16[768,1024]{1,0:T(8,128)(2,1)}, u32[]{:S(2)}, u32[]{:S(2)}) collective-permute-start(bf16[768,1024]{1,0:T(8,128)(2,1)S(1)} %pad_maximum_fusion.7), channel_id=1, source_target_pairs={{0,8},{4,12},{8,0},{12,4},{16,24},{20,28},{24,16},{28,20},{1,9},{5... | collective-permute-start | bytes 4718600 | tf_op jit(solution)/shard_map/ppermute | solution.py:32
  97.4 50.8 %collective-permute-start.10 = (bf16[768,768]{1,0:T(8,128)(2,1)}, bf16[768,768]{1,0:T(8,128)(2,1)}, u32[]{:S(2)}, u32[]{:S(2)}) collective-permute-start(bf16[768,768]{1,0:T(8,128)(2,1)} %collective-permute-done.2), channel_id=1, source_target_pairs={{0,3},{1,2},{2,1},{3,0},{4,7},{5,6},{6,5},{7,4},{8,11},{9,10},{10,... | collective-permute-start | bytes 3538952 | tf_op jit(solution)/shard_map/ppermute | solution.py:32
  99.9 51.7 %collective-permute-start.8 = (bf16[768,768]{1,0:T(8,128)(2,1)}, bf16[768,768]{1,0:T(8,128)(2,1)}, u32[]{:S(2)}, u32[]{:S(2)}) collective-permute-start(bf16[768,768]{1,0:T(8,128)(2,1)} %collective-permute-done.2), channel_id=1, source_target_pairs={{0,1},{1,0},{2,3},{3,2},{4,5},{5,4},{6,7},{7,6},{8,9},{9,8},{10,11... | collective-permute-start | bytes 3538952 | tf_op jit(solution)/shard_map/ppermute | solution.py:32
  100.5 51.2 %collective-permute-start.9 = (bf16[768,768]{1,0:T(8,128)(2,1)}, bf16[768,768]{1,0:T(8,128)(2,1)}, u32[]{:S(2)}, u32[]{:S(2)}) collective-permute-start(bf16[768,768]{1,0:T(8,128)(2,1)} %collective-permute-done.2), channel_id=1, source_target_pairs={{0,2},{1,3},{2,0},{3,1},{4,6},{5,7},{6,4},{7,5},{8,10},{9,11},{10,... | collective-permute-start | bytes 3538952 | tf_op jit(solution)/shard_map/ppermute | solution.py:32
  100.9 47.2 %collective-permute-start.7 = (bf16[768,512]{1,0:T(8,128)(2,1)}, bf16[768,512]{1,0:T(8,128)(2,1)}, u32[]{:S(2)}, u32[]{:S(2)}) collective-permute-start(bf16[768,512]{1,0:T(8,128)(2,1)} %maximum_select_fusion.2), channel_id=1, source_target_pairs={{0,16},{4,20},{8,24},{12,28},{16,0},{20,4},{24,8},{28,12},{1,17},{... | collective-permute-start | bytes 2359304 | tf_op jit(solution)/shard_map/ppermute | solution.py:32
  151.7 4.1 collective-permute-start.13
  151.8 38.4 %collective-permute-start.12 = (bf16[768,512]{1,0:T(8,128)(2,1)}, bf16[768,512]{1,0:T(8,128)(2,1)}, u32[]{:S(2)}, u32[]{:S(2)}) collective-permute-start(bf16[768,512]{1,0:T(8,128)(2,1)} %maximum_select_fusion.3), channel_id=1, source_target_pairs={{0,16},{4,20},{8,24},{12,28},{16,0},{20,4},{24,8},{28,12},{1,17},{... | collective-permute-start | bytes 2359304 | tf_op jit(solution)/shard_map/ppermute | solution.py:32
  154.8 35.8 %collective-permute-start.16 = (bf16[768,512]{1,0:T(8,128)(2,1)}, bf16[768,512]{1,0:T(8,128)(2,1)}, u32[]{:S(2)}, u32[]{:S(2)}) collective-permute-start(bf16[768,512]{1,0:T(8,128)(2,1)} %collective-permute-done.7), channel_id=1, source_target_pairs={{0,8},{4,12},{8,0},{12,4},{16,24},{20,28},{24,16},{28,20},{1,9},{5... | collective-permute-start | bytes 2359304 | tf_op jit(solution)/shard_map/ppermute | solution.py:32
  162.4 5.5 %collective-permute-start.14 = (bf16[384,3072]{1,0:T(8,128)(2,1)S(1)}, bf16[384,3072]{1,0:T(8,128)(2,1)S(1)}, u32[]{:S(2)}, u32[]{:S(2)}) collective-permute-start(bf16[384,3072]{1,0:T(8,128)(2,1)S(1)} %pad_maximum_fusion.3), channel_id=1, source_target_pairs={{0,4},{4,0},{8,12},{12,8},{16,20},{20,16},{24,28},{28,24},{1,5},{5... | collective-permute-start | bytes 7077896 | tf_op jit(solution)/shard_map/ppermute | solution.py:32
  163.1 11.7 %collective-permute-start.15 = (bf16[384,3072]{1,0:T(8,128)(2,1)S(1)}, bf16[384,3072]{1,0:T(8,128)(2,1)S(1)}, u32[]{:S(2)}, u32[]{:S(2)}) collective-permute-start(bf16[384,3072]{1,0:T(8,128)(2,1)S(1)} %pad_maximum_fusion.4), channel_id=1, source_target_pairs={{0,4},{4,0},{8,12},{12,8},{16,20},{20,16},{24,28},{28,24},{1,5},{5... | collective-permute-start | bytes 7077896 | tf_op jit(solution)/shard_map/ppermute | solution.py:32
  174.8 20.8 %copy-start = (bf16[1536,3072]{1,0:T(8,128)(2,1)}, bf16[1536,3072]{1,0:T(8,128)(2,1)S(1)}, u32[]{:S(2)}) copy-start(bf16[1536,3072]{1,0:T(8,128)(2,1)S(1)} %pad_maximum_fusion.in_ref) | copy-start | bytes 28311556
  182.3 20.7 %copy-start.1 = (bf16[1536,3072]{1,0:T(8,128)(2,1)}, bf16[1536,3072]{1,0:T(8,128)(2,1)S(1)}, u32[]{:S(2)}) copy-start(bf16[1536,3072]{1,0:T(8,128)(2,1)S(1)} %pad_maximum_fusion.1.out_ref) | copy-start | bytes 28311556
  190.7 18.9 %collective-permute-start.17 = (bf16[768,512]{1,0:T(8,128)(2,1)}, bf16[768,512]{1,0:T(8,128)(2,1)S(1)}, u32[]{:S(2)}, u32[]{:S(2)}) collective-permute-start(bf16[768,512]{1,0:T(8,128)(2,1)} %collective-permute-done.12), channel_id=1, source_target_pairs={{0,8},{4,12},{8,0},{12,4},{16,24},{20,28},{24,16},{28,20},{1,9},{5... | collective-permute-start | bytes 2359304 | tf_op jit(solution)/shard_map/ppermute | solution.py:32
  212.3 59.7 %collective-permute-start.18 = (bf16[768,512]{1,0:T(8,128)(2,1)S(1)}, bf16[768,512]{1,0:T(8,128)(2,1)S(1)}, u32[]{:S(2)}, u32[]{:S(2)}) collective-permute-start(bf16[768,512]{1,0:T(8,128)(2,1)S(1)} %get-tuple-element.274), channel_id=1, source_target_pairs={{0,8},{4,12},{8,0},{12,4},{16,24},{20,28},{24,16},{28,20},{1,9},{5... | collective-permute-start | bytes 2359304 | tf_op jit(solution)/shard_map/ppermute | solution.py:32
  213.8 58.2 %collective-permute-start.19 = (bf16[768,512]{1,0:T(8,128)(2,1)S(1)}, bf16[768,512]{1,0:T(8,128)(2,1)S(1)}, u32[]{:S(2)}, u32[]{:S(2)}) collective-permute-start(bf16[768,512]{1,0:T(8,128)(2,1)S(1)} %get-tuple-element.272), channel_id=1, source_target_pairs={{0,8},{4,12},{8,0},{12,4},{16,24},{20,28},{24,16},{28,20},{1,9},{5... | collective-permute-start | bytes 2359304 | tf_op jit(solution)/shard_map/ppermute | solution.py:32
  273.1 8.3 %collective-permute-start.22 = (bf16[768,3072]{1,0:T(8,128)(2,1)}, bf16[768,3072]{1,0:T(8,128)(2,1)}, u32[]{:S(2)}, u32[]{:S(2)}) collective-permute-start(bf16[768,3072]{1,0:T(8,128)(2,1)} %get-tuple-element.186), channel_id=1, source_target_pairs={{0,4},{4,0},{8,12},{12,8},{16,20},{20,16},{24,28},{28,24},{1,5},{5... | collective-permute-start | bytes 14155784 | tf_op jit(solution)/shard_map/ppermute | solution.py:32
  273.1 15.3 %collective-permute-start.21 = (bf16[768,3072]{1,0:T(8,128)(2,1)}, bf16[768,3072]{1,0:T(8,128)(2,1)}, u32[]{:S(2)}, u32[]{:S(2)}) collective-permute-start(bf16[768,3072]{1,0:T(8,128)(2,1)} %get-tuple-element.184), channel_id=1, source_target_pairs={{0,4},{4,0},{8,12},{12,8},{16,20},{20,16},{24,28},{28,24},{1,5},{5... | collective-permute-start | bytes 14155784 | tf_op jit(solution)/shard_map/ppermute | solution.py:32
  277.1 35.1 %collective-permute-start.23 = (bf16[768,512]{1,0:T(8,128)(2,1)}, bf16[768,512]{1,0:T(8,128)(2,1)}, u32[]{:S(2)}, u32[]{:S(2)}) collective-permute-start(bf16[768,512]{1,0:T(8,128)(2,1)} %get-tuple-element.266), channel_id=1, source_target_pairs={{0,8},{4,12},{8,0},{12,4},{16,24},{20,28},{24,16},{28,20},{1,9},{5... | collective-permute-start | bytes 2359304 | tf_op jit(solution)/shard_map/ppermute | solution.py:32
  278.6 37.3 %collective-permute-start.20 = (bf16[768,512]{1,0:T(8,128)(2,1)}, bf16[768,512]{1,0:T(8,128)(2,1)}, u32[]{:S(2)}, u32[]{:S(2)}) collective-permute-start(bf16[768,512]{1,0:T(8,128)(2,1)} %add_convert_fusion.7), channel_id=1, source_target_pairs={{0,16},{4,20},{8,24},{12,28},{16,0},{20,4},{24,8},{28,12},{1,17},{... | collective-permute-start | bytes 2359304 | tf_op jit(solution)/shard_map/ppermute | solution.py:32
  288.5 27.4 %copy-start.9 = (bf16[768,512]{1,0:T(8,128)(2,1)S(1)}, bf16[768,512]{1,0:T(8,128)(2,1)}, u32[]{:S(2)}) copy-start(bf16[768,512]{1,0:T(8,128)(2,1)} %get-tuple-element.189) | copy-start | bytes 2359300
  292.9 24.3 %copy-start.17 = (bf16[384,1536]{1,0:T(8,128)(2,1)S(1)}, bf16[384,1536]{1,0:T(8,128)(2,1)}, u32[]{:S(2)}) copy-start(bf16[384,1536]{1,0:T(8,128)(2,1)} %pad_maximum_fusion.10) | copy-start | bytes 3538948
  293.0 25.8 %copy-start.16 = (bf16[384,1536]{1,0:T(8,128)(2,1)S(1)}, bf16[384,1536]{1,0:T(8,128)(2,1)}, u32[]{:S(2)}) copy-start(bf16[384,1536]{1,0:T(8,128)(2,1)} %pad_maximum_fusion.11) | copy-start | bytes 3538948
  317.2 26.8 %collective-permute-start.25 = (bf16[384,1536]{1,0:T(8,128)(2,1)S(1)}, bf16[384,1536]{1,0:T(8,128)(2,1)S(1)}, u32[]{:S(2)}, u32[]{:S(2)}) collective-permute-start(bf16[384,1536]{1,0:T(8,128)(2,1)S(1)} %copy-done.17), channel_id=1, source_target_pairs={{0,1},{1,0},{2,3},{3,2},{4,5},{5,4},{6,7},{7,6},{8,9},{9,8},{10,11... | collective-permute-start | bytes 3538952 | tf_op jit(solution)/shard_map/ppermute | solution.py:32
  318.8 26.5 %collective-permute-start.26 = (bf16[384,1536]{1,0:T(8,128)(2,1)S(1)}, bf16[384,1536]{1,0:T(8,128)(2,1)S(1)}, u32[]{:S(2)}, u32[]{:S(2)}) collective-permute-start(bf16[384,1536]{1,0:T(8,128)(2,1)S(1)} %copy-done.16), channel_id=1, source_target_pairs={{0,2},{1,3},{2,0},{3,1},{4,6},{5,7},{6,4},{7,5},{8,10},{9,11},{10,... | collective-permute-start | bytes 3538952 | tf_op jit(solution)/shard_map/ppermute | solution.py:32
  320.4 34.3 %collective-permute-start.24 = (bf16[768,512]{1,0:T(8,128)(2,1)S(1)}, bf16[768,512]{1,0:T(8,128)(2,1)S(1)}, u32[]{:S(2)}, u32[]{:S(2)}) collective-permute-start(bf16[768,512]{1,0:T(8,128)(2,1)S(1)} %add_convert_fusion.6), channel_id=1, source_target_pairs={{0,16},{4,20},{8,24},{12,28},{16,0},{20,4},{24,8},{28,12},{1,17},{... | collective-permute-start | bytes 2359304 | tf_op jit(solution)/shard_map/ppermute | solution.py:32
  320.6 34.8 %collective-permute-start.27 = (bf16[768,512]{1,0:T(8,128)(2,1)}, bf16[768,512]{1,0:T(8,128)(2,1)S(1)}, u32[]{:S(2)}, u32[]{:S(2)}) collective-permute-start(bf16[768,512]{1,0:T(8,128)(2,1)} %get-tuple-element.201), channel_id=1, source_target_pairs={{0,8},{4,12},{8,0},{12,4},{16,24},{20,28},{24,16},{28,20},{1,9},{5... | collective-permute-start | bytes 2359304 | tf_op jit(solution)/shard_map/ppermute | solution.py:32
  354.7 42.2 %copy-start.20 = (bf16[768,512]{1,0:T(8,128)(2,1)}, bf16[768,512]{1,0:T(8,128)(2,1)S(1)}, u32[]{:S(2)}) copy-start(bf16[768,512]{1,0:T(8,128)(2,1)S(1)} %collective-permute-done.24) | copy-start | bytes 2359300
  355.6 39.8 %collective-permute-start.30 = (bf16[384,2304]{1,0:T(8,128)(2,1)S(1)}, bf16[384,2304]{1,0:T(8,128)(2,1)S(1)}, u32[]{:S(2)}, u32[]{:S(2)}) collective-permute-start(bf16[384,2304]{1,0:T(8,128)(2,1)S(1)} %pad_maximum_fusion.5), channel_id=1, source_target_pairs={{0,1},{1,0},{2,3},{3,2},{4,5},{5,4},{6,7},{7,6},{8,9},{9,8},{10,11... | collective-permute-start | bytes 5308424 | tf_op jit(solution)/shard_map/ppermute | solution.py:32
  356.2 40.7 %collective-permute-start.29 = (bf16[384,2304]{1,0:T(8,128)(2,1)S(1)}, bf16[384,2304]{1,0:T(8,128)(2,1)S(1)}, u32[]{:S(2)}, u32[]{:S(2)}) collective-permute-start(bf16[384,2304]{1,0:T(8,128)(2,1)S(1)} %pad_maximum_fusion.6), channel_id=1, source_target_pairs={{0,2},{1,3},{2,0},{3,1},{4,6},{5,7},{6,4},{7,5},{8,10},{9,11},{10,... | collective-permute-start | bytes 5308424 | tf_op jit(solution)/shard_map/ppermute | solution.py:32
  356.7 41.8 %collective-permute-start.28 = (bf16[768,512]{1,0:T(8,128)(2,1)S(1)}, bf16[768,512]{1,0:T(8,128)(2,1)}, u32[]{:S(2)}, u32[]{:S(2)}) collective-permute-start(bf16[768,512]{1,0:T(8,128)(2,1)S(1)} %add_convert_fusion.5), channel_id=1, source_target_pairs={{0,16},{4,20},{8,24},{12,28},{16,0},{20,4},{24,8},{28,12},{1,17},{... | collective-permute-start | bytes 2359304 | tf_op jit(solution)/shard_map/ppermute | solution.py:32
  356.7 41.8 %collective-permute-start.31 = (bf16[768,512]{1,0:T(8,128)(2,1)S(1)}, bf16[768,512]{1,0:T(8,128)(2,1)}, u32[]{:S(2)}, u32[]{:S(2)}) collective-permute-start(bf16[768,512]{1,0:T(8,128)(2,1)S(1)} %copy-done.22), channel_id=1, source_target_pairs={{0,8},{4,12},{8,0},{12,4},{16,24},{20,28},{24,16},{28,20},{1,9},{5... | collective-permute-start | bytes 2359304 | tf_op jit(solution)/shard_map/ppermute | solution.py:32
  398.5 13.8 %collective-permute-start.34 = (bf16[384,768]{1,0:T(8,128)(2,1)}, bf16[384,768]{1,0:T(8,128)(2,1)}, u32[]{:S(2)}, u32[]{:S(2)}) collective-permute-start(bf16[384,768]{1,0:T(8,128)(2,1)} %get-tuple-element.230), channel_id=1, source_target_pairs={{0,1},{1,0},{2,3},{3,2},{4,5},{5,4},{6,7},{7,6},{8,9},{9,8},{10,11... | collective-permute-start | bytes 1769480 | tf_op jit(solution)/shard_map/ppermute | solution.py:32
  399.0 14.7 %collective-permute-start.33 = (bf16[384,768]{1,0:T(8,128)(2,1)}, bf16[384,768]{1,0:T(8,128)(2,1)}, u32[]{:S(2)}, u32[]{:S(2)}) collective-permute-start(bf16[384,768]{1,0:T(8,128)(2,1)} %get-tuple-element.228), channel_id=1, source_target_pairs={{0,2},{1,3},{2,0},{3,1},{4,6},{5,7},{6,4},{7,5},{8,10},{9,11},{10,... | collective-permute-start | bytes 1769480 | tf_op jit(solution)/shard_map/ppermute | solution.py:32
  399.5 40.3 %collective-permute-start.39 = (bf16[768,512]{1,0:T(8,128)(2,1)}, bf16[768,512]{1,0:T(8,128)(2,1)S(1)}, u32[]{:S(2)}, u32[]{:S(2)}) collective-permute-start(bf16[768,512]{1,0:T(8,128)(2,1)} %get-tuple-element.246), channel_id=1, source_target_pairs={{0,8},{4,12},{8,0},{12,4},{16,24},{20,28},{24,16},{28,20},{1,9},{5... | collective-permute-start | bytes 2359304 | tf_op jit(solution)/shard_map/ppermute | solution.py:32
  399.5 28.0 %collective-permute-start.32 = (bf16[384,768]{1,0:T(8,128)(2,1)}, bf16[384,768]{1,0:T(8,128)(2,1)S(1)}, u32[]{:S(2)}, u32[]{:S(2)}) collective-permute-start(bf16[384,768]{1,0:T(8,128)(2,1)} %get-tuple-element.226), channel_id=1, source_target_pairs={{0,16},{4,20},{8,24},{12,28},{16,0},{20,4},{24,8},{28,12},{1,17},{... | collective-permute-start | bytes 1769480 | tf_op jit(solution)/shard_map/ppermute | solution.py:32
  418.4 39.8 %collective-permute-start.38 = (bf16[768,1024]{1,0:T(8,128)(2,1)S(1)}, bf16[768,1024]{1,0:T(8,128)(2,1)S(1)}, u32[]{:S(2)}, u32[]{:S(2)}) collective-permute-start(bf16[768,1024]{1,0:T(8,128)(2,1)S(1)} %pad_maximum_fusion.8), channel_id=1, source_target_pairs={{0,4},{4,0},{8,12},{12,8},{16,20},{20,16},{24,28},{28,24},{1,5},{5... | collective-permute-start | bytes 4718600 | tf_op jit(solution)/shard_map/ppermute | solution.py:32
  428.9 7.2 %collective-permute-start.36 = (f32[384]{0:T(512)S(1)}, f32[384]{0:T(512)S(1)}, u32[]{:S(2)}, u32[]{:S(2)}) collective-permute-start(f32[384]{0:T(512)S(1)} %multiply_reduce_fusion), channel_id=1, source_target_pairs={{0,1},{1,0},{2,3},{3,2},{4,5},{5,4},{6,7},{7,6},{8,9},{9,8},{10,11... | collective-permute-start | bytes 4616 | tf_op jit(solution)/shard_map/ppermute | solution.py:32
  430.3 26.0 %collective-permute-start.35 = (bf16[384,768]{1,0:T(8,128)(2,1)S(1)}, bf16[384,768]{1,0:T(8,128)(2,1)S(1)}, u32[]{:S(2)}, u32[]{:S(2)}) collective-permute-start(bf16[384,768]{1,0:T(8,128)(2,1)S(1)} %add_convert_fusion.9), channel_id=1, source_target_pairs={{0,16},{4,20},{8,24},{12,28},{16,0},{20,4},{24,8},{28,12},{1,17},{... | collective-permute-start | bytes 1769480 | tf_op jit(solution)/shard_map/ppermute | solution.py:32
  436.1 3.7 collective-permute-start.37
  441.3 16.9 %collective-permute-start.40 = (bf16[384,1024]{1,0:T(8,128)(2,1)S(1)}, bf16[384,1024]{1,0:T(8,128)(2,1)S(1)}, u32[]{:S(2)}, u32[]{:S(2)}) collective-permute-start(bf16[384,1024]{1,0:T(8,128)(2,1)S(1)} %get-tuple-element.300), channel_id=1, source_target_pairs={{0,4},{4,0},{8,12},{12,8},{16,20},{20,16},{24,28},{28,24},{1,5},{5... | collective-permute-start | bytes 2359304 | tf_op jit(solution)/shard_map/ppermute | solution.py:32
  (25 other events, 130.2 us)

commit v12 on v10

--- a/solution.py
+++ b/solution.py
@@ -244,10 +244,7 @@
 
     g_down_far = z_far(g_down_4)
     g_gate_4 = shrink(*g_gate_4)
-    input_got, in_all, gate_grad, up_grad, hidden = fence(
-        across(input_sib[:row_limit]), in_all, gate_grad, up_grad, hidden
-    )
-    input_got = cat(input_got, across(input_sib[row_limit:]))
+    input_got = across(input_sib)
     g_up = mm_first(in_all, up_grad).astype(BF16)
     expert_sum = (mm_last(hidden[:table], down) + expert_got.astype(F32)).astype(BF16)
     input_sum = (input_part(slice(None, table)) + input_got.astype(F32)).astype(BF16)

time: 453 us -> 456 us (level)
  other arithmetic: 45.5 us -> 55.5 us
  waiting for transfers between devices: 234 us -> 228 us
    another operation x1, other arithmetic: 2 us -> 12.5 us  [local(): gate_all = jnp.stack(gate_own + gate_far)]
    ppermute x42 -> x41, waiting for transfers between devices: 234 us -> 228 us  [swap(): return lax.ppermute(value, axis, [(i, i ^ distance) for i in range(size)])]
    ppermute x42 -> x41, starting transfers between devices: 41.8 us -> 41.6 us  [swap(): return lax.ppermute(value, axis, [(i, i ^ distance) for i in range(size)])]
  transfers between devices with their start and end apart: 42 -> 41, of which waited for: 20 -> 21; matrix products, arithmetic and copies ran while one was open for 33% -> 34% of each run, Pallas kernels for 0% -> 0%
where the time goes in v12:
time: 456 us; the launch traced here: 449 us
  waiting for transfers between devices  228 us (50%)
  matrix products  84.2 us (18%)
  other arithmetic  55.5 us (12%)
  starting transfers between devices  41.6 us (9%)
  local copies, waits for them, and re-layouts  37.9 us (8%)
    ppermute x41, waiting for transfers between devices, swap(): return lax.ppermute(value, axis, [(i, i ^ distance) for i in range(size)])  228 us
    dot_general x16, matrix products, dot(): lax.dot_general(left, right, (dims, ((), ())), preferred_element_type=F32)  84.2 us
    ppermute x41, starting transfers between devices, swap(): return lax.ppermute(value, axis, [(i, i ^ distance) for i in range(size)])  41.6 us
    concatenate x5, other arithmetic, cat(): return jnp.concatenate(values, axis=0)  13.5 us
    another operation x1, other arithmetic, local(): gate_all = jnp.stack(gate_own + gate_far)  12.5 us
  transfers between devices with their start and end apart: 41, of which 21 were waited for; matrix products, arithmetic and copies ran while one was open for 34% of the time, Pallas kernels for 0%

profile of v12, /device:TPU:0, one launch (start us, length us, event | category | flops | bytes accessed | tf_op | source)
XLA Modules:
  0.0 448.8 jit_solution(12102393821892807607)
XLA Ops:
  0.7 2.4 constant_dynamic-slice_fusion.18
  3.1 4.0 collective-permute-start
  9.7 5.9 %convolution_convert_fusion.5 = bf16[384,3072]{1,0:T(8,128)(2,1)} fusion(bf16[768,3072]{1,0:T(8,128)(2,1)} %param.7, s32[768]{0:T(1024)S(1)} %add_bitcast_fusion, pred[768]{0:T(1024)(128)(4,1)S(1)} %fusion.28), kind=kOutput, calls=%fused_computation.11 | convolution fusion | flops 1813708800 | bytes 7081728 | tf_op jit(solution)/shard_map/dot_general | solution.py:11
  15.6 4.2 multiply_convert_fusion
  25.7 16.2 %collective-permute-done = bf16[384,1024]{1,0:T(8,128)(2,1)} collective-permute-done((bf16[384,1024]{1,0:T(8,128)(2,1)}, bf16[384,1024]{1,0:T(8,128)(2,1)}, u32[]{:S(2)}, u32[]{:S(2)}) %collective-permute-start) | collective-permute-done | bytes 786464 | tf_op jit(solution)/shard_map/ppermute | solution.py:28
  44.0 2.4 collective-permute-start.6
  52.3 34.8 %collective-permute-done.6 = bf16[384,1024]{1,0:T(8,128)(2,1)S(1)} collective-permute-done((bf16[384,1024]{1,0:T(8,128)(2,1)}, bf16[384,1024]{1,0:T(8,128)(2,1)S(1)}, u32[]{:S(2)}, u32[]{:S(2)}) %collective-permute-start.6) | collective-permute-done | bytes 786464 | tf_op jit(solution)/shard_map/ppermute | solution.py:28
  87.1 10.2 %collective-permute-done.2 = bf16[768,768]{1,0:T(8,128)(2,1)} collective-permute-done((bf16[768,768]{1,0:T(8,128)(2,1)}, bf16[768,768]{1,0:T(8,128)(2,1)}, u32[]{:S(2)}, u32[]{:S(2)}) %collective-permute-start.2) | collective-permute-done | bytes 1179680 | tf_op jit(solution)/shard_map/ppermute | solution.py:28
  97.4 2.6 collective-permute-start.10
  100.9 3.0 collective-permute-start.7
  103.9 12.5 %pad_maximum_fusion.2 = bf16[4,384,1024]{2,1,0:T(8,128)(2,1)S(1)} fusion(bf16[1,384,1024]{2,1,0:T(8,128)(2,1)} %bitcast.100, bf16[1,384,1024]{2,1,0:T(8,128)(2,1)} %bitcast.4, bf16[1,384,1024]{2,1,0:T(8,128)(2,1)} %bitcast.3, bf16[1,384,1024]{2,1,0:T(8,128)(2,1)S(1)} %bitcast.96), kind=kLoop, calls=%fused_computation.12 | loop fusion | flops 4718592 | bytes 6291456 | tf_op jit(solution)/shard_map/stack | solution.py:182
  118.0 30.2 %collective-permute-done.7 = bf16[768,512]{1,0:T(8,128)(2,1)} collective-permute-done((bf16[768,512]{1,0:T(8,128)(2,1)}, bf16[768,512]{1,0:T(8,128)(2,1)}, u32[]{:S(2)}, u32[]{:S(2)}) %collective-permute-start.7) | collective-permute-done | bytes 786464 | tf_op jit(solution)/shard_map/ppermute | solution.py:28
  148.2 3.5 collective-permute-done.8
  151.8 3.1 collective-permute-start.12
  155.9 2.6 broadcast_select_fusion.10
  158.4 2.6 broadcast_select_fusion.11
  161.4 2.0 broadcast.31.clone
  169.4 6.1 %pad_maximum_fusion = bf16[1536,3072]{1,0:T(8,128)(2,1)S(1)} fusion(bf16[384,3072]{1,0:T(8,128)(2,1)S(1)} %collective-permute-done.14, bf16[384,3072]{1,0:T(8,128)(2,1)} %collective-permute-done.3, bf16[384,768]{1,0:T(8,128)(2,1)S(1)} %get-tuple-element.241, bf16[384,768]{1,0:T(8,128)(2,1)S(1)} %get-tuple-element.240, ...), kind=kLoop, calls=%fused_computation | loop fusion | flops 66060288 | bytes 18874368 | tf_op jit(solution)/shard_map/concatenate | solution.py:48
  175.5 6.1 %pad_maximum_fusion.1 = bf16[1536,3072]{1,0:T(8,128)(2,1)S(1)} fusion(bf16[384,3072]{1,0:T(8,128)(2,1)S(1)} %collective-permute-done.15, bf16[384,3072]{1,0:T(8,128)(2,1)} %collective-permute-done.4, bf16[384,768]{1,0:T(8,128)(2,1)S(1)} %get-tuple-element.244, bf16[384,768]{1,0:T(8,128)(2,1)S(1)} %get-tuple-element.243, ...), kind=kLoop, calls=%fused_computation.1 | loop fusion | flops 66060288 | bytes 18874368 | tf_op jit(solution)/shard_map/concatenate | solution.py:48
  181.6 5.1 %fusion.32 = f32[1536,512]{1,0:T(8,128)S(1)} fusion(bf16[1536,3072]{1,0:T(8,128)(2,1)S(1)} %pad_maximum_fusion, bf16[3072,512]{1,0:T(8,128)(2,1)S(1)} %bitcast.90), kind=kOutput, calls=%fused_computation.185 | convolution fusion | flops 4831838208 | bytes 15728640 | tf_op jit(solution)/shard_map/dot_general | solution.py:11
  186.7 3.5 collective-permute-done.12
  194.2 7.3 %multiply_convert_fusion.3 = (bf16[1536,512]{1,0:T(8,128)(2,1)S(1)}, f32[1536,512]{1,0:T(8,128)}) fusion(f32[1536,512]{1,0:T(8,128)S(1)} %fusion.32, bf16[1536,3072]{1,0:T(8,128)(2,1)S(1)} %pad_maximum_fusion, bf16[3072,512]{1,0:T(8,128)(2,1)S(1)} %bitcast.97), kind=kOutput, calls=%fused_computation.15 | convolution fusion | flops 4836556800 | bytes 20447232 | tf_op jit(solution)/shard_map/dot_general | solution.py:11
  201.5 5.5 %convolution_convert_fusion.3 = bf16[3072,512]{1,0:T(8,128)(2,1)S(1)} fusion(bf16[1536,3072]{1,0:T(8,128)(2,1)S(1)} %pad_maximum_fusion.1, bf16[1536,512]{1,0:T(8,128)(2,1)S(1)} %get-tuple-element.158), kind=kOutput, calls=%fused_computation.9 | convolution fusion | flops 4833411072 | bytes 14155776 | tf_op jit(solution)/shard_map/dot_general | solution.py:11
  207.0 2.5 collective-permute-done.17
  209.5 2.1 bitcast_dynamic-update-slice_fusion.2
  211.7 2.1 bitcast_dynamic-update-slice_fusion.1
  214.7 6.7 %convolution_convert_fusion = bf16[768,3072]{1,0:T(8,128)(2,1)} fusion(bf16[3072,512]{1,0:T(8,128)(2,1)} %bitcast.24, bf16[1536,512]{1,0:T(8,128)(2,1)S(1)} %get-tuple-element.158), kind=kOutput, calls=%fused_computation.5 | convolution fusion | flops 2418278400 | bytes 8650752 | tf_op jit(solution)/shard_map/dot_general | solution.py:11
  224.9 10.1 %multiply_convert_fusion.1 = (bf16[1536,512]{1,0:T(8,128)(2,1)S(1)}, bf16[1536,512]{1,0:T(8,128)(2,1)}) fusion(f32[1536,512]{1,0:T(8,128)} %copy-done.35, f32[1536,512]{1,0:T(8,128)} %get-tuple-element.157, bf16[1536,3072]{1,0:T(8,128)(2,1)S(1)} %pad_maximum_fusion.1, bf16[3072,512]{1,0:T(8,128)(2,1)} %bitcast.24), kind=kOutput, calls=%fused_computation.13 | convolution fusion | flops 4842061824 | bytes 22020096 | tf_op jit(solution)/shard_map/dot_general | solution.py:11
  235.1 5.2 %fusion.11 = f32[768,3072]{1,0:T(8,128)} fusion(bf16[3072,512]{1,0:T(8,128)(2,1)S(1)} %bitcast.98, bf16[1536,512]{1,0:T(8,128)(2,1)S(1)} %get-tuple-element.168), kind=kOutput, calls=%fused_computation.73 | convolution fusion | flops 2415919104 | bytes 13369344 | tf_op jit(solution)/shard_map/dot_general | solution.py:11
  240.3 5.5 %convolution_convert_fusion.2 = bf16[3072,512]{1,0:T(8,128)(2,1)S(1)} fusion(bf16[1536,3072]{1,0:T(8,128)(2,1)S(1)} %pad_maximum_fusion, bf16[1536,512]{1,0:T(8,128)(2,1)S(1)} %copy-done.11), kind=kOutput, calls=%fused_computation.8 | convolution fusion | flops 4833411072 | bytes 14155776 | tf_op jit(solution)/shard_map/dot_general | solution.py:11
  245.7 5.6 %add_convert_fusion.2 = bf16[768,3072]{1,0:T(8,128)(2,1)S(1)} fusion(f32[768,3072]{1,0:T(8,128)} %fusion.11, bf16[3072,512]{1,0:T(8,128)(2,1)S(1)} %bitcast.91, bf16[1536,512]{1,0:T(8,128)(2,1)} %get-tuple-element.167), kind=kOutput, calls=%fused_computation.4 | convolution fusion | flops 2420637696 | bytes 18087936 | tf_op jit(solution)/shard_map/dot_general | solution.py:11
  251.3 8.6 %collective-permute-done.20 = bf16[768,512]{1,0:T(8,128)(2,1)S(1)} collective-permute-done((bf16[768,512]{1,0:T(8,128)(2,1)}, bf16[768,512]{1,0:T(8,128)(2,1)S(1)}, u32[]{:S(2)}, u32[]{:S(2)}) %collective-permute-start.20) | collective-permute-done | bytes 786464 | tf_op jit(solution)/shard_map/ppermute | solution.py:28
  259.9 2.5 add_convert_fusion.8
  266.8 6.2 %add_convert_fusion = bf16[768,3072]{1,0:T(8,128)(2,1)S(1)} fusion(bf16[768,3072]{1,0:T(8,128)(2,1)} %collective-permute-done.18, bf16[3072,512]{1,0:T(8,128)(2,1)} %bitcast.24, bf16[1536,512]{1,0:T(8,128)(2,1)} %copy-done.34), kind=kOutput, calls=%fused_computation.2 | convolution fusion | flops 2422996992 | bytes 13369344 | tf_op jit(solution)/shard_map/dot_general | solution.py:11
  276.0 5.6 %convolution_convert_fusion.1 = bf16[3072,512]{1,0:T(8,128)(2,1)S(1)} fusion(bf16[1536,3072]{1,0:T(8,128)(2,1)S(1)} %pad_maximum_fusion, bf16[1536,512]{1,0:T(8,128)(2,1)S(1)} %copy-done.33), kind=kOutput, calls=%fused_computation.7 | convolution fusion | flops 4833411072 | bytes 14155776 | tf_op jit(solution)/shard_map/dot_general | solution.py:11
  286.1 2.6 fusion.15
  288.8 5.0 %add_convert_fusion.1 = bf16[768,3072]{1,0:T(8,128)(2,1)S(1)} fusion(bf16[768,3072]{1,0:T(8,128)(2,1)} %collective-permute-done.22, f32[768,3072]{1,0:T(8,128)S(1)} %fusion.15, bf16[3072,512]{1,0:T(8,128)(2,1)S(1)} %bitcast.92, bf16[1536,512]{1,0:T(8,128)(2,1)} %get-tuple-element.167), kind=kOutput, calls=%fused_computation.3 | convolution fusion | flops 2425356288 | bytes 22806528 | tf_op jit(solution)/shard_map/dot_general | solution.py:11
  293.8 5.9 %collective-permute-done.23 = bf16[768,512]{1,0:T(8,128)(2,1)} collective-permute-done((bf16[768,512]{1,0:T(8,128)(2,1)}, bf16[768,512]{1,0:T(8,128)(2,1)}, u32[]{:S(2)}, u32[]{:S(2)}) %collective-permute-start.23) | collective-permute-done | bytes 786464 | tf_op jit(solution)/shard_map/ppermute | solution.py:28
  299.7 3.7 collective-permute-done.21
  309.6 22.7 %collective-permute-done.25 = bf16[384,1536]{1,0:T(8,128)(2,1)S(1)} collective-permute-done((bf16[384,1536]{1,0:T(8,128)(2,1)S(1)}, bf16[384,1536]{1,0:T(8,128)(2,1)S(1)}, u32[]{:S(2)}, u32[]{:S(2)}) %collective-permute-start.25) | collective-permute-done | bytes 1179680 | tf_op jit(solution)/shard_map/ppermute | solution.py:28
  334.2 8.7 %collective-permute-done.24 = bf16[768,512]{1,0:T(8,128)(2,1)S(1)} collective-permute-done((bf16[768,512]{1,0:T(8,128)(2,1)S(1)}, bf16[768,512]{1,0:T(8,128)(2,1)S(1)}, u32[]{:S(2)}, u32[]{:S(2)}) %collective-permute-start.24) | collective-permute-done | bytes 786464 | tf_op jit(solution)/shard_map/ppermute | solution.py:28
  346.5 37.2 %collective-permute-done.30 = bf16[384,2304]{1,0:T(8,128)(2,1)S(1)} collective-permute-done((bf16[384,2304]{1,0:T(8,128)(2,1)S(1)}, bf16[384,2304]{1,0:T(8,128)(2,1)S(1)}, u32[]{:S(2)}, u32[]{:S(2)}) %collective-permute-start.30) | collective-permute-done | bytes 1769504 | tf_op jit(solution)/shard_map/ppermute | solution.py:28
  388.7 11.7 %collective-permute-done.34 = bf16[384,768]{1,0:T(8,128)(2,1)} collective-permute-done((bf16[384,768]{1,0:T(8,128)(2,1)}, bf16[384,768]{1,0:T(8,128)(2,1)}, u32[]{:S(2)}, u32[]{:S(2)}) %collective-permute-start.34) | collective-permute-done | bytes 589856 | tf_op jit(solution)/shard_map/ppermute | solution.py:28
  406.6 9.0 %collective-permute-done.32 = bf16[384,768]{1,0:T(8,128)(2,1)S(1)} collective-permute-done((bf16[384,768]{1,0:T(8,128)(2,1)}, bf16[384,768]{1,0:T(8,128)(2,1)S(1)}, u32[]{:S(2)}, u32[]{:S(2)}) %collective-permute-start.32) | collective-permute-done | bytes 589856 | tf_op jit(solution)/shard_map/ppermute | solution.py:28
  418.4 3.4 collective-permute-start.35
  421.8 2.0 convolution_convert_fusion.7
  425.7 2.0 collective-permute-done.37
  430.4 14.1 %collective-permute-done.35 = bf16[384,768]{1,0:T(8,128)(2,1)S(1)} collective-permute-done((bf16[384,768]{1,0:T(8,128)(2,1)S(1)}, bf16[384,768]{1,0:T(8,128)(2,1)S(1)}, u32[]{:S(2)}, u32[]{:S(2)}) %collective-permute-start.35) | collective-permute-done | bytes 589856 | tf_op jit(solution)/shard_map/ppermute | solution.py:28
  (217 shorter events, 80.9 us)
Async XLA Ops:
  3.1 38.8 %collective-permute-start = (bf16[384,1024]{1,0:T(8,128)(2,1)}, bf16[384,1024]{1,0:T(8,128)(2,1)}, u32[]{:S(2)}, u32[]{:S(2)}) collective-permute-start(bf16[384,1024]{1,0:T(8,128)(2,1)} %get-tuple-element.303), channel_id=1, source_target_pairs={{0,16},{4,20},{8,24},{12,28},{16,0},{20,4},{24,8},{28,12},{1,17},{... | collective-permute-start | bytes 2359304 | tf_op jit(solution)/shard_map/ppermute | solution.py:28
  7.1 34.8 %collective-permute-start.1 = (bf16[384,1024]{1,0:T(8,128)(2,1)S(1)}, bf16[384,1024]{1,0:T(8,128)(2,1)}, u32[]{:S(2)}, u32[]{:S(2)}) collective-permute-start(bf16[384,1024]{1,0:T(8,128)(2,1)S(1)} %get-tuple-element.125), channel_id=1, source_target_pairs={{0,8},{4,12},{8,0},{12,4},{16,24},{20,28},{24,16},{28,20},{1,9},{5... | collective-permute-start | bytes 2359304 | tf_op jit(solution)/shard_map/ppermute | solution.py:28
  41.9 5.8 %collective-permute-start.5 = (bf16[768,1024]{1,0:T(8,128)(2,1)S(1)}, bf16[768,1024]{1,0:T(8,128)(2,1)}, u32[]{:S(2)}, u32[]{:S(2)}) collective-permute-start(bf16[768,1024]{1,0:T(8,128)(2,1)S(1)} %maximum_maximum_fusion), channel_id=1, source_target_pairs={{0,4},{4,0},{8,12},{12,8},{16,20},{20,16},{24,28},{28,24},{1,5},{5... | collective-permute-start | bytes 4718600 | tf_op jit(solution)/shard_map/ppermute | solution.py:28
  41.9 55.4 %collective-permute-start.3 = (bf16[384,3072]{1,0:T(8,128)(2,1)}, bf16[384,3072]{1,0:T(8,128)(2,1)}, u32[]{:S(2)}, u32[]{:S(2)}) collective-permute-start(bf16[384,3072]{1,0:T(8,128)(2,1)} %convolution_convert_fusion.5), channel_id=1, source_target_pairs={{0,4},{4,0},{8,12},{12,8},{16,20},{20,16},{24,28},{28,24},{1,5},{5... | collective-permute-start | bytes 7077896 | tf_op jit(solution)/shard_map/ppermute | solution.py:28
  42.4 54.9 %collective-permute-start.4 = (bf16[384,3072]{1,0:T(8,128)(2,1)}, bf16[384,3072]{1,0:T(8,128)(2,1)}, u32[]{:S(2)}, u32[]{:S(2)}) collective-permute-start(bf16[384,3072]{1,0:T(8,128)(2,1)} %get-tuple-element.121), channel_id=1, source_target_pairs={{0,4},{4,0},{8,12},{12,8},{16,20},{20,16},{24,28},{28,24},{1,5},{5... | collective-permute-start | bytes 7077896 | tf_op jit(solution)/shard_map/ppermute | solution.py:28
  42.4 54.9 %collective-permute-start.2 = (bf16[768,768]{1,0:T(8,128)(2,1)}, bf16[768,768]{1,0:T(8,128)(2,1)}, u32[]{:S(2)}, u32[]{:S(2)}) collective-permute-start(bf16[768,768]{1,0:T(8,128)(2,1)} %pad_maximum_fusion.9), channel_id=1, source_target_pairs={{0,16},{4,20},{8,24},{12,28},{16,0},{20,4},{24,8},{28,12},{1,17},{... | collective-permute-start | bytes 3538952 | tf_op jit(solution)/shard_map/ppermute | solution.py:28
  44.0 43.1 %collective-permute-start.6 = (bf16[384,1024]{1,0:T(8,128)(2,1)}, bf16[384,1024]{1,0:T(8,128)(2,1)S(1)}, u32[]{:S(2)}, u32[]{:S(2)}) collective-permute-start(bf16[384,1024]{1,0:T(8,128)(2,1)} %collective-permute-done), channel_id=1, source_target_pairs={{0,8},{4,12},{8,0},{12,4},{16,24},{20,28},{24,16},{28,20},{1,9},{5... | collective-permute-start | bytes 2359304 | tf_op jit(solution)/shard_map/ppermute | solution.py:28
  97.3 54.4 %collective-permute-start.11 = (bf16[768,1024]{1,0:T(8,128)(2,1)S(1)}, bf16[768,1024]{1,0:T(8,128)(2,1)}, u32[]{:S(2)}, u32[]{:S(2)}) collective-permute-start(bf16[768,1024]{1,0:T(8,128)(2,1)S(1)} %pad_maximum_fusion.7), channel_id=1, source_target_pairs={{0,8},{4,12},{8,0},{12,4},{16,24},{20,28},{24,16},{28,20},{1,9},{5... | collective-permute-start | bytes 4718600 | tf_op jit(solution)/shard_map/ppermute | solution.py:28
  97.4 50.8 %collective-permute-start.10 = (bf16[768,768]{1,0:T(8,128)(2,1)}, bf16[768,768]{1,0:T(8,128)(2,1)}, u32[]{:S(2)}, u32[]{:S(2)}) collective-permute-start(bf16[768,768]{1,0:T(8,128)(2,1)} %collective-permute-done.2), channel_id=1, source_target_pairs={{0,3},{1,2},{2,1},{3,0},{4,7},{5,6},{6,5},{7,4},{8,11},{9,10},{10,... | collective-permute-start | bytes 3538952 | tf_op jit(solution)/shard_map/ppermute | solution.py:28
  99.9 51.7 %collective-permute-start.8 = (bf16[768,768]{1,0:T(8,128)(2,1)}, bf16[768,768]{1,0:T(8,128)(2,1)}, u32[]{:S(2)}, u32[]{:S(2)}) collective-permute-start(bf16[768,768]{1,0:T(8,128)(2,1)} %collective-permute-done.2), channel_id=1, source_target_pairs={{0,1},{1,0},{2,3},{3,2},{4,5},{5,4},{6,7},{7,6},{8,9},{9,8},{10,11... | collective-permute-start | bytes 3538952 | tf_op jit(solution)/shard_map/ppermute | solution.py:28
  100.5 51.2 %collective-permute-start.9 = (bf16[768,768]{1,0:T(8,128)(2,1)}, bf16[768,768]{1,0:T(8,128)(2,1)}, u32[]{:S(2)}, u32[]{:S(2)}) collective-permute-start(bf16[768,768]{1,0:T(8,128)(2,1)} %collective-permute-done.2), channel_id=1, source_target_pairs={{0,2},{1,3},{2,0},{3,1},{4,6},{5,7},{6,4},{7,5},{8,10},{9,11},{10,... | collective-permute-start | bytes 3538952 | tf_op jit(solution)/shard_map/ppermute | solution.py:28
  100.9 47.2 %collective-permute-start.7 = (bf16[768,512]{1,0:T(8,128)(2,1)}, bf16[768,512]{1,0:T(8,128)(2,1)}, u32[]{:S(2)}, u32[]{:S(2)}) collective-permute-start(bf16[768,512]{1,0:T(8,128)(2,1)} %maximum_select_fusion.2), channel_id=1, source_target_pairs={{0,16},{4,20},{8,24},{12,28},{16,0},{20,4},{24,8},{28,12},{1,17},{... | collective-permute-start | bytes 2359304 | tf_op jit(solution)/shard_map/ppermute | solution.py:28
  151.7 4.2 collective-permute-start.13
  151.8 38.4 %collective-permute-start.12 = (bf16[768,512]{1,0:T(8,128)(2,1)}, bf16[768,512]{1,0:T(8,128)(2,1)}, u32[]{:S(2)}, u32[]{:S(2)}) collective-permute-start(bf16[768,512]{1,0:T(8,128)(2,1)} %maximum_select_fusion.3), channel_id=1, source_target_pairs={{0,16},{4,20},{8,24},{12,28},{16,0},{20,4},{24,8},{28,12},{1,17},{... | collective-permute-start | bytes 2359304 | tf_op jit(solution)/shard_map/ppermute | solution.py:28
  154.8 35.7 %collective-permute-start.16 = (bf16[768,512]{1,0:T(8,128)(2,1)}, bf16[768,512]{1,0:T(8,128)(2,1)S(1)}, u32[]{:S(2)}, u32[]{:S(2)}) collective-permute-start(bf16[768,512]{1,0:T(8,128)(2,1)} %collective-permute-done.7), channel_id=1, source_target_pairs={{0,8},{4,12},{8,0},{12,4},{16,24},{20,28},{24,16},{28,20},{1,9},{5... | collective-permute-start | bytes 2359304 | tf_op jit(solution)/shard_map/ppermute | solution.py:28
  161.3 8.1 %collective-permute-start.14 = (bf16[384,3072]{1,0:T(8,128)(2,1)S(1)}, bf16[384,3072]{1,0:T(8,128)(2,1)S(1)}, u32[]{:S(2)}, u32[]{:S(2)}) collective-permute-start(bf16[384,3072]{1,0:T(8,128)(2,1)S(1)} %pad_maximum_fusion.3), channel_id=1, source_target_pairs={{0,4},{4,0},{8,12},{12,8},{16,20},{20,16},{24,28},{28,24},{1,5},{5... | collective-permute-start | bytes 7077896 | tf_op jit(solution)/shard_map/ppermute | solution.py:28
  164.6 10.9 %collective-permute-start.15 = (bf16[384,3072]{1,0:T(8,128)(2,1)S(1)}, bf16[384,3072]{1,0:T(8,128)(2,1)S(1)}, u32[]{:S(2)}, u32[]{:S(2)}) collective-permute-start(bf16[384,3072]{1,0:T(8,128)(2,1)S(1)} %pad_maximum_fusion.4), channel_id=1, source_target_pairs={{0,4},{4,0},{8,12},{12,8},{16,20},{20,16},{24,28},{28,24},{1,5},{5... | collective-permute-start | bytes 7077896 | tf_op jit(solution)/shard_map/ppermute | solution.py:28
  190.5 19.0 %collective-permute-start.17 = (bf16[768,512]{1,0:T(8,128)(2,1)}, bf16[768,512]{1,0:T(8,128)(2,1)S(1)}, u32[]{:S(2)}, u32[]{:S(2)}) collective-permute-start(bf16[768,512]{1,0:T(8,128)(2,1)} %collective-permute-done.12), channel_id=1, source_target_pairs={{0,8},{4,12},{8,0},{12,4},{16,24},{20,28},{24,16},{28,20},{1,9},{5... | collective-permute-start | bytes 2359304 | tf_op jit(solution)/shard_map/ppermute | solution.py:28
  201.5 13.2 %copy-start.34 = (bf16[1536,512]{1,0:T(8,128)(2,1)}, bf16[1536,512]{1,0:T(8,128)(2,1)S(1)}, u32[]{:S(2)}) copy-start(bf16[1536,512]{1,0:T(8,128)(2,1)S(1)} %get-tuple-element.158) | copy-start | bytes 4718596
  221.5 38.5 %collective-permute-start.18 = (bf16[768,3072]{1,0:T(8,128)(2,1)}, bf16[768,3072]{1,0:T(8,128)(2,1)}, u32[]{:S(2)}, u32[]{:S(2)}) collective-permute-start(bf16[768,3072]{1,0:T(8,128)(2,1)} %convolution_convert_fusion), channel_id=1, source_target_pairs={{0,4},{4,0},{8,12},{12,8},{16,20},{20,16},{24,28},{28,24},{1,5},{5... | collective-permute-start | bytes 14155784 | tf_op jit(solution)/shard_map/ppermute | solution.py:28
  222.9 28.4 %collective-permute-start.19 = (bf16[768,512]{1,0:T(8,128)(2,1)}, bf16[768,512]{1,0:T(8,128)(2,1)}, u32[]{:S(2)}, u32[]{:S(2)}) collective-permute-start(bf16[768,512]{1,0:T(8,128)(2,1)} %get-tuple-element.260), channel_id=1, source_target_pairs={{0,8},{4,12},{8,0},{12,4},{16,24},{20,28},{24,16},{28,20},{1,9},{5... | collective-permute-start | bytes 2359304 | tf_op jit(solution)/shard_map/ppermute | solution.py:28
  224.3 35.6 %collective-permute-start.20 = (bf16[768,512]{1,0:T(8,128)(2,1)}, bf16[768,512]{1,0:T(8,128)(2,1)S(1)}, u32[]{:S(2)}, u32[]{:S(2)}) collective-permute-start(bf16[768,512]{1,0:T(8,128)(2,1)} %get-tuple-element.258), channel_id=1, source_target_pairs={{0,8},{4,12},{8,0},{12,4},{16,24},{20,28},{24,16},{28,20},{1,9},{5... | collective-permute-start | bytes 2359304 | tf_op jit(solution)/shard_map/ppermute | solution.py:28
  262.5 26.3 %collective-permute-start.22 = (bf16[768,3072]{1,0:T(8,128)(2,1)S(1)}, bf16[768,3072]{1,0:T(8,128)(2,1)}, u32[]{:S(2)}, u32[]{:S(2)}) collective-permute-start(bf16[768,3072]{1,0:T(8,128)(2,1)S(1)} %add_convert_fusion.2), channel_id=1, source_target_pairs={{0,4},{4,0},{8,12},{12,8},{16,20},{20,16},{24,28},{28,24},{1,5},{5... | collective-permute-start | bytes 14155784 | tf_op jit(solution)/shard_map/ppermute | solution.py:28
  264.2 35.5 %collective-permute-start.23 = (bf16[768,512]{1,0:T(8,128)(2,1)}, bf16[768,512]{1,0:T(8,128)(2,1)}, u32[]{:S(2)}, u32[]{:S(2)}) collective-permute-start(bf16[768,512]{1,0:T(8,128)(2,1)} %get-tuple-element.252), channel_id=1, source_target_pairs={{0,8},{4,12},{8,0},{12,4},{16,24},{20,28},{24,16},{28,20},{1,9},{5... | collective-permute-start | bytes 2359304 | tf_op jit(solution)/shard_map/ppermute | solution.py:28
  265.6 37.8 %collective-permute-start.21 = (bf16[768,512]{1,0:T(8,128)(2,1)}, bf16[768,512]{1,0:T(8,128)(2,1)}, u32[]{:S(2)}, u32[]{:S(2)}) collective-permute-start(bf16[768,512]{1,0:T(8,128)(2,1)} %add_convert_fusion.8), channel_id=1, source_target_pairs={{0,16},{4,20},{8,24},{12,28},{16,0},{20,4},{24,8},{28,12},{1,17},{... | collective-permute-start | bytes 2359304 | tf_op jit(solution)/shard_map/ppermute | solution.py:28
  305.0 27.3 %collective-permute-start.25 = (bf16[384,1536]{1,0:T(8,128)(2,1)S(1)}, bf16[384,1536]{1,0:T(8,128)(2,1)S(1)}, u32[]{:S(2)}, u32[]{:S(2)}) collective-permute-start(bf16[384,1536]{1,0:T(8,128)(2,1)S(1)} %copy-done.18), channel_id=1, source_target_pairs={{0,1},{1,0},{2,3},{3,2},{4,5},{5,4},{6,7},{7,6},{8,9},{9,8},{10,11... | collective-permute-start | bytes 3538952 | tf_op jit(solution)/shard_map/ppermute | solution.py:28
  306.5 27.0 %collective-permute-start.26 = (bf16[384,1536]{1,0:T(8,128)(2,1)S(1)}, bf16[384,1536]{1,0:T(8,128)(2,1)S(1)}, u32[]{:S(2)}, u32[]{:S(2)}) collective-permute-start(bf16[384,1536]{1,0:T(8,128)(2,1)S(1)} %copy-done.17), channel_id=1, source_target_pairs={{0,2},{1,3},{2,0},{3,1},{4,6},{5,7},{6,4},{7,5},{8,10},{9,11},{10,... | collective-permute-start | bytes 3538952 | tf_op jit(solution)/shard_map/ppermute | solution.py:28
  308.1 34.8 %collective-permute-start.24 = (bf16[768,512]{1,0:T(8,128)(2,1)S(1)}, bf16[768,512]{1,0:T(8,128)(2,1)S(1)}, u32[]{:S(2)}, u32[]{:S(2)}) collective-permute-start(bf16[768,512]{1,0:T(8,128)(2,1)S(1)} %add_convert_fusion.7), channel_id=1, source_target_pairs={{0,16},{4,20},{8,24},{12,28},{16,0},{20,4},{24,8},{28,12},{1,17},{... | collective-permute-start | bytes 2359304 | tf_op jit(solution)/shard_map/ppermute | solution.py:28
  308.4 35.4 %collective-permute-start.27 = (bf16[768,512]{1,0:T(8,128)(2,1)}, bf16[768,512]{1,0:T(8,128)(2,1)S(1)}, u32[]{:S(2)}, u32[]{:S(2)}) collective-permute-start(bf16[768,512]{1,0:T(8,128)(2,1)} %get-tuple-element.185), channel_id=1, source_target_pairs={{0,8},{4,12},{8,0},{12,4},{16,24},{20,28},{24,16},{28,20},{1,9},{5... | collective-permute-start | bytes 2359304 | tf_op jit(solution)/shard_map/ppermute | solution.py:28
  309.0 23.3 %copy-start.3 = (bf16[384,3072]{1,0:T(8,128)(2,1)S(1)}, bf16[384,3072]{1,0:T(8,128)(2,1)}, u32[]{:S(2)}) copy-start(bf16[384,3072]{1,0:T(8,128)(2,1)} %copy-done.2) | copy-start | bytes 7077892
  309.6 23.9 %copy-start.1 = (bf16[384,3072]{1,0:T(8,128)(2,1)S(1)}, bf16[384,3072]{1,0:T(8,128)(2,1)}, u32[]{:S(2)}) copy-start(bf16[384,3072]{1,0:T(8,128)(2,1)} %copy-done) | copy-start | bytes 7077892
  344.0 39.7 %collective-permute-start.30 = (bf16[384,2304]{1,0:T(8,128)(2,1)S(1)}, bf16[384,2304]{1,0:T(8,128)(2,1)S(1)}, u32[]{:S(2)}, u32[]{:S(2)}) collective-permute-start(bf16[384,2304]{1,0:T(8,128)(2,1)S(1)} %pad_maximum_fusion.5), channel_id=1, source_target_pairs={{0,1},{1,0},{2,3},{3,2},{4,5},{5,4},{6,7},{7,6},{8,9},{9,8},{10,11... | collective-permute-start | bytes 5308424 | tf_op jit(solution)/shard_map/ppermute | solution.py:28
  344.6 40.6 %collective-permute-start.29 = (bf16[384,2304]{1,0:T(8,128)(2,1)S(1)}, bf16[384,2304]{1,0:T(8,128)(2,1)S(1)}, u32[]{:S(2)}, u32[]{:S(2)}) collective-permute-start(bf16[384,2304]{1,0:T(8,128)(2,1)S(1)} %pad_maximum_fusion.6), channel_id=1, source_target_pairs={{0,2},{1,3},{2,0},{3,1},{4,6},{5,7},{6,4},{7,5},{8,10},{9,11},{10,... | collective-permute-start | bytes 5308424 | tf_op jit(solution)/shard_map/ppermute | solution.py:28
  345.0 41.6 %collective-permute-start.28 = (bf16[768,512]{1,0:T(8,128)(2,1)S(1)}, bf16[768,512]{1,0:T(8,128)(2,1)}, u32[]{:S(2)}, u32[]{:S(2)}) collective-permute-start(bf16[768,512]{1,0:T(8,128)(2,1)S(1)} %add_convert_fusion.6), channel_id=1, source_target_pairs={{0,16},{4,20},{8,24},{12,28},{16,0},{20,4},{24,8},{28,12},{1,17},{... | collective-permute-start | bytes 2359304 | tf_op jit(solution)/shard_map/ppermute | solution.py:28
  345.0 41.6 %collective-permute-start.31 = (bf16[768,512]{1,0:T(8,128)(2,1)S(1)}, bf16[768,512]{1,0:T(8,128)(2,1)}, u32[]{:S(2)}, u32[]{:S(2)}) collective-permute-start(bf16[768,512]{1,0:T(8,128)(2,1)S(1)} %copy-done.22), channel_id=1, source_target_pairs={{0,8},{4,12},{8,0},{12,4},{16,24},{20,28},{24,16},{28,20},{1,9},{5... | collective-permute-start | bytes 2359304 | tf_op jit(solution)/shard_map/ppermute | solution.py:28
  386.6 16.4 %copy-start.9 = (bf16[768,512]{1,0:T(8,128)(2,1)S(1)}, bf16[768,512]{1,0:T(8,128)(2,1)}, u32[]{:S(2)}) copy-start(bf16[768,512]{1,0:T(8,128)(2,1)} %get-tuple-element.223) | copy-start | bytes 2359300
  386.6 13.8 %collective-permute-start.34 = (bf16[384,768]{1,0:T(8,128)(2,1)}, bf16[384,768]{1,0:T(8,128)(2,1)}, u32[]{:S(2)}, u32[]{:S(2)}) collective-permute-start(bf16[384,768]{1,0:T(8,128)(2,1)} %get-tuple-element.214), channel_id=1, source_target_pairs={{0,1},{1,0},{2,3},{3,2},{4,5},{5,4},{6,7},{7,6},{8,9},{9,8},{10,11... | collective-permute-start | bytes 1769480 | tf_op jit(solution)/shard_map/ppermute | solution.py:28
  387.2 14.4 %collective-permute-start.33 = (bf16[384,768]{1,0:T(8,128)(2,1)}, bf16[384,768]{1,0:T(8,128)(2,1)}, u32[]{:S(2)}, u32[]{:S(2)}) collective-permute-start(bf16[384,768]{1,0:T(8,128)(2,1)} %get-tuple-element.212), channel_id=1, source_target_pairs={{0,2},{1,3},{2,0},{3,1},{4,6},{5,7},{6,4},{7,5},{8,10},{9,11},{10,... | collective-permute-start | bytes 1769480 | tf_op jit(solution)/shard_map/ppermute | solution.py:28
  387.6 40.0 %collective-permute-start.39 = (bf16[768,512]{1,0:T(8,128)(2,1)}, bf16[768,512]{1,0:T(8,128)(2,1)S(1)}, u32[]{:S(2)}, u32[]{:S(2)}) collective-permute-start(bf16[768,512]{1,0:T(8,128)(2,1)} %get-tuple-element.230), channel_id=1, source_target_pairs={{0,8},{4,12},{8,0},{12,4},{16,24},{20,28},{24,16},{28,20},{1,9},{5... | collective-permute-start | bytes 2359304 | tf_op jit(solution)/shard_map/ppermute | solution.py:28
  387.6 27.9 %collective-permute-start.32 = (bf16[384,768]{1,0:T(8,128)(2,1)}, bf16[384,768]{1,0:T(8,128)(2,1)S(1)}, u32[]{:S(2)}, u32[]{:S(2)}) collective-permute-start(bf16[384,768]{1,0:T(8,128)(2,1)} %get-tuple-element.210), channel_id=1, source_target_pairs={{0,16},{4,20},{8,24},{12,28},{16,0},{20,4},{24,8},{28,12},{1,17},{... | collective-permute-start | bytes 1769480 | tf_op jit(solution)/shard_map/ppermute | solution.py:28
  406.2 40.3 %collective-permute-start.38 = (bf16[768,1024]{1,0:T(8,128)(2,1)S(1)}, bf16[768,1024]{1,0:T(8,128)(2,1)S(1)}, u32[]{:S(2)}, u32[]{:S(2)}) collective-permute-start(bf16[768,1024]{1,0:T(8,128)(2,1)S(1)} %pad_maximum_fusion.8), channel_id=1, source_target_pairs={{0,4},{4,0},{8,12},{12,8},{16,20},{20,16},{24,28},{28,24},{1,5},{5... | collective-permute-start | bytes 4718600 | tf_op jit(solution)/shard_map/ppermute | solution.py:28
  406.3 15.5 %copy-start.24 = (s32[768]{0:T(1024)S(1)}, s32[768]{0:T(1024)}, u32[]{:S(2)}) copy-start(s32[768]{0:T(1024)} %copy-done.23) | copy-start | bytes 9220
  406.3 15.5 %copy-start.27 = (pred[768]{0:T(1024)(128)(4,1)S(1)}, pred[768]{0:T(1024)(128)(4,1)}, u32[]{:S(2)}) copy-start(pred[768]{0:T(1024)(128)(4,1)} %copy-done.26) | copy-start | bytes 2308
  406.3 15.5 %copy-start.30 = (f32[384]{0:T(512)S(1)}, f32[384]{0:T(512)}, u32[]{:S(2)}) copy-start(f32[384]{0:T(512)} %copy-done.29) | copy-start | bytes 4612
  417.0 7.0 %collective-permute-start.36 = (f32[384]{0:T(512)S(1)}, f32[384]{0:T(512)S(1)}, u32[]{:S(2)}, u32[]{:S(2)}) collective-permute-start(f32[384]{0:T(512)S(1)} %multiply_reduce_fusion), channel_id=1, source_target_pairs={{0,1},{1,0},{2,3},{3,2},{4,5},{5,4},{6,7},{7,6},{8,9},{9,8},{10,11... | collective-permute-start | bytes 4616 | tf_op jit(solution)/shard_map/ppermute | solution.py:28
  418.4 26.1 %collective-permute-start.35 = (bf16[384,768]{1,0:T(8,128)(2,1)S(1)}, bf16[384,768]{1,0:T(8,128)(2,1)S(1)}, u32[]{:S(2)}, u32[]{:S(2)}) collective-permute-start(bf16[384,768]{1,0:T(8,128)(2,1)S(1)} %add_convert_fusion.10), channel_id=1, source_target_pairs={{0,16},{4,20},{8,24},{12,28},{16,0},{20,4},{24,8},{28,12},{1,17},{... | collective-permute-start | bytes 1769480 | tf_op jit(solution)/shard_map/ppermute | solution.py:28
  424.0 3.7 collective-permute-start.37
  429.2 17.2 %collective-permute-start.40 = (bf16[384,1024]{1,0:T(8,128)(2,1)S(1)}, bf16[384,1024]{1,0:T(8,128)(2,1)S(1)}, u32[]{:S(2)}, u32[]{:S(2)}) collective-permute-start(bf16[384,1024]{1,0:T(8,128)(2,1)S(1)} %get-tuple-element.286), channel_id=1, source_target_pairs={{0,4},{4,0},{8,12},{12,8},{16,20},{20,16},{24,28},{28,24},{1,5},{5... | collective-permute-start | bytes 2359304 | tf_op jit(solution)/shard_map/ppermute | solution.py:28
  (29 other events, 174.1 us)

commit v13 on v12

--- a/solution.py
+++ b/solution.py
@@ -93,12 +93,12 @@
             blocks = blocks + [got[i * rows : (i + 1) * rows] for i in range(count)]
         return blocks
 
-    def whole_panel(own, away):
-        full = jnp.zeros((n_chip, pair, hid), BF16)
-        for j in range(n_chip // 2):
-            full = lax.dynamic_update_index_in_dim(full, own[j], chip ^ j, 0)
-            full = lax.dynamic_update_index_in_dim(full, away[j], chip ^ j ^ (n_chip // 2), 0)
-        return full.reshape(depth, hid)
+    def put(full, blocks):
+        for j, block in blocks.items():
+            full = lax.dynamic_update_index_in_dim(full, block, chip ^ j, 0)
+        return full
+
+    half_n = n_chip // 2
 
     def block_of(panel, j):
         return lax.dynamic_index_in_dim(panel.reshape(n_chip, pair, hid), chip ^ j, 0, False)
@@ -182,8 +182,11 @@
     gate_all = jnp.stack(gate_own + gate_far)
     gate_mine = lax.dynamic_slice_in_dim(gate_all, core * hid, hid, 2)
     gate_send = lax.dynamic_slice_in_dim(gate_all, (1 - core) * hid, hid, 2)
-    up_4, gate_mine, gate_send, down_1, *rest = fence(
-        up_4, gate_mine, gate_send, down_1, *quarters, *own
+    empty = jnp.zeros((n_chip, pair, hid), BF16)
+    up = put(empty, {0: own[0][:, :hid]})
+    down = put(empty, {0: own[0][:, hid:]})
+    up_4, gate_mine, gate_send, down_1, up, down, *rest = fence(
+        up_4, gate_mine, gate_send, down_1, up, down, *quarters, *own
     )
     quarters, own = rest[: len(quarters)], rest[len(quarters) :]
     up_own, down_own = [b[:, :hid] for b in own], [b[:, hid:] for b in own]
@@ -195,6 +198,9 @@
     for j in range(n_chip):
         gate = lax.dynamic_update_slice(gate, gate_mine[j][None, None], (chip ^ j, core, 0, 0))
         gate = lax.dynamic_update_slice(gate, gate_got[j][None, None], (chip ^ j, 1 - core, 0, 0))
+    up = put(up, {j: up_own[j] for j in range(1, half_n)})
+    up = put(up, {half_n: up_4})
+    down = put(down, {j: down_own[j] for j in range(1, half_n)})
     gate = gate.reshape(depth, hid)
 
     def true_rows(first):
@@ -205,24 +211,27 @@
     in_all = cat(rows_in, in_away, in_sib, in_away_sib)
     out_all = cat(out_grad, out_away, out_sib, out_away_sib)
     gate_pre = mm(in_all, gate)
-    down_4, in_all, out_all, gate_pre, gate, *up_far = fence(
-        down_4, in_all, out_all, gate_pre, gate, *up_far
+    down_4, in_all, out_all, gate_pre, gate, up, down, *up_far = fence(
+        down_4, in_all, out_all, gate_pre, gate, up, down, *up_far
     )
 
     down_far = grow(down_4)
-    up = whole_panel(up_own, up_far)
+    up = put(up, {j + half_n: up_far[j] for j in range(1, half_n)}).reshape(depth, hid)
+    down = put(down, {half_n: down_4})
     up_pre = mm(in_all, up)
     sigmoid_gate = jax.nn.sigmoid(gate_pre)
     hidden = (gate_pre * sigmoid_gate * up_pre).astype(BF16)
     g_down = mm_first(out_all, hidden).astype(BF16)
-    g_down, hidden, up_pre, up, *down_far = fence(g_down, hidden, up_pre, up, *down_far)
+    g_down, hidden, up_pre, up, down, *down_far = fence(
+        g_down, hidden, up_pre, up, down, *down_far
+    )
 
     table = 2 * row_limit
     g_down_4 = first_send(blocks_far(g_down))
     n_kept = len(g_down_4)
     g_down_4 = shrink(*g_down_4)
     g_down_own = shrink(*first_send(blocks_own(g_down)))
-    down = whole_panel(down_own, down_far)
+    down = put(down, {j + half_n: down_far[j] for j in range(1, half_n)}).reshape(depth, hid)
     hidden_grad = mm(out_all, down)
     gate_grad = (
         hidden_grad * up_pre * sigmoid_gate * (1.0 + gate_pre * (1.0 - sigmoid_gate))

time: 456 us -> 451 us (0.989)
  other arithmetic: 55.5 us -> 45.2 us
  waiting for transfers between devices: 228 us -> 235 us
  local copies, waits for them, and re-layouts: 37.9 us -> 32.6 us
    another operation x1, other arithmetic: 12.5 us -> 2.25 us  [local(): gate_all = jnp.stack(gate_own + gate_far)]
    ppermute x41, waiting for transfers between devices: 228 us -> 235 us  [swap(): return lax.ppermute(value, axis, [(i, i ^ distance) for i in range(size)])]
  transfers between devices with their start and end apart: 41 -> 41, of which waited for: 21 -> 22; matrix products, arithmetic and copies ran while one was open for 34% -> 33% of each run, Pallas kernels for 0% -> 0%
where the time goes in v13:
time: 451 us; the launch traced here: 444 us
  waiting for transfers between devices  235 us (52%)
  matrix products  88.1 us (20%)
  other arithmetic  45.2 us (10%)
  starting transfers between devices  41.3 us (9%)
  local copies, waits for them, and re-layouts  32.6 us (7%)
    ppermute x41, waiting for transfers between devices, swap(): return lax.ppermute(value, axis, [(i, i ^ distance) for i in range(size)])  235 us
    dot_general x16, matrix products, dot(): lax.dot_general(left, right, (dims, ((), ())), preferred_element_type=F32)  88.1 us
    ppermute x41, starting transfers between devices, swap(): return lax.ppermute(value, axis, [(i, i ^ distance) for i in range(size)])  41.3 us
    concatenate x5, other arithmetic, cat(): return jnp.concatenate(values, axis=0)  13.6 us
  transfers between devices with their start and end apart: 41, of which 22 were waited for; matrix products, arithmetic and copies ran while one was open for 33% of the time, Pallas kernels for 0%

profile of v13, /device:TPU:0, one launch (start us, length us, event | category | flops | bytes accessed | tf_op | source)
XLA Modules:
  0.0 444.4 jit_solution(15273621708908164285)
XLA Ops:
  0.7 2.4 constant_dynamic-slice_fusion.18
  3.1 4.0 collective-permute-start
  9.7 6.0 %convolution_convert_fusion.5 = bf16[384,3072]{1,0:T(8,128)(2,1)} fusion(bf16[768,3072]{1,0:T(8,128)(2,1)} %param.7, s32[768]{0:T(1024)S(1)} %add_bitcast_fusion, pred[768]{0:T(1024)(128)(4,1)S(1)} %fusion.28), kind=kOutput, calls=%fused_computation.11 | convolution fusion | flops 1813708800 | bytes 7081728 | tf_op jit(solution)/shard_map/dot_general | solution.py:11
  15.6 4.2 multiply_convert_fusion
  25.3 16.6 %collective-permute-done = bf16[384,1024]{1,0:T(8,128)(2,1)} collective-permute-done((bf16[384,1024]{1,0:T(8,128)(2,1)}, bf16[384,1024]{1,0:T(8,128)(2,1)}, u32[]{:S(2)}, u32[]{:S(2)}) %collective-permute-start) | collective-permute-done | bytes 786464 | tf_op jit(solution)/shard_map/ppermute | solution.py:28
  44.0 2.4 collective-permute-start.6
  52.7 34.4 %collective-permute-done.6 = bf16[384,1024]{1,0:T(8,128)(2,1)S(1)} collective-permute-done((bf16[384,1024]{1,0:T(8,128)(2,1)}, bf16[384,1024]{1,0:T(8,128)(2,1)S(1)}, u32[]{:S(2)}, u32[]{:S(2)}) %collective-permute-start.6) | collective-permute-done | bytes 786464 | tf_op jit(solution)/shard_map/ppermute | solution.py:28
  87.1 10.2 %collective-permute-done.2 = bf16[768,768]{1,0:T(8,128)(2,1)} collective-permute-done((bf16[768,768]{1,0:T(8,128)(2,1)}, bf16[768,768]{1,0:T(8,128)(2,1)}, u32[]{:S(2)}, u32[]{:S(2)}) %collective-permute-start.2) | collective-permute-done | bytes 1179680 | tf_op jit(solution)/shard_map/ppermute | solution.py:28
  97.4 2.6 collective-permute-start.10
  100.9 3.0 collective-permute-start.7
  103.9 2.3 pad_maximum_fusion.2
  107.7 2.0 broadcast_in_dim.67.clone.1
  111.0 37.2 %collective-permute-done.7 = bf16[768,512]{1,0:T(8,128)(2,1)S(1)} collective-permute-done((bf16[768,512]{1,0:T(8,128)(2,1)}, bf16[768,512]{1,0:T(8,128)(2,1)S(1)}, u32[]{:S(2)}, u32[]{:S(2)}) %collective-permute-start.7) | collective-permute-done | bytes 786464 | tf_op jit(solution)/shard_map/ppermute | solution.py:28
  148.2 3.5 collective-permute-done.8
  151.9 3.1 collective-permute-start.12
  155.6 2.4 bitcast_dynamic-update-slice_fusion.3
  158.0 2.6 broadcast_select_fusion.10
  160.6 2.6 broadcast_select_fusion.11
  165.0 3.0 collective-permute-done.14
  168.0 6.1 %pad_maximum_fusion = bf16[1536,3072]{1,0:T(8,128)(2,1)S(1)} fusion(bf16[384,3072]{1,0:T(8,128)(2,1)S(1)} %collective-permute-done.14, bf16[384,3072]{1,0:T(8,128)(2,1)} %collective-permute-done.3, bf16[384,768]{1,0:T(8,128)(2,1)S(1)} %get-tuple-element.245, bf16[384,768]{1,0:T(8,128)(2,1)S(1)} %get-tuple-element.244, ...), kind=kLoop, calls=%fused_computation | loop fusion | flops 66060288 | bytes 18874368 | tf_op jit(solution)/shard_map/concatenate | solution.py:48
  174.1 6.1 %pad_maximum_fusion.1 = bf16[1536,3072]{1,0:T(8,128)(2,1)S(1)} fusion(bf16[384,3072]{1,0:T(8,128)(2,1)S(1)} %collective-permute-done.15, bf16[384,3072]{1,0:T(8,128)(2,1)} %collective-permute-done.4, bf16[384,768]{1,0:T(8,128)(2,1)S(1)} %get-tuple-element.248, bf16[384,768]{1,0:T(8,128)(2,1)S(1)} %get-tuple-element.247, ...), kind=kLoop, calls=%fused_computation.1 | loop fusion | flops 66060288 | bytes 18874368 | tf_op jit(solution)/shard_map/concatenate | solution.py:48
  180.2 6.8 %fusion.32 = f32[1536,512]{1,0:T(8,128)} fusion(bf16[1536,3072]{1,0:T(8,128)(2,1)S(1)} %pad_maximum_fusion, bf16[3072,512]{1,0:T(8,128)(2,1)S(1)} %bitcast.90), kind=kOutput, calls=%fused_computation.185 | convolution fusion | flops 4831838208 | bytes 15728640 | tf_op jit(solution)/shard_map/dot_general | solution.py:11
  187.0 3.2 collective-permute-done.12
  191.9 9.2 %multiply_convert_fusion.3 = (bf16[1536,512]{1,0:T(8,128)(2,1)S(1)}, f32[1536,512]{1,0:T(8,128)}) fusion(f32[1536,512]{1,0:T(8,128)} %fusion.32, bf16[1536,3072]{1,0:T(8,128)(2,1)S(1)} %pad_maximum_fusion, bf16[3072,512]{1,0:T(8,128)(2,1)S(1)} %bitcast.97), kind=kOutput, calls=%fused_computation.15 | convolution fusion | flops 4836556800 | bytes 20447232 | tf_op jit(solution)/shard_map/dot_general | solution.py:11
  201.1 5.6 %convolution_convert_fusion.3 = bf16[3072,512]{1,0:T(8,128)(2,1)S(1)} fusion(bf16[1536,3072]{1,0:T(8,128)(2,1)S(1)} %pad_maximum_fusion.1, bf16[1536,512]{1,0:T(8,128)(2,1)S(1)} %get-tuple-element.162), kind=kOutput, calls=%fused_computation.9 | convolution fusion | flops 4833411072 | bytes 14155776 | tf_op jit(solution)/shard_map/dot_general | solution.py:11
  206.8 2.1 bitcast_dynamic-update-slice_fusion.1
  210.6 6.3 %convolution_convert_fusion = bf16[768,3072]{1,0:T(8,128)(2,1)} fusion(bf16[3072,512]{1,0:T(8,128)(2,1)} %bitcast.24, bf16[1536,512]{1,0:T(8,128)(2,1)S(1)} %get-tuple-element.162), kind=kOutput, calls=%fused_computation.5 | convolution fusion | flops 2418278400 | bytes 8650752 | tf_op jit(solution)/shard_map/dot_general | solution.py:11
  220.4 10.2 %multiply_convert_fusion.1 = (bf16[1536,512]{1,0:T(8,128)(2,1)S(1)}, bf16[1536,512]{1,0:T(8,128)(2,1)}) fusion(f32[1536,512]{1,0:T(8,128)} %fusion.32, f32[1536,512]{1,0:T(8,128)} %get-tuple-element.161, bf16[1536,3072]{1,0:T(8,128)(2,1)S(1)} %pad_maximum_fusion.1, bf16[3072,512]{1,0:T(8,128)(2,1)} %bitcast.24), kind=kOutput, calls=%fused_computation.13 | convolution fusion | flops 4842061824 | bytes 22020096 | tf_op jit(solution)/shard_map/dot_general | solution.py:11
  230.6 5.2 %fusion.11 = f32[768,3072]{1,0:T(8,128)} fusion(bf16[3072,512]{1,0:T(8,128)(2,1)S(1)} %bitcast.98, bf16[1536,512]{1,0:T(8,128)(2,1)S(1)} %get-tuple-element.172), kind=kOutput, calls=%fused_computation.73 | convolution fusion | flops 2415919104 | bytes 13369344 | tf_op jit(solution)/shard_map/dot_general | solution.py:11
  235.8 5.5 %convolution_convert_fusion.2 = bf16[3072,512]{1,0:T(8,128)(2,1)S(1)} fusion(bf16[1536,3072]{1,0:T(8,128)(2,1)S(1)} %pad_maximum_fusion, bf16[1536,512]{1,0:T(8,128)(2,1)S(1)} %copy-done.13), kind=kOutput, calls=%fused_computation.8 | convolution fusion | flops 4833411072 | bytes 14155776 | tf_op jit(solution)/shard_map/dot_general | solution.py:11
  241.2 5.8 %add_convert_fusion.2 = bf16[768,3072]{1,0:T(8,128)(2,1)S(1)} fusion(f32[768,3072]{1,0:T(8,128)} %fusion.11, bf16[3072,512]{1,0:T(8,128)(2,1)S(1)} %bitcast.91, bf16[1536,512]{1,0:T(8,128)(2,1)} %get-tuple-element.171), kind=kOutput, calls=%fused_computation.4 | convolution fusion | flops 2420637696 | bytes 18087936 | tf_op jit(solution)/shard_map/dot_general | solution.py:11
  247.0 8.4 %collective-permute-done.20 = bf16[768,512]{1,0:T(8,128)(2,1)S(1)} collective-permute-done((bf16[768,512]{1,0:T(8,128)(2,1)}, bf16[768,512]{1,0:T(8,128)(2,1)S(1)}, u32[]{:S(2)}, u32[]{:S(2)}) %collective-permute-start.20) | collective-permute-done | bytes 786464 | tf_op jit(solution)/shard_map/ppermute | solution.py:28
  255.4 2.5 add_convert_fusion.8
  262.3 6.2 %add_convert_fusion = bf16[768,3072]{1,0:T(8,128)(2,1)S(1)} fusion(bf16[768,3072]{1,0:T(8,128)(2,1)} %collective-permute-done.18, bf16[3072,512]{1,0:T(8,128)(2,1)} %bitcast.24, bf16[1536,512]{1,0:T(8,128)(2,1)} %copy-done.40), kind=kOutput, calls=%fused_computation.2 | convolution fusion | flops 2422996992 | bytes 13369344 | tf_op jit(solution)/shard_map/dot_general | solution.py:11
  271.4 5.5 %convolution_convert_fusion.1 = bf16[3072,512]{1,0:T(8,128)(2,1)S(1)} fusion(bf16[1536,3072]{1,0:T(8,128)(2,1)S(1)} %pad_maximum_fusion, bf16[1536,512]{1,0:T(8,128)(2,1)S(1)} %copy-done.39), kind=kOutput, calls=%fused_computation.7 | convolution fusion | flops 4833411072 | bytes 14155776 | tf_op jit(solution)/shard_map/dot_general | solution.py:11
  281.4 2.6 fusion.15
  284.1 5.2 %add_convert_fusion.1 = bf16[768,3072]{1,0:T(8,128)(2,1)S(1)} fusion(bf16[768,3072]{1,0:T(8,128)(2,1)} %collective-permute-done.22, f32[768,3072]{1,0:T(8,128)S(1)} %fusion.15, bf16[3072,512]{1,0:T(8,128)(2,1)S(1)} %bitcast.92, bf16[1536,512]{1,0:T(8,128)(2,1)} %get-tuple-element.171), kind=kOutput, calls=%fused_computation.3 | convolution fusion | flops 2425356288 | bytes 22806528 | tf_op jit(solution)/shard_map/dot_general | solution.py:11
  289.3 5.8 %collective-permute-done.23 = bf16[768,512]{1,0:T(8,128)(2,1)} collective-permute-done((bf16[768,512]{1,0:T(8,128)(2,1)}, bf16[768,512]{1,0:T(8,128)(2,1)}, u32[]{:S(2)}, u32[]{:S(2)}) %collective-permute-start.23) | collective-permute-done | bytes 786464 | tf_op jit(solution)/shard_map/ppermute | solution.py:28
  295.2 3.7 collective-permute-done.21
  304.9 22.8 %collective-permute-done.25 = bf16[384,1536]{1,0:T(8,128)(2,1)S(1)} collective-permute-done((bf16[384,1536]{1,0:T(8,128)(2,1)S(1)}, bf16[384,1536]{1,0:T(8,128)(2,1)S(1)}, u32[]{:S(2)}, u32[]{:S(2)}) %collective-permute-start.25) | collective-permute-done | bytes 1179680 | tf_op jit(solution)/shard_map/ppermute | solution.py:28
  329.6 8.6 %collective-permute-done.24 = bf16[768,512]{1,0:T(8,128)(2,1)S(1)} collective-permute-done((bf16[768,512]{1,0:T(8,128)(2,1)S(1)}, bf16[768,512]{1,0:T(8,128)(2,1)S(1)}, u32[]{:S(2)}, u32[]{:S(2)}) %collective-permute-start.24) | collective-permute-done | bytes 786464 | tf_op jit(solution)/shard_map/ppermute | solution.py:28
  341.9 37.0 %collective-permute-done.30 = bf16[384,2304]{1,0:T(8,128)(2,1)S(1)} collective-permute-done((bf16[384,2304]{1,0:T(8,128)(2,1)S(1)}, bf16[384,2304]{1,0:T(8,128)(2,1)S(1)}, u32[]{:S(2)}, u32[]{:S(2)}) %collective-permute-start.30) | collective-permute-done | bytes 1769504 | tf_op jit(solution)/shard_map/ppermute | solution.py:28
  384.1 11.5 %collective-permute-done.34 = bf16[384,768]{1,0:T(8,128)(2,1)} collective-permute-done((bf16[384,768]{1,0:T(8,128)(2,1)}, bf16[384,768]{1,0:T(8,128)(2,1)}, u32[]{:S(2)}, u32[]{:S(2)}) %collective-permute-start.34) | collective-permute-done | bytes 589856 | tf_op jit(solution)/shard_map/ppermute | solution.py:28
  401.8 9.2 %collective-permute-done.32 = bf16[384,768]{1,0:T(8,128)(2,1)S(1)} collective-permute-done((bf16[384,768]{1,0:T(8,128)(2,1)}, bf16[384,768]{1,0:T(8,128)(2,1)S(1)}, u32[]{:S(2)}, u32[]{:S(2)}) %collective-permute-start.32) | collective-permute-done | bytes 589856 | tf_op jit(solution)/shard_map/ppermute | solution.py:28
  413.8 3.4 collective-permute-start.35
  417.2 2.0 convolution_convert_fusion.7
  421.0 2.1 collective-permute-done.37
  425.9 14.0 %collective-permute-done.35 = bf16[384,768]{1,0:T(8,128)(2,1)S(1)} collective-permute-done((bf16[384,768]{1,0:T(8,128)(2,1)S(1)}, bf16[384,768]{1,0:T(8,128)(2,1)S(1)}, u32[]{:S(2)}, u32[]{:S(2)}) %collective-permute-start.35) | collective-permute-done | bytes 589856 | tf_op jit(solution)/shard_map/ppermute | solution.py:28
  (226 shorter events, 75.5 us)
Async XLA Ops:
  3.1 38.8 %collective-permute-start = (bf16[384,1024]{1,0:T(8,128)(2,1)}, bf16[384,1024]{1,0:T(8,128)(2,1)}, u32[]{:S(2)}, u32[]{:S(2)}) collective-permute-start(bf16[384,1024]{1,0:T(8,128)(2,1)} %get-tuple-element.309), channel_id=1, source_target_pairs={{0,16},{4,20},{8,24},{12,28},{16,0},{20,4},{24,8},{28,12},{1,17},{... | collective-permute-start | bytes 2359304 | tf_op jit(solution)/shard_map/ppermute | solution.py:28
  7.1 34.8 %collective-permute-start.1 = (bf16[384,1024]{1,0:T(8,128)(2,1)S(1)}, bf16[384,1024]{1,0:T(8,128)(2,1)}, u32[]{:S(2)}, u32[]{:S(2)}) collective-permute-start(bf16[384,1024]{1,0:T(8,128)(2,1)S(1)} %get-tuple-element.127), channel_id=1, source_target_pairs={{0,8},{4,12},{8,0},{12,4},{16,24},{20,28},{24,16},{28,20},{1,9},{5... | collective-permute-start | bytes 2359304 | tf_op jit(solution)/shard_map/ppermute | solution.py:28
  41.9 5.8 %collective-permute-start.5 = (bf16[768,1024]{1,0:T(8,128)(2,1)S(1)}, bf16[768,1024]{1,0:T(8,128)(2,1)}, u32[]{:S(2)}, u32[]{:S(2)}) collective-permute-start(bf16[768,1024]{1,0:T(8,128)(2,1)S(1)} %maximum_maximum_fusion), channel_id=1, source_target_pairs={{0,4},{4,0},{8,12},{12,8},{16,20},{20,16},{24,28},{28,24},{1,5},{5... | collective-permute-start | bytes 4718600 | tf_op jit(solution)/shard_map/ppermute | solution.py:28
  41.9 55.4 %collective-permute-start.3 = (bf16[384,3072]{1,0:T(8,128)(2,1)}, bf16[384,3072]{1,0:T(8,128)(2,1)}, u32[]{:S(2)}, u32[]{:S(2)}) collective-permute-start(bf16[384,3072]{1,0:T(8,128)(2,1)} %convolution_convert_fusion.5), channel_id=1, source_target_pairs={{0,4},{4,0},{8,12},{12,8},{16,20},{20,16},{24,28},{28,24},{1,5},{5... | collective-permute-start | bytes 7077896 | tf_op jit(solution)/shard_map/ppermute | solution.py:28
  42.4 54.9 %collective-permute-start.4 = (bf16[384,3072]{1,0:T(8,128)(2,1)}, bf16[384,3072]{1,0:T(8,128)(2,1)}, u32[]{:S(2)}, u32[]{:S(2)}) collective-permute-start(bf16[384,3072]{1,0:T(8,128)(2,1)} %get-tuple-element.123), channel_id=1, source_target_pairs={{0,4},{4,0},{8,12},{12,8},{16,20},{20,16},{24,28},{28,24},{1,5},{5... | collective-permute-start | bytes 7077896 | tf_op jit(solution)/shard_map/ppermute | solution.py:28
  42.4 54.9 %collective-permute-start.2 = (bf16[768,768]{1,0:T(8,128)(2,1)}, bf16[768,768]{1,0:T(8,128)(2,1)}, u32[]{:S(2)}, u32[]{:S(2)}) collective-permute-start(bf16[768,768]{1,0:T(8,128)(2,1)} %pad_maximum_fusion.9), channel_id=1, source_target_pairs={{0,16},{4,20},{8,24},{12,28},{16,0},{20,4},{24,8},{28,12},{1,17},{... | collective-permute-start | bytes 3538952 | tf_op jit(solution)/shard_map/ppermute | solution.py:28
  44.0 43.1 %collective-permute-start.6 = (bf16[384,1024]{1,0:T(8,128)(2,1)}, bf16[384,1024]{1,0:T(8,128)(2,1)S(1)}, u32[]{:S(2)}, u32[]{:S(2)}) collective-permute-start(bf16[384,1024]{1,0:T(8,128)(2,1)} %collective-permute-done), channel_id=1, source_target_pairs={{0,8},{4,12},{8,0},{12,4},{16,24},{20,28},{24,16},{28,20},{1,9},{5... | collective-permute-start | bytes 2359304 | tf_op jit(solution)/shard_map/ppermute | solution.py:28
  97.3 54.4 %collective-permute-start.11 = (bf16[768,1024]{1,0:T(8,128)(2,1)S(1)}, bf16[768,1024]{1,0:T(8,128)(2,1)}, u32[]{:S(2)}, u32[]{:S(2)}) collective-permute-start(bf16[768,1024]{1,0:T(8,128)(2,1)S(1)} %pad_maximum_fusion.7), channel_id=1, source_target_pairs={{0,8},{4,12},{8,0},{12,4},{16,24},{20,28},{24,16},{28,20},{1,9},{5... | collective-permute-start | bytes 4718600 | tf_op jit(solution)/shard_map/ppermute | solution.py:28
  97.4 50.8 %collective-permute-start.10 = (bf16[768,768]{1,0:T(8,128)(2,1)}, bf16[768,768]{1,0:T(8,128)(2,1)}, u32[]{:S(2)}, u32[]{:S(2)}) collective-permute-start(bf16[768,768]{1,0:T(8,128)(2,1)} %collective-permute-done.2), channel_id=1, source_target_pairs={{0,3},{1,2},{2,1},{3,0},{4,7},{5,6},{6,5},{7,4},{8,11},{9,10},{10,... | collective-permute-start | bytes 3538952 | tf_op jit(solution)/shard_map/ppermute | solution.py:28
  99.9 51.7 %collective-permute-start.8 = (bf16[768,768]{1,0:T(8,128)(2,1)}, bf16[768,768]{1,0:T(8,128)(2,1)}, u32[]{:S(2)}, u32[]{:S(2)}) collective-permute-start(bf16[768,768]{1,0:T(8,128)(2,1)} %collective-permute-done.2), channel_id=1, source_target_pairs={{0,1},{1,0},{2,3},{3,2},{4,5},{5,4},{6,7},{7,6},{8,9},{9,8},{10,11... | collective-permute-start | bytes 3538952 | tf_op jit(solution)/shard_map/ppermute | solution.py:28
  100.5 51.2 %collective-permute-start.9 = (bf16[768,768]{1,0:T(8,128)(2,1)}, bf16[768,768]{1,0:T(8,128)(2,1)}, u32[]{:S(2)}, u32[]{:S(2)}) collective-permute-start(bf16[768,768]{1,0:T(8,128)(2,1)} %collective-permute-done.2), channel_id=1, source_target_pairs={{0,2},{1,3},{2,0},{3,1},{4,6},{5,7},{6,4},{7,5},{8,10},{9,11},{10,... | collective-permute-start | bytes 3538952 | tf_op jit(solution)/shard_map/ppermute | solution.py:28
  100.9 47.2 %collective-permute-start.7 = (bf16[768,512]{1,0:T(8,128)(2,1)}, bf16[768,512]{1,0:T(8,128)(2,1)S(1)}, u32[]{:S(2)}, u32[]{:S(2)}) collective-permute-start(bf16[768,512]{1,0:T(8,128)(2,1)} %maximum_select_fusion.2), channel_id=1, source_target_pairs={{0,16},{4,20},{8,24},{12,28},{16,0},{20,4},{24,8},{28,12},{1,17},{... | collective-permute-start | bytes 2359304 | tf_op jit(solution)/shard_map/ppermute | solution.py:28
  110.9 40.7 %copy-start.4 = (bf16[4,768,512]{2,1,0:T(8,128)(2,1)}, bf16[4,768,512]{2,1,0:T(8,128)(2,1)S(1)}, u32[]{:S(2)}) copy-start(bf16[4,768,512]{2,1,0:T(8,128)(2,1)S(1)} %bitcast_dynamic-update-slice_fusion.7) | copy-start | bytes 9437188
  151.7 6.3 %collective-permute-start.13 = (bf16[4,384,512]{2,1,0:T(8,128)(2,1)}, bf16[4,384,512]{2,1,0:T(8,128)(2,1)S(1)}, u32[]{:S(2)}, u32[]{:S(2)}) collective-permute-start(bf16[4,384,512]{2,1,0:T(8,128)(2,1)} %get-tuple-element.135), channel_id=1, source_target_pairs={{0,4},{4,0},{8,12},{12,8},{16,20},{20,16},{24,28},{28,24},{1,5},{5... | collective-permute-start | bytes 4718600 | tf_op jit(solution)/shard_map/ppermute | solution.py:28
  151.9 38.4 %collective-permute-start.12 = (bf16[768,512]{1,0:T(8,128)(2,1)}, bf16[768,512]{1,0:T(8,128)(2,1)}, u32[]{:S(2)}, u32[]{:S(2)}) collective-permute-start(bf16[768,512]{1,0:T(8,128)(2,1)} %maximum_select_fusion.3), channel_id=1, source_target_pairs={{0,16},{4,20},{8,24},{12,28},{16,0},{20,4},{24,8},{28,12},{1,17},{... | collective-permute-start | bytes 2359304 | tf_op jit(solution)/shard_map/ppermute | solution.py:28
  154.9 35.7 %collective-permute-start.16 = (bf16[768,512]{1,0:T(8,128)(2,1)}, bf16[768,512]{1,0:T(8,128)(2,1)S(1)}, u32[]{:S(2)}, u32[]{:S(2)}) collective-permute-start(bf16[768,512]{1,0:T(8,128)(2,1)} %copy-done.24), channel_id=1, source_target_pairs={{0,8},{4,12},{8,0},{12,4},{16,24},{20,28},{24,16},{28,20},{1,9},{5... | collective-permute-start | bytes 2359304 | tf_op jit(solution)/shard_map/ppermute | solution.py:28
  163.4 4.6 %collective-permute-start.14 = (bf16[384,3072]{1,0:T(8,128)(2,1)S(1)}, bf16[384,3072]{1,0:T(8,128)(2,1)S(1)}, u32[]{:S(2)}, u32[]{:S(2)}) collective-permute-start(bf16[384,3072]{1,0:T(8,128)(2,1)S(1)} %pad_maximum_fusion.3), channel_id=1, source_target_pairs={{0,4},{4,0},{8,12},{12,8},{16,20},{20,16},{24,28},{28,24},{1,5},{5... | collective-permute-start | bytes 7077896 | tf_op jit(solution)/shard_map/ppermute | solution.py:28
  164.6 9.5 %collective-permute-start.15 = (bf16[384,3072]{1,0:T(8,128)(2,1)S(1)}, bf16[384,3072]{1,0:T(8,128)(2,1)S(1)}, u32[]{:S(2)}, u32[]{:S(2)}) collective-permute-start(bf16[384,3072]{1,0:T(8,128)(2,1)S(1)} %pad_maximum_fusion.4), channel_id=1, source_target_pairs={{0,4},{4,0},{8,12},{12,8},{16,20},{20,16},{24,28},{28,24},{1,5},{5... | collective-permute-start | bytes 7077896 | tf_op jit(solution)/shard_map/ppermute | solution.py:28
  190.6 19.0 %collective-permute-start.17 = (bf16[768,512]{1,0:T(8,128)(2,1)}, bf16[768,512]{1,0:T(8,128)(2,1)S(1)}, u32[]{:S(2)}, u32[]{:S(2)}) collective-permute-start(bf16[768,512]{1,0:T(8,128)(2,1)} %collective-permute-done.12), channel_id=1, source_target_pairs={{0,8},{4,12},{8,0},{12,4},{16,24},{20,28},{24,16},{28,20},{1,9},{5... | collective-permute-start | bytes 2359304 | tf_op jit(solution)/shard_map/ppermute | solution.py:28
  216.9 38.5 %collective-permute-start.18 = (bf16[768,3072]{1,0:T(8,128)(2,1)}, bf16[768,3072]{1,0:T(8,128)(2,1)}, u32[]{:S(2)}, u32[]{:S(2)}) collective-permute-start(bf16[768,3072]{1,0:T(8,128)(2,1)} %convolution_convert_fusion), channel_id=1, source_target_pairs={{0,4},{4,0},{8,12},{12,8},{16,20},{20,16},{24,28},{28,24},{1,5},{5... | collective-permute-start | bytes 14155784 | tf_op jit(solution)/shard_map/ppermute | solution.py:28
  218.4 28.6 %collective-permute-start.19 = (bf16[768,512]{1,0:T(8,128)(2,1)}, bf16[768,512]{1,0:T(8,128)(2,1)}, u32[]{:S(2)}, u32[]{:S(2)}) collective-permute-start(bf16[768,512]{1,0:T(8,128)(2,1)} %get-tuple-element.264), channel_id=1, source_target_pairs={{0,8},{4,12},{8,0},{12,4},{16,24},{20,28},{24,16},{28,20},{1,9},{5... | collective-permute-start | bytes 2359304 | tf_op jit(solution)/shard_map/ppermute | solution.py:28
  219.8 35.6 %collective-permute-start.20 = (bf16[768,512]{1,0:T(8,128)(2,1)}, bf16[768,512]{1,0:T(8,128)(2,1)S(1)}, u32[]{:S(2)}, u32[]{:S(2)}) collective-permute-start(bf16[768,512]{1,0:T(8,128)(2,1)} %get-tuple-element.262), channel_id=1, source_target_pairs={{0,8},{4,12},{8,0},{12,4},{16,24},{20,28},{24,16},{28,20},{1,9},{5... | collective-permute-start | bytes 2359304 | tf_op jit(solution)/shard_map/ppermute | solution.py:28
  257.9 26.2 %collective-permute-start.22 = (bf16[768,3072]{1,0:T(8,128)(2,1)S(1)}, bf16[768,3072]{1,0:T(8,128)(2,1)}, u32[]{:S(2)}, u32[]{:S(2)}) collective-permute-start(bf16[768,3072]{1,0:T(8,128)(2,1)S(1)} %add_convert_fusion.2), channel_id=1, source_target_pairs={{0,4},{4,0},{8,12},{12,8},{16,20},{20,16},{24,28},{28,24},{1,5},{5... | collective-permute-start | bytes 14155784 | tf_op jit(solution)/shard_map/ppermute | solution.py:28
  259.6 35.5 %collective-permute-start.23 = (bf16[768,512]{1,0:T(8,128)(2,1)}, bf16[768,512]{1,0:T(8,128)(2,1)}, u32[]{:S(2)}, u32[]{:S(2)}) collective-permute-start(bf16[768,512]{1,0:T(8,128)(2,1)} %get-tuple-element.256), channel_id=1, source_target_pairs={{0,8},{4,12},{8,0},{12,4},{16,24},{20,28},{24,16},{28,20},{1,9},{5... | collective-permute-start | bytes 2359304 | tf_op jit(solution)/shard_map/ppermute | solution.py:28
  261.0 37.8 %collective-permute-start.21 = (bf16[768,512]{1,0:T(8,128)(2,1)}, bf16[768,512]{1,0:T(8,128)(2,1)}, u32[]{:S(2)}, u32[]{:S(2)}) collective-permute-start(bf16[768,512]{1,0:T(8,128)(2,1)} %add_convert_fusion.8), channel_id=1, source_target_pairs={{0,16},{4,20},{8,24},{12,28},{16,0},{20,4},{24,8},{28,12},{1,17},{... | collective-permute-start | bytes 2359304 | tf_op jit(solution)/shard_map/ppermute | solution.py:28
  300.4 27.3 %collective-permute-start.25 = (bf16[384,1536]{1,0:T(8,128)(2,1)S(1)}, bf16[384,1536]{1,0:T(8,128)(2,1)S(1)}, u32[]{:S(2)}, u32[]{:S(2)}) collective-permute-start(bf16[384,1536]{1,0:T(8,128)(2,1)S(1)} %copy-done.22), channel_id=1, source_target_pairs={{0,1},{1,0},{2,3},{3,2},{4,5},{5,4},{6,7},{7,6},{8,9},{9,8},{10,11... | collective-permute-start | bytes 3538952 | tf_op jit(solution)/shard_map/ppermute | solution.py:28
  302.0 27.0 %collective-permute-start.26 = (bf16[384,1536]{1,0:T(8,128)(2,1)S(1)}, bf16[384,1536]{1,0:T(8,128)(2,1)S(1)}, u32[]{:S(2)}, u32[]{:S(2)}) collective-permute-start(bf16[384,1536]{1,0:T(8,128)(2,1)S(1)} %copy-done.21), channel_id=1, source_target_pairs={{0,2},{1,3},{2,0},{3,1},{4,6},{5,7},{6,4},{7,5},{8,10},{9,11},{10,... | collective-permute-start | bytes 3538952 | tf_op jit(solution)/shard_map/ppermute | solution.py:28
  303.4 34.8 %collective-permute-start.24 = (bf16[768,512]{1,0:T(8,128)(2,1)S(1)}, bf16[768,512]{1,0:T(8,128)(2,1)S(1)}, u32[]{:S(2)}, u32[]{:S(2)}) collective-permute-start(bf16[768,512]{1,0:T(8,128)(2,1)S(1)} %add_convert_fusion.7), channel_id=1, source_target_pairs={{0,16},{4,20},{8,24},{12,28},{16,0},{20,4},{24,8},{28,12},{1,17},{... | collective-permute-start | bytes 2359304 | tf_op jit(solution)/shard_map/ppermute | solution.py:28
  303.6 35.4 %collective-permute-start.27 = (bf16[768,512]{1,0:T(8,128)(2,1)}, bf16[768,512]{1,0:T(8,128)(2,1)S(1)}, u32[]{:S(2)}, u32[]{:S(2)}) collective-permute-start(bf16[768,512]{1,0:T(8,128)(2,1)} %get-tuple-element.189), channel_id=1, source_target_pairs={{0,8},{4,12},{8,0},{12,4},{16,24},{20,28},{24,16},{28,20},{1,9},{5... | collective-permute-start | bytes 2359304 | tf_op jit(solution)/shard_map/ppermute | solution.py:28
  304.3 23.4 %copy-start.3 = (bf16[384,3072]{1,0:T(8,128)(2,1)S(1)}, bf16[384,3072]{1,0:T(8,128)(2,1)}, u32[]{:S(2)}) copy-start(bf16[384,3072]{1,0:T(8,128)(2,1)} %copy-done.2) | copy-start | bytes 7077892
  304.9 24.1 %copy-start.1 = (bf16[384,3072]{1,0:T(8,128)(2,1)S(1)}, bf16[384,3072]{1,0:T(8,128)(2,1)}, u32[]{:S(2)}) copy-start(bf16[384,3072]{1,0:T(8,128)(2,1)} %copy-done) | copy-start | bytes 7077892
  339.3 39.7 %collective-permute-start.30 = (bf16[384,2304]{1,0:T(8,128)(2,1)S(1)}, bf16[384,2304]{1,0:T(8,128)(2,1)S(1)}, u32[]{:S(2)}, u32[]{:S(2)}) collective-permute-start(bf16[384,2304]{1,0:T(8,128)(2,1)S(1)} %pad_maximum_fusion.5), channel_id=1, source_target_pairs={{0,1},{1,0},{2,3},{3,2},{4,5},{5,4},{6,7},{7,6},{8,9},{9,8},{10,11... | collective-permute-start | bytes 5308424 | tf_op jit(solution)/shard_map/ppermute | solution.py:28
  339.9 40.6 %collective-permute-start.29 = (bf16[384,2304]{1,0:T(8,128)(2,1)S(1)}, bf16[384,2304]{1,0:T(8,128)(2,1)S(1)}, u32[]{:S(2)}, u32[]{:S(2)}) collective-permute-start(bf16[384,2304]{1,0:T(8,128)(2,1)S(1)} %pad_maximum_fusion.6), channel_id=1, source_target_pairs={{0,2},{1,3},{2,0},{3,1},{4,6},{5,7},{6,4},{7,5},{8,10},{9,11},{10,... | collective-permute-start | bytes 5308424 | tf_op jit(solution)/shard_map/ppermute | solution.py:28
  340.5 41.3 %collective-permute-start.28 = (bf16[768,512]{1,0:T(8,128)(2,1)S(1)}, bf16[768,512]{1,0:T(8,128)(2,1)}, u32[]{:S(2)}, u32[]{:S(2)}) collective-permute-start(bf16[768,512]{1,0:T(8,128)(2,1)S(1)} %add_convert_fusion.6), channel_id=1, source_target_pairs={{0,16},{4,20},{8,24},{12,28},{16,0},{20,4},{24,8},{28,12},{1,17},{... | collective-permute-start | bytes 2359304 | tf_op jit(solution)/shard_map/ppermute | solution.py:28
  340.5 41.3 %collective-permute-start.31 = (bf16[768,512]{1,0:T(8,128)(2,1)S(1)}, bf16[768,512]{1,0:T(8,128)(2,1)}, u32[]{:S(2)}, u32[]{:S(2)}) collective-permute-start(bf16[768,512]{1,0:T(8,128)(2,1)S(1)} %copy-done.28), channel_id=1, source_target_pairs={{0,8},{4,12},{8,0},{12,4},{16,24},{20,28},{24,16},{28,20},{1,9},{5... | collective-permute-start | bytes 2359304 | tf_op jit(solution)/shard_map/ppermute | solution.py:28
  381.8 16.4 %copy-start.11 = (bf16[768,512]{1,0:T(8,128)(2,1)S(1)}, bf16[768,512]{1,0:T(8,128)(2,1)}, u32[]{:S(2)}) copy-start(bf16[768,512]{1,0:T(8,128)(2,1)} %get-tuple-element.227) | copy-start | bytes 2359300
  381.8 13.8 %collective-permute-start.34 = (bf16[384,768]{1,0:T(8,128)(2,1)}, bf16[384,768]{1,0:T(8,128)(2,1)}, u32[]{:S(2)}, u32[]{:S(2)}) collective-permute-start(bf16[384,768]{1,0:T(8,128)(2,1)} %get-tuple-element.218), channel_id=1, source_target_pairs={{0,1},{1,0},{2,3},{3,2},{4,5},{5,4},{6,7},{7,6},{8,9},{9,8},{10,11... | collective-permute-start | bytes 1769480 | tf_op jit(solution)/shard_map/ppermute | solution.py:28
  382.4 14.5 %collective-permute-start.33 = (bf16[384,768]{1,0:T(8,128)(2,1)}, bf16[384,768]{1,0:T(8,128)(2,1)}, u32[]{:S(2)}, u32[]{:S(2)}) collective-permute-start(bf16[384,768]{1,0:T(8,128)(2,1)} %get-tuple-element.216), channel_id=1, source_target_pairs={{0,2},{1,3},{2,0},{3,1},{4,6},{5,7},{6,4},{7,5},{8,10},{9,11},{10,... | collective-permute-start | bytes 1769480 | tf_op jit(solution)/shard_map/ppermute | solution.py:28
  383.0 40.1 %collective-permute-start.39 = (bf16[768,512]{1,0:T(8,128)(2,1)}, bf16[768,512]{1,0:T(8,128)(2,1)S(1)}, u32[]{:S(2)}, u32[]{:S(2)}) collective-permute-start(bf16[768,512]{1,0:T(8,128)(2,1)} %get-tuple-element.234), channel_id=1, source_target_pairs={{0,8},{4,12},{8,0},{12,4},{16,24},{20,28},{24,16},{28,20},{1,9},{5... | collective-permute-start | bytes 2359304 | tf_op jit(solution)/shard_map/ppermute | solution.py:28
  383.0 28.0 %collective-permute-start.32 = (bf16[384,768]{1,0:T(8,128)(2,1)}, bf16[384,768]{1,0:T(8,128)(2,1)S(1)}, u32[]{:S(2)}, u32[]{:S(2)}) collective-permute-start(bf16[384,768]{1,0:T(8,128)(2,1)} %get-tuple-element.214), channel_id=1, source_target_pairs={{0,16},{4,20},{8,24},{12,28},{16,0},{20,4},{24,8},{28,12},{1,17},{... | collective-permute-start | bytes 1769480 | tf_op jit(solution)/shard_map/ppermute | solution.py:28
  401.5 40.4 %collective-permute-start.38 = (bf16[768,1024]{1,0:T(8,128)(2,1)S(1)}, bf16[768,1024]{1,0:T(8,128)(2,1)S(1)}, u32[]{:S(2)}, u32[]{:S(2)}) collective-permute-start(bf16[768,1024]{1,0:T(8,128)(2,1)S(1)} %pad_maximum_fusion.8), channel_id=1, source_target_pairs={{0,4},{4,0},{8,12},{12,8},{16,20},{20,16},{24,28},{28,24},{1,5},{5... | collective-permute-start | bytes 4718600 | tf_op jit(solution)/shard_map/ppermute | solution.py:28
  401.5 15.7 %copy-start.30 = (s32[768]{0:T(1024)S(1)}, s32[768]{0:T(1024)}, u32[]{:S(2)}) copy-start(s32[768]{0:T(1024)} %copy-done.29) | copy-start | bytes 9220
  401.6 15.7 %copy-start.33 = (pred[768]{0:T(1024)(128)(4,1)S(1)}, pred[768]{0:T(1024)(128)(4,1)}, u32[]{:S(2)}) copy-start(pred[768]{0:T(1024)(128)(4,1)} %copy-done.32) | copy-start | bytes 2308
  401.6 15.6 %copy-start.36 = (f32[384]{0:T(512)S(1)}, f32[384]{0:T(512)}, u32[]{:S(2)}) copy-start(f32[384]{0:T(512)} %copy-done.35) | copy-start | bytes 4612
  412.4 7.0 %collective-permute-start.36 = (f32[384]{0:T(512)S(1)}, f32[384]{0:T(512)S(1)}, u32[]{:S(2)}, u32[]{:S(2)}) collective-permute-start(f32[384]{0:T(512)S(1)} %multiply_reduce_fusion), channel_id=1, source_target_pairs={{0,1},{1,0},{2,3},{3,2},{4,5},{5,4},{6,7},{7,6},{8,9},{9,8},{10,11... | collective-permute-start | bytes 4616 | tf_op jit(solution)/shard_map/ppermute | solution.py:28
  413.8 26.0 %collective-permute-start.35 = (bf16[384,768]{1,0:T(8,128)(2,1)S(1)}, bf16[384,768]{1,0:T(8,128)(2,1)S(1)}, u32[]{:S(2)}, u32[]{:S(2)}) collective-permute-start(bf16[384,768]{1,0:T(8,128)(2,1)S(1)} %add_convert_fusion.10), channel_id=1, source_target_pairs={{0,16},{4,20},{8,24},{12,28},{16,0},{20,4},{24,8},{28,12},{1,17},{... | collective-permute-start | bytes 1769480 | tf_op jit(solution)/shard_map/ppermute | solution.py:28
  419.4 3.7 collective-permute-start.37
  424.6 17.1 %collective-permute-start.40 = (bf16[384,1024]{1,0:T(8,128)(2,1)S(1)}, bf16[384,1024]{1,0:T(8,128)(2,1)S(1)}, u32[]{:S(2)}, u32[]{:S(2)}) collective-permute-start(bf16[384,1024]{1,0:T(8,128)(2,1)S(1)} %get-tuple-element.290), channel_id=1, source_target_pairs={{0,4},{4,0},{8,12},{12,8},{16,20},{20,16},{24,28},{28,24},{1,5},{5... | collective-permute-start | bytes 2359304 | tf_op jit(solution)/shard_map/ppermute | solution.py:28
  (34 other events, 190.6 us)

commit v14 on v13

--- a/solution.py
+++ b/solution.py
@@ -230,13 +230,16 @@
     g_down_4 = first_send(blocks_far(g_down))
     n_kept = len(g_down_4)
     g_down_4 = shrink(*g_down_4)
-    g_down_own = shrink(*first_send(blocks_own(g_down)))
+    own_send = first_send(blocks_own(g_down))
     down = put(down, {j + half_n: down_far[j] for j in range(1, half_n)}).reshape(depth, hid)
     hidden_grad = mm(out_all, down)
     gate_grad = (
         hidden_grad * up_pre * sigmoid_gate * (1.0 + gate_pre * (1.0 - sigmoid_gate))
     ).astype(BF16)
     up_grad = (hidden_grad * gate_pre * sigmoid_gate).astype(BF16)
+    gate_grad, up_grad, *rest = fence(gate_grad, up_grad, *g_down_4, *own_send)
+    g_down_4, own_send = done(*rest[:2]), rest[2:]
+    g_down_own = shrink(*own_send)
     g_gate = mm_first(in_all, gate_grad).astype(BF16)
     expert_got = across(mm_last(hidden[table:], down).astype(BF16))
 
@@ -244,11 +247,9 @@
         return mm_last(gate_grad[rows], gate) + mm_last(up_grad[rows], up)
 
     input_sib = input_part(slice(table, None)).astype(BF16)
-    down, gate_grad, up_grad, g_gate, expert_got, input_sib, *rest = fence(
-        down, gate_grad, up_grad, g_gate, expert_got, input_sib, *g_down_4, *g_down_own
-    )
-    g_down_own = rest[2:]
-    g_down_4, input_sib, g_gate = fence(done(*rest[:2]), input_sib, g_gate)
+    down, gate_grad, up_grad, g_gate, expert_got, input_sib, g_down_4, *g_down_own = fence(
+        down, gate_grad, up_grad, g_gate, expert_got, input_sib, g_down_4, *g_down_own
+    )
     g_gate_4, g_gate_own = first_send(blocks_far(g_gate)), first_send(blocks_own(g_gate))
 
     g_down_far = z_far(g_down_4)

time: 451 us -> 442 us (0.980)
  waiting for transfers between devices: 235 us -> 223 us
  matrix products: 88.1 us -> 77.1 us
  starting transfers between devices: 41.3 us -> 48.4 us
  other arithmetic: 45.2 us -> 51.9 us
    ppermute x41, waiting for transfers between devices: 235 us -> 223 us  [swap(): return lax.ppermute(value, axis, [(i, i ^ distance) for i in range(size)])]
    dot_general x16, matrix products: 88.1 us -> 77.1 us  [dot(): lax.dot_general(left, right, (dims, ((), ())), preferred_element_type=F32)]
    ppermute x41, starting transfers between devices: 41.3 us -> 48.4 us  [swap(): return lax.ppermute(value, axis, [(i, i ^ distance) for i in range(size)])]
    convert_element_type x0 -> x1, other arithmetic: none -> 4.7 us  [local(): (input_part(slice(None, table)) + input_got.astype(F32)).astype(BF16)]
  transfers between devices with their start and end apart: 41 -> 41, of which waited for: 22 -> 21; matrix products, arithmetic and copies ran while one was open for 33% -> 34% of each run, Pallas kernels for 0% -> 0%
where the time goes in v14:
time: 442 us; the launch traced here: 436 us
  waiting for transfers between devices  223 us (50%)
  matrix products  77.1 us (17%)
  other arithmetic  51.9 us (12%)
  starting transfers between devices  48.4 us (11%)
  local copies, waits for them, and re-layouts  33.2 us (8%)
    ppermute x41, waiting for transfers between devices, swap(): return lax.ppermute(value, axis, [(i, i ^ distance) for i in range(size)])  223 us
    dot_general x16, matrix products, dot(): lax.dot_general(left, right, (dims, ((), ())), preferred_element_type=F32)  77.1 us
    ppermute x41, starting transfers between devices, swap(): return lax.ppermute(value, axis, [(i, i ^ distance) for i in range(size)])  48.4 us
    concatenate x5, other arithmetic, cat(): return jnp.concatenate(values, axis=0)  13.6 us
  transfers between devices with their start and end apart: 41, of which 21 were waited for; matrix products, arithmetic and copies ran while one was open for 34% of the time, Pallas kernels for 0%

profile of v14, /device:TPU:0, one launch (start us, length us, event | category | flops | bytes accessed | tf_op | source)
XLA Modules:
  0.0 435.6 jit_solution(12211796388943183068)
XLA Ops:
  0.7 2.4 constant_dynamic-slice_fusion.18
  3.1 4.0 collective-permute-start
  9.7 5.9 %convolution_convert_fusion.5 = bf16[384,3072]{1,0:T(8,128)(2,1)} fusion(bf16[768,3072]{1,0:T(8,128)(2,1)} %param.7, s32[768]{0:T(1024)S(1)} %add_bitcast_fusion, pred[768]{0:T(1024)(128)(4,1)S(1)} %fusion.29), kind=kOutput, calls=%fused_computation.11 | convolution fusion | flops 1813708800 | bytes 7081728 | tf_op jit(solution)/shard_map/dot_general | solution.py:11
  15.5 4.3 multiply_convert_fusion
  25.5 16.4 %collective-permute-done = bf16[384,1024]{1,0:T(8,128)(2,1)} collective-permute-done((bf16[384,1024]{1,0:T(8,128)(2,1)}, bf16[384,1024]{1,0:T(8,128)(2,1)}, u32[]{:S(2)}, u32[]{:S(2)}) %collective-permute-start) | collective-permute-done | bytes 786464 | tf_op jit(solution)/shard_map/ppermute | solution.py:28
  44.0 2.4 collective-permute-start.6
  53.5 33.6 %collective-permute-done.6 = bf16[384,1024]{1,0:T(8,128)(2,1)S(1)} collective-permute-done((bf16[384,1024]{1,0:T(8,128)(2,1)}, bf16[384,1024]{1,0:T(8,128)(2,1)S(1)}, u32[]{:S(2)}, u32[]{:S(2)}) %collective-permute-start.6) | collective-permute-done | bytes 786464 | tf_op jit(solution)/shard_map/ppermute | solution.py:28
  87.1 10.2 %collective-permute-done.2 = bf16[768,768]{1,0:T(8,128)(2,1)} collective-permute-done((bf16[768,768]{1,0:T(8,128)(2,1)}, bf16[768,768]{1,0:T(8,128)(2,1)}, u32[]{:S(2)}, u32[]{:S(2)}) %collective-permute-start.2) | collective-permute-done | bytes 1179680 | tf_op jit(solution)/shard_map/ppermute | solution.py:28
  97.4 2.6 collective-permute-start.10
  100.9 3.0 collective-permute-start.7
  103.9 2.3 pad_maximum_fusion.2
  109.7 38.5 %collective-permute-done.7 = bf16[768,512]{1,0:T(8,128)(2,1)S(1)} collective-permute-done((bf16[768,512]{1,0:T(8,128)(2,1)}, bf16[768,512]{1,0:T(8,128)(2,1)S(1)}, u32[]{:S(2)}, u32[]{:S(2)}) %collective-permute-start.7) | collective-permute-done | bytes 786464 | tf_op jit(solution)/shard_map/ppermute | solution.py:28
  148.2 3.5 collective-permute-done.8
  151.9 3.1 collective-permute-start.12
  155.6 2.4 bitcast_dynamic-update-slice_fusion.3
  158.0 2.6 broadcast_select_fusion.10
  160.6 2.6 broadcast_select_fusion.11
  165.9 2.1 collective-permute-done.14
  168.0 6.1 %pad_maximum_fusion = bf16[1536,3072]{1,0:T(8,128)(2,1)S(1)} fusion(bf16[384,3072]{1,0:T(8,128)(2,1)S(1)} %collective-permute-done.14, bf16[384,3072]{1,0:T(8,128)(2,1)} %collective-permute-done.3, bf16[384,768]{1,0:T(8,128)(2,1)S(1)} %get-tuple-element.249, bf16[384,768]{1,0:T(8,128)(2,1)S(1)} %get-tuple-element.248, ...), kind=kLoop, calls=%fused_computation | loop fusion | flops 66060288 | bytes 18874368 | tf_op jit(solution)/shard_map/concatenate | solution.py:48
  174.1 6.1 %pad_maximum_fusion.1 = bf16[1536,3072]{1,0:T(8,128)(2,1)S(1)} fusion(bf16[384,3072]{1,0:T(8,128)(2,1)S(1)} %collective-permute-done.15, bf16[384,3072]{1,0:T(8,128)(2,1)} %collective-permute-done.4, bf16[384,768]{1,0:T(8,128)(2,1)S(1)} %get-tuple-element.252, bf16[384,768]{1,0:T(8,128)(2,1)S(1)} %get-tuple-element.251, ...), kind=kLoop, calls=%fused_computation.1 | loop fusion | flops 66060288 | bytes 18874368 | tf_op jit(solution)/shard_map/concatenate | solution.py:48
  180.2 5.1 %fusion.33 = f32[1536,512]{1,0:T(8,128)S(1)} fusion(bf16[1536,3072]{1,0:T(8,128)(2,1)S(1)} %pad_maximum_fusion, bf16[3072,512]{1,0:T(8,128)(2,1)S(1)} %bitcast.90), kind=kOutput, calls=%fused_computation.186 | convolution fusion | flops 4831838208 | bytes 15728640 | tf_op jit(solution)/shard_map/dot_general | solution.py:11
  185.4 4.9 %collective-permute-done.12 = bf16[768,512]{1,0:T(8,128)(2,1)} collective-permute-done((bf16[768,512]{1,0:T(8,128)(2,1)}, bf16[768,512]{1,0:T(8,128)(2,1)}, u32[]{:S(2)}, u32[]{:S(2)}) %collective-permute-start.12) | collective-permute-done | bytes 786464 | tf_op jit(solution)/shard_map/ppermute | solution.py:28
  193.1 7.0 %multiply_convert_fusion.3 = (bf16[1536,512]{1,0:T(8,128)(2,1)}, f32[1536,512]{1,0:T(8,128)}) fusion(f32[1536,512]{1,0:T(8,128)S(1)} %fusion.33, bf16[1536,3072]{1,0:T(8,128)(2,1)S(1)} %pad_maximum_fusion, bf16[3072,512]{1,0:T(8,128)(2,1)S(1)} %bitcast.100), kind=kOutput, calls=%fused_computation.15 | convolution fusion | flops 4836556800 | bytes 20447232 | tf_op jit(solution)/shard_map/dot_general | solution.py:11
  200.1 7.1 %convolution_convert_fusion.3 = bf16[3072,512]{1,0:T(8,128)(2,1)S(1)} fusion(bf16[1536,3072]{1,0:T(8,128)(2,1)S(1)} %pad_maximum_fusion.1, bf16[1536,512]{1,0:T(8,128)(2,1)} %get-tuple-element.167), kind=kOutput, calls=%fused_computation.9 | convolution fusion | flops 4833411072 | bytes 14155776 | tf_op jit(solution)/shard_map/dot_general | solution.py:11
  212.7 4.4 %convolution_convert_fusion = bf16[768,3072]{1,0:T(8,128)(2,1)} fusion(bf16[3072,512]{1,0:T(8,128)(2,1)S(1)} %bitcast.97, bf16[1536,512]{1,0:T(8,128)(2,1)S(1)} %copy-done.43), kind=kOutput, calls=%fused_computation.5 | convolution fusion | flops 2418278400 | bytes 8650752 | tf_op jit(solution)/shard_map/dot_general | solution.py:11
  217.1 9.3 %multiply_convert_fusion.1 = (bf16[1536,512]{1,0:T(8,128)(2,1)}, bf16[1536,512]{1,0:T(8,128)(2,1)}) fusion(f32[1536,512]{1,0:T(8,128)} %copy-done.45, f32[1536,512]{1,0:T(8,128)} %get-tuple-element.163, bf16[1536,3072]{1,0:T(8,128)(2,1)S(1)} %pad_maximum_fusion.1, bf16[3072,512]{1,0:T(8,128)(2,1)S(1)} %bitcast.98), kind=kOutput, calls=%fused_computation.13 | convolution fusion | flops 4842061824 | bytes 22020096 | tf_op jit(solution)/shard_map/dot_general | solution.py:11
  226.3 2.9 collective-permute-done.18
  231.0 2.3 add_convert_fusion.8
  233.3 2.6 fusion.16
  235.9 6.6 %convolution_convert_fusion.2 = bf16[3072,512]{1,0:T(8,128)(2,1)} fusion(bf16[1536,3072]{1,0:T(8,128)(2,1)S(1)} %pad_maximum_fusion, bf16[1536,512]{1,0:T(8,128)(2,1)S(1)} %copy-done.30), kind=kOutput, calls=%fused_computation.8 | convolution fusion | flops 4833411072 | bytes 14155776 | tf_op jit(solution)/shard_map/dot_general | solution.py:11
  242.6 5.7 %add_convert_fusion.2 = bf16[768,3072]{1,0:T(8,128)(2,1)} fusion(f32[768,3072]{1,0:T(8,128)S(1)} %fusion.16, bf16[3072,512]{1,0:T(8,128)(2,1)S(1)} %bitcast.91, bf16[1536,512]{1,0:T(8,128)(2,1)} %get-tuple-element.175), kind=kOutput, calls=%fused_computation.4 | convolution fusion | flops 2420637696 | bytes 18087936 | tf_op jit(solution)/shard_map/dot_general | solution.py:11
  248.4 3.7 dynamic-slice_bitcast_fusion
  253.7 4.5 %add_convert_fusion = bf16[768,3072]{1,0:T(8,128)(2,1)S(1)} fusion(bf16[768,3072]{1,0:T(8,128)(2,1)} %collective-permute-done.19, bf16[3072,512]{1,0:T(8,128)(2,1)S(1)} %bitcast.99, bf16[1536,512]{1,0:T(8,128)(2,1)S(1)} %copy-done.44), kind=kOutput, calls=%fused_computation.2 | convolution fusion | flops 2422996992 | bytes 13369344 | tf_op jit(solution)/shard_map/dot_general | solution.py:11
  261.2 5.5 %convolution_convert_fusion.1 = bf16[3072,512]{1,0:T(8,128)(2,1)S(1)} fusion(bf16[1536,3072]{1,0:T(8,128)(2,1)S(1)} %pad_maximum_fusion, bf16[1536,512]{1,0:T(8,128)(2,1)S(1)} %copy-done.42), kind=kOutput, calls=%fused_computation.7 | convolution fusion | flops 4833411072 | bytes 14155776 | tf_op jit(solution)/shard_map/dot_general | solution.py:11
  271.1 2.6 fusion.12
  273.8 2.6 fusion.14
  276.5 4.7 %add_convert_fusion.1 = bf16[768,3072]{1,0:T(8,128)(2,1)S(1)} fusion(bf16[768,3072]{1,0:T(8,128)(2,1)} %collective-permute-done.22, f32[768,3072]{1,0:T(8,128)S(1)} %fusion.14, f32[768,3072]{1,0:T(8,128)S(1)} %fusion.12), kind=kLoop, calls=%fused_computation.3 | loop fusion | flops 9437184 | bytes 28311552 | tf_op jit(solution)/shard_map/convert_element_type | solution.py:260
  281.2 7.8 %collective-permute-done.23 = bf16[768,512]{1,0:T(8,128)(2,1)} collective-permute-done((bf16[768,512]{1,0:T(8,128)(2,1)}, bf16[768,512]{1,0:T(8,128)(2,1)}, u32[]{:S(2)}, u32[]{:S(2)}) %collective-permute-start.23) | collective-permute-done | bytes 786464 | tf_op jit(solution)/shard_map/ppermute | solution.py:28
  295.0 2.6 collective-permute-start.27
  298.6 19.6 %collective-permute-done.25 = bf16[384,1536]{1,0:T(8,128)(2,1)S(1)} collective-permute-done((bf16[384,1536]{1,0:T(8,128)(2,1)S(1)}, bf16[384,1536]{1,0:T(8,128)(2,1)S(1)}, u32[]{:S(2)}, u32[]{:S(2)}) %collective-permute-start.25) | collective-permute-done | bytes 1179680 | tf_op jit(solution)/shard_map/ppermute | solution.py:28
  320.0 9.9 %collective-permute-done.24 = bf16[768,512]{1,0:T(8,128)(2,1)S(1)} collective-permute-done((bf16[768,512]{1,0:T(8,128)(2,1)S(1)}, bf16[768,512]{1,0:T(8,128)(2,1)S(1)}, u32[]{:S(2)}, u32[]{:S(2)}) %collective-permute-start.24) | collective-permute-done | bytes 786464 | tf_op jit(solution)/shard_map/ppermute | solution.py:28
  334.7 35.0 %collective-permute-done.30 = bf16[384,2304]{1,0:T(8,128)(2,1)S(1)} collective-permute-done((bf16[384,2304]{1,0:T(8,128)(2,1)S(1)}, bf16[384,2304]{1,0:T(8,128)(2,1)S(1)}, u32[]{:S(2)}, u32[]{:S(2)}) %collective-permute-start.30) | collective-permute-done | bytes 1769504 | tf_op jit(solution)/shard_map/ppermute | solution.py:28
  374.4 3.4 collective-permute-start.32
  377.7 8.6 %collective-permute-done.34 = bf16[384,768]{1,0:T(8,128)(2,1)} collective-permute-done((bf16[384,768]{1,0:T(8,128)(2,1)}, bf16[384,768]{1,0:T(8,128)(2,1)}, u32[]{:S(2)}, u32[]{:S(2)}) %collective-permute-start.34) | collective-permute-done | bytes 589856 | tf_op jit(solution)/shard_map/ppermute | solution.py:28
  393.6 8.3 %collective-permute-done.32 = bf16[384,768]{1,0:T(8,128)(2,1)S(1)} collective-permute-done((bf16[384,768]{1,0:T(8,128)(2,1)}, bf16[384,768]{1,0:T(8,128)(2,1)S(1)}, u32[]{:S(2)}, u32[]{:S(2)}) %collective-permute-start.32) | collective-permute-done | bytes 589856 | tf_op jit(solution)/shard_map/ppermute | solution.py:28
  404.7 3.3 collective-permute-start.35
  411.7 2.1 collective-permute-done.37
  416.7 14.4 %collective-permute-done.35 = bf16[384,768]{1,0:T(8,128)(2,1)S(1)} collective-permute-done((bf16[384,768]{1,0:T(8,128)(2,1)S(1)}, bf16[384,768]{1,0:T(8,128)(2,1)S(1)}, u32[]{:S(2)}, u32[]{:S(2)}) %collective-permute-start.35) | collective-permute-done | bytes 589856 | tf_op jit(solution)/shard_map/ppermute | solution.py:28
  (237 shorter events, 82.9 us)
Async XLA Ops:
  3.1 38.8 %collective-permute-start = (bf16[384,1024]{1,0:T(8,128)(2,1)}, bf16[384,1024]{1,0:T(8,128)(2,1)}, u32[]{:S(2)}, u32[]{:S(2)}) collective-permute-start(bf16[384,1024]{1,0:T(8,128)(2,1)} %get-tuple-element.313), channel_id=1, source_target_pairs={{0,16},{4,20},{8,24},{12,28},{16,0},{20,4},{24,8},{28,12},{1,17},{... | collective-permute-start | bytes 2359304 | tf_op jit(solution)/shard_map/ppermute | solution.py:28
  7.1 34.8 %collective-permute-start.1 = (bf16[384,1024]{1,0:T(8,128)(2,1)S(1)}, bf16[384,1024]{1,0:T(8,128)(2,1)}, u32[]{:S(2)}, u32[]{:S(2)}) collective-permute-start(bf16[384,1024]{1,0:T(8,128)(2,1)S(1)} %get-tuple-element.129), channel_id=1, source_target_pairs={{0,8},{4,12},{8,0},{12,4},{16,24},{20,28},{24,16},{28,20},{1,9},{5... | collective-permute-start | bytes 2359304 | tf_op jit(solution)/shard_map/ppermute | solution.py:28
  41.9 5.8 %collective-permute-start.5 = (bf16[768,1024]{1,0:T(8,128)(2,1)S(1)}, bf16[768,1024]{1,0:T(8,128)(2,1)}, u32[]{:S(2)}, u32[]{:S(2)}) collective-permute-start(bf16[768,1024]{1,0:T(8,128)(2,1)S(1)} %maximum_maximum_fusion), channel_id=1, source_target_pairs={{0,4},{4,0},{8,12},{12,8},{16,20},{20,16},{24,28},{28,24},{1,5},{5... | collective-permute-start | bytes 4718600 | tf_op jit(solution)/shard_map/ppermute | solution.py:28
  41.9 55.4 %collective-permute-start.3 = (bf16[384,3072]{1,0:T(8,128)(2,1)}, bf16[384,3072]{1,0:T(8,128)(2,1)}, u32[]{:S(2)}, u32[]{:S(2)}) collective-permute-start(bf16[384,3072]{1,0:T(8,128)(2,1)} %convolution_convert_fusion.5), channel_id=1, source_target_pairs={{0,4},{4,0},{8,12},{12,8},{16,20},{20,16},{24,28},{28,24},{1,5},{5... | collective-permute-start | bytes 7077896 | tf_op jit(solution)/shard_map/ppermute | solution.py:28
  42.4 54.9 %collective-permute-start.4 = (bf16[384,3072]{1,0:T(8,128)(2,1)}, bf16[384,3072]{1,0:T(8,128)(2,1)}, u32[]{:S(2)}, u32[]{:S(2)}) collective-permute-start(bf16[384,3072]{1,0:T(8,128)(2,1)} %get-tuple-element.125), channel_id=1, source_target_pairs={{0,4},{4,0},{8,12},{12,8},{16,20},{20,16},{24,28},{28,24},{1,5},{5... | collective-permute-start | bytes 7077896 | tf_op jit(solution)/shard_map/ppermute | solution.py:28
  42.4 54.9 %collective-permute-start.2 = (bf16[768,768]{1,0:T(8,128)(2,1)}, bf16[768,768]{1,0:T(8,128)(2,1)}, u32[]{:S(2)}, u32[]{:S(2)}) collective-permute-start(bf16[768,768]{1,0:T(8,128)(2,1)} %pad_maximum_fusion.9), channel_id=1, source_target_pairs={{0,16},{4,20},{8,24},{12,28},{16,0},{20,4},{24,8},{28,12},{1,17},{... | collective-permute-start | bytes 3538952 | tf_op jit(solution)/shard_map/ppermute | solution.py:28
  44.0 43.1 %collective-permute-start.6 = (bf16[384,1024]{1,0:T(8,128)(2,1)}, bf16[384,1024]{1,0:T(8,128)(2,1)S(1)}, u32[]{:S(2)}, u32[]{:S(2)}) collective-permute-start(bf16[384,1024]{1,0:T(8,128)(2,1)} %collective-permute-done), channel_id=1, source_target_pairs={{0,8},{4,12},{8,0},{12,4},{16,24},{20,28},{24,16},{28,20},{1,9},{5... | collective-permute-start | bytes 2359304 | tf_op jit(solution)/shard_map/ppermute | solution.py:28
  97.3 54.4 %collective-permute-start.11 = (bf16[768,1024]{1,0:T(8,128)(2,1)S(1)}, bf16[768,1024]{1,0:T(8,128)(2,1)}, u32[]{:S(2)}, u32[]{:S(2)}) collective-permute-start(bf16[768,1024]{1,0:T(8,128)(2,1)S(1)} %pad_maximum_fusion.7), channel_id=1, source_target_pairs={{0,8},{4,12},{8,0},{12,4},{16,24},{20,28},{24,16},{28,20},{1,9},{5... | collective-permute-start | bytes 4718600 | tf_op jit(solution)/shard_map/ppermute | solution.py:28
  97.4 50.8 %collective-permute-start.10 = (bf16[768,768]{1,0:T(8,128)(2,1)}, bf16[768,768]{1,0:T(8,128)(2,1)}, u32[]{:S(2)}, u32[]{:S(2)}) collective-permute-start(bf16[768,768]{1,0:T(8,128)(2,1)} %collective-permute-done.2), channel_id=1, source_target_pairs={{0,3},{1,2},{2,1},{3,0},{4,7},{5,6},{6,5},{7,4},{8,11},{9,10},{10,... | collective-permute-start | bytes 3538952 | tf_op jit(solution)/shard_map/ppermute | solution.py:28
  99.9 51.7 %collective-permute-start.8 = (bf16[768,768]{1,0:T(8,128)(2,1)}, bf16[768,768]{1,0:T(8,128)(2,1)}, u32[]{:S(2)}, u32[]{:S(2)}) collective-permute-start(bf16[768,768]{1,0:T(8,128)(2,1)} %collective-permute-done.2), channel_id=1, source_target_pairs={{0,1},{1,0},{2,3},{3,2},{4,5},{5,4},{6,7},{7,6},{8,9},{9,8},{10,11... | collective-permute-start | bytes 3538952 | tf_op jit(solution)/shard_map/ppermute | solution.py:28
  100.5 51.2 %collective-permute-start.9 = (bf16[768,768]{1,0:T(8,128)(2,1)}, bf16[768,768]{1,0:T(8,128)(2,1)}, u32[]{:S(2)}, u32[]{:S(2)}) collective-permute-start(bf16[768,768]{1,0:T(8,128)(2,1)} %collective-permute-done.2), channel_id=1, source_target_pairs={{0,2},{1,3},{2,0},{3,1},{4,6},{5,7},{6,4},{7,5},{8,10},{9,11},{10,... | collective-permute-start | bytes 3538952 | tf_op jit(solution)/shard_map/ppermute | solution.py:28
  100.9 47.2 %collective-permute-start.7 = (bf16[768,512]{1,0:T(8,128)(2,1)}, bf16[768,512]{1,0:T(8,128)(2,1)S(1)}, u32[]{:S(2)}, u32[]{:S(2)}) collective-permute-start(bf16[768,512]{1,0:T(8,128)(2,1)} %maximum_select_fusion.2), channel_id=1, source_target_pairs={{0,16},{4,20},{8,24},{12,28},{16,0},{20,4},{24,8},{28,12},{1,17},{... | collective-permute-start | bytes 2359304 | tf_op jit(solution)/shard_map/ppermute | solution.py:28
  109.7 42.0 %copy-start.8 = (bf16[4,768,512]{2,1,0:T(8,128)(2,1)}, bf16[4,768,512]{2,1,0:T(8,128)(2,1)S(1)}, u32[]{:S(2)}) copy-start(bf16[4,768,512]{2,1,0:T(8,128)(2,1)S(1)} %bitcast_dynamic-update-slice_fusion.7) | copy-start | bytes 9437188
  151.7 6.3 %collective-permute-start.13 = (bf16[4,384,512]{2,1,0:T(8,128)(2,1)}, bf16[4,384,512]{2,1,0:T(8,128)(2,1)S(1)}, u32[]{:S(2)}, u32[]{:S(2)}) collective-permute-start(bf16[4,384,512]{2,1,0:T(8,128)(2,1)} %get-tuple-element.137), channel_id=1, source_target_pairs={{0,4},{4,0},{8,12},{12,8},{16,20},{20,16},{24,28},{28,24},{1,5},{5... | collective-permute-start | bytes 4718600 | tf_op jit(solution)/shard_map/ppermute | solution.py:28
  151.9 38.4 %collective-permute-start.12 = (bf16[768,512]{1,0:T(8,128)(2,1)}, bf16[768,512]{1,0:T(8,128)(2,1)}, u32[]{:S(2)}, u32[]{:S(2)}) collective-permute-start(bf16[768,512]{1,0:T(8,128)(2,1)} %maximum_select_fusion.3), channel_id=1, source_target_pairs={{0,16},{4,20},{8,24},{12,28},{16,0},{20,4},{24,8},{28,12},{1,17},{... | collective-permute-start | bytes 2359304 | tf_op jit(solution)/shard_map/ppermute | solution.py:28
  154.9 35.8 %collective-permute-start.16 = (bf16[768,512]{1,0:T(8,128)(2,1)}, bf16[768,512]{1,0:T(8,128)(2,1)}, u32[]{:S(2)}, u32[]{:S(2)}) collective-permute-start(bf16[768,512]{1,0:T(8,128)(2,1)} %copy-done.27), channel_id=1, source_target_pairs={{0,8},{4,12},{8,0},{12,4},{16,24},{20,28},{24,16},{28,20},{1,9},{5... | collective-permute-start | bytes 2359304 | tf_op jit(solution)/shard_map/ppermute | solution.py:28
  163.4 4.6 %collective-permute-start.14 = (bf16[384,3072]{1,0:T(8,128)(2,1)S(1)}, bf16[384,3072]{1,0:T(8,128)(2,1)S(1)}, u32[]{:S(2)}, u32[]{:S(2)}) collective-permute-start(bf16[384,3072]{1,0:T(8,128)(2,1)S(1)} %pad_maximum_fusion.3), channel_id=1, source_target_pairs={{0,4},{4,0},{8,12},{12,8},{16,20},{20,16},{24,28},{28,24},{1,5},{5... | collective-permute-start | bytes 7077896 | tf_op jit(solution)/shard_map/ppermute | solution.py:28
  165.6 8.6 %collective-permute-start.15 = (bf16[384,3072]{1,0:T(8,128)(2,1)S(1)}, bf16[384,3072]{1,0:T(8,128)(2,1)S(1)}, u32[]{:S(2)}, u32[]{:S(2)}) collective-permute-start(bf16[384,3072]{1,0:T(8,128)(2,1)S(1)} %pad_maximum_fusion.4), channel_id=1, source_target_pairs={{0,4},{4,0},{8,12},{12,8},{16,20},{20,16},{24,28},{28,24},{1,5},{5... | collective-permute-start | bytes 7077896 | tf_op jit(solution)/shard_map/ppermute | solution.py:28
  185.4 14.8 %copy-start.45 = (f32[1536,512]{1,0:T(8,128)}, f32[1536,512]{1,0:T(8,128)S(1)}, u32[]{:S(2)}) copy-start(f32[1536,512]{1,0:T(8,128)S(1)} %fusion.33) | copy-start | bytes 9437188
  190.7 18.9 %collective-permute-start.17 = (bf16[768,512]{1,0:T(8,128)(2,1)}, bf16[768,512]{1,0:T(8,128)(2,1)S(1)}, u32[]{:S(2)}, u32[]{:S(2)}) collective-permute-start(bf16[768,512]{1,0:T(8,128)(2,1)} %collective-permute-done.12), channel_id=1, source_target_pairs={{0,8},{4,12},{8,0},{12,4},{16,24},{20,28},{24,16},{28,20},{1,9},{5... | collective-permute-start | bytes 2359304 | tf_op jit(solution)/shard_map/ppermute | solution.py:28
  211.1 18.1 %collective-permute-start.18 = (bf16[768,512]{1,0:T(8,128)(2,1)}, bf16[768,512]{1,0:T(8,128)(2,1)}, u32[]{:S(2)}, u32[]{:S(2)}) collective-permute-start(bf16[768,512]{1,0:T(8,128)(2,1)} %get-tuple-element.268), channel_id=1, source_target_pairs={{0,8},{4,12},{8,0},{12,4},{16,24},{20,28},{24,16},{28,20},{1,9},{5... | collective-permute-start | bytes 2359304 | tf_op jit(solution)/shard_map/ppermute | solution.py:28
  217.1 31.2 %collective-permute-start.19 = (bf16[768,3072]{1,0:T(8,128)(2,1)}, bf16[768,3072]{1,0:T(8,128)(2,1)}, u32[]{:S(2)}, u32[]{:S(2)}) collective-permute-start(bf16[768,3072]{1,0:T(8,128)(2,1)} %convolution_convert_fusion), channel_id=1, source_target_pairs={{0,4},{4,0},{8,12},{12,8},{16,20},{20,16},{24,28},{28,24},{1,5},{5... | collective-permute-start | bytes 14155784 | tf_op jit(solution)/shard_map/ppermute | solution.py:28
  217.1 16.2 %copy-start.11 = (bf16[4,768,512]{2,1,0:T(8,128)(2,1)S(1)}, bf16[4,768,512]{2,1,0:T(8,128)(2,1)}, u32[]{:S(2)}) copy-start(bf16[4,768,512]{2,1,0:T(8,128)(2,1)} %copy-done.10) | copy-start | bytes 9437188
  229.2 19.1 %collective-permute-start.20 = (bf16[768,512]{1,0:T(8,128)(2,1)}, bf16[768,512]{1,0:T(8,128)(2,1)}, u32[]{:S(2)}, u32[]{:S(2)}) collective-permute-start(bf16[768,512]{1,0:T(8,128)(2,1)} %get-tuple-element.173), channel_id=1, source_target_pairs={{0,8},{4,12},{8,0},{12,4},{16,24},{20,28},{24,16},{28,20},{1,9},{5... | collective-permute-start | bytes 2359304 | tf_op jit(solution)/shard_map/ppermute | solution.py:28
  248.3 28.2 %collective-permute-start.22 = (bf16[768,3072]{1,0:T(8,128)(2,1)}, bf16[768,3072]{1,0:T(8,128)(2,1)}, u32[]{:S(2)}, u32[]{:S(2)}) collective-permute-start(bf16[768,3072]{1,0:T(8,128)(2,1)} %add_convert_fusion.2), channel_id=1, source_target_pairs={{0,4},{4,0},{8,12},{12,8},{16,20},{20,16},{24,28},{28,24},{1,5},{5... | collective-permute-start | bytes 14155784 | tf_op jit(solution)/shard_map/ppermute | solution.py:28
  252.1 36.9 %collective-permute-start.23 = (bf16[768,512]{1,0:T(8,128)(2,1)}, bf16[768,512]{1,0:T(8,128)(2,1)}, u32[]{:S(2)}, u32[]{:S(2)}) collective-permute-start(bf16[768,512]{1,0:T(8,128)(2,1)} %get-tuple-element.260), channel_id=1, source_target_pairs={{0,8},{4,12},{8,0},{12,4},{16,24},{20,28},{24,16},{28,20},{1,9},{5... | collective-permute-start | bytes 2359304 | tf_op jit(solution)/shard_map/ppermute | solution.py:28
  252.4 37.7 %collective-permute-start.21 = (bf16[768,512]{1,0:T(8,128)(2,1)}, bf16[768,512]{1,0:T(8,128)(2,1)}, u32[]{:S(2)}, u32[]{:S(2)}) collective-permute-start(bf16[768,512]{1,0:T(8,128)(2,1)} %add_convert_fusion.8), channel_id=1, source_target_pairs={{0,16},{4,20},{8,24},{12,28},{16,0},{20,4},{24,8},{28,12},{1,17},{... | collective-permute-start | bytes 2359304 | tf_op jit(solution)/shard_map/ppermute | solution.py:28
  291.7 26.5 %collective-permute-start.25 = (bf16[384,1536]{1,0:T(8,128)(2,1)S(1)}, bf16[384,1536]{1,0:T(8,128)(2,1)S(1)}, u32[]{:S(2)}, u32[]{:S(2)}) collective-permute-start(bf16[384,1536]{1,0:T(8,128)(2,1)S(1)} %copy-done.25), channel_id=1, source_target_pairs={{0,1},{1,0},{2,3},{3,2},{4,5},{5,4},{6,7},{7,6},{8,9},{9,8},{10,11... | collective-permute-start | bytes 3538952 | tf_op jit(solution)/shard_map/ppermute | solution.py:28
  293.3 26.1 %collective-permute-start.26 = (bf16[384,1536]{1,0:T(8,128)(2,1)S(1)}, bf16[384,1536]{1,0:T(8,128)(2,1)S(1)}, u32[]{:S(2)}, u32[]{:S(2)}) collective-permute-start(bf16[384,1536]{1,0:T(8,128)(2,1)S(1)} %copy-done.24), channel_id=1, source_target_pairs={{0,2},{1,3},{2,0},{3,1},{4,6},{5,7},{6,4},{7,5},{8,10},{9,11},{10,... | collective-permute-start | bytes 3538952 | tf_op jit(solution)/shard_map/ppermute | solution.py:28
  294.7 35.3 %collective-permute-start.24 = (bf16[768,512]{1,0:T(8,128)(2,1)S(1)}, bf16[768,512]{1,0:T(8,128)(2,1)S(1)}, u32[]{:S(2)}, u32[]{:S(2)}) collective-permute-start(bf16[768,512]{1,0:T(8,128)(2,1)S(1)} %add_convert_fusion.7), channel_id=1, source_target_pairs={{0,16},{4,20},{8,24},{12,28},{16,0},{20,4},{24,8},{28,12},{1,17},{... | collective-permute-start | bytes 2359304 | tf_op jit(solution)/shard_map/ppermute | solution.py:28
  295.0 34.9 %collective-permute-start.27 = (bf16[768,512]{1,0:T(8,128)(2,1)}, bf16[768,512]{1,0:T(8,128)(2,1)S(1)}, u32[]{:S(2)}, u32[]{:S(2)}) collective-permute-start(bf16[768,512]{1,0:T(8,128)(2,1)} %get-tuple-element.193), channel_id=1, source_target_pairs={{0,8},{4,12},{8,0},{12,4},{16,24},{20,28},{24,16},{28,20},{1,9},{5... | collective-permute-start | bytes 2359304 | tf_op jit(solution)/shard_map/ppermute | solution.py:28
  298.0 20.2 %copy-start.3 = (bf16[384,3072]{1,0:T(8,128)(2,1)S(1)}, bf16[384,3072]{1,0:T(8,128)(2,1)}, u32[]{:S(2)}) copy-start(bf16[384,3072]{1,0:T(8,128)(2,1)} %copy-done.2) | copy-start | bytes 7077892
  298.6 20.8 %copy-start.1 = (bf16[384,3072]{1,0:T(8,128)(2,1)S(1)}, bf16[384,3072]{1,0:T(8,128)(2,1)}, u32[]{:S(2)}) copy-start(bf16[384,3072]{1,0:T(8,128)(2,1)} %copy-done) | copy-start | bytes 7077892
  330.2 39.6 %collective-permute-start.30 = (bf16[384,2304]{1,0:T(8,128)(2,1)S(1)}, bf16[384,2304]{1,0:T(8,128)(2,1)S(1)}, u32[]{:S(2)}, u32[]{:S(2)}) collective-permute-start(bf16[384,2304]{1,0:T(8,128)(2,1)S(1)} %pad_maximum_fusion.5), channel_id=1, source_target_pairs={{0,1},{1,0},{2,3},{3,2},{4,5},{5,4},{6,7},{7,6},{8,9},{9,8},{10,11... | collective-permute-start | bytes 5308424 | tf_op jit(solution)/shard_map/ppermute | solution.py:28
  330.8 40.5 %collective-permute-start.29 = (bf16[384,2304]{1,0:T(8,128)(2,1)S(1)}, bf16[384,2304]{1,0:T(8,128)(2,1)S(1)}, u32[]{:S(2)}, u32[]{:S(2)}) collective-permute-start(bf16[384,2304]{1,0:T(8,128)(2,1)S(1)} %pad_maximum_fusion.6), channel_id=1, source_target_pairs={{0,2},{1,3},{2,0},{3,1},{4,6},{5,7},{6,4},{7,5},{8,10},{9,11},{10,... | collective-permute-start | bytes 5308424 | tf_op jit(solution)/shard_map/ppermute | solution.py:28
  331.4 41.3 %collective-permute-start.28 = (bf16[768,512]{1,0:T(8,128)(2,1)S(1)}, bf16[768,512]{1,0:T(8,128)(2,1)}, u32[]{:S(2)}, u32[]{:S(2)}) collective-permute-start(bf16[768,512]{1,0:T(8,128)(2,1)S(1)} %add_convert_fusion.6), channel_id=1, source_target_pairs={{0,16},{4,20},{8,24},{12,28},{16,0},{20,4},{24,8},{28,12},{1,17},{... | collective-permute-start | bytes 2359304 | tf_op jit(solution)/shard_map/ppermute | solution.py:28
  332.8 39.9 %collective-permute-start.31 = (bf16[768,512]{1,0:T(8,128)(2,1)S(1)}, bf16[768,512]{1,0:T(8,128)(2,1)}, u32[]{:S(2)}, u32[]{:S(2)}) collective-permute-start(bf16[768,512]{1,0:T(8,128)(2,1)S(1)} %copy-done.29), channel_id=1, source_target_pairs={{0,8},{4,12},{8,0},{12,4},{16,24},{20,28},{24,16},{28,20},{1,9},{5... | collective-permute-start | bytes 2359304 | tf_op jit(solution)/shard_map/ppermute | solution.py:28
  372.7 16.2 %copy-start.15 = (bf16[768,512]{1,0:T(8,128)(2,1)S(1)}, bf16[768,512]{1,0:T(8,128)(2,1)}, u32[]{:S(2)}) copy-start(bf16[768,512]{1,0:T(8,128)(2,1)} %get-tuple-element.231) | copy-start | bytes 2359300
  372.7 13.7 %collective-permute-start.34 = (bf16[384,768]{1,0:T(8,128)(2,1)}, bf16[384,768]{1,0:T(8,128)(2,1)}, u32[]{:S(2)}, u32[]{:S(2)}) collective-permute-start(bf16[384,768]{1,0:T(8,128)(2,1)} %get-tuple-element.222), channel_id=1, source_target_pairs={{0,1},{1,0},{2,3},{3,2},{4,5},{5,4},{6,7},{7,6},{8,9},{9,8},{10,11... | collective-permute-start | bytes 1769480 | tf_op jit(solution)/shard_map/ppermute | solution.py:28
  373.2 14.3 %collective-permute-start.33 = (bf16[384,768]{1,0:T(8,128)(2,1)}, bf16[384,768]{1,0:T(8,128)(2,1)}, u32[]{:S(2)}, u32[]{:S(2)}) collective-permute-start(bf16[384,768]{1,0:T(8,128)(2,1)} %get-tuple-element.220), channel_id=1, source_target_pairs={{0,2},{1,3},{2,0},{3,1},{4,6},{5,7},{6,4},{7,5},{8,10},{9,11},{10,... | collective-permute-start | bytes 1769480 | tf_op jit(solution)/shard_map/ppermute | solution.py:28
  373.9 40.0 %collective-permute-start.39 = (bf16[768,512]{1,0:T(8,128)(2,1)}, bf16[768,512]{1,0:T(8,128)(2,1)S(1)}, u32[]{:S(2)}, u32[]{:S(2)}) collective-permute-start(bf16[768,512]{1,0:T(8,128)(2,1)} %get-tuple-element.238), channel_id=1, source_target_pairs={{0,8},{4,12},{8,0},{12,4},{16,24},{20,28},{24,16},{28,20},{1,9},{5... | collective-permute-start | bytes 2359304 | tf_op jit(solution)/shard_map/ppermute | solution.py:28
  374.4 27.6 %collective-permute-start.32 = (bf16[384,768]{1,0:T(8,128)(2,1)}, bf16[384,768]{1,0:T(8,128)(2,1)S(1)}, u32[]{:S(2)}, u32[]{:S(2)}) collective-permute-start(bf16[384,768]{1,0:T(8,128)(2,1)} %get-tuple-element.218), channel_id=1, source_target_pairs={{0,16},{4,20},{8,24},{12,28},{16,0},{20,4},{24,8},{28,12},{1,17},{... | collective-permute-start | bytes 1769480 | tf_op jit(solution)/shard_map/ppermute | solution.py:28
  393.2 39.8 %collective-permute-start.38 = (bf16[768,1024]{1,0:T(8,128)(2,1)S(1)}, bf16[768,1024]{1,0:T(8,128)(2,1)S(1)}, u32[]{:S(2)}, u32[]{:S(2)}) collective-permute-start(bf16[768,1024]{1,0:T(8,128)(2,1)S(1)} %pad_maximum_fusion.8), channel_id=1, source_target_pairs={{0,4},{4,0},{8,12},{12,8},{16,20},{20,16},{24,28},{28,24},{1,5},{5... | collective-permute-start | bytes 4718600 | tf_op jit(solution)/shard_map/ppermute | solution.py:28
  393.3 14.7 %copy-start.33 = (s32[768]{0:T(1024)S(1)}, s32[768]{0:T(1024)}, u32[]{:S(2)}) copy-start(s32[768]{0:T(1024)} %copy-done.32) | copy-start | bytes 9220
  403.3 6.9 %collective-permute-start.36 = (f32[384]{0:T(512)S(1)}, f32[384]{0:T(512)S(1)}, u32[]{:S(2)}, u32[]{:S(2)}) collective-permute-start(f32[384]{0:T(512)S(1)} %multiply_reduce_fusion), channel_id=1, source_target_pairs={{0,1},{1,0},{2,3},{3,2},{4,5},{5,4},{6,7},{7,6},{8,9},{9,8},{10,11... | collective-permute-start | bytes 4616 | tf_op jit(solution)/shard_map/ppermute | solution.py:28
  404.7 26.3 %collective-permute-start.35 = (bf16[384,768]{1,0:T(8,128)(2,1)S(1)}, bf16[384,768]{1,0:T(8,128)(2,1)S(1)}, u32[]{:S(2)}, u32[]{:S(2)}) collective-permute-start(bf16[384,768]{1,0:T(8,128)(2,1)S(1)} %add_convert_fusion.10), channel_id=1, source_target_pairs={{0,16},{4,20},{8,24},{12,28},{16,0},{20,4},{24,8},{28,12},{1,17},{... | collective-permute-start | bytes 1769480 | tf_op jit(solution)/shard_map/ppermute | solution.py:28
  410.2 3.7 collective-permute-start.37
  415.4 17.5 %collective-permute-start.40 = (bf16[384,1024]{1,0:T(8,128)(2,1)S(1)}, bf16[384,1024]{1,0:T(8,128)(2,1)S(1)}, u32[]{:S(2)}, u32[]{:S(2)}) collective-permute-start(bf16[384,1024]{1,0:T(8,128)(2,1)S(1)} %get-tuple-element.294), channel_id=1, source_target_pairs={{0,4},{4,0},{8,12},{12,8},{16,20},{20,16},{24,28},{28,24},{1,5},{5... | collective-permute-start | bytes 2359304 | tf_op jit(solution)/shard_map/ppermute | solution.py:28
  (39 other events, 217.5 us)

commit v15 on v14

--- a/solution.py
+++ b/solution.py
@@ -240,6 +240,7 @@
     gate_grad, up_grad, *rest = fence(gate_grad, up_grad, *g_down_4, *own_send)
     g_down_4, own_send = done(*rest[:2]), rest[2:]
     g_down_own = shrink(*own_send)
+    g_down_far = z_far(g_down_4)
     g_gate = mm_first(in_all, gate_grad).astype(BF16)
     expert_got = across(mm_last(hidden[table:], down).astype(BF16))
 
@@ -247,12 +248,8 @@
         return mm_last(gate_grad[rows], gate) + mm_last(up_grad[rows], up)
 
     input_sib = input_part(slice(table, None)).astype(BF16)
-    down, gate_grad, up_grad, g_gate, expert_got, input_sib, g_down_4, *g_down_own = fence(
-        down, gate_grad, up_grad, g_gate, expert_got, input_sib, g_down_4, *g_down_own
-    )
     g_gate_4, g_gate_own = first_send(blocks_far(g_gate)), first_send(blocks_own(g_gate))
 
-    g_down_far = z_far(g_down_4)
     g_gate_4 = shrink(*g_gate_4)
     input_got = across(input_sib)
     g_up = mm_first(in_all, up_grad).astype(BF16)
@@ -289,8 +286,9 @@
     send_low, send_high = gone(expert_mine, low), gone(expert_other, high)
     g_up_4, g_up_own = first_send(blocks_far(g_up)), first_send(blocks_own(g_up))
     g_down_far, input_sum, send_low, send_high, *rest = fence(
-        g_down_far, input_sum, send_low, send_high, *g_gate_4, *g_up_4, *g_up_own
-    )
+        g_down_far, input_sum, send_low, send_high, *g_down_own, *g_gate_4, *g_up_4, *g_up_own
+    )
+    g_down_own, rest = rest[:2], rest[2:]
     g_up_own = rest[2 + n_kept :]
     g_gate_4, send_low, send_high, input_sum, *g_up_4 = fence(
         done(*rest[:2]), send_low, send_high, input_sum, *rest[2 : 2 + n_kept]

time: 442 us -> 442 us (level)
  starting transfers between devices: 48.4 us -> 40.2 us
  matrix products: 77.1 us -> 82.1 us
    ppermute x41, starting transfers between devices: 48.4 us -> 40.2 us  [swap(): return lax.ppermute(value, axis, [(i, i ^ distance) for i in range(size)])]
    dot_general x16, matrix products: 77.1 us -> 82.1 us  [dot(): lax.dot_general(left, right, (dims, ((), ())), preferred_element_type=F32)]
  transfers between devices with their start and end apart: 41 -> 41, of which waited for: 21 -> 20; matrix products, arithmetic and copies ran while one was open for 34% -> 35% of each run, Pallas kernels for 0% -> 0%
where the time goes in v15:
time: 442 us; the launch traced here: 435 us
  waiting for transfers between devices  227 us (51%)
  matrix products  82.1 us (19%)
  other arithmetic  48.6 us (11%)
  starting transfers between devices  40.2 us (9%)
  local copies, waits for them, and re-layouts  35 us (8%)
    ppermute x41, waiting for transfers between devices, swap(): return lax.ppermute(value, axis, [(i, i ^ distance) for i in range(size)])  227 us
    dot_general x16, matrix products, dot(): lax.dot_general(left, right, (dims, ((), ())), preferred_element_type=F32)  82.1 us
    ppermute x41, starting transfers between devices, swap(): return lax.ppermute(value, axis, [(i, i ^ distance) for i in range(size)])  40.2 us
    concatenate x5, other arithmetic, cat(): return jnp.concatenate(values, axis=0)  13.6 us
  transfers between devices with their start and end apart: 41, of which 20 were waited for; matrix products, arithmetic and copies ran while one was open for 35% of the time, Pallas kernels for 0%

profile of v15, /device:TPU:0, one launch (start us, length us, event | category | flops | bytes accessed | tf_op | source)
XLA Modules:
  0.0 434.9 jit_solution(11319625324410542813)
XLA Ops:
  0.7 2.4 constant_dynamic-slice_fusion.18
  3.1 4.0 collective-permute-start
  9.7 6.0 %convolution_convert_fusion.5 = bf16[384,3072]{1,0:T(8,128)(2,1)} fusion(bf16[768,3072]{1,0:T(8,128)(2,1)} %param.7, s32[768]{0:T(1024)S(1)} %add_bitcast_fusion, pred[768]{0:T(1024)(128)(4,1)S(1)} %fusion.29), kind=kOutput, calls=%fused_computation.11 | convolution fusion | flops 1813708800 | bytes 7081728 | tf_op jit(solution)/shard_map/dot_general | solution.py:11
  15.6 4.2 multiply_convert_fusion
  25.5 16.4 %collective-permute-done = bf16[384,1024]{1,0:T(8,128)(2,1)} collective-permute-done((bf16[384,1024]{1,0:T(8,128)(2,1)}, bf16[384,1024]{1,0:T(8,128)(2,1)}, u32[]{:S(2)}, u32[]{:S(2)}) %collective-permute-start) | collective-permute-done | bytes 786464 | tf_op jit(solution)/shard_map/ppermute | solution.py:28
  44.0 2.4 collective-permute-start.6
  52.7 34.4 %collective-permute-done.6 = bf16[384,1024]{1,0:T(8,128)(2,1)} collective-permute-done((bf16[384,1024]{1,0:T(8,128)(2,1)}, bf16[384,1024]{1,0:T(8,128)(2,1)}, u32[]{:S(2)}, u32[]{:S(2)}) %collective-permute-start.6) | collective-permute-done | bytes 786464 | tf_op jit(solution)/shard_map/ppermute | solution.py:28
  87.1 10.2 %collective-permute-done.2 = bf16[768,768]{1,0:T(8,128)(2,1)} collective-permute-done((bf16[768,768]{1,0:T(8,128)(2,1)}, bf16[768,768]{1,0:T(8,128)(2,1)}, u32[]{:S(2)}, u32[]{:S(2)}) %collective-permute-start.2) | collective-permute-done | bytes 1179680 | tf_op jit(solution)/shard_map/ppermute | solution.py:28
  100.9 3.0 collective-permute-start.7
  103.8 2.3 pad_maximum_fusion.2
  107.9 2.1 broadcast_in_dim.67.clone.1
  111.1 37.0 %collective-permute-done.7 = bf16[768,512]{1,0:T(8,128)(2,1)S(1)} collective-permute-done((bf16[768,512]{1,0:T(8,128)(2,1)}, bf16[768,512]{1,0:T(8,128)(2,1)S(1)}, u32[]{:S(2)}, u32[]{:S(2)}) %collective-permute-start.7) | collective-permute-done | bytes 786464 | tf_op jit(solution)/shard_map/ppermute | solution.py:28
  148.1 3.7 collective-permute-done.9
  152.0 3.1 collective-permute-start.12
  155.7 2.4 bitcast_dynamic-update-slice_fusion.3
  158.1 2.5 broadcast_select_fusion.11
  160.7 2.6 broadcast_select_fusion.10
  165.1 3.0 collective-permute-done.14
  168.2 6.1 %pad_maximum_fusion = bf16[1536,3072]{1,0:T(8,128)(2,1)S(1)} fusion(bf16[384,3072]{1,0:T(8,128)(2,1)S(1)} %collective-permute-done.14, bf16[384,3072]{1,0:T(8,128)(2,1)} %collective-permute-done.3, bf16[384,768]{1,0:T(8,128)(2,1)S(1)} %get-tuple-element.235, bf16[384,768]{1,0:T(8,128)(2,1)S(1)} %get-tuple-element.234, ...), kind=kLoop, calls=%fused_computation | loop fusion | flops 66060288 | bytes 18874368 | tf_op jit(solution)/shard_map/concatenate | solution.py:48
  174.3 6.1 %pad_maximum_fusion.1 = bf16[1536,3072]{1,0:T(8,128)(2,1)S(1)} fusion(bf16[384,3072]{1,0:T(8,128)(2,1)S(1)} %collective-permute-done.15, bf16[384,3072]{1,0:T(8,128)(2,1)} %collective-permute-done.4, bf16[384,768]{1,0:T(8,128)(2,1)S(1)} %get-tuple-element.238, bf16[384,768]{1,0:T(8,128)(2,1)S(1)} %get-tuple-element.237, ...), kind=kLoop, calls=%fused_computation.1 | loop fusion | flops 66060288 | bytes 18874368 | tf_op jit(solution)/shard_map/concatenate | solution.py:48
  180.4 5.1 %fusion.33 = f32[1536,512]{1,0:T(8,128)S(1)} fusion(bf16[1536,3072]{1,0:T(8,128)(2,1)S(1)} %pad_maximum_fusion, bf16[3072,512]{1,0:T(8,128)(2,1)S(1)} %bitcast.90), kind=kOutput, calls=%fused_computation.186 | convolution fusion | flops 4831838208 | bytes 15728640 | tf_op jit(solution)/shard_map/dot_general | solution.py:11
  185.5 4.9 %collective-permute-done.12 = bf16[768,512]{1,0:T(8,128)(2,1)} collective-permute-done((bf16[768,512]{1,0:T(8,128)(2,1)}, bf16[768,512]{1,0:T(8,128)(2,1)}, u32[]{:S(2)}, u32[]{:S(2)}) %collective-permute-start.12) | collective-permute-done | bytes 786464 | tf_op jit(solution)/shard_map/ppermute | solution.py:28
  193.3 7.4 %multiply_convert_fusion.3 = (bf16[1536,512]{1,0:T(8,128)(2,1)S(1)}, f32[1536,512]{1,0:T(8,128)}) fusion(f32[1536,512]{1,0:T(8,128)S(1)} %fusion.33, bf16[1536,3072]{1,0:T(8,128)(2,1)S(1)} %pad_maximum_fusion, bf16[3072,512]{1,0:T(8,128)(2,1)S(1)} %bitcast.97), kind=kOutput, calls=%fused_computation.15 | convolution fusion | flops 4836556800 | bytes 20447232 | tf_op jit(solution)/shard_map/dot_general | solution.py:11
  200.6 5.5 %convolution_convert_fusion.3 = bf16[3072,512]{1,0:T(8,128)(2,1)S(1)} fusion(bf16[1536,3072]{1,0:T(8,128)(2,1)S(1)} %pad_maximum_fusion.1, bf16[1536,512]{1,0:T(8,128)(2,1)S(1)} %get-tuple-element.164), kind=kOutput, calls=%fused_computation.9 | convolution fusion | flops 4833411072 | bytes 14155776 | tf_op jit(solution)/shard_map/dot_general | solution.py:11
  206.1 2.2 bitcast_dynamic-update-slice_fusion.1
  213.7 10.0 %multiply_convert_fusion.1 = (bf16[1536,512]{1,0:T(8,128)(2,1)S(1)}, bf16[1536,512]{1,0:T(8,128)(2,1)}) fusion(f32[1536,512]{1,0:T(8,128)} %copy-done.39, f32[1536,512]{1,0:T(8,128)} %get-tuple-element.156, bf16[1536,3072]{1,0:T(8,128)(2,1)S(1)} %pad_maximum_fusion.1, bf16[3072,512]{1,0:T(8,128)(2,1)} %bitcast.24), kind=kOutput, calls=%fused_computation.13 | convolution fusion | flops 4842061824 | bytes 22020096 | tf_op jit(solution)/shard_map/dot_general | solution.py:11
  223.7 7.5 %convolution_convert_fusion = bf16[768,3072]{1,0:T(8,128)(2,1)} fusion(bf16[3072,512]{1,0:T(8,128)(2,1)} %bitcast.24, bf16[1536,512]{1,0:T(8,128)(2,1)} %copy-done.37), kind=kOutput, calls=%fused_computation.5 | convolution fusion | flops 2418278400 | bytes 8650752 | tf_op jit(solution)/shard_map/dot_general | solution.py:11
  233.5 2.6 fusion.13
  236.1 5.6 %add_convert_fusion.2 = bf16[768,3072]{1,0:T(8,128)(2,1)} fusion(f32[768,3072]{1,0:T(8,128)S(1)} %fusion.13, bf16[3072,512]{1,0:T(8,128)(2,1)S(1)} %bitcast.91, bf16[1536,512]{1,0:T(8,128)(2,1)} %get-tuple-element.160), kind=kOutput, calls=%fused_computation.4 | convolution fusion | flops 2420637696 | bytes 18087936 | tf_op jit(solution)/shard_map/dot_general | solution.py:11
  242.4 6.9 %convolution_convert_fusion.2 = bf16[3072,512]{1,0:T(8,128)(2,1)S(1)} fusion(bf16[1536,3072]{1,0:T(8,128)(2,1)S(1)} %pad_maximum_fusion, bf16[1536,512]{1,0:T(8,128)(2,1)} %get-tuple-element.160), kind=kOutput, calls=%fused_computation.8 | convolution fusion | flops 4833411072 | bytes 14155776 | tf_op jit(solution)/shard_map/dot_general | solution.py:11
  249.3 1.7 dynamic-slice_bitcast_fusion
  252.7 5.7 %convolution_convert_fusion.1 = bf16[3072,512]{1,0:T(8,128)(2,1)S(1)} fusion(bf16[1536,3072]{1,0:T(8,128)(2,1)S(1)} %pad_maximum_fusion, bf16[1536,512]{1,0:T(8,128)(2,1)S(1)} %copy-done.36), kind=kOutput, calls=%fused_computation.7 | convolution fusion | flops 4833411072 | bytes 14155776 | tf_op jit(solution)/shard_map/dot_general | solution.py:11
  258.3 1.7 dynamic-slice_bitcast_fusion.2
  260.7 2.6 fusion.18
  263.3 2.6 fusion.16
  266.0 5.5 %add_convert_fusion = bf16[768,3072]{1,0:T(8,128)(2,1)S(1)} fusion(bf16[768,3072]{1,0:T(8,128)(2,1)} %collective-permute-done.21, bf16[3072,512]{1,0:T(8,128)(2,1)} %bitcast.24, bf16[1536,512]{1,0:T(8,128)(2,1)S(1)} %copy-done.38), kind=kOutput, calls=%fused_computation.2 | convolution fusion | flops 2422996992 | bytes 13369344 | tf_op jit(solution)/shard_map/dot_general | solution.py:11
  276.3 4.7 %add_convert_fusion.1 = bf16[768,3072]{1,0:T(8,128)(2,1)S(1)} fusion(bf16[768,3072]{1,0:T(8,128)(2,1)} %collective-permute-done.20, f32[768,3072]{1,0:T(8,128)S(1)} %fusion.18, f32[768,3072]{1,0:T(8,128)S(1)} %fusion.16), kind=kLoop, calls=%fused_computation.3 | loop fusion | flops 9437184 | bytes 28311552 | tf_op jit(solution)/shard_map/convert_element_type | solution.py:257
  281.0 14.6 %collective-permute-done.23 = bf16[768,512]{1,0:T(8,128)(2,1)} collective-permute-done((bf16[768,512]{1,0:T(8,128)(2,1)}, bf16[768,512]{1,0:T(8,128)(2,1)}, u32[]{:S(2)}, u32[]{:S(2)}) %collective-permute-start.23) | collective-permute-done | bytes 786464 | tf_op jit(solution)/shard_map/ppermute | solution.py:28
  301.7 22.9 %collective-permute-done.25 = bf16[384,1536]{1,0:T(8,128)(2,1)S(1)} collective-permute-done((bf16[384,1536]{1,0:T(8,128)(2,1)S(1)}, bf16[384,1536]{1,0:T(8,128)(2,1)S(1)}, u32[]{:S(2)}, u32[]{:S(2)}) %collective-permute-start.25) | collective-permute-done | bytes 1179680 | tf_op jit(solution)/shard_map/ppermute | solution.py:28
  326.2 7.8 %collective-permute-done.24 = bf16[768,512]{1,0:T(8,128)(2,1)S(1)} collective-permute-done((bf16[768,512]{1,0:T(8,128)(2,1)S(1)}, bf16[768,512]{1,0:T(8,128)(2,1)S(1)}, u32[]{:S(2)}, u32[]{:S(2)}) %collective-permute-start.24) | collective-permute-done | bytes 786464 | tf_op jit(solution)/shard_map/ppermute | solution.py:28
  337.1 2.3 collective-permute-start.31
  339.4 35.3 %collective-permute-done.29 = bf16[384,2304]{1,0:T(8,128)(2,1)S(1)} collective-permute-done((bf16[384,2304]{1,0:T(8,128)(2,1)S(1)}, bf16[384,2304]{1,0:T(8,128)(2,1)S(1)}, u32[]{:S(2)}, u32[]{:S(2)}) %collective-permute-start.29) | collective-permute-done | bytes 1769504 | tf_op jit(solution)/shard_map/ppermute | solution.py:28
  381.7 9.7 %collective-permute-done.33 = bf16[384,768]{1,0:T(8,128)(2,1)} collective-permute-done((bf16[384,768]{1,0:T(8,128)(2,1)}, bf16[384,768]{1,0:T(8,128)(2,1)}, u32[]{:S(2)}, u32[]{:S(2)}) %collective-permute-start.33) | collective-permute-done | bytes 589856 | tf_op jit(solution)/shard_map/ppermute | solution.py:28
  393.9 11.4 %collective-permute-done.32 = bf16[384,768]{1,0:T(8,128)(2,1)} collective-permute-done((bf16[384,768]{1,0:T(8,128)(2,1)}, bf16[384,768]{1,0:T(8,128)(2,1)}, u32[]{:S(2)}, u32[]{:S(2)}) %collective-permute-start.32) | collective-permute-done | bytes 589856 | tf_op jit(solution)/shard_map/ppermute | solution.py:28
  413.3 3.0 convolution_convert_fusion.7
  417.6 2.6 collective-permute-done.37
  421.9 8.4 %collective-permute-done.35 = bf16[384,768]{1,0:T(8,128)(2,1)S(1)} collective-permute-done((bf16[384,768]{1,0:T(8,128)(2,1)S(1)}, bf16[384,768]{1,0:T(8,128)(2,1)S(1)}, u32[]{:S(2)}, u32[]{:S(2)}) %collective-permute-start.35) | collective-permute-done | bytes 589856 | tf_op jit(solution)/shard_map/ppermute | solution.py:28
  430.3 1.9 convolution_convert_fusion.6
  (225 shorter events, 76.7 us)
Async XLA Ops:
  3.1 38.8 %collective-permute-start = (bf16[384,1024]{1,0:T(8,128)(2,1)}, bf16[384,1024]{1,0:T(8,128)(2,1)}, u32[]{:S(2)}, u32[]{:S(2)}) collective-permute-start(bf16[384,1024]{1,0:T(8,128)(2,1)} %get-tuple-element.299), channel_id=1, source_target_pairs={{0,16},{4,20},{8,24},{12,28},{16,0},{20,4},{24,8},{28,12},{1,17},{... | collective-permute-start | bytes 2359304 | tf_op jit(solution)/shard_map/ppermute | solution.py:28
  7.1 34.8 %collective-permute-start.1 = (bf16[384,1024]{1,0:T(8,128)(2,1)S(1)}, bf16[384,1024]{1,0:T(8,128)(2,1)}, u32[]{:S(2)}, u32[]{:S(2)}) collective-permute-start(bf16[384,1024]{1,0:T(8,128)(2,1)S(1)} %get-tuple-element.122), channel_id=1, source_target_pairs={{0,8},{4,12},{8,0},{12,4},{16,24},{20,28},{24,16},{28,20},{1,9},{5... | collective-permute-start | bytes 2359304 | tf_op jit(solution)/shard_map/ppermute | solution.py:28
  25.5 23.6 %copy-start.17 = (bf16[384,512]{1,0:T(8,128)(2,1)S(1)}, bf16[384,512]{1,0:T(8,128)(2,1)}, u32[]{:S(2)}) copy-start(bf16[384,512]{1,0:T(8,128)(2,1)} %get-tuple-element.289) | copy-start | bytes 1179652
  41.9 5.8 %collective-permute-start.5 = (bf16[768,1024]{1,0:T(8,128)(2,1)S(1)}, bf16[768,1024]{1,0:T(8,128)(2,1)}, u32[]{:S(2)}, u32[]{:S(2)}) collective-permute-start(bf16[768,1024]{1,0:T(8,128)(2,1)S(1)} %maximum_maximum_fusion), channel_id=1, source_target_pairs={{0,4},{4,0},{8,12},{12,8},{16,20},{20,16},{24,28},{28,24},{1,5},{5... | collective-permute-start | bytes 4718600 | tf_op jit(solution)/shard_map/ppermute | solution.py:28
  41.9 55.4 %collective-permute-start.3 = (bf16[384,3072]{1,0:T(8,128)(2,1)}, bf16[384,3072]{1,0:T(8,128)(2,1)}, u32[]{:S(2)}, u32[]{:S(2)}) collective-permute-start(bf16[384,3072]{1,0:T(8,128)(2,1)} %convolution_convert_fusion.5), channel_id=1, source_target_pairs={{0,4},{4,0},{8,12},{12,8},{16,20},{20,16},{24,28},{28,24},{1,5},{5... | collective-permute-start | bytes 7077896 | tf_op jit(solution)/shard_map/ppermute | solution.py:28
  42.4 54.9 %collective-permute-start.4 = (bf16[384,3072]{1,0:T(8,128)(2,1)}, bf16[384,3072]{1,0:T(8,128)(2,1)}, u32[]{:S(2)}, u32[]{:S(2)}) collective-permute-start(bf16[384,3072]{1,0:T(8,128)(2,1)} %get-tuple-element.118), channel_id=1, source_target_pairs={{0,4},{4,0},{8,12},{12,8},{16,20},{20,16},{24,28},{28,24},{1,5},{5... | collective-permute-start | bytes 7077896 | tf_op jit(solution)/shard_map/ppermute | solution.py:28
  42.4 54.9 %collective-permute-start.2 = (bf16[768,768]{1,0:T(8,128)(2,1)}, bf16[768,768]{1,0:T(8,128)(2,1)}, u32[]{:S(2)}, u32[]{:S(2)}) collective-permute-start(bf16[768,768]{1,0:T(8,128)(2,1)} %pad_maximum_fusion.9), channel_id=1, source_target_pairs={{0,16},{4,20},{8,24},{12,28},{16,0},{20,4},{24,8},{28,12},{1,17},{... | collective-permute-start | bytes 3538952 | tf_op jit(solution)/shard_map/ppermute | solution.py:28
  44.0 43.1 %collective-permute-start.6 = (bf16[384,1024]{1,0:T(8,128)(2,1)}, bf16[384,1024]{1,0:T(8,128)(2,1)}, u32[]{:S(2)}, u32[]{:S(2)}) collective-permute-start(bf16[384,1024]{1,0:T(8,128)(2,1)} %collective-permute-done), channel_id=1, source_target_pairs={{0,8},{4,12},{8,0},{12,4},{16,24},{20,28},{24,16},{28,20},{1,9},{5... | collective-permute-start | bytes 2359304 | tf_op jit(solution)/shard_map/ppermute | solution.py:28
  97.3 54.5 %collective-permute-start.11 = (bf16[768,1024]{1,0:T(8,128)(2,1)S(1)}, bf16[768,1024]{1,0:T(8,128)(2,1)}, u32[]{:S(2)}, u32[]{:S(2)}) collective-permute-start(bf16[768,1024]{1,0:T(8,128)(2,1)S(1)} %pad_maximum_fusion.7), channel_id=1, source_target_pairs={{0,8},{4,12},{8,0},{12,4},{16,24},{20,28},{24,16},{28,20},{1,9},{5... | collective-permute-start | bytes 4718600 | tf_op jit(solution)/shard_map/ppermute | solution.py:28
  97.3 50.8 %collective-permute-start.8 = (bf16[768,768]{1,0:T(8,128)(2,1)}, bf16[768,768]{1,0:T(8,128)(2,1)}, u32[]{:S(2)}, u32[]{:S(2)}) collective-permute-start(bf16[768,768]{1,0:T(8,128)(2,1)} %collective-permute-done.2), channel_id=1, source_target_pairs={{0,1},{1,0},{2,3},{3,2},{4,5},{5,4},{6,7},{7,6},{8,9},{9,8},{10,11... | collective-permute-start | bytes 3538952 | tf_op jit(solution)/shard_map/ppermute | solution.py:28
  98.9 52.9 %collective-permute-start.9 = (bf16[768,768]{1,0:T(8,128)(2,1)}, bf16[768,768]{1,0:T(8,128)(2,1)}, u32[]{:S(2)}, u32[]{:S(2)}) collective-permute-start(bf16[768,768]{1,0:T(8,128)(2,1)} %collective-permute-done.2), channel_id=1, source_target_pairs={{0,2},{1,3},{2,0},{3,1},{4,6},{5,7},{6,4},{7,5},{8,10},{9,11},{10,... | collective-permute-start | bytes 3538952 | tf_op jit(solution)/shard_map/ppermute | solution.py:28
  100.4 51.4 %collective-permute-start.10 = (bf16[768,768]{1,0:T(8,128)(2,1)}, bf16[768,768]{1,0:T(8,128)(2,1)}, u32[]{:S(2)}, u32[]{:S(2)}) collective-permute-start(bf16[768,768]{1,0:T(8,128)(2,1)} %collective-permute-done.2), channel_id=1, source_target_pairs={{0,3},{1,2},{2,1},{3,0},{4,7},{5,6},{6,5},{7,4},{8,11},{9,10},{10,... | collective-permute-start | bytes 3538952 | tf_op jit(solution)/shard_map/ppermute | solution.py:28
  100.9 47.2 %collective-permute-start.7 = (bf16[768,512]{1,0:T(8,128)(2,1)}, bf16[768,512]{1,0:T(8,128)(2,1)S(1)}, u32[]{:S(2)}, u32[]{:S(2)}) collective-permute-start(bf16[768,512]{1,0:T(8,128)(2,1)} %maximum_select_fusion.2), channel_id=1, source_target_pairs={{0,16},{4,20},{8,24},{12,28},{16,0},{20,4},{24,8},{28,12},{1,17},{... | collective-permute-start | bytes 2359304 | tf_op jit(solution)/shard_map/ppermute | solution.py:28
  151.8 6.3 %collective-permute-start.13 = (bf16[4,384,512]{2,1,0:T(8,128)(2,1)}, bf16[4,384,512]{2,1,0:T(8,128)(2,1)S(1)}, u32[]{:S(2)}, u32[]{:S(2)}) collective-permute-start(bf16[4,384,512]{2,1,0:T(8,128)(2,1)} %get-tuple-element.130), channel_id=1, source_target_pairs={{0,4},{4,0},{8,12},{12,8},{16,20},{20,16},{24,28},{28,24},{1,5},{5... | collective-permute-start | bytes 4718600 | tf_op jit(solution)/shard_map/ppermute | solution.py:28
  152.0 38.4 %collective-permute-start.12 = (bf16[768,512]{1,0:T(8,128)(2,1)}, bf16[768,512]{1,0:T(8,128)(2,1)}, u32[]{:S(2)}, u32[]{:S(2)}) collective-permute-start(bf16[768,512]{1,0:T(8,128)(2,1)} %maximum_select_fusion.3), channel_id=1, source_target_pairs={{0,16},{4,20},{8,24},{12,28},{16,0},{20,4},{24,8},{28,12},{1,17},{... | collective-permute-start | bytes 2359304 | tf_op jit(solution)/shard_map/ppermute | solution.py:28
  155.1 35.8 %collective-permute-start.16 = (bf16[768,512]{1,0:T(8,128)(2,1)}, bf16[768,512]{1,0:T(8,128)(2,1)}, u32[]{:S(2)}, u32[]{:S(2)}) collective-permute-start(bf16[768,512]{1,0:T(8,128)(2,1)} %copy-done.22), channel_id=1, source_target_pairs={{0,8},{4,12},{8,0},{12,4},{16,24},{20,28},{24,16},{28,20},{1,9},{5... | collective-permute-start | bytes 2359304 | tf_op jit(solution)/shard_map/ppermute | solution.py:28
  163.6 4.6 %collective-permute-start.14 = (bf16[384,3072]{1,0:T(8,128)(2,1)S(1)}, bf16[384,3072]{1,0:T(8,128)(2,1)S(1)}, u32[]{:S(2)}, u32[]{:S(2)}) collective-permute-start(bf16[384,3072]{1,0:T(8,128)(2,1)S(1)} %pad_maximum_fusion.3), channel_id=1, source_target_pairs={{0,4},{4,0},{8,12},{12,8},{16,20},{20,16},{24,28},{28,24},{1,5},{5... | collective-permute-start | bytes 7077896 | tf_op jit(solution)/shard_map/ppermute | solution.py:28
  164.7 9.5 %collective-permute-start.15 = (bf16[384,3072]{1,0:T(8,128)(2,1)S(1)}, bf16[384,3072]{1,0:T(8,128)(2,1)S(1)}, u32[]{:S(2)}, u32[]{:S(2)}) collective-permute-start(bf16[384,3072]{1,0:T(8,128)(2,1)S(1)} %pad_maximum_fusion.4), channel_id=1, source_target_pairs={{0,4},{4,0},{8,12},{12,8},{16,20},{20,16},{24,28},{28,24},{1,5},{5... | collective-permute-start | bytes 7077896 | tf_op jit(solution)/shard_map/ppermute | solution.py:28
  190.9 18.9 %collective-permute-start.17 = (bf16[768,512]{1,0:T(8,128)(2,1)}, bf16[768,512]{1,0:T(8,128)(2,1)S(1)}, u32[]{:S(2)}, u32[]{:S(2)}) collective-permute-start(bf16[768,512]{1,0:T(8,128)(2,1)} %collective-permute-done.12), channel_id=1, source_target_pairs={{0,8},{4,12},{8,0},{12,4},{16,24},{20,28},{24,16},{28,20},{1,9},{5... | collective-permute-start | bytes 2359304 | tf_op jit(solution)/shard_map/ppermute | solution.py:28
  193.2 40.2 %copy-start.6 = (bf16[4,768,512]{2,1,0:T(8,128)(2,1)}, bf16[4,768,512]{2,1,0:T(8,128)(2,1)S(1)}, u32[]{:S(2)}) copy-start(bf16[4,768,512]{2,1,0:T(8,128)(2,1)S(1)} %bitcast_dynamic-update-slice_fusion.2) | copy-start | bytes 9437188
  211.2 20.0 %collective-permute-start.18 = (bf16[768,512]{1,0:T(8,128)(2,1)}, bf16[768,512]{1,0:T(8,128)(2,1)S(1)}, u32[]{:S(2)}, u32[]{:S(2)}) collective-permute-start(bf16[768,512]{1,0:T(8,128)(2,1)} %get-tuple-element.254), channel_id=1, source_target_pairs={{0,8},{4,12},{8,0},{12,4},{16,24},{20,28},{24,16},{28,20},{1,9},{5... | collective-permute-start | bytes 2359304 | tf_op jit(solution)/shard_map/ppermute | solution.py:28
  231.2 34.8 %collective-permute-start.21 = (bf16[768,3072]{1,0:T(8,128)(2,1)}, bf16[768,3072]{1,0:T(8,128)(2,1)}, u32[]{:S(2)}, u32[]{:S(2)}) collective-permute-start(bf16[768,3072]{1,0:T(8,128)(2,1)} %convolution_convert_fusion), channel_id=1, source_target_pairs={{0,4},{4,0},{8,12},{12,8},{16,20},{20,16},{24,28},{28,24},{1,5},{5... | collective-permute-start | bytes 14155784 | tf_op jit(solution)/shard_map/ppermute | solution.py:28
  232.3 48.7 %collective-permute-start.19 = (bf16[768,512]{1,0:T(8,128)(2,1)}, bf16[768,512]{1,0:T(8,128)(2,1)}, u32[]{:S(2)}, u32[]{:S(2)}) collective-permute-start(bf16[768,512]{1,0:T(8,128)(2,1)} %add_convert_fusion.8), channel_id=1, source_target_pairs={{0,16},{4,20},{8,24},{12,28},{16,0},{20,4},{24,8},{28,12},{1,17},{... | collective-permute-start | bytes 2359304 | tf_op jit(solution)/shard_map/ppermute | solution.py:28
  241.7 34.5 %collective-permute-start.20 = (bf16[768,3072]{1,0:T(8,128)(2,1)}, bf16[768,3072]{1,0:T(8,128)(2,1)}, u32[]{:S(2)}, u32[]{:S(2)}) collective-permute-start(bf16[768,3072]{1,0:T(8,128)(2,1)} %add_convert_fusion.2), channel_id=1, source_target_pairs={{0,4},{4,0},{8,12},{12,8},{16,20},{20,16},{24,28},{28,24},{1,5},{5... | collective-permute-start | bytes 14155784 | tf_op jit(solution)/shard_map/ppermute | solution.py:28
  242.0 39.0 %collective-permute-start.22 = (bf16[768,512]{1,0:T(8,128)(2,1)}, bf16[768,512]{1,0:T(8,128)(2,1)}, u32[]{:S(2)}, u32[]{:S(2)}) collective-permute-start(bf16[768,512]{1,0:T(8,128)(2,1)} %get-tuple-element.166), channel_id=1, source_target_pairs={{0,8},{4,12},{8,0},{12,4},{16,24},{20,28},{24,16},{28,20},{1,9},{5... | collective-permute-start | bytes 2359304 | tf_op jit(solution)/shard_map/ppermute | solution.py:28
  251.0 44.6 %collective-permute-start.23 = (bf16[768,512]{1,0:T(8,128)(2,1)}, bf16[768,512]{1,0:T(8,128)(2,1)}, u32[]{:S(2)}, u32[]{:S(2)}) collective-permute-start(bf16[768,512]{1,0:T(8,128)(2,1)} %get-tuple-element.246), channel_id=1, source_target_pairs={{0,8},{4,12},{8,0},{12,4},{16,24},{20,28},{24,16},{28,20},{1,9},{5... | collective-permute-start | bytes 2359304 | tf_op jit(solution)/shard_map/ppermute | solution.py:28
  281.0 16.2 %copy-start.21 = (bf16[384,1536]{1,0:T(8,128)(2,1)S(1)}, bf16[384,1536]{1,0:T(8,128)(2,1)}, u32[]{:S(2)}) copy-start(bf16[384,1536]{1,0:T(8,128)(2,1)} %pad_maximum_fusion.10) | copy-start | bytes 3538948
  281.0 17.5 %copy-start.20 = (bf16[384,1536]{1,0:T(8,128)(2,1)S(1)}, bf16[384,1536]{1,0:T(8,128)(2,1)}, u32[]{:S(2)}) copy-start(bf16[384,1536]{1,0:T(8,128)(2,1)} %pad_maximum_fusion.11) | copy-start | bytes 3538948
  297.2 27.4 %collective-permute-start.25 = (bf16[384,1536]{1,0:T(8,128)(2,1)S(1)}, bf16[384,1536]{1,0:T(8,128)(2,1)S(1)}, u32[]{:S(2)}, u32[]{:S(2)}) collective-permute-start(bf16[384,1536]{1,0:T(8,128)(2,1)S(1)} %copy-done.21), channel_id=1, source_target_pairs={{0,1},{1,0},{2,3},{3,2},{4,5},{5,4},{6,7},{7,6},{8,9},{9,8},{10,11... | collective-permute-start | bytes 3538952 | tf_op jit(solution)/shard_map/ppermute | solution.py:28
  298.4 35.5 %collective-permute-start.24 = (bf16[768,512]{1,0:T(8,128)(2,1)S(1)}, bf16[768,512]{1,0:T(8,128)(2,1)S(1)}, u32[]{:S(2)}, u32[]{:S(2)}) collective-permute-start(bf16[768,512]{1,0:T(8,128)(2,1)S(1)} %add_convert_fusion.7), channel_id=1, source_target_pairs={{0,16},{4,20},{8,24},{12,28},{16,0},{20,4},{24,8},{28,12},{1,17},{... | collective-permute-start | bytes 2359304 | tf_op jit(solution)/shard_map/ppermute | solution.py:28
  298.5 27.1 %collective-permute-start.26 = (bf16[384,1536]{1,0:T(8,128)(2,1)S(1)}, bf16[384,1536]{1,0:T(8,128)(2,1)S(1)}, u32[]{:S(2)}, u32[]{:S(2)}) collective-permute-start(bf16[384,1536]{1,0:T(8,128)(2,1)S(1)} %copy-done.20), channel_id=1, source_target_pairs={{0,2},{1,3},{2,0},{3,1},{4,6},{5,7},{6,4},{7,5},{8,10},{9,11},{10,... | collective-permute-start | bytes 3538952 | tf_op jit(solution)/shard_map/ppermute | solution.py:28
  299.3 35.4 %collective-permute-start.27 = (bf16[768,512]{1,0:T(8,128)(2,1)}, bf16[768,512]{1,0:T(8,128)(2,1)S(1)}, u32[]{:S(2)}, u32[]{:S(2)}) collective-permute-start(bf16[768,512]{1,0:T(8,128)(2,1)} %get-tuple-element.179), channel_id=1, source_target_pairs={{0,8},{4,12},{8,0},{12,4},{16,24},{20,28},{24,16},{28,20},{1,9},{5... | collective-permute-start | bytes 2359304 | tf_op jit(solution)/shard_map/ppermute | solution.py:28
  301.1 23.5 %copy-start.3 = (bf16[384,3072]{1,0:T(8,128)(2,1)S(1)}, bf16[384,3072]{1,0:T(8,128)(2,1)}, u32[]{:S(2)}) copy-start(bf16[384,3072]{1,0:T(8,128)(2,1)} %copy-done.2) | copy-start | bytes 7077892
  301.7 23.8 %copy-start.1 = (bf16[384,3072]{1,0:T(8,128)(2,1)S(1)}, bf16[384,3072]{1,0:T(8,128)(2,1)}, u32[]{:S(2)}) copy-start(bf16[384,3072]{1,0:T(8,128)(2,1)} %copy-done) | copy-start | bytes 7077892
  335.0 39.7 %collective-permute-start.29 = (bf16[384,2304]{1,0:T(8,128)(2,1)S(1)}, bf16[384,2304]{1,0:T(8,128)(2,1)S(1)}, u32[]{:S(2)}, u32[]{:S(2)}) collective-permute-start(bf16[384,2304]{1,0:T(8,128)(2,1)S(1)} %pad_maximum_fusion.6), channel_id=1, source_target_pairs={{0,2},{1,3},{2,0},{3,1},{4,6},{5,7},{6,4},{7,5},{8,10},{9,11},{10,... | collective-permute-start | bytes 5308424 | tf_op jit(solution)/shard_map/ppermute | solution.py:28
  336.2 39.9 %collective-permute-start.30 = (bf16[384,2304]{1,0:T(8,128)(2,1)S(1)}, bf16[384,2304]{1,0:T(8,128)(2,1)S(1)}, u32[]{:S(2)}, u32[]{:S(2)}) collective-permute-start(bf16[384,2304]{1,0:T(8,128)(2,1)S(1)} %pad_maximum_fusion.5), channel_id=1, source_target_pairs={{0,1},{1,0},{2,3},{3,2},{4,5},{5,4},{6,7},{7,6},{8,9},{9,8},{10,11... | collective-permute-start | bytes 5308424 | tf_op jit(solution)/shard_map/ppermute | solution.py:28
  337.1 40.5 %collective-permute-start.28 = (bf16[768,512]{1,0:T(8,128)(2,1)S(1)}, bf16[768,512]{1,0:T(8,128)(2,1)S(1)}, u32[]{:S(2)}, u32[]{:S(2)}) collective-permute-start(bf16[768,512]{1,0:T(8,128)(2,1)S(1)} %add_convert_fusion.6), channel_id=1, source_target_pairs={{0,16},{4,20},{8,24},{12,28},{16,0},{20,4},{24,8},{28,12},{1,17},{... | collective-permute-start | bytes 2359304 | tf_op jit(solution)/shard_map/ppermute | solution.py:28
  337.1 40.5 %collective-permute-start.31 = (bf16[768,512]{1,0:T(8,128)(2,1)S(1)}, bf16[768,512]{1,0:T(8,128)(2,1)}, u32[]{:S(2)}, u32[]{:S(2)}) collective-permute-start(bf16[768,512]{1,0:T(8,128)(2,1)S(1)} %copy-done.24), channel_id=1, source_target_pairs={{0,8},{4,12},{8,0},{12,4},{16,24},{20,28},{24,16},{28,20},{1,9},{5... | collective-permute-start | bytes 2359304 | tf_op jit(solution)/shard_map/ppermute | solution.py:28
  377.6 13.8 %collective-permute-start.33 = (bf16[384,768]{1,0:T(8,128)(2,1)}, bf16[384,768]{1,0:T(8,128)(2,1)}, u32[]{:S(2)}, u32[]{:S(2)}) collective-permute-start(bf16[384,768]{1,0:T(8,128)(2,1)} %get-tuple-element.206), channel_id=1, source_target_pairs={{0,2},{1,3},{2,0},{3,1},{4,6},{5,7},{6,4},{7,5},{8,10},{9,11},{10,... | collective-permute-start | bytes 1769480 | tf_op jit(solution)/shard_map/ppermute | solution.py:28
  378.5 14.1 %collective-permute-start.34 = (bf16[384,768]{1,0:T(8,128)(2,1)}, bf16[384,768]{1,0:T(8,128)(2,1)}, u32[]{:S(2)}, u32[]{:S(2)}) collective-permute-start(bf16[384,768]{1,0:T(8,128)(2,1)} %get-tuple-element.208), channel_id=1, source_target_pairs={{0,1},{1,0},{2,3},{3,2},{4,5},{5,4},{6,7},{7,6},{8,9},{9,8},{10,11... | collective-permute-start | bytes 1769480 | tf_op jit(solution)/shard_map/ppermute | solution.py:28
  380.0 25.3 %collective-permute-start.32 = (bf16[384,768]{1,0:T(8,128)(2,1)}, bf16[384,768]{1,0:T(8,128)(2,1)}, u32[]{:S(2)}, u32[]{:S(2)}) collective-permute-start(bf16[384,768]{1,0:T(8,128)(2,1)} %get-tuple-element.204), channel_id=1, source_target_pairs={{0,16},{4,20},{8,24},{12,28},{16,0},{20,4},{24,8},{28,12},{1,17},{... | collective-permute-start | bytes 1769480 | tf_op jit(solution)/shard_map/ppermute | solution.py:28
  380.0 27.3 %copy-start.8 = (bf16[768,512]{1,0:T(8,128)(2,1)S(1)}, bf16[768,512]{1,0:T(8,128)(2,1)}, u32[]{:S(2)}) copy-start(bf16[768,512]{1,0:T(8,128)(2,1)} %get-tuple-element.220) | copy-start | bytes 2359300
  380.0 40.3 %collective-permute-start.39 = (bf16[768,512]{1,0:T(8,128)(2,1)}, bf16[768,512]{1,0:T(8,128)(2,1)S(1)}, u32[]{:S(2)}, u32[]{:S(2)}) collective-permute-start(bf16[768,512]{1,0:T(8,128)(2,1)} %get-tuple-element.224), channel_id=1, source_target_pairs={{0,8},{4,12},{8,0},{12,4},{16,24},{20,28},{24,16},{28,20},{1,9},{5... | collective-permute-start | bytes 2359304 | tf_op jit(solution)/shard_map/ppermute | solution.py:28
  393.8 36.5 %collective-permute-start.35 = (bf16[384,768]{1,0:T(8,128)(2,1)S(1)}, bf16[384,768]{1,0:T(8,128)(2,1)S(1)}, u32[]{:S(2)}, u32[]{:S(2)}) collective-permute-start(bf16[384,768]{1,0:T(8,128)(2,1)S(1)} %add_convert_fusion.10), channel_id=1, source_target_pairs={{0,16},{4,20},{8,24},{12,28},{16,0},{20,4},{24,8},{28,12},{1,17},{... | collective-permute-start | bytes 1769480 | tf_op jit(solution)/shard_map/ppermute | solution.py:28
  406.8 9.8 %collective-permute-start.36 = (f32[384]{0:T(512)S(1)}, f32[384]{0:T(512)S(1)}, u32[]{:S(2)}, u32[]{:S(2)}) collective-permute-start(f32[384]{0:T(512)S(1)} %multiply_reduce_fusion), channel_id=1, source_target_pairs={{0,1},{1,0},{2,3},{3,2},{4,5},{5,4},{6,7},{7,6},{8,9},{9,8},{10,11... | collective-permute-start | bytes 4616 | tf_op jit(solution)/shard_map/ppermute | solution.py:28
  412.8 19.5 %collective-permute-start.38 = (bf16[768,1024]{1,0:T(8,128)(2,1)S(1)}, bf16[768,1024]{1,0:T(8,128)(2,1)S(1)}, u32[]{:S(2)}, u32[]{:S(2)}) collective-permute-start(bf16[768,1024]{1,0:T(8,128)(2,1)S(1)} %pad_maximum_fusion.8), channel_id=1, source_target_pairs={{0,4},{4,0},{8,12},{12,8},{16,20},{20,16},{24,28},{28,24},{1,5},{5... | collective-permute-start | bytes 4718600 | tf_op jit(solution)/shard_map/ppermute | solution.py:28
  416.6 3.7 collective-permute-start.37
  420.7 11.5 %collective-permute-start.40 = (bf16[384,1024]{1,0:T(8,128)(2,1)S(1)}, bf16[384,1024]{1,0:T(8,128)(2,1)S(1)}, u32[]{:S(2)}, u32[]{:S(2)}) collective-permute-start(bf16[384,1024]{1,0:T(8,128)(2,1)S(1)} %get-tuple-element.280), channel_id=1, source_target_pairs={{0,4},{4,0},{8,12},{12,8},{16,20},{20,16},{24,28},{28,24},{1,5},{5... | collective-permute-start | bytes 2359304 | tf_op jit(solution)/shard_map/ppermute | solution.py:28
  (33 other events, 145.2 us)

commit v16 on v15

--- a/solution.py
+++ b/solution.py
@@ -285,14 +285,13 @@
     expert_mine, expert_other = split_rows(expert_sum)
     send_low, send_high = gone(expert_mine, low), gone(expert_other, high)
     g_up_4, g_up_own = first_send(blocks_far(g_up)), first_send(blocks_own(g_up))
-    g_down_far, input_sum, send_low, send_high, *rest = fence(
-        g_down_far, input_sum, send_low, send_high, *g_down_own, *g_gate_4, *g_up_4, *g_up_own
+    got_low, got_high = swap(send_low, "tensor", low), swap(send_high, "tensor", high)
+    g_down_far, input_sum, *rest = fence(
+        g_down_far, input_sum, *g_down_own, *g_gate_4, *g_up_4, *g_up_own
     )
     g_down_own, rest = rest[:2], rest[2:]
     g_up_own = rest[2 + n_kept :]
-    g_gate_4, send_low, send_high, input_sum, *g_up_4 = fence(
-        done(*rest[:2]), send_low, send_high, input_sum, *rest[2 : 2 + n_kept]
-    )
+    g_gate_4, input_sum, *g_up_4 = fence(done(*rest[:2]), input_sum, *rest[2 : 2 + n_kept])
 
     def halves_of(own, other):
         both = beside(own, other)
@@ -312,8 +311,8 @@
 
     g_gate_far = z_far(g_gate_4)
     g_up_4 = shrink(*g_up_4)
-    expert_mine = kept(expert_mine, low, swap(send_low, "tensor", low))
-    expert_other = kept(expert_other, high, swap(send_high, "tensor", high))
+    expert_mine = kept(expert_mine, low, got_low)
+    expert_other = kept(expert_other, high, got_high)
     input_mine, input_other = split_rows(input_sum)
     merged = len(t_bits) == 2
     if merged:

time: 442 us -> 441 us (level)
  transfers between devices with their start and end apart: 41 -> 41, of which waited for: 20 -> 21; matrix products, arithmetic and copies ran while one was open for 35% -> 36% of each run, Pallas kernels for 0% -> 0%
where the time goes in v16:
time: 441 us; the launch traced here: 435 us
  waiting for transfers between devices  224 us (51%)
  matrix products  82 us (19%)
  other arithmetic  51 us (12%)
  starting transfers between devices  40.5 us (9%)
  local copies, waits for them, and re-layouts  34.9 us (8%)
    ppermute x41, waiting for transfers between devices, swap(): return lax.ppermute(value, axis, [(i, i ^ distance) for i in range(size)])  224 us
    dot_general x16, matrix products, dot(): lax.dot_general(left, right, (dims, ((), ())), preferred_element_type=F32)  82 us
    ppermute x41, starting transfers between devices, swap(): return lax.ppermute(value, axis, [(i, i ^ distance) for i in range(size)])  40.5 us
    concatenate x5, other arithmetic, cat(): return jnp.concatenate(values, axis=0)  13.6 us
  transfers between devices with their start and end apart: 41, of which 21 were waited for; matrix products, arithmetic and copies ran while one was open for 36% of the time, Pallas kernels for 0%

profile of v16, /device:TPU:0, one launch (start us, length us, event | category | flops | bytes accessed | tf_op | source)
XLA Modules:
  0.0 434.6 jit_solution(4382866430581814178)
XLA Ops:
  0.7 2.4 constant_dynamic-slice_fusion.18
  3.1 4.0 collective-permute-start
  9.7 6.0 %convolution_convert_fusion.5 = bf16[384,3072]{1,0:T(8,128)(2,1)} fusion(bf16[768,3072]{1,0:T(8,128)(2,1)} %param.7, s32[768]{0:T(1024)S(1)} %add_bitcast_fusion, pred[768]{0:T(1024)(128)(4,1)S(1)} %fusion.29), kind=kOutput, calls=%fused_computation.11 | convolution fusion | flops 1813708800 | bytes 7081728 | tf_op jit(solution)/shard_map/dot_general | solution.py:11
  15.6 4.2 multiply_convert_fusion
  25.5 16.4 %collective-permute-done = bf16[384,1024]{1,0:T(8,128)(2,1)} collective-permute-done((bf16[384,1024]{1,0:T(8,128)(2,1)}, bf16[384,1024]{1,0:T(8,128)(2,1)}, u32[]{:S(2)}, u32[]{:S(2)}) %collective-permute-start) | collective-permute-done | bytes 786464 | tf_op jit(solution)/shard_map/ppermute | solution.py:28
  44.0 2.4 collective-permute-start.6
  52.7 34.4 %collective-permute-done.6 = bf16[384,1024]{1,0:T(8,128)(2,1)S(1)} collective-permute-done((bf16[384,1024]{1,0:T(8,128)(2,1)}, bf16[384,1024]{1,0:T(8,128)(2,1)S(1)}, u32[]{:S(2)}, u32[]{:S(2)}) %collective-permute-start.6) | collective-permute-done | bytes 786464 | tf_op jit(solution)/shard_map/ppermute | solution.py:28
  87.1 10.2 %collective-permute-done.2 = bf16[768,768]{1,0:T(8,128)(2,1)} collective-permute-done((bf16[768,768]{1,0:T(8,128)(2,1)}, bf16[768,768]{1,0:T(8,128)(2,1)}, u32[]{:S(2)}, u32[]{:S(2)}) %collective-permute-start.2) | collective-permute-done | bytes 1179680 | tf_op jit(solution)/shard_map/ppermute | solution.py:28
  100.9 3.0 collective-permute-start.7
  103.9 2.3 pad_maximum_fusion.2
  108.0 2.1 broadcast_in_dim.67.clone.1
  111.1 37.0 %collective-permute-done.7 = bf16[768,512]{1,0:T(8,128)(2,1)S(1)} collective-permute-done((bf16[768,512]{1,0:T(8,128)(2,1)}, bf16[768,512]{1,0:T(8,128)(2,1)S(1)}, u32[]{:S(2)}, u32[]{:S(2)}) %collective-permute-start.7) | collective-permute-done | bytes 786464 | tf_op jit(solution)/shard_map/ppermute | solution.py:28
  148.2 3.7 collective-permute-done.9
  152.1 3.1 collective-permute-start.12
  155.8 2.4 bitcast_dynamic-update-slice_fusion.3
  158.2 2.5 broadcast_select_fusion.11
  160.7 2.6 broadcast_select_fusion.10
  165.2 3.0 collective-permute-done.14
  168.2 6.1 %pad_maximum_fusion = bf16[1536,3072]{1,0:T(8,128)(2,1)S(1)} fusion(bf16[384,3072]{1,0:T(8,128)(2,1)S(1)} %collective-permute-done.14, bf16[384,3072]{1,0:T(8,128)(2,1)} %collective-permute-done.3, bf16[384,768]{1,0:T(8,128)(2,1)S(1)} %get-tuple-element.227, bf16[384,768]{1,0:T(8,128)(2,1)S(1)} %get-tuple-element.226, ...), kind=kLoop, calls=%fused_computation | loop fusion | flops 66060288 | bytes 18874368 | tf_op jit(solution)/shard_map/concatenate | solution.py:48
  174.3 6.1 %pad_maximum_fusion.1 = bf16[1536,3072]{1,0:T(8,128)(2,1)S(1)} fusion(bf16[384,3072]{1,0:T(8,128)(2,1)S(1)} %collective-permute-done.15, bf16[384,3072]{1,0:T(8,128)(2,1)} %collective-permute-done.4, bf16[384,768]{1,0:T(8,128)(2,1)S(1)} %get-tuple-element.230, bf16[384,768]{1,0:T(8,128)(2,1)S(1)} %get-tuple-element.229, ...), kind=kLoop, calls=%fused_computation.1 | loop fusion | flops 66060288 | bytes 18874368 | tf_op jit(solution)/shard_map/concatenate | solution.py:48
  180.4 5.1 %fusion.33 = f32[1536,512]{1,0:T(8,128)S(1)} fusion(bf16[1536,3072]{1,0:T(8,128)(2,1)S(1)} %pad_maximum_fusion, bf16[3072,512]{1,0:T(8,128)(2,1)S(1)} %bitcast.90), kind=kOutput, calls=%fused_computation.186 | convolution fusion | flops 4831838208 | bytes 15728640 | tf_op jit(solution)/shard_map/dot_general | solution.py:11
  185.6 4.9 %collective-permute-done.12 = bf16[768,512]{1,0:T(8,128)(2,1)} collective-permute-done((bf16[768,512]{1,0:T(8,128)(2,1)}, bf16[768,512]{1,0:T(8,128)(2,1)}, u32[]{:S(2)}, u32[]{:S(2)}) %collective-permute-start.12) | collective-permute-done | bytes 786464 | tf_op jit(solution)/shard_map/ppermute | solution.py:28
  193.3 7.4 %multiply_convert_fusion.3 = (bf16[1536,512]{1,0:T(8,128)(2,1)S(1)}, f32[1536,512]{1,0:T(8,128)}) fusion(f32[1536,512]{1,0:T(8,128)S(1)} %fusion.33, bf16[1536,3072]{1,0:T(8,128)(2,1)S(1)} %pad_maximum_fusion, bf16[3072,512]{1,0:T(8,128)(2,1)S(1)} %bitcast.97), kind=kOutput, calls=%fused_computation.15 | convolution fusion | flops 4836556800 | bytes 20447232 | tf_op jit(solution)/shard_map/dot_general | solution.py:11
  200.7 5.5 %convolution_convert_fusion.3 = bf16[3072,512]{1,0:T(8,128)(2,1)S(1)} fusion(bf16[1536,3072]{1,0:T(8,128)(2,1)S(1)} %pad_maximum_fusion.1, bf16[1536,512]{1,0:T(8,128)(2,1)S(1)} %get-tuple-element.168), kind=kOutput, calls=%fused_computation.9 | convolution fusion | flops 4833411072 | bytes 14155776 | tf_op jit(solution)/shard_map/dot_general | solution.py:11
  206.2 2.1 bitcast_dynamic-update-slice_fusion.1
  213.8 10.0 %multiply_convert_fusion.1 = (bf16[1536,512]{1,0:T(8,128)(2,1)S(1)}, bf16[1536,512]{1,0:T(8,128)(2,1)}) fusion(f32[1536,512]{1,0:T(8,128)} %copy-done.39, f32[1536,512]{1,0:T(8,128)} %get-tuple-element.152, bf16[1536,3072]{1,0:T(8,128)(2,1)S(1)} %pad_maximum_fusion.1, bf16[3072,512]{1,0:T(8,128)(2,1)} %bitcast.24), kind=kOutput, calls=%fused_computation.13 | convolution fusion | flops 4842061824 | bytes 22020096 | tf_op jit(solution)/shard_map/dot_general | solution.py:11
  223.8 7.4 %convolution_convert_fusion = bf16[768,3072]{1,0:T(8,128)(2,1)} fusion(bf16[3072,512]{1,0:T(8,128)(2,1)} %bitcast.24, bf16[1536,512]{1,0:T(8,128)(2,1)} %copy-done.37), kind=kOutput, calls=%fused_computation.5 | convolution fusion | flops 2418278400 | bytes 8650752 | tf_op jit(solution)/shard_map/dot_general | solution.py:11
  233.5 2.6 fusion.13
  236.2 5.6 %add_convert_fusion.2 = bf16[768,3072]{1,0:T(8,128)(2,1)} fusion(f32[768,3072]{1,0:T(8,128)S(1)} %fusion.13, bf16[3072,512]{1,0:T(8,128)(2,1)S(1)} %bitcast.91, bf16[1536,512]{1,0:T(8,128)(2,1)} %get-tuple-element.156), kind=kOutput, calls=%fused_computation.4 | convolution fusion | flops 2420637696 | bytes 18087936 | tf_op jit(solution)/shard_map/dot_general | solution.py:11
  242.4 6.9 %convolution_convert_fusion.2 = bf16[3072,512]{1,0:T(8,128)(2,1)S(1)} fusion(bf16[1536,3072]{1,0:T(8,128)(2,1)S(1)} %pad_maximum_fusion, bf16[1536,512]{1,0:T(8,128)(2,1)} %get-tuple-element.156), kind=kOutput, calls=%fused_computation.8 | convolution fusion | flops 4833411072 | bytes 14155776 | tf_op jit(solution)/shard_map/dot_general | solution.py:11
  252.7 5.7 %convolution_convert_fusion.1 = bf16[3072,512]{1,0:T(8,128)(2,1)S(1)} fusion(bf16[1536,3072]{1,0:T(8,128)(2,1)S(1)} %pad_maximum_fusion, bf16[1536,512]{1,0:T(8,128)(2,1)S(1)} %copy-done.36), kind=kOutput, calls=%fused_computation.7 | convolution fusion | flops 4833411072 | bytes 14155776 | tf_op jit(solution)/shard_map/dot_general | solution.py:11
  258.4 1.8 dynamic-slice_bitcast_fusion.2
  260.8 2.6 fusion.18
  263.4 2.6 fusion.16
  266.1 5.5 %add_convert_fusion = bf16[768,3072]{1,0:T(8,128)(2,1)S(1)} fusion(bf16[768,3072]{1,0:T(8,128)(2,1)} %collective-permute-done.24, bf16[3072,512]{1,0:T(8,128)(2,1)} %bitcast.24, bf16[1536,512]{1,0:T(8,128)(2,1)S(1)} %copy-done.38), kind=kOutput, calls=%fused_computation.2 | convolution fusion | flops 2422996992 | bytes 13369344 | tf_op jit(solution)/shard_map/dot_general | solution.py:11
  278.4 4.7 %add_convert_fusion.1 = bf16[768,3072]{1,0:T(8,128)(2,1)S(1)} fusion(bf16[768,3072]{1,0:T(8,128)(2,1)} %collective-permute-done.20, f32[768,3072]{1,0:T(8,128)S(1)} %fusion.18, f32[768,3072]{1,0:T(8,128)S(1)} %fusion.16), kind=kLoop, calls=%fused_computation.3 | loop fusion | flops 9437184 | bytes 28311552 | tf_op jit(solution)/shard_map/convert_element_type | solution.py:257
  283.1 12.6 %collective-permute-done.22 = bf16[768,512]{1,0:T(8,128)(2,1)} collective-permute-done((bf16[768,512]{1,0:T(8,128)(2,1)}, bf16[768,512]{1,0:T(8,128)(2,1)}, u32[]{:S(2)}, u32[]{:S(2)}) %collective-permute-start.22) | collective-permute-done | bytes 786464 | tf_op jit(solution)/shard_map/ppermute | solution.py:28
  299.5 3.6 collective-permute-done.25
  307.0 26.1 %collective-permute-done.23 = bf16[768,512]{1,0:T(8,128)(2,1)S(1)} collective-permute-done((bf16[768,512]{1,0:T(8,128)(2,1)S(1)}, bf16[768,512]{1,0:T(8,128)(2,1)S(1)}, u32[]{:S(2)}, u32[]{:S(2)}) %collective-permute-start.23) | collective-permute-done | bytes 786464 | tf_op jit(solution)/shard_map/ppermute | solution.py:28
  335.9 2.0 collective-permute-start.31
  338.0 35.9 %collective-permute-done.29 = bf16[384,2304]{1,0:T(8,128)(2,1)S(1)} collective-permute-done((bf16[384,2304]{1,0:T(8,128)(2,1)S(1)}, bf16[384,2304]{1,0:T(8,128)(2,1)S(1)}, u32[]{:S(2)}, u32[]{:S(2)}) %collective-permute-start.29) | collective-permute-done | bytes 1769504 | tf_op jit(solution)/shard_map/ppermute | solution.py:28
  378.8 2.1 collective-permute-start.39
  380.9 10.4 %collective-permute-done.33 = bf16[384,768]{1,0:T(8,128)(2,1)} collective-permute-done((bf16[384,768]{1,0:T(8,128)(2,1)}, bf16[384,768]{1,0:T(8,128)(2,1)}, u32[]{:S(2)}, u32[]{:S(2)}) %collective-permute-start.33) | collective-permute-done | bytes 589856 | tf_op jit(solution)/shard_map/ppermute | solution.py:28
  393.8 11.2 %collective-permute-done.32 = bf16[384,768]{1,0:T(8,128)(2,1)} collective-permute-done((bf16[384,768]{1,0:T(8,128)(2,1)}, bf16[384,768]{1,0:T(8,128)(2,1)}, u32[]{:S(2)}, u32[]{:S(2)}) %collective-permute-start.32) | collective-permute-done | bytes 589856 | tf_op jit(solution)/shard_map/ppermute | solution.py:28
  413.5 3.0 convolution_convert_fusion.7
  417.6 2.9 collective-permute-done.37
  422.1 7.9 %collective-permute-done.35 = bf16[384,768]{1,0:T(8,128)(2,1)S(1)} collective-permute-done((bf16[384,768]{1,0:T(8,128)(2,1)S(1)}, bf16[384,768]{1,0:T(8,128)(2,1)S(1)}, u32[]{:S(2)}, u32[]{:S(2)}) %collective-permute-start.35) | collective-permute-done | bytes 589856 | tf_op jit(solution)/shard_map/ppermute | solution.py:28
  430.0 1.9 convolution_convert_fusion.6
  (224 shorter events, 78.6 us)
Async XLA Ops:
  3.1 38.8 %collective-permute-start = (bf16[384,1024]{1,0:T(8,128)(2,1)}, bf16[384,1024]{1,0:T(8,128)(2,1)}, u32[]{:S(2)}, u32[]{:S(2)}) collective-permute-start(bf16[384,1024]{1,0:T(8,128)(2,1)} %get-tuple-element.291), channel_id=1, source_target_pairs={{0,16},{4,20},{8,24},{12,28},{16,0},{20,4},{24,8},{28,12},{1,17},{... | collective-permute-start | bytes 2359304 | tf_op jit(solution)/shard_map/ppermute | solution.py:28
  7.1 34.8 %collective-permute-start.1 = (bf16[384,1024]{1,0:T(8,128)(2,1)S(1)}, bf16[384,1024]{1,0:T(8,128)(2,1)}, u32[]{:S(2)}, u32[]{:S(2)}) collective-permute-start(bf16[384,1024]{1,0:T(8,128)(2,1)S(1)} %get-tuple-element.118), channel_id=1, source_target_pairs={{0,8},{4,12},{8,0},{12,4},{16,24},{20,28},{24,16},{28,20},{1,9},{5... | collective-permute-start | bytes 2359304 | tf_op jit(solution)/shard_map/ppermute | solution.py:28
  25.4 23.7 %copy-start.17 = (bf16[384,512]{1,0:T(8,128)(2,1)S(1)}, bf16[384,512]{1,0:T(8,128)(2,1)}, u32[]{:S(2)}) copy-start(bf16[384,512]{1,0:T(8,128)(2,1)} %get-tuple-element.281) | copy-start | bytes 1179652
  41.9 5.8 %collective-permute-start.5 = (bf16[768,1024]{1,0:T(8,128)(2,1)S(1)}, bf16[768,1024]{1,0:T(8,128)(2,1)}, u32[]{:S(2)}, u32[]{:S(2)}) collective-permute-start(bf16[768,1024]{1,0:T(8,128)(2,1)S(1)} %maximum_maximum_fusion), channel_id=1, source_target_pairs={{0,4},{4,0},{8,12},{12,8},{16,20},{20,16},{24,28},{28,24},{1,5},{5... | collective-permute-start | bytes 4718600 | tf_op jit(solution)/shard_map/ppermute | solution.py:28
  41.9 55.4 %collective-permute-start.3 = (bf16[384,3072]{1,0:T(8,128)(2,1)}, bf16[384,3072]{1,0:T(8,128)(2,1)}, u32[]{:S(2)}, u32[]{:S(2)}) collective-permute-start(bf16[384,3072]{1,0:T(8,128)(2,1)} %convolution_convert_fusion.5), channel_id=1, source_target_pairs={{0,4},{4,0},{8,12},{12,8},{16,20},{20,16},{24,28},{28,24},{1,5},{5... | collective-permute-start | bytes 7077896 | tf_op jit(solution)/shard_map/ppermute | solution.py:28
  42.4 54.9 %collective-permute-start.4 = (bf16[384,3072]{1,0:T(8,128)(2,1)}, bf16[384,3072]{1,0:T(8,128)(2,1)}, u32[]{:S(2)}, u32[]{:S(2)}) collective-permute-start(bf16[384,3072]{1,0:T(8,128)(2,1)} %get-tuple-element.114), channel_id=1, source_target_pairs={{0,4},{4,0},{8,12},{12,8},{16,20},{20,16},{24,28},{28,24},{1,5},{5... | collective-permute-start | bytes 7077896 | tf_op jit(solution)/shard_map/ppermute | solution.py:28
  42.4 54.9 %collective-permute-start.2 = (bf16[768,768]{1,0:T(8,128)(2,1)}, bf16[768,768]{1,0:T(8,128)(2,1)}, u32[]{:S(2)}, u32[]{:S(2)}) collective-permute-start(bf16[768,768]{1,0:T(8,128)(2,1)} %pad_maximum_fusion.9), channel_id=1, source_target_pairs={{0,16},{4,20},{8,24},{12,28},{16,0},{20,4},{24,8},{28,12},{1,17},{... | collective-permute-start | bytes 3538952 | tf_op jit(solution)/shard_map/ppermute | solution.py:28
  44.0 43.1 %collective-permute-start.6 = (bf16[384,1024]{1,0:T(8,128)(2,1)}, bf16[384,1024]{1,0:T(8,128)(2,1)S(1)}, u32[]{:S(2)}, u32[]{:S(2)}) collective-permute-start(bf16[384,1024]{1,0:T(8,128)(2,1)} %collective-permute-done), channel_id=1, source_target_pairs={{0,8},{4,12},{8,0},{12,4},{16,24},{20,28},{24,16},{28,20},{1,9},{5... | collective-permute-start | bytes 2359304 | tf_op jit(solution)/shard_map/ppermute | solution.py:28
  97.3 54.6 %collective-permute-start.11 = (bf16[768,1024]{1,0:T(8,128)(2,1)S(1)}, bf16[768,1024]{1,0:T(8,128)(2,1)}, u32[]{:S(2)}, u32[]{:S(2)}) collective-permute-start(bf16[768,1024]{1,0:T(8,128)(2,1)S(1)} %pad_maximum_fusion.7), channel_id=1, source_target_pairs={{0,8},{4,12},{8,0},{12,4},{16,24},{20,28},{24,16},{28,20},{1,9},{5... | collective-permute-start | bytes 4718600 | tf_op jit(solution)/shard_map/ppermute | solution.py:28
  97.4 50.8 %collective-permute-start.8 = (bf16[768,768]{1,0:T(8,128)(2,1)}, bf16[768,768]{1,0:T(8,128)(2,1)}, u32[]{:S(2)}, u32[]{:S(2)}) collective-permute-start(bf16[768,768]{1,0:T(8,128)(2,1)} %collective-permute-done.2), channel_id=1, source_target_pairs={{0,1},{1,0},{2,3},{3,2},{4,5},{5,4},{6,7},{7,6},{8,9},{9,8},{10,11... | collective-permute-start | bytes 3538952 | tf_op jit(solution)/shard_map/ppermute | solution.py:28
  99.0 52.9 %collective-permute-start.9 = (bf16[768,768]{1,0:T(8,128)(2,1)}, bf16[768,768]{1,0:T(8,128)(2,1)}, u32[]{:S(2)}, u32[]{:S(2)}) collective-permute-start(bf16[768,768]{1,0:T(8,128)(2,1)} %collective-permute-done.2), channel_id=1, source_target_pairs={{0,2},{1,3},{2,0},{3,1},{4,6},{5,7},{6,4},{7,5},{8,10},{9,11},{10,... | collective-permute-start | bytes 3538952 | tf_op jit(solution)/shard_map/ppermute | solution.py:28
  100.5 51.4 %collective-permute-start.10 = (bf16[768,768]{1,0:T(8,128)(2,1)}, bf16[768,768]{1,0:T(8,128)(2,1)}, u32[]{:S(2)}, u32[]{:S(2)}) collective-permute-start(bf16[768,768]{1,0:T(8,128)(2,1)} %collective-permute-done.2), channel_id=1, source_target_pairs={{0,3},{1,2},{2,1},{3,0},{4,7},{5,6},{6,5},{7,4},{8,11},{9,10},{10,... | collective-permute-start | bytes 3538952 | tf_op jit(solution)/shard_map/ppermute | solution.py:28
  100.9 47.2 %collective-permute-start.7 = (bf16[768,512]{1,0:T(8,128)(2,1)}, bf16[768,512]{1,0:T(8,128)(2,1)S(1)}, u32[]{:S(2)}, u32[]{:S(2)}) collective-permute-start(bf16[768,512]{1,0:T(8,128)(2,1)} %maximum_select_fusion.2), channel_id=1, source_target_pairs={{0,16},{4,20},{8,24},{12,28},{16,0},{20,4},{24,8},{28,12},{1,17},{... | collective-permute-start | bytes 2359304 | tf_op jit(solution)/shard_map/ppermute | solution.py:28
  151.9 6.3 %collective-permute-start.13 = (bf16[4,384,512]{2,1,0:T(8,128)(2,1)}, bf16[4,384,512]{2,1,0:T(8,128)(2,1)S(1)}, u32[]{:S(2)}, u32[]{:S(2)}) collective-permute-start(bf16[4,384,512]{2,1,0:T(8,128)(2,1)} %get-tuple-element.126), channel_id=1, source_target_pairs={{0,4},{4,0},{8,12},{12,8},{16,20},{20,16},{24,28},{28,24},{1,5},{5... | collective-permute-start | bytes 4718600 | tf_op jit(solution)/shard_map/ppermute | solution.py:28
  152.1 38.4 %collective-permute-start.12 = (bf16[768,512]{1,0:T(8,128)(2,1)}, bf16[768,512]{1,0:T(8,128)(2,1)}, u32[]{:S(2)}, u32[]{:S(2)}) collective-permute-start(bf16[768,512]{1,0:T(8,128)(2,1)} %maximum_select_fusion.3), channel_id=1, source_target_pairs={{0,16},{4,20},{8,24},{12,28},{16,0},{20,4},{24,8},{28,12},{1,17},{... | collective-permute-start | bytes 2359304 | tf_op jit(solution)/shard_map/ppermute | solution.py:28
  155.1 35.8 %collective-permute-start.16 = (bf16[768,512]{1,0:T(8,128)(2,1)}, bf16[768,512]{1,0:T(8,128)(2,1)}, u32[]{:S(2)}, u32[]{:S(2)}) collective-permute-start(bf16[768,512]{1,0:T(8,128)(2,1)} %copy-done.21), channel_id=1, source_target_pairs={{0,8},{4,12},{8,0},{12,4},{16,24},{20,28},{24,16},{28,20},{1,9},{5... | collective-permute-start | bytes 2359304 | tf_op jit(solution)/shard_map/ppermute | solution.py:28
  163.6 4.6 %collective-permute-start.14 = (bf16[384,3072]{1,0:T(8,128)(2,1)S(1)}, bf16[384,3072]{1,0:T(8,128)(2,1)S(1)}, u32[]{:S(2)}, u32[]{:S(2)}) collective-permute-start(bf16[384,3072]{1,0:T(8,128)(2,1)S(1)} %pad_maximum_fusion.3), channel_id=1, source_target_pairs={{0,4},{4,0},{8,12},{12,8},{16,20},{20,16},{24,28},{28,24},{1,5},{5... | collective-permute-start | bytes 7077896 | tf_op jit(solution)/shard_map/ppermute | solution.py:28
  164.8 9.5 %collective-permute-start.15 = (bf16[384,3072]{1,0:T(8,128)(2,1)S(1)}, bf16[384,3072]{1,0:T(8,128)(2,1)S(1)}, u32[]{:S(2)}, u32[]{:S(2)}) collective-permute-start(bf16[384,3072]{1,0:T(8,128)(2,1)S(1)} %pad_maximum_fusion.4), channel_id=1, source_target_pairs={{0,4},{4,0},{8,12},{12,8},{16,20},{20,16},{24,28},{28,24},{1,5},{5... | collective-permute-start | bytes 7077896 | tf_op jit(solution)/shard_map/ppermute | solution.py:28
  185.6 15.2 %copy-start.39 = (f32[1536,512]{1,0:T(8,128)}, f32[1536,512]{1,0:T(8,128)S(1)}, u32[]{:S(2)}) copy-start(f32[1536,512]{1,0:T(8,128)S(1)} %fusion.33) | copy-start | bytes 9437188
  190.9 18.9 %collective-permute-start.17 = (bf16[768,512]{1,0:T(8,128)(2,1)}, bf16[768,512]{1,0:T(8,128)(2,1)S(1)}, u32[]{:S(2)}, u32[]{:S(2)}) collective-permute-start(bf16[768,512]{1,0:T(8,128)(2,1)} %collective-permute-done.12), channel_id=1, source_target_pairs={{0,8},{4,12},{8,0},{12,4},{16,24},{20,28},{24,16},{28,20},{1,9},{5... | collective-permute-start | bytes 2359304 | tf_op jit(solution)/shard_map/ppermute | solution.py:28
  193.3 40.2 %copy-start.6 = (bf16[4,768,512]{2,1,0:T(8,128)(2,1)}, bf16[4,768,512]{2,1,0:T(8,128)(2,1)S(1)}, u32[]{:S(2)}) copy-start(bf16[4,768,512]{2,1,0:T(8,128)(2,1)S(1)} %bitcast_dynamic-update-slice_fusion.2) | copy-start | bytes 9437188
  211.3 20.0 %collective-permute-start.18 = (bf16[768,512]{1,0:T(8,128)(2,1)}, bf16[768,512]{1,0:T(8,128)(2,1)S(1)}, u32[]{:S(2)}, u32[]{:S(2)}) collective-permute-start(bf16[768,512]{1,0:T(8,128)(2,1)} %get-tuple-element.246), channel_id=1, source_target_pairs={{0,8},{4,12},{8,0},{12,4},{16,24},{20,28},{24,16},{28,20},{1,9},{5... | collective-permute-start | bytes 2359304 | tf_op jit(solution)/shard_map/ppermute | solution.py:28
  231.2 34.8 %collective-permute-start.24 = (bf16[768,3072]{1,0:T(8,128)(2,1)}, bf16[768,3072]{1,0:T(8,128)(2,1)}, u32[]{:S(2)}, u32[]{:S(2)}) collective-permute-start(bf16[768,3072]{1,0:T(8,128)(2,1)} %convolution_convert_fusion), channel_id=1, source_target_pairs={{0,4},{4,0},{8,12},{12,8},{16,20},{20,16},{24,28},{28,24},{1,5},{5... | collective-permute-start | bytes 14155784 | tf_op jit(solution)/shard_map/ppermute | solution.py:28
  232.4 50.7 %collective-permute-start.19 = (bf16[768,512]{1,0:T(8,128)(2,1)}, bf16[768,512]{1,0:T(8,128)(2,1)}, u32[]{:S(2)}, u32[]{:S(2)}) collective-permute-start(bf16[768,512]{1,0:T(8,128)(2,1)} %add_convert_fusion.8), channel_id=1, source_target_pairs={{0,16},{4,20},{8,24},{12,28},{16,0},{20,4},{24,8},{28,12},{1,17},{... | collective-permute-start | bytes 2359304 | tf_op jit(solution)/shard_map/ppermute | solution.py:28
  241.8 35.7 %collective-permute-start.20 = (bf16[768,3072]{1,0:T(8,128)(2,1)}, bf16[768,3072]{1,0:T(8,128)(2,1)}, u32[]{:S(2)}, u32[]{:S(2)}) collective-permute-start(bf16[768,3072]{1,0:T(8,128)(2,1)} %add_convert_fusion.2), channel_id=1, source_target_pairs={{0,4},{4,0},{8,12},{12,8},{16,20},{20,16},{24,28},{28,24},{1,5},{5... | collective-permute-start | bytes 14155784 | tf_op jit(solution)/shard_map/ppermute | solution.py:28
  242.0 41.1 %collective-permute-start.21 = (bf16[768,512]{1,0:T(8,128)(2,1)}, bf16[768,512]{1,0:T(8,128)(2,1)}, u32[]{:S(2)}, u32[]{:S(2)}) collective-permute-start(bf16[768,512]{1,0:T(8,128)(2,1)} %get-tuple-element.161), channel_id=1, source_target_pairs={{0,8},{4,12},{8,0},{12,4},{16,24},{20,28},{24,16},{28,20},{1,9},{5... | collective-permute-start | bytes 2359304 | tf_op jit(solution)/shard_map/ppermute | solution.py:28
  251.1 44.5 %collective-permute-start.22 = (bf16[768,512]{1,0:T(8,128)(2,1)}, bf16[768,512]{1,0:T(8,128)(2,1)}, u32[]{:S(2)}, u32[]{:S(2)}) collective-permute-start(bf16[768,512]{1,0:T(8,128)(2,1)} %get-tuple-element.238), channel_id=1, source_target_pairs={{0,8},{4,12},{8,0},{12,4},{16,24},{20,28},{24,16},{28,20},{1,9},{5... | collective-permute-start | bytes 2359304 | tf_op jit(solution)/shard_map/ppermute | solution.py:28
  275.2 27.9 %collective-permute-start.25 = (bf16[384,1536]{1,0:T(8,128)(2,1)}, bf16[384,1536]{1,0:T(8,128)(2,1)}, u32[]{:S(2)}, u32[]{:S(2)}) collective-permute-start(bf16[384,1536]{1,0:T(8,128)(2,1)} %pad_maximum_fusion.10), channel_id=1, source_target_pairs={{0,1},{1,0},{2,3},{3,2},{4,5},{5,4},{6,7},{7,6},{8,9},{9,8},{10,11... | collective-permute-start | bytes 3538952 | tf_op jit(solution)/shard_map/ppermute | solution.py:28
  277.5 27.6 %collective-permute-start.26 = (bf16[384,1536]{1,0:T(8,128)(2,1)}, bf16[384,1536]{1,0:T(8,128)(2,1)}, u32[]{:S(2)}, u32[]{:S(2)}) collective-permute-start(bf16[384,1536]{1,0:T(8,128)(2,1)} %pad_maximum_fusion.11), channel_id=1, source_target_pairs={{0,2},{1,3},{2,0},{3,1},{4,6},{5,7},{6,4},{7,5},{8,10},{9,11},{10,... | collective-permute-start | bytes 3538952 | tf_op jit(solution)/shard_map/ppermute | solution.py:28
  283.1 14.3 %copy-start.24 = (bf16[768,512]{1,0:T(8,128)(2,1)S(1)}, bf16[768,512]{1,0:T(8,128)(2,1)}, u32[]{:S(2)}) copy-start(bf16[768,512]{1,0:T(8,128)(2,1)} %get-tuple-element.171) | copy-start | bytes 2359300
  297.2 35.8 %collective-permute-start.23 = (bf16[768,512]{1,0:T(8,128)(2,1)S(1)}, bf16[768,512]{1,0:T(8,128)(2,1)S(1)}, u32[]{:S(2)}, u32[]{:S(2)}) collective-permute-start(bf16[768,512]{1,0:T(8,128)(2,1)S(1)} %add_convert_fusion.7), channel_id=1, source_target_pairs={{0,16},{4,20},{8,24},{12,28},{16,0},{20,4},{24,8},{28,12},{1,17},{... | collective-permute-start | bytes 2359304 | tf_op jit(solution)/shard_map/ppermute | solution.py:28
  297.3 35.8 %collective-permute-start.27 = (bf16[768,512]{1,0:T(8,128)(2,1)S(1)}, bf16[768,512]{1,0:T(8,128)(2,1)S(1)}, u32[]{:S(2)}, u32[]{:S(2)}) collective-permute-start(bf16[768,512]{1,0:T(8,128)(2,1)S(1)} %copy-done.24), channel_id=1, source_target_pairs={{0,8},{4,12},{8,0},{12,4},{16,24},{20,28},{24,16},{28,20},{1,9},{5... | collective-permute-start | bytes 2359304 | tf_op jit(solution)/shard_map/ppermute | solution.py:28
  306.9 26.3 %copy-start.11 = (bf16[768,512]{1,0:T(8,128)(2,1)S(1)}, bf16[768,512]{1,0:T(8,128)(2,1)}, u32[]{:S(2)}) copy-start(bf16[768,512]{1,0:T(8,128)(2,1)} %get-tuple-element.172) | copy-start | bytes 2359300
  306.9 29.1 %copy-start.23 = (bf16[768,512]{1,0:T(8,128)(2,1)S(1)}, bf16[768,512]{1,0:T(8,128)(2,1)}, u32[]{:S(2)}) copy-start(bf16[768,512]{1,0:T(8,128)(2,1)} %get-tuple-element.190) | copy-start | bytes 2359300
  333.4 40.4 %collective-permute-start.29 = (bf16[384,2304]{1,0:T(8,128)(2,1)S(1)}, bf16[384,2304]{1,0:T(8,128)(2,1)S(1)}, u32[]{:S(2)}, u32[]{:S(2)}) collective-permute-start(bf16[384,2304]{1,0:T(8,128)(2,1)S(1)} %pad_maximum_fusion.6), channel_id=1, source_target_pairs={{0,2},{1,3},{2,0},{3,1},{4,6},{5,7},{6,4},{7,5},{8,10},{9,11},{10,... | collective-permute-start | bytes 5308424 | tf_op jit(solution)/shard_map/ppermute | solution.py:28
  335.0 40.2 %collective-permute-start.30 = (bf16[384,2304]{1,0:T(8,128)(2,1)S(1)}, bf16[384,2304]{1,0:T(8,128)(2,1)S(1)}, u32[]{:S(2)}, u32[]{:S(2)}) collective-permute-start(bf16[384,2304]{1,0:T(8,128)(2,1)S(1)} %pad_maximum_fusion.5), channel_id=1, source_target_pairs={{0,1},{1,0},{2,3},{3,2},{4,5},{5,4},{6,7},{7,6},{8,9},{9,8},{10,11... | collective-permute-start | bytes 5308424 | tf_op jit(solution)/shard_map/ppermute | solution.py:28
  335.5 41.2 %collective-permute-start.28 = (bf16[768,512]{1,0:T(8,128)(2,1)S(1)}, bf16[768,512]{1,0:T(8,128)(2,1)S(1)}, u32[]{:S(2)}, u32[]{:S(2)}) collective-permute-start(bf16[768,512]{1,0:T(8,128)(2,1)S(1)} %add_convert_fusion.6), channel_id=1, source_target_pairs={{0,16},{4,20},{8,24},{12,28},{16,0},{20,4},{24,8},{28,12},{1,17},{... | collective-permute-start | bytes 2359304 | tf_op jit(solution)/shard_map/ppermute | solution.py:28
  335.9 40.8 %collective-permute-start.31 = (bf16[768,512]{1,0:T(8,128)(2,1)S(1)}, bf16[768,512]{1,0:T(8,128)(2,1)}, u32[]{:S(2)}, u32[]{:S(2)}) collective-permute-start(bf16[768,512]{1,0:T(8,128)(2,1)S(1)} %copy-done.23), channel_id=1, source_target_pairs={{0,8},{4,12},{8,0},{12,4},{16,24},{20,28},{24,16},{28,20},{1,9},{5... | collective-permute-start | bytes 2359304 | tf_op jit(solution)/shard_map/ppermute | solution.py:28
  376.7 14.5 %collective-permute-start.33 = (bf16[384,768]{1,0:T(8,128)(2,1)}, bf16[384,768]{1,0:T(8,128)(2,1)}, u32[]{:S(2)}, u32[]{:S(2)}) collective-permute-start(bf16[384,768]{1,0:T(8,128)(2,1)} %get-tuple-element.198), channel_id=1, source_target_pairs={{0,2},{1,3},{2,0},{3,1},{4,6},{5,7},{6,4},{7,5},{8,10},{9,11},{10,... | collective-permute-start | bytes 1769480 | tf_op jit(solution)/shard_map/ppermute | solution.py:28
  378.3 14.3 %collective-permute-start.34 = (bf16[384,768]{1,0:T(8,128)(2,1)}, bf16[384,768]{1,0:T(8,128)(2,1)}, u32[]{:S(2)}, u32[]{:S(2)}) collective-permute-start(bf16[384,768]{1,0:T(8,128)(2,1)} %get-tuple-element.200), channel_id=1, source_target_pairs={{0,1},{1,0},{2,3},{3,2},{4,5},{5,4},{6,7},{7,6},{8,9},{9,8},{10,11... | collective-permute-start | bytes 1769480 | tf_op jit(solution)/shard_map/ppermute | solution.py:28
  378.8 26.2 %collective-permute-start.32 = (bf16[384,768]{1,0:T(8,128)(2,1)}, bf16[384,768]{1,0:T(8,128)(2,1)}, u32[]{:S(2)}, u32[]{:S(2)}) collective-permute-start(bf16[384,768]{1,0:T(8,128)(2,1)} %get-tuple-element.196), channel_id=1, source_target_pairs={{0,16},{4,20},{8,24},{12,28},{16,0},{20,4},{24,8},{28,12},{1,17},{... | collective-permute-start | bytes 1769480 | tf_op jit(solution)/shard_map/ppermute | solution.py:28
  378.8 28.7 %copy-start.8 = (bf16[768,512]{1,0:T(8,128)(2,1)S(1)}, bf16[768,512]{1,0:T(8,128)(2,1)}, u32[]{:S(2)}) copy-start(bf16[768,512]{1,0:T(8,128)(2,1)} %get-tuple-element.212) | copy-start | bytes 2359300
  378.8 41.7 %collective-permute-start.39 = (bf16[768,512]{1,0:T(8,128)(2,1)}, bf16[768,512]{1,0:T(8,128)(2,1)S(1)}, u32[]{:S(2)}, u32[]{:S(2)}) collective-permute-start(bf16[768,512]{1,0:T(8,128)(2,1)} %get-tuple-element.216), channel_id=1, source_target_pairs={{0,8},{4,12},{8,0},{12,4},{16,24},{20,28},{24,16},{28,20},{1,9},{5... | collective-permute-start | bytes 2359304 | tf_op jit(solution)/shard_map/ppermute | solution.py:28
  393.7 36.3 %collective-permute-start.35 = (bf16[384,768]{1,0:T(8,128)(2,1)S(1)}, bf16[384,768]{1,0:T(8,128)(2,1)S(1)}, u32[]{:S(2)}, u32[]{:S(2)}) collective-permute-start(bf16[384,768]{1,0:T(8,128)(2,1)S(1)} %add_convert_fusion.10), channel_id=1, source_target_pairs={{0,16},{4,20},{8,24},{12,28},{16,0},{20,4},{24,8},{28,12},{1,17},{... | collective-permute-start | bytes 1769480 | tf_op jit(solution)/shard_map/ppermute | solution.py:28
  406.6 10.2 %collective-permute-start.36 = (f32[384]{0:T(512)S(1)}, f32[384]{0:T(512)S(1)}, u32[]{:S(2)}, u32[]{:S(2)}) collective-permute-start(f32[384]{0:T(512)S(1)} %multiply_reduce_fusion), channel_id=1, source_target_pairs={{0,1},{1,0},{2,3},{3,2},{4,5},{5,4},{6,7},{7,6},{8,9},{9,8},{10,11... | collective-permute-start | bytes 4616 | tf_op jit(solution)/shard_map/ppermute | solution.py:28
  413.0 19.0 %collective-permute-start.38 = (bf16[768,1024]{1,0:T(8,128)(2,1)S(1)}, bf16[768,1024]{1,0:T(8,128)(2,1)S(1)}, u32[]{:S(2)}, u32[]{:S(2)}) collective-permute-start(bf16[768,1024]{1,0:T(8,128)(2,1)S(1)} %pad_maximum_fusion.8), channel_id=1, source_target_pairs={{0,4},{4,0},{8,12},{12,8},{16,20},{20,16},{24,28},{28,24},{1,5},{5... | collective-permute-start | bytes 4718600 | tf_op jit(solution)/shard_map/ppermute | solution.py:28
  416.8 3.7 collective-permute-start.37
  420.9 11.0 %collective-permute-start.40 = (bf16[384,1024]{1,0:T(8,128)(2,1)S(1)}, bf16[384,1024]{1,0:T(8,128)(2,1)S(1)}, u32[]{:S(2)}, u32[]{:S(2)}) collective-permute-start(bf16[384,1024]{1,0:T(8,128)(2,1)S(1)} %get-tuple-element.272), channel_id=1, source_target_pairs={{0,4},{4,0},{8,12},{12,8},{16,20},{20,16},{24,28},{28,24},{1,5},{5... | collective-permute-start | bytes 2359304 | tf_op jit(solution)/shard_map/ppermute | solution.py:28
  (33 other events, 130.1 us)
